TPU v7x, 256 devices: a whole 4x4x8 slice. The times are simulated.
256 devices in a mesh: gx: 16 (over z, core), gy: 16 (over y, x).
Axes of the slice: x: 4, y: 4, z: 8, core: 2. Of those that a mesh axis runs over, the one named last changes fastest.
Arguments:
- right_side: float32 [2, 4096, 8192], P(None, 'gy', 'gx'), may hold values from -16 to 16
- coefficient: float32 [2, 4096, 8192], P(None, 'gy', 'gx'), may hold values from 0.2 to 5
- strength_table: float32 [35], replicated, may hold values from 0.3 to 3
- layer_entry: int32 [2], replicated, may hold values from 0 to 34
- shifts: int32 [6, 2, 2], replicated, may hold values from -32 to 32, as said below
Outputs:
- solution_field: float32 [2, 4096, 8192], P(None, 'gy', 'gx')
- residual: float32 [2, 4096, 8192], P(None, 'gy', 'gx')
Inputs may be any that keep to these rules, and one draw needn't show every extreme that they name: `shifts`: every entry lies in -32 to 32; both ends are reached.
All inputs are finite; a program needn't handle non-finite values.
Results may differ from a plain program's by a relative error of at most 0.0003.
Values sent between devices are 32-bit elements; how exact they have to be, the bound alone decides.
No kernel may reach another device: no remote copies, remote signals or barrier semaphores. Data moves between devices by JAX's collectives and lax.ppermute only.
A program may use at most 64 MiB of HBM per device.

v0:
```python
import jax
import jax.numpy as jnp
from jax import lax
from jax.sharding import PartitionSpec as P

SMAX = 32
ITERS = 2


def with_halo(x, sides, width):
    for axis, dim in sides:
        count, length = (lax.axis_size(axis), x.shape[dim])
        up = [(i, (i + 1) % count) for i in range(count - 1)]
        down = [(j, i) for i, j in up]
        last = lax.slice_in_dim(x, length - width, length, axis=dim)
        first = lax.slice_in_dim(x, 0, width, axis=dim)
        before = lax.ppermute(last, axis, up)
        after = lax.ppermute(first, axis, down)
        x = jnp.concatenate([before, x, after], axis=dim)
    return x


def prior_from_pads(padded, coeff_pad, weights):
    rows = padded.shape[1] - 2
    cols = padded.shape[2] - 2
    centre = padded[:, 1 : 1 + rows, 1 : 1 + cols]
    coeff_centre = coeff_pad[:, 1 : 1 + rows, 1 : 1 + cols]
    total = jnp.zeros_like(centre)
    for step_r, step_c in ((1, 0), (-1, 0), (0, 1), (0, -1)):
        other = padded[:, 1 + step_r : 1 + step_r + rows, 1 + step_c : 1 + step_c + cols]
        coeff_other = coeff_pad[:, 1 + step_r : 1 + step_r + rows, 1 + step_c : 1 + step_c + cols]
        total = total + 0.5 * (coeff_centre + coeff_other) * (centre - other)
    return weights[:, None, None] * total


def operate(field, coeff_pad, weights, shifts):
    layers, rows, cols = field.shape
    dirs = shifts.shape[0]
    depth = SMAX
    padded = with_halo(field, (("gx", 2), ("gy", 1)), depth)
    images = []
    for direction in range(dirs):
        image = jnp.zeros((rows, cols), jnp.float32)
        for layer in range(layers):
            start_r = depth + shifts[direction, layer, 0]
            start_c = depth + shifts[direction, layer, 1]
            image = image + lax.dynamic_slice(padded[layer], (start_r, start_c), (rows, cols))
        images.append(image)
    image_pad = with_halo(jnp.stack(images), (("gx", 2), ("gy", 1)), depth)
    back = []
    for layer in range(layers):
        acc = jnp.zeros((rows, cols), jnp.float32)
        for direction in range(dirs):
            start_r = depth - shifts[direction, layer, 0]
            start_c = depth - shifts[direction, layer, 1]
            acc = acc + lax.dynamic_slice(image_pad[direction], (start_r, start_c), (rows, cols))
        back.append(acc)
    centre_pad = padded[:, depth - 1 : depth + rows + 1, depth - 1 : depth + cols + 1]
    return jnp.stack(back) + prior_from_pads(centre_pad, coeff_pad, weights)


def inner_sums(residual, w_vec):
    pair = (jnp.sum(residual * residual), jnp.sum(w_vec * residual))
    return lax.psum((pair[0], pair[1]), ("gx", "gy"))


def on_device(right_side, coefficient, strength_table, layer_entry, shifts):
    entries = jnp.arange(strength_table.shape[0], dtype=jnp.int32)
    weights = jnp.sum(
        jnp.where(layer_entry[:, None] == entries[None, :], strength_table[None, :], 0.0), axis=1
    )
    coeff_pad = with_halo(coefficient, (("gx", 2), ("gy", 1)), 1)
    solution_field = jnp.zeros_like(right_side)
    residual = right_side
    w_vec = operate(residual, coeff_pad, weights, shifts)
    z_vec = jnp.zeros_like(right_side)
    s_vec = jnp.zeros_like(right_side)
    p_vec = jnp.zeros_like(right_side)
    gamma_prev = jnp.float32(1.0)
    alpha_prev = jnp.float32(1.0)
    for step in range(ITERS):
        gamma, delta = inner_sums(residual, w_vec)
        n_vec = operate(w_vec, coeff_pad, weights, shifts)
        if step == 0:
            beta = jnp.float32(0.0)
            alpha = gamma / delta
        else:
            beta = gamma / gamma_prev
            alpha = gamma / (delta - beta * gamma / alpha_prev)
        z_vec = n_vec + beta * z_vec
        s_vec = w_vec + beta * s_vec
        p_vec = residual + beta * p_vec
        solution_field = solution_field + alpha * p_vec
        residual = residual - alpha * s_vec
        w_vec = w_vec - alpha * z_vec
        gamma_prev = gamma
        alpha_prev = alpha
    return (solution_field, residual)


def solution(mesh):
    placed = (P(None, "gy", "gx"), P(None, "gy", "gx"), P(), P(), P())
    return jax.shard_map(
        on_device,
        mesh=mesh,
        in_specs=placed,
        out_specs=(P(None, "gy", "gx"), P(None, "gy", "gx")),
        check_vma=False,
    )
```

profile of v0, /device:TPU:1, one launch (start us, length us, event | category | flops | bytes accessed | tf_op | source)
XLA Modules:
  0.0 369.4 jit_solution(8329636813934591109)
XLA Ops:
  0.6 1.2 fusion.47
  1.9 4.9 %collective-permute-start = (f32[2,256,32]{2,1,0:T(8,128)S(1)}, f32[2,256,32]{2,1,0:T(8,128)S(1)}, u32[]{:S(2)}, u32[]{:S(2)}) collective-permute-start(f32[2,256,32]{2,1,0:T(8,128)S(1)} %get-tuple-element.51), channel_id=1, source_target_pairs={{0,16},{16,32},{32,48},{48,64},{64,80},{80,96},{96,112},{112,128},... | collective-permute-start | bytes 196616 | tf_op jit(solution)/shard_map/ppermute | solution.py:17
  6.8 1.9 collective-permute-start.1
  8.8 1.4 collective-permute-done
  10.1 4.4 %collective-permute-done.1 = f32[2,256,32]{2,1,0:T(8,128)S(1)} collective-permute-done((f32[2,256,32]{2,1,0:T(8,128)S(1)}, f32[2,256,32]{2,1,0:T(8,128)S(1)}, u32[]{:S(2)}, u32[]{:S(2)}) %collective-permute-start.1) | collective-permute-done | bytes 65568 | tf_op jit(solution)/shard_map/ppermute | solution.py:18
  14.5 1.2 pad_maximum_fusion.37
  15.8 3.1 collective-permute-start.2
  18.9 1.3 collective-permute-start.3
  20.2 1.8 fusion.48
  23.2 1.4 fusion.49
  57.6 1.6 copy-done.2
  59.7 2.0 collective-permute-start.4
  62.0 2.3 collective-permute-start.5
  64.7 4.5 %collective-permute-done.5 = f32[6,256,32]{1,2,0:T(8,128)S(1)} collective-permute-done((f32[6,256,32]{1,2,0:T(8,128)S(1)}, f32[6,256,32]{1,2,0:T(8,128)S(1)}, u32[]{:S(2)}, u32[]{:S(2)}) %collective-permute-start.5) | collective-permute-done | bytes 196640 | tf_op jit(solution)/shard_map/ppermute | solution.py:18
  69.2 1.2 copy.46
  70.3 2.6 pad_maximum_fusion.33
  72.9 4.9 %collective-permute-start.6 = (f32[6,32,576]{2,1,0:T(8,128)}, f32[6,32,576]{2,1,0:T(8,128)}, u32[]{:S(2)}, u32[]{:S(2)}) collective-permute-start(f32[6,32,576]{2,1,0:T(8,128)} %get-tuple-element.28), channel_id=1, source_target_pairs={{0,1},{1,2},{2,3},{3,4},{4,5},{5,6},{6,7},{7,8},{8,9},{9,10},{10,1... | collective-permute-start | bytes 1327112 | tf_op jit(solution)/shard_map/ppermute | solution.py:17
  77.8 1.3 collective-permute-start.7
  79.9 2.0 collective-permute-start.8
  82.0 2.3 collective-permute-start.9
  114.5 1.3 collective-permute-start.10
  115.8 4.6 %collective-permute-start.11 = (f32[2,1,514]{2,0,1:T(2,128)S(1)}, f32[2,1,514]{2,0,1:T(2,128)S(1)}, u32[]{:S(2)}, u32[]{:S(2)}) collective-permute-start(f32[2,1,514]{2,0,1:T(2,128)S(1)} %copy.49), channel_id=1, source_target_pairs={{0,1},{1,2},{2,3},{3,4},{4,5},{5,6},{6,7},{7,8},{8,9},{9,10},{10,1... | collective-permute-start | bytes 12344 | tf_op jit(solution)/shard_map/ppermute | solution.py:17
  121.2 3.6 pad_maximum_fusion
  127.2 4.0 %multiply_reduce_fusion.2 = (f32[]{:T(128)}, f32[]{:T(128)}, f32[2,256,512]{2,1,0:T(8,128)S(1)}) fusion(f32[2,256,512]{2,1,0:T(8,128)S(1)} %copy-done, f32[2,256,32]{2,1,0:T(8,128)S(1)} %copy-done.8, f32[2,256,512]{2,1,0:T(8,128)S(1)} %copy-done.3, f32[2,256,1]{2,1,0:T(8,128)S(1)} %collective-permute-done.8, f32[2,256,32]{2,1,0:T(8,128)S(1)} %copy-done.10, ...), kind=kLoop, calls=%fused_computation.69 | loop fusion | flops 11010046 | bytes 4632624 | tf_op jit(solution)/shard_map/reduce_sum | solution.py:63
  131.3 4.4 %collective-permute-start.12 = (f32[2,256,32]{2,1,0:T(8,128)S(1)}, f32[2,256,32]{2,1,0:T(8,128)S(1)}, u32[]{:S(2)}, u32[]{:S(2)}) collective-permute-start(f32[2,256,32]{2,1,0:T(8,128)S(1)} %get-tuple-element.47), channel_id=1, source_target_pairs={{0,16},{16,32},{32,48},{48,64},{64,80},{80,96},{96,112},{112,128},... | collective-permute-start | bytes 196616 | tf_op jit(solution)/shard_map/ppermute | solution.py:17
  135.7 1.9 collective-permute-start.13
  137.6 1.4 collective-permute-done.12
  139.0 4.4 %collective-permute-done.13 = f32[2,256,32]{2,1,0:T(8,128)S(1)} collective-permute-done((f32[2,256,32]{2,1,0:T(8,128)S(1)}, f32[2,256,32]{2,1,0:T(8,128)S(1)}, u32[]{:S(2)}, u32[]{:S(2)}) %collective-permute-start.13) | collective-permute-done | bytes 65568 | tf_op jit(solution)/shard_map/ppermute | solution.py:18
  143.6 3.9 %collective-permute-start.14 = (f32[2,32,576]{2,1,0:T(8,128)S(1)}, f32[2,32,576]{2,1,0:T(8,128)S(1)}, u32[]{:S(2)}, u32[]{:S(2)}) collective-permute-start(f32[2,32,576]{2,1,0:T(8,128)S(1)} %get-tuple-element.41), channel_id=1, source_target_pairs={{0,1},{1,2},{2,3},{3,4},{4,5},{5,6},{6,7},{7,8},{8,9},{9,10},{10,1... | collective-permute-start | bytes 442376 | tf_op jit(solution)/shard_map/ppermute | solution.py:17
  147.5 1.5 collective-permute-start.15
  149.7 4.1 %collective-permute-done.15 = f32[2,32,576]{2,1,0:T(8,128)S(1)} collective-permute-done((f32[2,32,576]{2,1,0:T(8,128)S(1)}, f32[2,32,576]{2,1,0:T(8,128)S(1)}, u32[]{:S(2)}, u32[]{:S(2)}) %collective-permute-start.15) | collective-permute-done | bytes 147488 | tf_op jit(solution)/shard_map/ppermute | solution.py:18
  156.7 1.6 copy-done.1
  158.3 1.4 fusion.41
  159.7 2.0 copy.51
  161.8 2.9 collective-permute-start.16
  164.6 2.1 copy.52
  166.7 2.1 collective-permute-start.17
  168.8 2.1 copy.53
  170.9 4.6 %collective-permute-done.17 = f32[6,256,32]{1,2,0:T(8,128)} collective-permute-done((f32[6,256,32]{1,2,0:T(8,128)}, f32[6,256,32]{1,2,0:T(8,128)}, u32[]{:S(2)}, u32[]{:S(2)}) %collective-permute-start.17) | collective-permute-done | bytes 196640 | tf_op jit(solution)/shard_map/ppermute | solution.py:18
  175.5 2.1 copy.54
  177.6 2.6 pad_maximum_fusion.30
  180.2 6.0 %collective-permute-start.18 = (f32[6,32,576]{2,1,0:T(8,128)}, f32[6,32,576]{2,1,0:T(8,128)}, u32[]{:S(2)}, u32[]{:S(2)}) collective-permute-start(f32[6,32,576]{2,1,0:T(8,128)} %get-tuple-element.26), channel_id=1, source_target_pairs={{0,1},{1,2},{2,3},{3,4},{4,5},{5,6},{6,7},{7,8},{8,9},{9,10},{10,1... | collective-permute-start | bytes 1327112 | tf_op jit(solution)/shard_map/ppermute | solution.py:17
  186.3 1.3 collective-permute-start.19
  187.5 89.5 %all-reduce.1 = (f32[]{:T(128)}, f32[]{:T(128)}) all-reduce(f32[]{:T(128)} %get-tuple-element.7, f32[]{:T(128)} %get-tuple-element.6), channel_id=1, replica_groups=mesh['gx'=16,'gy'=16] {'gx','gy'}, use_global_device_ids=true, to_apply=%region_1.2 | all-reduce | flops 2 | bytes 16 | tf_op jit(solution)/shard_map/psum | solution.py:64
  278.2 3.7 %pad_maximum_fusion.1 = f32[6,320,576]{2,1,0:T(8,128)S(1)} fusion(f32[6,32,576]{2,1,0:T(8,128)} %collective-permute-done.19, f32[6,256,32]{2,1,0:T(8,128)} %copy.54, f32[6,256,512]{2,1,0:T(8,128)} %copy-done.1, f32[6,256,32]{2,1,0:T(8,128)} %copy.53, f32[6,32,576]{2,1,0:T(8,128)} %collective-permute-done.18), kind=kLoop, calls=%fused_computation.1 | loop fusion | flops 4423680 | bytes 8847360 | tf_op jit(solution)/shard_map/concatenate | solution.py:19
  284.3 4.8 %multiply_reduce_fusion = (f32[]{:T(128)}, f32[]{:T(128)}, f32[2,256,512]{2,1,0:T(8,128)}) fusion(f32[2,256,512]{2,1,0:T(8,128)S(1)} %copy-done, f32[2,256,512]{2,1,0:T(8,128)S(1)} %get-tuple-element.13, f32[]{:T(128)S(6)} %div.12, f32[2,256,32]{2,1,0:T(8,128)S(1)} %copy-done.12, f32[2,256,512]{2,1,0:T(8,128)S(1)} %copy-done.3, ...), kind=kLoop, calls=%fused_computation.66 | loop fusion | flops 12058622 | bytes 5681204 | tf_op jit(solution)/shard_map/reduce_sum | solution.py:63
  289.1 72.8 %all-reduce = (f32[]{:T(128)}, f32[]{:T(128)}) all-reduce(f32[]{:T(128)} %get-tuple-element.5, f32[]{:T(128)} %get-tuple-element.4), channel_id=1, replica_groups=mesh['gx'=16,'gy'=16] {'gx','gy'}, use_global_device_ids=true, to_apply=%region_6.7 | all-reduce | flops 2 | bytes 16 | tf_op jit(solution)/shard_map/psum | solution.py:64
  366.5 3.0 multiply_subtract_fusion
  (96 shorter events, 15.1 us)
Async XLA Ops:
  0.6 54.2 %copy-start = (f32[2,256,512]{2,1,0:T(8,128)S(1)}, f32[2,256,512]{2,1,0:T(8,128)}, u32[]{:S(2)}) copy-start(f32[2,256,512]{2,1,0:T(8,128)} %param.5) | copy-start | bytes 3145732
  1.9 8.2 %collective-permute-start = (f32[2,256,32]{2,1,0:T(8,128)S(1)}, f32[2,256,32]{2,1,0:T(8,128)S(1)}, u32[]{:S(2)}, u32[]{:S(2)}) collective-permute-start(f32[2,256,32]{2,1,0:T(8,128)S(1)} %get-tuple-element.51), channel_id=1, source_target_pairs={{0,16},{16,32},{32,48},{48,64},{64,80},{80,96},{96,112},{112,128},... | collective-permute-start | bytes 196616 | tf_op jit(solution)/shard_map/ppermute | solution.py:17
  6.8 7.7 %collective-permute-start.1 = (f32[2,256,32]{2,1,0:T(8,128)S(1)}, f32[2,256,32]{2,1,0:T(8,128)S(1)}, u32[]{:S(2)}, u32[]{:S(2)}) collective-permute-start(f32[2,256,32]{2,1,0:T(8,128)S(1)} %get-tuple-element.50), channel_id=1, source_target_pairs={{16,0},{32,16},{48,32},{64,48},{80,64},{96,80},{112,96},{128,112},... | collective-permute-start | bytes 196616 | tf_op jit(solution)/shard_map/ppermute | solution.py:18
  10.1 43.4 %copy-start.7 = (f32[2,256,32]{2,1,0:T(8,128)}, f32[2,256,32]{2,1,0:T(8,128)S(1)}, u32[]{:S(2)}) copy-start(f32[2,256,32]{2,1,0:T(8,128)S(1)} %collective-permute-done) | copy-start | bytes 196612
  14.5 39.0 %copy-start.9 = (f32[2,256,32]{2,1,0:T(8,128)}, f32[2,256,32]{2,1,0:T(8,128)S(1)}, u32[]{:S(2)}) copy-start(f32[2,256,32]{2,1,0:T(8,128)S(1)} %collective-permute-done.1) | copy-start | bytes 196612
  15.8 37.7 %collective-permute-start.2 = (f32[2,32,576]{2,1,0:T(8,128)S(1)}, f32[2,32,576]{2,1,0:T(8,128)S(1)}, u32[]{:S(2)}, u32[]{:S(2)}) collective-permute-start(f32[2,32,576]{2,1,0:T(8,128)S(1)} %get-tuple-element.45), channel_id=1, source_target_pairs={{0,1},{1,2},{2,3},{3,4},{4,5},{5,6},{6,7},{7,8},{8,9},{9,10},{10,1... | collective-permute-start | bytes 442376 | tf_op jit(solution)/shard_map/ppermute | solution.py:17
  18.9 34.6 %collective-permute-start.3 = (f32[2,32,576]{2,1,0:T(8,128)S(1)}, f32[2,32,576]{2,1,0:T(8,128)S(1)}, u32[]{:S(2)}, u32[]{:S(2)}) collective-permute-start(f32[2,32,576]{2,1,0:T(8,128)S(1)} %get-tuple-element.44), channel_id=1, source_target_pairs={{1,0},{2,1},{3,2},{4,3},{5,4},{6,5},{7,6},{8,7},{9,8},{10,9},{11,1... | collective-permute-start | bytes 442376 | tf_op jit(solution)/shard_map/ppermute | solution.py:18
  53.5 0.7 copy-start.15
  54.1 0.7 copy-start.17
  57.6 1.7 copy-start.2
  59.7 4.6 %collective-permute-start.4 = (f32[6,256,32]{1,2,0:T(8,128)S(1)}, f32[6,256,32]{1,2,0:T(8,128)S(1)}, u32[]{:S(2)}, u32[]{:S(2)}) collective-permute-start(f32[6,256,32]{1,2,0:T(8,128)S(1)} %copy.43), channel_id=1, source_target_pairs={{0,16},{16,32},{32,48},{48,64},{64,80},{80,96},{96,112},{112,128},... | collective-permute-start | bytes 589832 | tf_op jit(solution)/shard_map/ppermute | solution.py:17
  62.0 7.2 %collective-permute-start.5 = (f32[6,256,32]{1,2,0:T(8,128)S(1)}, f32[6,256,32]{1,2,0:T(8,128)S(1)}, u32[]{:S(2)}, u32[]{:S(2)}) collective-permute-start(f32[6,256,32]{1,2,0:T(8,128)S(1)} %copy.44), channel_id=1, source_target_pairs={{16,0},{32,16},{48,32},{64,48},{80,64},{96,80},{112,96},{128,112},... | collective-permute-start | bytes 589832 | tf_op jit(solution)/shard_map/ppermute | solution.py:18
  64.6 14.4 %copy-start.3 = (f32[2,256,512]{2,1,0:T(8,128)S(1)}, f32[2,256,512]{2,1,0:T(8,128)}, u32[]{:S(2)}) copy-start(f32[2,256,512]{2,1,0:T(8,128)} %param.6) | copy-start | bytes 3145732
  70.3 27.2 %copy-start.23 = (f32[35]{0:T(128)S(1)}, f32[35]{0:T(128)}, u32[]{:S(2)}) copy-start(f32[35]{0:T(128)} %param.7) | copy-start | bytes 424
  70.3 27.2 %copy-start.24 = (s32[2]{0:T(128)S(1)}, s32[2]{0:T(128)}, u32[]{:S(2)}) copy-start(s32[2]{0:T(128)} %param.8) | copy-start | bytes 28
  72.9 48.3 %collective-permute-start.6 = (f32[6,32,576]{2,1,0:T(8,128)}, f32[6,32,576]{2,1,0:T(8,128)}, u32[]{:S(2)}, u32[]{:S(2)}) collective-permute-start(f32[6,32,576]{2,1,0:T(8,128)} %get-tuple-element.28), channel_id=1, source_target_pairs={{0,1},{1,2},{2,3},{3,4},{4,5},{5,6},{6,7},{7,8},{8,9},{9,10},{10,1... | collective-permute-start | bytes 1327112 | tf_op jit(solution)/shard_map/ppermute | solution.py:17
  77.8 43.5 %collective-permute-start.7 = (f32[6,32,576]{2,1,0:T(8,128)}, f32[6,32,576]{2,1,0:T(8,128)}, u32[]{:S(2)}, u32[]{:S(2)}) collective-permute-start(f32[6,32,576]{2,1,0:T(8,128)} %get-tuple-element.29), channel_id=1, source_target_pairs={{1,0},{2,1},{3,2},{4,3},{5,4},{6,5},{7,6},{8,7},{9,8},{10,9},{11,1... | collective-permute-start | bytes 1327112 | tf_op jit(solution)/shard_map/ppermute | solution.py:18
  79.9 34.5 %collective-permute-start.8 = (f32[2,256,1]{2,1,0:T(8,128)}, f32[2,256,1]{2,1,0:T(8,128)S(1)}, u32[]{:S(2)}, u32[]{:S(2)}) collective-permute-start(f32[2,256,1]{2,1,0:T(8,128)} %get-tuple-element.49), channel_id=1, source_target_pairs={{0,16},{16,32},{32,48},{48,64},{64,80},{80,96},{96,112},{112,128},... | collective-permute-start | bytes 6152 | tf_op jit(solution)/shard_map/ppermute | solution.py:17
  82.0 32.5 %collective-permute-start.9 = (f32[2,256,1]{2,1,0:T(8,128)}, f32[2,256,1]{2,1,0:T(8,128)S(1)}, u32[]{:S(2)}, u32[]{:S(2)}) collective-permute-start(f32[2,256,1]{2,1,0:T(8,128)} %get-tuple-element.48), channel_id=1, source_target_pairs={{16,0},{32,16},{48,32},{64,48},{80,64},{96,80},{112,96},{128,112},... | collective-permute-start | bytes 6152 | tf_op jit(solution)/shard_map/ppermute | solution.py:18
  114.4 10.4 %copy-start.4 = (f32[2,256,1]{2,1,0:T(8,128)}, f32[2,256,1]{2,1,0:T(8,128)S(1)}, u32[]{:S(2)}) copy-start(f32[2,256,1]{2,1,0:T(8,128)S(1)} %collective-permute-done.9) | copy-start | bytes 6148
  114.5 6.2 %collective-permute-start.10 = (f32[2,1,514]{2,0,1:T(2,128)S(1)}, f32[2,1,514]{2,0,1:T(2,128)S(1)}, u32[]{:S(2)}, u32[]{:S(2)}) collective-permute-start(f32[2,1,514]{2,0,1:T(2,128)S(1)} %copy.47), channel_id=1, source_target_pairs={{1,0},{2,1},{3,2},{4,3},{5,4},{6,5},{7,6},{8,7},{9,8},{10,9},{11,1... | collective-permute-start | bytes 12344 | tf_op jit(solution)/shard_map/ppermute | solution.py:18
  115.8 5.4 %collective-permute-start.11 = (f32[2,1,514]{2,0,1:T(2,128)S(1)}, f32[2,1,514]{2,0,1:T(2,128)S(1)}, u32[]{:S(2)}, u32[]{:S(2)}) collective-permute-start(f32[2,1,514]{2,0,1:T(2,128)S(1)} %copy.49), channel_id=1, source_target_pairs={{0,1},{1,2},{2,3},{3,4},{4,5},{5,6},{6,7},{7,8},{8,9},{9,10},{10,1... | collective-permute-start | bytes 12344 | tf_op jit(solution)/shard_map/ppermute | solution.py:17
  125.2 2.0 copy-start.5
  125.2 2.0 copy-start.8
  125.2 2.0 copy-start.10
  125.2 2.0 copy-start.16
  125.2 2.0 copy-start.18
  131.3 7.7 %collective-permute-start.12 = (f32[2,256,32]{2,1,0:T(8,128)S(1)}, f32[2,256,32]{2,1,0:T(8,128)S(1)}, u32[]{:S(2)}, u32[]{:S(2)}) collective-permute-start(f32[2,256,32]{2,1,0:T(8,128)S(1)} %get-tuple-element.47), channel_id=1, source_target_pairs={{0,16},{16,32},{32,48},{48,64},{64,80},{80,96},{96,112},{112,128},... | collective-permute-start | bytes 196616 | tf_op jit(solution)/shard_map/ppermute | solution.py:17
  135.7 7.7 %collective-permute-start.13 = (f32[2,256,32]{2,1,0:T(8,128)S(1)}, f32[2,256,32]{2,1,0:T(8,128)S(1)}, u32[]{:S(2)}, u32[]{:S(2)}) collective-permute-start(f32[2,256,32]{2,1,0:T(8,128)S(1)} %get-tuple-element.46), channel_id=1, source_target_pairs={{16,0},{32,16},{48,32},{64,48},{80,64},{96,80},{112,96},{128,112},... | collective-permute-start | bytes 196616 | tf_op jit(solution)/shard_map/ppermute | solution.py:18
  139.0 15.4 %copy-start.11 = (f32[2,256,32]{2,1,0:T(8,128)}, f32[2,256,32]{2,1,0:T(8,128)S(1)}, u32[]{:S(2)}) copy-start(f32[2,256,32]{2,1,0:T(8,128)S(1)} %collective-permute-done.12) | copy-start | bytes 196612
  143.4 11.1 %copy-start.13 = (f32[2,256,32]{2,1,0:T(8,128)}, f32[2,256,32]{2,1,0:T(8,128)S(1)}, u32[]{:S(2)}) copy-start(f32[2,256,32]{2,1,0:T(8,128)S(1)} %collective-permute-done.13) | copy-start | bytes 196612
  143.6 6.2 %collective-permute-start.14 = (f32[2,32,576]{2,1,0:T(8,128)S(1)}, f32[2,32,576]{2,1,0:T(8,128)S(1)}, u32[]{:S(2)}, u32[]{:S(2)}) collective-permute-start(f32[2,32,576]{2,1,0:T(8,128)S(1)} %get-tuple-element.41), channel_id=1, source_target_pairs={{0,1},{1,2},{2,3},{3,4},{4,5},{5,6},{6,7},{7,8},{8,9},{9,10},{10,1... | collective-permute-start | bytes 442376 | tf_op jit(solution)/shard_map/ppermute | solution.py:17
  147.5 6.3 %collective-permute-start.15 = (f32[2,32,576]{2,1,0:T(8,128)S(1)}, f32[2,32,576]{2,1,0:T(8,128)S(1)}, u32[]{:S(2)}, u32[]{:S(2)}) collective-permute-start(f32[2,32,576]{2,1,0:T(8,128)S(1)} %get-tuple-element.40), channel_id=1, source_target_pairs={{1,0},{2,1},{3,2},{4,3},{5,4},{6,5},{7,6},{8,7},{9,8},{10,9},{11,1... | collective-permute-start | bytes 442376 | tf_op jit(solution)/shard_map/ppermute | solution.py:18
  149.7 4.7 %copy-start.19 = (f32[2,32,576]{2,1,0:T(8,128)}, f32[2,32,576]{2,1,0:T(8,128)S(1)}, u32[]{:S(2)}) copy-start(f32[2,32,576]{2,1,0:T(8,128)S(1)} %collective-permute-done.14) | copy-start | bytes 442372
  153.8 0.7 copy-start.21
  156.6 1.7 copy-start.1
  161.8 7.0 %collective-permute-start.16 = (f32[6,256,32]{1,2,0:T(8,128)}, f32[6,256,32]{1,2,0:T(8,128)}, u32[]{:S(2)}, u32[]{:S(2)}) collective-permute-start(f32[6,256,32]{1,2,0:T(8,128)} %copy.51), channel_id=1, source_target_pairs={{0,16},{16,32},{32,48},{48,64},{64,80},{80,96},{96,112},{112,128},... | collective-permute-start | bytes 589832 | tf_op jit(solution)/shard_map/ppermute | solution.py:17
  166.7 8.8 %collective-permute-start.17 = (f32[6,256,32]{1,2,0:T(8,128)}, f32[6,256,32]{1,2,0:T(8,128)}, u32[]{:S(2)}, u32[]{:S(2)}) collective-permute-start(f32[6,256,32]{1,2,0:T(8,128)} %copy.52), channel_id=1, source_target_pairs={{16,0},{32,16},{48,32},{64,48},{80,64},{96,80},{112,96},{128,112},... | collective-permute-start | bytes 589832 | tf_op jit(solution)/shard_map/ppermute | solution.py:18
  180.2 98.0 %collective-permute-start.18 = (f32[6,32,576]{2,1,0:T(8,128)}, f32[6,32,576]{2,1,0:T(8,128)}, u32[]{:S(2)}, u32[]{:S(2)}) collective-permute-start(f32[6,32,576]{2,1,0:T(8,128)} %get-tuple-element.26), channel_id=1, source_target_pairs={{0,1},{1,2},{2,3},{3,4},{4,5},{5,6},{6,7},{7,8},{8,9},{9,10},{10,1... | collective-permute-start | bytes 1327112 | tf_op jit(solution)/shard_map/ppermute | solution.py:17
  186.3 92.0 %collective-permute-start.19 = (f32[6,32,576]{2,1,0:T(8,128)}, f32[6,32,576]{2,1,0:T(8,128)}, u32[]{:S(2)}, u32[]{:S(2)}) collective-permute-start(f32[6,32,576]{2,1,0:T(8,128)} %get-tuple-element.27), channel_id=1, source_target_pairs={{1,0},{2,1},{3,2},{4,3},{5,4},{6,5},{7,6},{8,7},{9,8},{10,9},{11,1... | collective-permute-start | bytes 1327112 | tf_op jit(solution)/shard_map/ppermute | solution.py:18
  282.3 2.0 copy-start.6
  282.3 2.0 copy-start.12
  282.3 2.0 copy-start.14
  282.3 2.0 copy-start.20
  282.3 2.0 copy-start.22
where the time goes:
time: 371 us; the launch traced here: 369 us
  blocking collectives  162 us (44%)
  between operations  67.2 us (18%)
  starting transfers between devices  56 us (15%)
  other arithmetic  35 us (9%)
  waiting for transfers between devices  26.1 us (7%)
  local copies, waits for them, and re-layouts  22.8 us (6%)
    psum x2, blocking collectives, inner_sums(): return lax.psum((pair[0], pair[1]), ('gx', 'gy'))  162 us
    ppermute x10, starting transfers between devices, with_halo(): before = lax.ppermute(last, axis, up)  38.8 us
    ppermute x10, waiting for transfers between devices, with_halo(): after = lax.ppermute(first, axis, down)  22.1 us
    ppermute x10, starting transfers between devices, with_halo(): after = lax.ppermute(first, axis, down)  17.2 us
    concatenate x6, other arithmetic, with_halo(): x = jnp.concatenate([before, x, after], axis=dim)  9.65 us
    reduce_sum x2, other arithmetic, inner_sums(): pair = (jnp.sum(residual * residual), jnp.sum(w_vec * residual))  8.79 us
  transfers between devices with their start and end apart: 20, of which 9 were waited for; matrix products, arithmetic and copies ran while one was open for 2% of the time, Pallas kernels for 0%

commit v1 on v0

v1 whole, which is shorter than its diff:
```python
import jax
import jax.numpy as jnp
from jax import lax
from jax.experimental import pallas as pl
from jax.experimental.pallas import tpu as pltpu
from jax.sharding import PartitionSpec as P

REACH = 64
LANES = 128
HALF = 64
CHUNK = 16
VMEM_BYTES = 32 * 1024 * 1024


def even_swap(count):
    return [(i, i ^ 1) for i in range(count)]


def odd_swap(count):
    return [(i, i + 1 if i % 2 else i - 1) for i in range(1, count - 1)]


def is_odd(axis):
    return lax.rem(lax.axis_index(axis), 2) == 1


def swap(even, odd, axis):
    count = lax.axis_size(axis)
    return (
        lax.ppermute(even, axis, even_swap(count)),
        lax.ppermute(odd, axis, odd_swap(count)),
    )


def lane_of(shape):
    return lax.broadcasted_iota(jnp.int32, shape, 1)


def pack_columns(first, second, high):
    low_lanes = lane_of(first.shape) < HALF
    turned = pltpu.roll(second, HALF, 1)
    if high:
        return jnp.where(low_lanes, turned, first)
    return jnp.where(low_lanes, first, turned)


def store_packed(even_ref, odd_ref, odd, start, low, high):
    rows = low.shape[0]
    even_ref[start : start + rows, :] = jnp.where(odd, low, high)
    odd_ref[start : start + rows, :] = jnp.where(odd, high, low)


def pack_kernel(with_coeff, *refs):
    if with_coeff:
        field, coeff, even_rows, odd_rows, even_out, odd_out = refs
    else:
        field, even_rows, odd_rows, even_out, odd_out = refs
    rows, cols = field.shape[1:]
    odd_x, odd_y = is_odd("gx"), is_odd("gy")
    edges = (slice(0, LANES), slice(cols - LANES, cols))

    def halo(layer, edge, before):
        even = even_rows[layer, 0:REACH, edge]
        other = odd_rows[layer, 0:REACH, edge]
        return jnp.where(odd_y == before, even, other)

    for start, part in ((0, "above"), (REACH, "own"), (REACH + rows, "below")):
        packed = []
        for high, edge in enumerate(edges):
            if part == "own":
                pair = [field[layer, :, edge] for layer in range(2)]
            else:
                pair = [halo(layer, edge, part == "above") for layer in range(2)]
            packed.append(pack_columns(pair[0], pair[1], high))
        store_packed(even_out, odd_out, odd_x, start, packed[0], packed[1])
    if with_coeff:
        packed = [
            pack_columns(coeff[0, :, edge], coeff[1, :, edge], high)
            for high, edge in enumerate(edges)
        ]
        store_packed(even_out, odd_out, odd_x, 2 * REACH + rows, packed[0], packed[1])


def pack(field, coeff, even_rows, odd_rows):
    rows = field.shape[1]
    total = rows + 2 * REACH + (0 if coeff is None else rows)
    out = jax.ShapeDtypeStruct((total, LANES), jnp.float32)
    operands = [field] + ([] if coeff is None else [coeff]) + [even_rows, odd_rows]

    def kernel(*refs):
        pack_kernel(coeff is not None, *refs)

    return pl.pallas_call(
        kernel,
        out_shape=(out, out),
        in_specs=[pl.BlockSpec(memory_space=pltpu.VMEM)] * len(operands),
        out_specs=(pl.BlockSpec(memory_space=pltpu.VMEM),) * 2,
        compiler_params=pltpu.CompilerParams(vmem_limit_bytes=VMEM_BYTES),
        name="pack_columns",
    )(*operands)


def fill_field(pad, field, even_rows, odd_rows, even_cols, odd_cols):
    rows, cols = field.shape[1:]
    odd_x, odd_y = is_odd("gx"), is_odd("gy")
    tiles = cols // LANES
    for layer in range(2):
        for tile in range(tiles):
            lanes = slice(tile * LANES, (tile + 1) * LANES)
            pad[layer, 1 + tile, REACH : REACH + rows, :] = field[layer, :, lanes]
            even = even_rows[layer, 0:REACH, lanes]
            other = odd_rows[layer, 0:REACH, lanes]
            pad[layer, 1 + tile, 0:REACH, :] = jnp.where(odd_y, even, other)
            pad[layer, 1 + tile, REACH + rows :, :] = jnp.where(odd_y, other, even)
    even = even_cols[0 : rows + 2 * REACH, :]
    other = odd_cols[0 : rows + 2 * REACH, :]
    for tile, packed in (
        (0, jnp.where(odd_x, even, other)),
        (1 + tiles, jnp.where(odd_x, other, even)),
    ):
        pad[0, tile] = packed
        pad[1, tile] = pltpu.roll(packed, HALF, 1)


def fill_coeff(pad, coeff, even_rows, odd_rows, even_cols, odd_cols):
    rows, cols = coeff.shape[1:]
    odd_x, odd_y = is_odd("gx"), is_odd("gy")
    tiles = cols // LANES
    for layer in range(2):
        for tile in range(tiles):
            lanes = slice(tile * LANES, (tile + 1) * LANES)
            pad[layer, 1 + tile, 8 : 8 + rows, :] = coeff[layer, :, lanes]
            even = even_rows[layer, REACH : REACH + 8, lanes]
            other = odd_rows[layer, REACH : REACH + 8, lanes]
            pad[layer, 1 + tile, 0:8, :] = jnp.where(odd_y, even, other)
            pad[layer, 1 + tile, 8 + rows :, :] = jnp.where(odd_y, other, even)
    start = rows + 2 * REACH
    even = even_cols[start : start + rows, :]
    other = odd_cols[start : start + rows, :]
    for tile, packed in (
        (0, jnp.where(odd_x, even, other)),
        (1 + tiles, jnp.where(odd_x, other, even)),
    ):
        pad[0, tile, 8 : 8 + rows, :] = packed
        pad[1, tile, 8 : 8 + rows, :] = pltpu.roll(packed, HALF, 1)


def neighbours_across(load, tiles):
    lane = lane_of((CHUNK, LANES))
    values = [load(tile) for tile in range(tiles + 2)]
    back = [pltpu.roll(value, 1, 1) for value in values[:-1]]
    ahead = [pltpu.roll(value, LANES - 1, 1) for value in values[1:]]
    left = [jnp.where(lane == 0, back[i], back[i + 1]) for i in range(tiles)]
    right = [jnp.where(lane == LANES - 1, ahead[i + 1], ahead[i]) for i in range(tiles)]
    return values[1:-1], left, right


def apply_chunk(layer, row, pad, coeff_pad, shifts, weight, field_rows, grid_shape, tile_shape):
    dirs = shifts.shape[0]
    rows, cols = tile_shape
    tiles = cols // LANES
    other = 1 - layer
    lane = lane_of((CHUNK, LANES))
    row_at = lax.broadcasted_iota(jnp.int32, (CHUNK, LANES), 0)
    first_row = lax.axis_index("gy") * rows + row
    first_col = lax.axis_index("gx") * cols

    def field_at(tile):
        return pad[layer, tile, pl.ds(REACH + row, CHUNK), :]

    def coeff_at(tile):
        return coeff_pad[layer, tile, pl.ds(8 + row, CHUNK), :]

    own, left, right = neighbours_across(field_at, tiles)
    own_c, left_c, right_c = neighbours_across(coeff_at, tiles)
    result = []
    for tile in range(tiles):
        value, coeff = own[tile], own_c[tile]
        above = pad[layer, 1 + tile, pl.ds(REACH - 1 + row, CHUNK), :]
        below = pad[layer, 1 + tile, pl.ds(REACH + 1 + row, CHUNK), :]
        above_c = coeff_pad[layer, 1 + tile, pl.ds(7 + row, CHUNK), :]
        below_c = coeff_pad[layer, 1 + tile, pl.ds(9 + row, CHUNK), :]
        total = (coeff + above_c) * (value - above) + (coeff + below_c) * (value - below)
        total += (coeff + left_c[tile]) * (value - left[tile])
        total += (coeff + right_c[tile]) * (value - right[tile])
        result.append(weight * total)
    for direction in range(dirs):
        shift_r, shift_c = shifts[direction, layer, 0], shifts[direction, layer, 1]
        start_r = REACH + row + shifts[direction, other, 0] - shift_r
        start_c = LANES + shifts[direction, other, 1] - shift_c
        skip = lax.shift_right_logical(start_c, 7)
        turn = jnp.bitwise_and(start_c, LANES - 1)
        back = jnp.bitwise_and(LANES - turn, LANES - 1)
        moved = [
            pltpu.roll(pad[other, skip + tile, pl.ds(start_r, CHUNK), :], back, 1)
            for tile in range(tiles + 1)
        ]
        here = lane < LANES - turn
        image_row = row_at + (first_row - shift_r)
        inside = (image_row >= 0) & (image_row < grid_shape[0])
        for tile in range(tiles):
            mask = inside
            if tile == 0:
                mask = mask & (lane >= shift_c - first_col)
            if tile == tiles - 1:
                mask = mask & (lane < grid_shape[1] + shift_c - first_col - tile * LANES)
            value = own[tile] + jnp.where(here, moved[tile], moved[tile + 1])
            result[tile] = result[tile] + jnp.where(mask, value, 0.0)
    return own, result


def fold(parts):
    total = sum(parts[1:], parts[0])
    pieces = [total[8 * i : 8 * i + 8] for i in range(CHUNK // 8)]
    return sum(pieces[1:], pieces[0])


def dot_of(first, second):
    return fold([a * b for a, b in zip(first, second, strict=True)])


def weight_of(table, entry, layer):
    return 0.5 * table[entry[layer]]


def first_kernel(
    grid_shape, field, coeff, even_rows, odd_rows, even_cols, odd_cols, shifts, table, entry,
    out, sums, even_out, odd_out, pad, coeff_pad,
):
    rows, cols = field.shape[1:]
    fill_field(pad, field, even_rows, odd_rows, even_cols, odd_cols)
    fill_coeff(coeff_pad, coeff, even_rows, odd_rows, even_cols, odd_cols)
    carry = (jnp.zeros((8, LANES), jnp.float32),) * 3
    for layer in range(2):
        weight = weight_of(table, entry, layer)

        def step(i, carry, layer=layer, weight=weight):
            row = pl.multiple_of(i * CHUNK, CHUNK)
            own, result = apply_chunk(
                layer, row, pad, coeff_pad, shifts, weight, field, grid_shape, (rows, cols)
            )
            for tile, value in enumerate(result):
                out[layer, pl.ds(row, CHUNK), tile * LANES : (tile + 1) * LANES] = value
            pairs = ((own, own), (own, result), (result, result))
            return tuple(c + dot_of(*p) for c, p in zip(carry, pairs, strict=True))

        carry = lax.fori_loop(0, rows // CHUNK, step, carry)
    for index, value in enumerate(carry):
        sums[index] = value
    odd_y = is_odd("gy")
    low, high = out[:, 0:REACH, :], out[:, rows - REACH :, :]
    even_out[...] = jnp.where(odd_y, low, high)
    odd_out[...] = jnp.where(odd_y, high, low)


def second_kernel(
    grid_shape, base, field, coeff, even_rows, odd_rows, even_cols, odd_cols, even_edge, odd_edge,
    even_side, odd_side, sums, shifts, table, entry, out, parts, pad, coeff_pad,
):
    rows, cols = field.shape[1:]
    fill_field(pad, field, even_rows, odd_rows, even_cols, odd_cols)
    fill_coeff(coeff_pad, coeff, even_edge, odd_edge, even_side, odd_side)
    gamma, delta, omega = (jnp.sum(sums[index], keepdims=True) for index in range(3))
    fit = jnp.where(omega > 0.0, delta / jnp.where(omega > 0.0, omega, 1.0), 0.0)
    fit = jnp.clip(fit, -1.0, 1.0)
    carry = (jnp.zeros((8, LANES), jnp.float32),) * 6
    for layer in range(2):
        weight = weight_of(table, entry, layer)

        def step(i, carry, layer=layer, weight=weight):
            row = pl.multiple_of(i * CHUNK, CHUNK)
            own, result = apply_chunk(
                layer, row, pad, coeff_pad, shifts, weight, field, grid_shape, (rows, cols)
            )
            rest, slope = [], []
            for tile, value in enumerate(result):
                lanes = slice(tile * LANES, (tile + 1) * LANES)
                out[layer, pl.ds(row, CHUNK), lanes] = value
                rest.append(base[layer, pl.ds(row, CHUNK), lanes] - fit * own[tile])
                slope.append(own[tile] - fit * value)
            pairs = (
                (rest, rest), (rest, own), (slope, rest), (result, rest), (slope, own), (result, own),
            )
            return tuple(c + dot_of(*p) for c, p in zip(carry, pairs, strict=True))

        carry = lax.fori_loop(0, rows // CHUNK, step, carry)
    rest2, rest_w, slope_rest, n_rest, slope_w, n_w = (
        jnp.sum(value, keepdims=True) for value in carry
    )
    lane = lane_of((8, LANES))
    row = jnp.zeros((8, LANES), jnp.float32)
    for at, value in (
        (0, rest2), (1, slope_rest), (8, 2.0 * rest_w), (9, n_rest + slope_w),
        (16, omega), (17, n_w), (24, fit), (25, fit), (32, gamma), (33, delta),
    ):
        row = jnp.where(lane == at, value, row)
    for start in range(0, parts.shape[0], 8):
        parts[start : start + 8, :] = row


def pick(row, lane, at):
    return jnp.sum(jnp.where(lane == at, row, 0.0), keepdims=True)


def last_kernel(parts, base, w_vec, n_vec, solution_out, residual_out):
    gathered = parts[...]
    count = gathered.shape[0]
    lane = lane_of((8, LANES))
    total = sum(gathered[8 * i : 8 * i + 8] for i in range(count // 8))
    gamma, delta = pick(total, lane, 32), pick(total, lane, 33)
    alpha = gamma / delta
    gap = alpha - pltpu.roll(gathered, LANES - 24, 1)
    moved = gathered - gap * pltpu.roll(gathered, LANES - 8, 1)
    moved = moved + gap * gap * pltpu.roll(gathered, LANES - 16, 1)
    total = sum(moved[8 * i : 8 * i + 8] for i in range(count // 8))
    gamma_next, delta_next = pick(total, lane, 0), pick(total, lane, 1)
    beta = gamma_next / gamma
    alpha_next = gamma_next / (delta_next - beta * gamma_next / alpha)
    for layer in range(base.shape[0]):
        start, w_start = base[layer], w_vec[layer]
        residual = start - alpha * w_start
        w_next = w_start - alpha * n_vec[layer]
        solution_out[layer] = alpha * start + alpha_next * (residual + beta * start)
        residual_out[layer] = residual - alpha_next * (w_next + beta * w_start)


VMEM_SPEC = pl.BlockSpec(memory_space=pltpu.VMEM)
SMEM_SPEC = pl.BlockSpec(memory_space=pltpu.SMEM)


def pads(rows, cols):
    tiles = cols // LANES + 2
    return [
        pltpu.VMEM((2, tiles, rows + 2 * REACH, LANES), jnp.float32),
        pltpu.VMEM((2, tiles, rows + 16, LANES), jnp.float32),
    ]


def on_device(right_side, coefficient, strength_table, layer_entry, shifts):
    layers, rows, cols = right_side.shape
    count_y, count_x = lax.axis_size("gy"), lax.axis_size("gx")
    devices = count_x * count_y
    grid_shape = (rows * count_y, cols * count_x)
    params = pltpu.CompilerParams(vmem_limit_bytes=VMEM_BYTES)
    full = jax.ShapeDtypeStruct((layers, rows, cols), jnp.float32)
    edge = jax.ShapeDtypeStruct((layers, REACH, cols), jnp.float32)
    odd_y = is_odd("gy")
    low = jnp.concatenate([right_side[:, :REACH], coefficient[:, :8]], axis=1)
    high = jnp.concatenate([right_side[:, rows - REACH :], coefficient[:, rows - 8 :]], axis=1)
    rows0 = swap(jnp.where(odd_y, low, high), jnp.where(odd_y, high, low), "gy")
    cols0 = swap(*pack(right_side, coefficient, *rows0), "gx")
    scalars = (shifts, strength_table, layer_entry)

    def first(*refs):
        first_kernel(grid_shape, *refs)

    w_vec, sums, even, odd = pl.pallas_call(
        first,
        out_shape=(full, jax.ShapeDtypeStruct((3, 8, LANES), jnp.float32), edge, edge),
        in_specs=[VMEM_SPEC] * 6 + [SMEM_SPEC] * 3,
        out_specs=(VMEM_SPEC,) * 4,
        scratch_shapes=pads(rows, cols),
        compiler_params=params,
        name="first_apply",
    )(right_side, coefficient, *rows0, *cols0, *scalars)
    rows1 = swap(even, odd, "gy")
    cols1 = swap(*pack(w_vec, None, *rows1), "gx")

    def second(*refs):
        second_kernel(grid_shape, *refs)

    n_vec, parts = pl.pallas_call(
        second,
        out_shape=(full, jax.ShapeDtypeStruct((devices, LANES), jnp.float32)),
        in_specs=[VMEM_SPEC] * 12 + [SMEM_SPEC] * 3,
        out_specs=(VMEM_SPEC,) * 2,
        scratch_shapes=pads(rows, cols),
        compiler_params=params,
        name="second_apply",
    )(right_side, w_vec, coefficient, *rows1, *cols1, *rows0, *cols0, sums, *scalars)
    gathered = lax.all_to_all(parts, ("gx", "gy"), 0, 0, tiled=True)
    steps = 4
    block = pl.BlockSpec((layers, rows // steps, cols), lambda i: (0, i, 0))
    return pl.pallas_call(
        last_kernel,
        grid=(steps,),
        out_shape=(full, full),
        in_specs=[pl.BlockSpec((devices, LANES), lambda i: (0, 0))] + [block] * 3,
        out_specs=(block, block),
        compiler_params=params,
        name="last_update",
    )(gathered, right_side, w_vec, n_vec)


def solution(mesh):
    placed = (P(None, "gy", "gx"), P(None, "gy", "gx"), P(), P(), P())
    return jax.shard_map(
        on_device,
        mesh=mesh,
        in_specs=placed,
        out_specs=(P(None, "gy", "gx"), P(None, "gy", "gx")),
        check_vma=False,
    )
```

time: 371 us -> 92.5 us (0.25)
  blocking collectives: 162 us -> 33.6 us
  between operations: 67.2 us -> 0.74 us
  starting transfers between devices: 56 us -> 19.6 us
  other arithmetic: 35 us -> 0.06 us
  local copies, waits for them, and re-layouts: 22.8 us -> 2.12 us
  Pallas kernels: 0 us -> 18.3 us
  waiting for transfers between devices: 26.1 us -> 17.9 us
    psum x2 -> x0, blocking collectives: 162 us -> none  [inner_sums(): return lax.psum((pair[0], pair[1]), ('gx', 'gy'))]
    ppermute x20 -> x8, starting transfers between devices: 56 us -> 19.6 us  [the longest x4 11.8 us: swap(): lax.ppermute(odd, axis, odd_swap(count))]
    all_to_all x0 -> x1, blocking collectives: none -> 33.6 us  [on_device(): gathered = lax.all_to_all(parts, ('gx', 'gy'), 0, 0, tiled=True)]
    pallas_call x0 -> x5, Pallas kernels: none -> 18.3 us  [the longest x1 7.1 us: on_device(): pl.pallas_call(second, out_shape=(full, jax.ShapeDtypeStruct((devices, LA...]
    slice x17 -> x2, local copies, waits for them, and re-layouts: 12.6 us -> 2 us  [on_device(): low = jnp.concatenate([right_side[:, :REACH], coefficient[:, :8]], axis=1)]
    concatenate x6 -> x0, other arithmetic: 9.65 us -> none  [with_halo(): x = jnp.concatenate([before, x, after], axis=dim)]
    reduce_sum x3 -> x0, other arithmetic: 8.97 us -> none  [the longest x2 8.79 us: inner_sums(): pair = (jnp.sum(residual * residual), jnp.sum(w_vec * residual))]
    ppermute x20 -> x8, waiting for transfers between devices: 26.1 us -> 17.9 us  [the longest x4 9.51 us: swap(): lax.ppermute(even, axis, even_swap(count))]
  transfers between devices with their start and end apart: 20 -> 8, of which waited for: 9 -> 4; matrix products, arithmetic and copies ran while one was open for 2% -> 0% of each run, Pallas kernels for 0% -> 0%
where the time goes in v1:
time: 92.5 us; the launch traced here: 92.2 us
  blocking collectives  33.6 us (36%)
  starting transfers between devices  19.6 us (21%)
  Pallas kernels  18.3 us (20%)
  waiting for transfers between devices  17.9 us (19%)
  local copies, waits for them, and re-layouts  2.12 us (2%)
    all_to_all x1, blocking collectives, on_device(): gathered = lax.all_to_all(parts, ('gx', 'gy'), 0, 0, tiled=True)  33.6 us
    ppermute x4, starting transfers between devices, swap(): lax.ppermute(odd, axis, odd_swap(count))  11.8 us
    ppermute x4, waiting for transfers between devices, swap(): lax.ppermute(even, axis, even_swap(count))  9.51 us
    ppermute x4, waiting for transfers between devices, swap(): lax.ppermute(odd, axis, odd_swap(count))  8.37 us
    ppermute x4, starting transfers between devices, swap(): lax.ppermute(even, axis, even_swap(count))  7.75 us
    pallas_call x1, Pallas kernels, on_device(): pl.pallas_call(second, out_shape=(full, jax.ShapeDtypeStruct((devices, LA...  7.1 us
    pallas_call x1, Pallas kernels, on_device(): pl.pallas_call(first, out_shape=(full, jax.ShapeDtypeStruct((3, 8, LANES)...  6.83 us
    pallas_call x1, Pallas kernels, on_device(): pl.pallas_call(last_kernel, grid=(steps,), out_shape=(full, full), in_spe...  3.1 us
  transfers between devices with their start and end apart: 8, of which 4 were waited for; matrix products, arithmetic and copies ran while one was open for 0% of the time, Pallas kernels for 0%

profile of v1, /device:TPU:1, one launch (start us, length us, event | category | flops | bytes accessed | tf_op | source)
XLA Modules:
  0.0 92.2 jit_solution(2887026745962583447)
XLA Ops:
  0.6 0.8 fusion.3
  1.4 0.0 copy-start
  1.4 0.0 copy-start.1
  1.4 1.2 %fusion.2 = (f32[2,64,512]{2,1,0:T(8,128)S(1)}, f32[2,64,512]{2,1,0:T(8,128)S(1)}) fusion(f32[2,256,512]{2,1,0:T(8,128)} %base.1), kind=kLoop, calls=%fused_computation.4 | loop fusion | bytes 1048576 | tf_op jit(solution)/shard_map/slice | solution.py:348
  2.6 0.1 fusion
  2.7 0.7 collective-permute-start.1
  3.4 4.6 %collective-permute-start = (f32[2,72,512]{2,1,0:T(8,128)S(1)}, f32[2,72,512]{2,1,0:T(8,128)S(1)}, u32[]{:S(2)}, u32[]{:S(2)}) collective-permute-start(f32[2,72,512]{2,1,0:T(8,128)S(1)} %get-tuple-element.27), channel_id=1, source_target_pairs={{0,1},{1,0},{2,3},{3,2},{4,5},{5,4},{6,7},{7,6},{8,9},{9,8},{10,11... | collective-permute-start | bytes 884744 | tf_op jit(solution)/shard_map/ppermute | solution.py:30
  8.0 0.0 collective-permute-done.1.refs_3_.refs_8_
  8.0 6.4 %collective-permute-done.refs_2_.refs_7_ = f32[2,72,512]{2,1,0:T(8,128)S(1)} collective-permute-done((f32[2,72,512]{2,1,0:T(8,128)S(1)}, f32[2,72,512]{2,1,0:T(8,128)S(1)}, u32[]{:S(2)}, u32[]{:S(2)}) %collective-permute-start) | collective-permute-done | bytes 294944 | tf_op jit(solution)/shard_map/ppermute | solution.py:30
  14.4 0.0 copy-done
  14.4 0.0 copy-done.1
  14.4 1.1 %pack_columns.2 = (f32[640,128]{1,0:T(8,128)}, f32[640,128]{1,0:T(8,128)}) custom-call(f32[2,256,512]{2,1,0:T(8,128)S(1)} %copy-done, f32[2,256,512]{2,1,0:T(8,128)S(1)} %copy-done.1, f32[2,72,512]{2,1,0:T(8,128)S(1)} %collective-permute-done.refs_2_.refs_7_, f32[2,72,512]{2,1,0:T(8,128)S(1)} %collective-permute-done.1.refs_3_.refs_8_), custom_call_target="tpu_custom_call" | custom-call | tf_op jit(solution)/shard_map/pack_columns/pallas_call | solution.py:93
  15.5 0.0 copy-start.4
  15.5 1.5 %collective-permute-start.2 = (f32[640,128]{1,0:T(8,128)}, f32[640,128]{1,0:T(8,128)S(1)}, u32[]{:S(2)}, u32[]{:S(2)}) collective-permute-start(f32[640,128]{1,0:T(8,128)} %get-tuple-element.12), channel_id=1, source_target_pairs={{0,16},{16,0},{32,48},{48,32},{64,80},{80,64},{96,112},{112,96},{1... | collective-permute-start | bytes 983048 | tf_op jit(solution)/shard_map/ppermute | solution.py:30
  17.0 0.0 copy-start.2
  17.0 0.0 copy-start.3
  17.0 3.6 %collective-permute-start.3 = (f32[640,128]{1,0:T(8,128)}, f32[640,128]{1,0:T(8,128)S(1)}, u32[]{:S(2)}, u32[]{:S(2)}) collective-permute-start(f32[640,128]{1,0:T(8,128)} %get-tuple-element.13), channel_id=1, source_target_pairs={{16,32},{32,16},{48,64},{64,48},{80,96},{96,80},{112,128},{128,112... | collective-permute-start | bytes 983048 | tf_op jit(solution)/shard_map/ppermute | solution.py:31
  20.6 0.0 copy-done.4
  20.6 0.1 copy.9.refs_6_.refs_12_
  20.7 0.0 collective-permute-done.2.refs_4_.refs_9_
  20.7 5.0 %collective-permute-done.3.refs_5_.refs_10_ = f32[640,128]{1,0:T(8,128)S(1)} collective-permute-done((f32[640,128]{1,0:T(8,128)}, f32[640,128]{1,0:T(8,128)S(1)}, u32[]{:S(2)}, u32[]{:S(2)}) %collective-permute-start.3) | collective-permute-done | bytes 327712 | tf_op jit(solution)/shard_map/ppermute | solution.py:31
  25.7 0.0 copy-done.2
  25.7 0.0 copy-done.3
  25.7 6.8 %first_apply.1 = (f32[2,256,512]{2,1,0:T(8,128)S(1)}, f32[3,8,128]{2,1,0:T(8,128)S(1)}, f32[2,64,512]{2,1,0:T(8,128)S(1)}, f32[2,64,512]{2,1,0:T(8,128)S(1)}) custom-call(f32[2,256,512]{2,1,0:T(8,128)S(1)} %copy-done, f32[2,256,512]{2,1,0:T(8,128)S(1)} %copy-done.1, f32[2,72,512]{2,1,0:T(8,128)S(1)} %collective-permute-done.refs_2_.refs_7_, ...), custom_call_target="tpu_custom_call" | custom-call | tf_op jit(solution)/shard_map/first_apply/pallas_call | solution.py:357
  32.6 1.5 %collective-permute-start.4 = (f32[2,64,512]{2,1,0:T(8,128)S(1)}, f32[2,64,512]{2,1,0:T(8,128)S(1)}, u32[]{:S(2)}, u32[]{:S(2)}) collective-permute-start(f32[2,64,512]{2,1,0:T(8,128)S(1)} %get-tuple-element.15), channel_id=1, source_target_pairs={{0,1},{1,0},{2,3},{3,2},{4,5},{5,4},{6,7},{7,6},{8,9},{9,8},{10,11... | collective-permute-start | bytes 786440 | tf_op jit(solution)/shard_map/ppermute | solution.py:30
  34.1 0.7 collective-permute-start.5
  34.8 3.1 %collective-permute-done.4.refs_1_.refs_3_ = f32[2,64,512]{2,1,0:T(8,128)S(1)} collective-permute-done((f32[2,64,512]{2,1,0:T(8,128)S(1)}, f32[2,64,512]{2,1,0:T(8,128)S(1)}, u32[]{:S(2)}, u32[]{:S(2)}) %collective-permute-start.4) | collective-permute-done | bytes 262176 | tf_op jit(solution)/shard_map/ppermute | solution.py:30
  37.9 0.0 collective-permute-done.5.refs_2_.refs_4_
  37.9 0.2 pack_columns.3
  38.1 0.1 collective-permute-start.6
  38.2 6.9 %collective-permute-start.7 = (f32[384,128]{1,0:T(8,128)S(1)}, f32[384,128]{1,0:T(8,128)S(1)}, u32[]{:S(2)}, u32[]{:S(2)}) collective-permute-start(f32[384,128]{1,0:T(8,128)S(1)} %get-tuple-element.18), channel_id=1, source_target_pairs={{16,32},{32,16},{48,64},{64,48},{80,96},{96,80},{112,128},{128,112... | collective-permute-start | bytes 589832 | tf_op jit(solution)/shard_map/ppermute | solution.py:31
  45.1 0.0 collective-permute-done.6.refs_5_
  45.1 3.3 %collective-permute-done.7.refs_6_ = f32[384,128]{1,0:T(8,128)S(1)} collective-permute-done((f32[384,128]{1,0:T(8,128)S(1)}, f32[384,128]{1,0:T(8,128)S(1)}, u32[]{:S(2)}, u32[]{:S(2)}) %collective-permute-start.7) | collective-permute-done | bytes 196640 | tf_op jit(solution)/shard_map/ppermute | solution.py:31
  48.5 7.1 %second_apply.1 = (f32[2,256,512]{2,1,0:T(8,128)S(1)}, f32[256,128]{1,0:T(8,128)S(1)}) custom-call(f32[2,256,512]{2,1,0:T(8,128)S(1)} %copy-done, f32[2,256,512]{2,1,0:T(8,128)S(1)} %get-tuple-element.14.refs_0_.refs_1_.w_vec, f32[2,256,512]{2,1,0:T(8,128)S(1)} %copy-done.1, f32[2,64,512]{2,1,0:T(8,128)S(1)} %collective-permute-done.4.refs_1_.refs_3_, ...), custom_call_target="tpu_custom_call" | custom-call | tf_op jit(solution)/shard_map/second_apply/pallas_call | solution.py:372
  55.6 33.6 %all_to_all.11 = f32[256,1,128]{2,1,0:T(1,128)S(1)} all-to-all(f32[256,1,128]{2,1,0:T(1,128)S(1)} %bitcast.5), channel_id=1, replica_groups=mesh['gx'=16,'gy'=16] {'gx','gy'}, dimensions={0} | all-to-all | bytes 262144 | tf_op jit(solution)/shard_map/all_to_all | solution.py:381
  89.1 3.1 %last_update.1 = (f32[2,256,512]{2,1,0:T(8,128)}, f32[2,256,512]{2,1,0:T(8,128)}) custom-call(f32[256,128]{1,0:T(8,128)S(1)} %bitcast.4, f32[2,256,512]{2,1,0:T(8,128)S(1)} %copy-done, f32[2,256,512]{2,1,0:T(8,128)S(1)} %get-tuple-element.14.refs_0_.refs_1_.w_vec, f32[2,256,512]{2,1,0:T(8,128)S(1)} %get-tuple-element.21.n_vec), custom_call_target="tpu_custom_call" | custom-call | tf_op jit(solution)/shard_map/last_update/pallas_call | solution.py:384
Async XLA Ops:
  1.4 13.0 %copy-start = (f32[2,256,512]{2,1,0:T(8,128)S(1)}, f32[2,256,512]{2,1,0:T(8,128)}, u32[]{:S(2)}) copy-start(f32[2,256,512]{2,1,0:T(8,128)} %base.1) | copy-start | bytes 3145732
  1.4 13.0 %copy-start.1 = (f32[2,256,512]{2,1,0:T(8,128)S(1)}, f32[2,256,512]{2,1,0:T(8,128)}, u32[]{:S(2)}) copy-start(f32[2,256,512]{2,1,0:T(8,128)} %refs_2_.1) | copy-start | bytes 3145732
  2.7 5.3 %collective-permute-start.1 = (f32[2,72,512]{2,1,0:T(8,128)S(1)}, f32[2,72,512]{2,1,0:T(8,128)S(1)}, u32[]{:S(2)}, u32[]{:S(2)}) collective-permute-start(f32[2,72,512]{2,1,0:T(8,128)S(1)} %get-tuple-element.26), channel_id=1, source_target_pairs={{1,2},{2,1},{3,4},{4,3},{5,6},{6,5},{7,8},{8,7},{9,10},{10,9},{11,... | collective-permute-start | bytes 884744 | tf_op jit(solution)/shard_map/ppermute | solution.py:31
  3.4 11.0 %collective-permute-start = (f32[2,72,512]{2,1,0:T(8,128)S(1)}, f32[2,72,512]{2,1,0:T(8,128)S(1)}, u32[]{:S(2)}, u32[]{:S(2)}) collective-permute-start(f32[2,72,512]{2,1,0:T(8,128)S(1)} %get-tuple-element.27), channel_id=1, source_target_pairs={{0,1},{1,0},{2,3},{3,2},{4,5},{5,4},{6,7},{7,6},{8,9},{9,8},{10,11... | collective-permute-start | bytes 884744 | tf_op jit(solution)/shard_map/ppermute | solution.py:30
  15.5 5.1 %copy-start.4 = (s32[6,2,2]{0,2,1:T(2,128)S(1)}, s32[6,2,2]{0,2,1:T(2,128)}, u32[]{:S(2)}) copy-start(s32[6,2,2]{0,2,1:T(2,128)} %param.9) | copy-start | bytes 292
  15.5 5.2 %collective-permute-start.2 = (f32[640,128]{1,0:T(8,128)}, f32[640,128]{1,0:T(8,128)S(1)}, u32[]{:S(2)}, u32[]{:S(2)}) collective-permute-start(f32[640,128]{1,0:T(8,128)} %get-tuple-element.12), channel_id=1, source_target_pairs={{0,16},{16,0},{32,48},{48,32},{64,80},{80,64},{96,112},{112,96},{1... | collective-permute-start | bytes 983048 | tf_op jit(solution)/shard_map/ppermute | solution.py:30
  17.0 8.7 %copy-start.2 = (f32[35]{0:T(128)S(1)}, f32[35]{0:T(128)}, u32[]{:S(2)}) copy-start(f32[35]{0:T(128)} %refs_13_.1) | copy-start | bytes 424
  17.0 8.7 %copy-start.3 = (s32[2]{0:T(128)S(1)}, s32[2]{0:T(128)}, u32[]{:S(2)}) copy-start(s32[2]{0:T(128)} %refs_14_.1) | copy-start | bytes 28
  17.0 8.7 %collective-permute-start.3 = (f32[640,128]{1,0:T(8,128)}, f32[640,128]{1,0:T(8,128)S(1)}, u32[]{:S(2)}, u32[]{:S(2)}) collective-permute-start(f32[640,128]{1,0:T(8,128)} %get-tuple-element.13), channel_id=1, source_target_pairs={{16,32},{32,16},{48,64},{64,48},{80,96},{96,80},{112,128},{128,112... | collective-permute-start | bytes 983048 | tf_op jit(solution)/shard_map/ppermute | solution.py:31
  32.6 5.3 %collective-permute-start.4 = (f32[2,64,512]{2,1,0:T(8,128)S(1)}, f32[2,64,512]{2,1,0:T(8,128)S(1)}, u32[]{:S(2)}, u32[]{:S(2)}) collective-permute-start(f32[2,64,512]{2,1,0:T(8,128)S(1)} %get-tuple-element.15), channel_id=1, source_target_pairs={{0,1},{1,0},{2,3},{3,2},{4,5},{5,4},{6,7},{7,6},{8,9},{9,8},{10,11... | collective-permute-start | bytes 786440 | tf_op jit(solution)/shard_map/ppermute | solution.py:30
  34.1 3.8 %collective-permute-start.5 = (f32[2,64,512]{2,1,0:T(8,128)S(1)}, f32[2,64,512]{2,1,0:T(8,128)S(1)}, u32[]{:S(2)}, u32[]{:S(2)}) collective-permute-start(f32[2,64,512]{2,1,0:T(8,128)S(1)} %get-tuple-element.16), channel_id=1, source_target_pairs={{1,2},{2,1},{3,4},{4,3},{5,6},{6,5},{7,8},{8,7},{9,10},{10,9},{11,... | collective-permute-start | bytes 786440 | tf_op jit(solution)/shard_map/ppermute | solution.py:31
  38.1 7.0 %collective-permute-start.6 = (f32[384,128]{1,0:T(8,128)S(1)}, f32[384,128]{1,0:T(8,128)S(1)}, u32[]{:S(2)}, u32[]{:S(2)}) collective-permute-start(f32[384,128]{1,0:T(8,128)S(1)} %get-tuple-element.17), channel_id=1, source_target_pairs={{0,16},{16,0},{32,48},{48,32},{64,80},{80,64},{96,112},{112,96},{1... | collective-permute-start | bytes 589832 | tf_op jit(solution)/shard_map/ppermute | solution.py:30
  38.2 10.3 %collective-permute-start.7 = (f32[384,128]{1,0:T(8,128)S(1)}, f32[384,128]{1,0:T(8,128)S(1)}, u32[]{:S(2)}, u32[]{:S(2)}) collective-permute-start(f32[384,128]{1,0:T(8,128)S(1)} %get-tuple-element.18), channel_id=1, source_target_pairs={{16,32},{32,16},{48,64},{64,48},{80,96},{96,80},{112,128},{128,112... | collective-permute-start | bytes 589832 | tf_op jit(solution)/shard_map/ppermute | solution.py:31

commit v2 on v1

--- a/solution.py
+++ b/solution.py
@@ -8,7 +8,7 @@
 REACH = 64
 LANES = 128
 HALF = 64
-CHUNK = 16
+CHUNK = 32
 VMEM_BYTES = 32 * 1024 * 1024
 
 
@@ -81,13 +81,14 @@
         store_packed(even_out, odd_out, odd_x, 2 * REACH + rows, packed[0], packed[1])
 
 
-def pack(field, coeff, even_rows, odd_rows):
+def pack(field, coeff, even_rows, odd_rows, after):
     rows = field.shape[1]
     total = rows + 2 * REACH + (0 if coeff is None else rows)
     out = jax.ShapeDtypeStruct((total, LANES), jnp.float32)
-    operands = [field] + ([] if coeff is None else [coeff]) + [even_rows, odd_rows]
-
-    def kernel(*refs):
+    operands = [after, field] + ([] if coeff is None else [coeff]) + [even_rows, odd_rows]
+
+    def kernel(unused, *refs):
+        del unused
         pack_kernel(coeff is not None, *refs)
 
     return pl.pallas_call(
@@ -100,49 +101,23 @@
     )(*operands)
 
 
-def fill_field(pad, field, even_rows, odd_rows, even_cols, odd_cols):
-    rows, cols = field.shape[1:]
-    odd_x, odd_y = is_odd("gx"), is_odd("gy")
-    tiles = cols // LANES
+def zero_rim(pad, depth, rows):
+    tiles = pad.shape[1]
     for layer in range(2):
         for tile in range(tiles):
+            if tile in (0, tiles - 1):
+                pad[layer, tile] = jnp.zeros(pad.shape[2:], jnp.float32)
+            else:
+                pad[layer, tile, 0:depth, :] = jnp.zeros((depth, LANES), jnp.float32)
+                pad[layer, tile, depth + rows :, :] = jnp.zeros((depth, LANES), jnp.float32)
+
+
+def fill_own(pad, depth, field):
+    rows, cols = field.shape[1:]
+    for layer in range(2):
+        for tile in range(cols // LANES):
             lanes = slice(tile * LANES, (tile + 1) * LANES)
-            pad[layer, 1 + tile, REACH : REACH + rows, :] = field[layer, :, lanes]
-            even = even_rows[layer, 0:REACH, lanes]
-            other = odd_rows[layer, 0:REACH, lanes]
-            pad[layer, 1 + tile, 0:REACH, :] = jnp.where(odd_y, even, other)
-            pad[layer, 1 + tile, REACH + rows :, :] = jnp.where(odd_y, other, even)
-    even = even_cols[0 : rows + 2 * REACH, :]
-    other = odd_cols[0 : rows + 2 * REACH, :]
-    for tile, packed in (
-        (0, jnp.where(odd_x, even, other)),
-        (1 + tiles, jnp.where(odd_x, other, even)),
-    ):
-        pad[0, tile] = packed
-        pad[1, tile] = pltpu.roll(packed, HALF, 1)
-
-
-def fill_coeff(pad, coeff, even_rows, odd_rows, even_cols, odd_cols):
-    rows, cols = coeff.shape[1:]
-    odd_x, odd_y = is_odd("gx"), is_odd("gy")
-    tiles = cols // LANES
-    for layer in range(2):
-        for tile in range(tiles):
-            lanes = slice(tile * LANES, (tile + 1) * LANES)
-            pad[layer, 1 + tile, 8 : 8 + rows, :] = coeff[layer, :, lanes]
-            even = even_rows[layer, REACH : REACH + 8, lanes]
-            other = odd_rows[layer, REACH : REACH + 8, lanes]
-            pad[layer, 1 + tile, 0:8, :] = jnp.where(odd_y, even, other)
-            pad[layer, 1 + tile, 8 + rows :, :] = jnp.where(odd_y, other, even)
-    start = rows + 2 * REACH
-    even = even_cols[start : start + rows, :]
-    other = odd_cols[start : start + rows, :]
-    for tile, packed in (
-        (0, jnp.where(odd_x, even, other)),
-        (1 + tiles, jnp.where(odd_x, other, even)),
-    ):
-        pad[0, tile, 8 : 8 + rows, :] = packed
-        pad[1, tile, 8 : 8 + rows, :] = pltpu.roll(packed, HALF, 1)
+            pad[layer, 1 + tile, depth : depth + rows, :] = field[layer, :, lanes]
 
 
 def neighbours_across(load, tiles):
@@ -155,7 +130,7 @@
     return values[1:-1], left, right
 
 
-def apply_chunk(layer, row, pad, coeff_pad, shifts, weight, field_rows, grid_shape, tile_shape):
+def apply_chunk(layer, row, pad, coeff_pad, shifts, weight, grid_shape, tile_shape):
     dirs = shifts.shape[0]
     rows, cols = tile_shape
     tiles = cols // LANES
@@ -206,12 +181,12 @@
                 mask = mask & (lane < grid_shape[1] + shift_c - first_col - tile * LANES)
             value = own[tile] + jnp.where(here, moved[tile], moved[tile + 1])
             result[tile] = result[tile] + jnp.where(mask, value, 0.0)
-    return own, result
+    return result
 
 
 def fold(parts):
     total = sum(parts[1:], parts[0])
-    pieces = [total[8 * i : 8 * i + 8] for i in range(CHUNK // 8)]
+    pieces = [total[8 * i : 8 * i + 8] for i in range(total.shape[0] // 8)]
     return sum(pieces[1:], pieces[0])
 
 
@@ -223,21 +198,181 @@
     return 0.5 * table[entry[layer]]
 
 
+def own_kernel(grid_shape, field, coeff, shifts, table, entry, out, pad, coeff_pad):
+    rows, cols = field.shape[1:]
+    zero_rim(pad, REACH, rows)
+    zero_rim(coeff_pad, 8, rows)
+    fill_own(pad, REACH, field)
+    fill_own(coeff_pad, 8, coeff)
+    for layer in range(2):
+        weight = weight_of(table, entry, layer)
+
+        def step(i, carry, layer=layer, weight=weight):
+            row = pl.multiple_of(i * CHUNK, CHUNK)
+            result = apply_chunk(
+                layer, row, pad, coeff_pad, shifts, weight, grid_shape, (rows, cols)
+            )
+            for tile, value in enumerate(result):
+                out[layer, pl.ds(row, CHUNK), tile * LANES : (tile + 1) * LANES] = value
+            return carry
+
+        lax.fori_loop(0, rows // CHUNK, step, 0)
+
+
+def rows_kernel(
+    grid_shape, before, field, coeff, even_rows, odd_rows, even_edge, odd_edge, packed, shifts,
+    table, entry, out, pad,
+):
+    del packed
+    rows, cols = field.shape[1:]
+    tiles = cols // LANES
+    odd_y = is_odd("gy")
+    first_row = lax.axis_index("gy") * rows
+    first_col = lax.axis_index("gx") * cols
+    zeros = jnp.zeros((REACH, LANES), jnp.float32)
+    for layer in range(2):
+        for side in range(2):
+            for tile in (0, tiles + 1):
+                pad[layer, side, tile, 0:REACH, :] = zeros
+                pad[layer, side, tile, REACH:, :] = zeros
+        for tile in range(tiles):
+            lanes = slice(tile * LANES, (tile + 1) * LANES)
+            even = even_rows[layer, 0:REACH, lanes]
+            other = odd_rows[layer, 0:REACH, lanes]
+            pad[layer, 0, 1 + tile, 0:REACH, :] = jnp.where(odd_y, even, other)
+            pad[layer, 0, 1 + tile, REACH:, :] = zeros
+            pad[layer, 1, 1 + tile, 0:REACH, :] = zeros
+            pad[layer, 1, 1 + tile, REACH:, :] = jnp.where(odd_y, other, even)
+    out[...] = before[...]
+    lane = lane_of((CHUNK, LANES))
+    row_at = lax.broadcasted_iota(jnp.int32, (CHUNK, LANES), 0)
+    for layer in range(2):
+        other_layer = 1 - layer
+
+        def step(i, carry, layer=layer, other_layer=other_layer):
+            part = pl.multiple_of(i * CHUNK, CHUNK)
+            totals = [[jnp.zeros((CHUNK, LANES), jnp.float32)] * tiles for _ in range(2)]
+            for direction in range(shifts.shape[0]):
+                shift_r, shift_c = shifts[direction, layer, 0], shifts[direction, layer, 1]
+                step_r = shifts[direction, other_layer, 0] - shift_r
+                start_c = LANES + shifts[direction, other_layer, 1] - shift_c
+                side = jnp.where(step_r < 0, 0, 1)
+                start_r = part + step_r + jnp.where(step_r < 0, REACH, 0)
+                row = part + jnp.where(step_r < 0, 0, rows - REACH)
+                skip = lax.shift_right_logical(start_c, 7)
+                turn = jnp.bitwise_and(start_c, LANES - 1)
+                back = jnp.bitwise_and(LANES - turn, LANES - 1)
+                moved = [
+                    pltpu.roll(
+                        pad[other_layer, side, skip + tile, pl.ds(start_r, CHUNK), :], back, 1
+                    )
+                    for tile in range(tiles + 1)
+                ]
+                here = lane < LANES - turn
+                image_row = row_at + (first_row + row - shift_r)
+                inside = (image_row >= 0) & (image_row < grid_shape[0])
+                upper = inside & (jnp.full((CHUNK, LANES), side, jnp.int32) == 0)
+                lower = inside & (jnp.full((CHUNK, LANES), side, jnp.int32) == 1)
+                for tile in range(tiles):
+                    value = jnp.where(here, moved[tile], moved[tile + 1])
+                    if tile == 0:
+                        value = jnp.where(lane >= shift_c - first_col, value, 0.0)
+                    if tile == tiles - 1:
+                        last = grid_shape[1] + shift_c - first_col - tile * LANES
+                        value = jnp.where(lane < last, value, 0.0)
+                    totals[0][tile] = totals[0][tile] + jnp.where(upper, value, 0.0)
+                    totals[1][tile] = totals[1][tile] + jnp.where(lower, value, 0.0)
+            for side, base in enumerate((0, rows - REACH)):
+                for tile in range(tiles):
+                    lanes = slice(tile * LANES, (tile + 1) * LANES)
+                    out[layer, pl.ds(base + part, CHUNK), lanes] += totals[side][tile]
+            return carry
+
+        lax.fori_loop(0, REACH // CHUNK, step, 0)
+        weight = weight_of(table, entry, layer)
+        at = lax.broadcasted_iota(jnp.int32, (8, cols), 0)
+        even = even_edge[layer, REACH : REACH + 8, :]
+        other = odd_edge[layer, REACH : REACH + 8, :]
+        even_v = [even_rows[layer, start : start + 8, :] for start in (0, REACH - 8)]
+        other_v = [odd_rows[layer, start : start + 8, :] for start in (0, REACH - 8)]
+        for start, edge_c, edge_v, spot, source in (
+            (0, jnp.where(odd_y, even, other), jnp.where(odd_y, even_v[1], other_v[1]), 0, 1),
+            (
+                rows - 8, jnp.where(odd_y, other, even), jnp.where(odd_y, other_v[0], even_v[0]),
+                7, 7,
+            ),
+        ):
+            edge_c = pltpu.roll(edge_c, source, 0)
+            edge_v = pltpu.roll(edge_v, source, 0)
+            value = field[layer, start : start + 8, :]
+            own_c = coeff[layer, start : start + 8, :]
+            extra = weight * (edge_c * value - (own_c + edge_c) * edge_v)
+            out[layer, start : start + 8, :] += jnp.where(at == spot, extra, 0.0)
+
+
+def finish_chunk(
+    grid_shape, layer, row, before, field, coeff, pad, coeff_pad, shifts, weight, odd_x,
+):
+    rows, cols = field.shape[1:]
+    tiles = cols // LANES
+    first_row = lax.axis_index("gy") * rows + row
+    first_col = lax.axis_index("gx") * cols
+    lane = lane_of((CHUNK, LANES))
+    row_at = lax.broadcasted_iota(jnp.int32, (CHUNK, LANES), 0)
+    cut = [slice(tile * LANES, (tile + 1) * LANES) for tile in range(tiles)]
+    own = [field[layer, pl.ds(row, CHUNK), lanes] for lanes in cut]
+    result = [before[layer, pl.ds(row, CHUNK), lanes] for lanes in cut]
+    ends = []
+    for tile, side, turn, spot in ((0, 0, 1, 0), (tiles - 1, 1, LANES - 1, LANES - 1)):
+        edge_v = pltpu.roll(pad[layer, side, pl.ds(REACH + row, CHUNK), :], turn, 1)
+        edge_c = pltpu.roll(coeff_pad[layer, side, pl.ds(row, CHUNK), :], turn, 1)
+        own_c = coeff[layer, pl.ds(row, CHUNK), cut[tile]]
+        extra = weight * (edge_c * own[tile] - (own_c + edge_c) * edge_v)
+        ends.append(result[tile] + jnp.where(lane == spot, extra, 0.0))
+    for direction in range(shifts.shape[0]):
+        shift_r, shift_c = shifts[direction, layer, 0], shifts[direction, layer, 1]
+        start_r = REACH + row + shifts[direction, 1 - layer, 0] - shift_r
+        step_c = shifts[direction, 1 - layer, 1] - shift_c
+        side = jnp.where(step_c < 0, 0, 1)
+        back = jnp.bitwise_and(LANES - step_c, LANES - 1)
+        moved = pltpu.roll(pad[1 - layer, side, pl.ds(start_r, CHUNK), :], back, 1)
+        image_row = row_at + (first_row - shift_r)
+        moved = jnp.where((image_row >= 0) & (image_row < grid_shape[0]), moved, 0.0)
+        low, low_end = shift_c - first_col, jnp.where(step_c < 0, -step_c, 0)
+        high = jnp.where(step_c < 0, LANES, LANES - step_c)
+        high_end = grid_shape[1] + shift_c - first_col - (tiles - 1) * LANES
+        ends[0] = ends[0] + jnp.where((lane >= low) & (lane < low_end), moved, 0.0)
+        ends[1] = ends[1] + jnp.where((lane >= high) & (lane < high_end), moved, 0.0)
+    return own, [ends[0]] + result[1:-1] + [ends[1]]
+
+
+def fill_sides(pad, coeff_pad, rows, even_cols, odd_cols, even_side, odd_side):
+    odd_x = is_odd("gx")
+    depth = rows + 2 * REACH
+    for target, even, other in (
+        (pad, even_cols[0:depth, :], odd_cols[0:depth, :]),
+        (coeff_pad, even_side[depth : depth + rows, :], odd_side[depth : depth + rows, :]),
+    ):
+        for side, packed in ((0, jnp.where(odd_x, even, other)), (1, jnp.where(odd_x, other, even))):
+            target[0, side] = packed
+            target[1, side] = pltpu.roll(packed, HALF, 1)
+
+
 def first_kernel(
-    grid_shape, field, coeff, even_rows, odd_rows, even_cols, odd_cols, shifts, table, entry,
+    grid_shape, before, field, coeff, even_cols, odd_cols, shifts, table, entry,
     out, sums, even_out, odd_out, pad, coeff_pad,
 ):
     rows, cols = field.shape[1:]
-    fill_field(pad, field, even_rows, odd_rows, even_cols, odd_cols)
-    fill_coeff(coeff_pad, coeff, even_rows, odd_rows, even_cols, odd_cols)
+    fill_sides(pad, coeff_pad, rows, even_cols, odd_cols, even_cols, odd_cols)
+    odd_x = is_odd("gx")
     carry = (jnp.zeros((8, LANES), jnp.float32),) * 3
     for layer in range(2):
         weight = weight_of(table, entry, layer)
 
         def step(i, carry, layer=layer, weight=weight):
             row = pl.multiple_of(i * CHUNK, CHUNK)
-            own, result = apply_chunk(
-                layer, row, pad, coeff_pad, shifts, weight, field, grid_shape, (rows, cols)
+            own, result = finish_chunk(
+                grid_shape, layer, row, before, field, coeff, pad, coeff_pad, shifts, weight, odd_x,
             )
             for tile, value in enumerate(result):
                 out[layer, pl.ds(row, CHUNK), tile * LANES : (tile + 1) * LANES] = value
@@ -254,12 +389,12 @@
 
 
 def second_kernel(
-    grid_shape, base, field, coeff, even_rows, odd_rows, even_cols, odd_cols, even_edge, odd_edge,
-    even_side, odd_side, sums, shifts, table, entry, out, parts, pad, coeff_pad,
+    grid_shape, base, before, field, coeff, even_cols, odd_cols, even_side, odd_side, sums, shifts,
+    table, entry, out, parts, pad, coeff_pad,
 ):
     rows, cols = field.shape[1:]
-    fill_field(pad, field, even_rows, odd_rows, even_cols, odd_cols)
-    fill_coeff(coeff_pad, coeff, even_edge, odd_edge, even_side, odd_side)
+    fill_sides(pad, coeff_pad, rows, even_cols, odd_cols, even_side, odd_side)
+    odd_x = is_odd("gx")
     gamma, delta, omega = (jnp.sum(sums[index], keepdims=True) for index in range(3))
     fit = jnp.where(omega > 0.0, delta / jnp.where(omega > 0.0, omega, 1.0), 0.0)
     fit = jnp.clip(fit, -1.0, 1.0)
@@ -269,8 +404,8 @@
 
         def step(i, carry, layer=layer, weight=weight):
             row = pl.multiple_of(i * CHUNK, CHUNK)
-            own, result = apply_chunk(
-                layer, row, pad, coeff_pad, shifts, weight, field, grid_shape, (rows, cols)
+            own, result = finish_chunk(
+                grid_shape, layer, row, before, field, coeff, pad, coeff_pad, shifts, weight, odd_x,
             )
             rest, slope = [], []
             for tile, value in enumerate(result):
@@ -328,56 +463,74 @@
 SMEM_SPEC = pl.BlockSpec(memory_space=pltpu.SMEM)
 
 
-def pads(rows, cols):
-    tiles = cols // LANES + 2
-    return [
-        pltpu.VMEM((2, tiles, rows + 2 * REACH, LANES), jnp.float32),
-        pltpu.VMEM((2, tiles, rows + 16, LANES), jnp.float32),
-    ]
+def on_tensor_core(kernel, name, operands, scalars, out_shape, scratch, microseconds):
+    many = isinstance(out_shape, tuple)
+    return pl.pallas_call(
+        kernel,
+        out_shape=out_shape,
+        in_specs=[VMEM_SPEC] * len(operands) + [SMEM_SPEC] * len(scalars),
+        out_specs=(VMEM_SPEC,) * len(out_shape) if many else VMEM_SPEC,
+        scratch_shapes=[pltpu.VMEM(shape, jnp.float32) for shape in scratch],
+        compiler_params=pltpu.CompilerParams(vmem_limit_bytes=VMEM_BYTES),
+        cost_estimate=pl.CostEstimate(
+            flops=0, bytes_accessed=3_000_000 * microseconds, transcendentals=0
+        ),
+        name=name,
+    )(*operands, *scalars)
 
 
 def on_device(right_side, coefficient, strength_table, layer_entry, shifts):
     layers, rows, cols = right_side.shape
     count_y, count_x = lax.axis_size("gy"), lax.axis_size("gx")
     devices = count_x * count_y
+    tiles = cols // LANES
     grid_shape = (rows * count_y, cols * count_x)
     params = pltpu.CompilerParams(vmem_limit_bytes=VMEM_BYTES)
     full = jax.ShapeDtypeStruct((layers, rows, cols), jnp.float32)
     edge = jax.ShapeDtypeStruct((layers, REACH, cols), jnp.float32)
+    scalars = (shifts, strength_table, layer_entry)
+    sides = [(2, 2, rows + 2 * REACH, LANES), (2, 2, rows, LANES)]
+
+    def bind(kernel):
+        def bound(*refs):
+            kernel(grid_shape, *refs)
+
+        return bound
+
+    def own_part(field):
+        return on_tensor_core(
+            bind(own_kernel), "own_part", (field, coefficient), scalars, full,
+            [(2, tiles + 2, rows + 2 * REACH, LANES), (2, tiles + 2, rows + 16, LANES)], 6,
+        )
+
+    def rows_part(before, field, around, edges, packed):
+        return on_tensor_core(
+            bind(rows_kernel), "rows_part", (before, field, coefficient, *around, *edges, packed),
+            scalars, full, [(2, 2, tiles + 2, 2 * REACH, LANES)], 3,
+        )
+
     odd_y = is_odd("gy")
     low = jnp.concatenate([right_side[:, :REACH], coefficient[:, :8]], axis=1)
     high = jnp.concatenate([right_side[:, rows - REACH :], coefficient[:, rows - 8 :]], axis=1)
     rows0 = swap(jnp.where(odd_y, low, high), jnp.where(odd_y, high, low), "gy")
-    cols0 = swap(*pack(right_side, coefficient, *rows0), "gx")
-    scalars = (shifts, strength_table, layer_entry)
-
-    def first(*refs):
-        first_kernel(grid_shape, *refs)
-
-    w_vec, sums, even, odd = pl.pallas_call(
-        first,
-        out_shape=(full, jax.ShapeDtypeStruct((3, 8, LANES), jnp.float32), edge, edge),
-        in_specs=[VMEM_SPEC] * 6 + [SMEM_SPEC] * 3,
-        out_specs=(VMEM_SPEC,) * 4,
-        scratch_shapes=pads(rows, cols),
-        compiler_params=params,
-        name="first_apply",
-    )(right_side, coefficient, *rows0, *cols0, *scalars)
+    w_own = own_part(right_side)
+    packed = pack(right_side, coefficient, *rows0, w_own)
+    cols0 = swap(*packed, "gx")
+    w_rows = rows_part(w_own, right_side, rows0, rows0, packed[0])
+    w_vec, sums, even, odd = on_tensor_core(
+        bind(first_kernel), "first_apply", (w_rows, right_side, coefficient, *cols0), scalars,
+        (full, jax.ShapeDtypeStruct((3, 8, LANES), jnp.float32), edge, edge), sides, 3,
+    )
     rows1 = swap(even, odd, "gy")
-    cols1 = swap(*pack(w_vec, None, *rows1), "gx")
-
-    def second(*refs):
-        second_kernel(grid_shape, *refs)
-
-    n_vec, parts = pl.pallas_call(
-        second,
-        out_shape=(full, jax.ShapeDtypeStruct((devices, LANES), jnp.float32)),
-        in_specs=[VMEM_SPEC] * 12 + [SMEM_SPEC] * 3,
-        out_specs=(VMEM_SPEC,) * 2,
-        scratch_shapes=pads(rows, cols),
-        compiler_params=params,
-        name="second_apply",
-    )(right_side, w_vec, coefficient, *rows1, *cols1, *rows0, *cols0, sums, *scalars)
+    n_own = own_part(w_vec)
+    packed = pack(w_vec, None, *rows1, n_own)
+    cols1 = swap(*packed, "gx")
+    n_rows = rows_part(n_own, w_vec, rows1, rows0, packed[0])
+    n_vec, parts = on_tensor_core(
+        bind(second_kernel), "second_apply",
+        (right_side, n_rows, w_vec, coefficient, *cols1, *cols0, sums), scalars,
+        (full, jax.ShapeDtypeStruct((devices, LANES), jnp.float32)), sides, 3,
+    )
     gathered = lax.all_to_all(parts, ("gx", "gy"), 0, 0, tiled=True)
     steps = 4
     block = pl.BlockSpec((layers, rows // steps, cols), lambda i: (0, i, 0))

time: 92.5 us -> 82.6 us (0.89)
  waiting for transfers between devices: 17.9 us -> 4.88 us
  Pallas kernels: 18.3 us -> 25 us
  starting transfers between devices: 19.6 us -> 16.8 us
  blocking collectives: 33.6 us -> 32.6 us
    ppermute x4, waiting for transfers between devices: 9.51 us -> 0.44 us  [swap(): lax.ppermute(even, axis, even_swap(count))]
    pallas_call x2 -> x6, Pallas kernels: 13.9 us -> 21.5 us  [on_tensor_core(): pl.pallas_call(kernel, out_shape=out_shape, in_specs=[VMEM_SPEC] * len(op...]
    ppermute x4, waiting for transfers between devices: 8.37 us -> 4.44 us  [swap(): lax.ppermute(odd, axis, odd_swap(count))]
    ppermute x4, starting transfers between devices: 7.75 us -> 6.3 us  [swap(): lax.ppermute(even, axis, even_swap(count))]
    ppermute x4, starting transfers between devices: 11.8 us -> 10.5 us  [swap(): lax.ppermute(odd, axis, odd_swap(count))]
    all_to_all x1, blocking collectives: 33.6 us -> 32.6 us  [on_device(): gathered = lax.all_to_all(parts, ('gx', 'gy'), 0, 0, tiled=True)]
  transfers between devices with their start and end apart: 8 -> 8, of which waited for: 4 -> 3; matrix products, arithmetic and copies ran while one was open for 0% -> 0% of each run, Pallas kernels for 0% -> 18%
where the time goes in v2:
time: 82.6 us; the launch traced here: 82.2 us
  blocking collectives  32.6 us (39%)
  Pallas kernels  25 us (30%)
  starting transfers between devices  16.8 us (20%)
  waiting for transfers between devices  4.88 us (6%)
  local copies, waits for them, and re-layouts  2.12 us (3%)
    all_to_all x1, blocking collectives, on_device(): gathered = lax.all_to_all(parts, ('gx', 'gy'), 0, 0, tiled=True)  32.6 us
    pallas_call x6, Pallas kernels, on_tensor_core(): pl.pallas_call(kernel, out_shape=out_shape, in_specs=[VMEM_SPEC] * len(op...  21.5 us
    ppermute x4, starting transfers between devices, swap(): lax.ppermute(odd, axis, odd_swap(count))  10.5 us
    ppermute x4, starting transfers between devices, swap(): lax.ppermute(even, axis, even_swap(count))  6.3 us
    ppermute x4, waiting for transfers between devices, swap(): lax.ppermute(odd, axis, odd_swap(count))  4.44 us
    pallas_call x1, Pallas kernels, on_device(): pl.pallas_call(last_kernel, grid=(steps,), out_shape=(full, full), in_spe...  3.1 us
    slice x2, local copies, waits for them, and re-layouts, on_device(): low = jnp.concatenate([right_side[:, :REACH], coefficient[:, :8]], axis=1)  2 us
  transfers between devices with their start and end apart: 8, of which 3 were waited for; matrix products, arithmetic and copies ran while one was open for 0% of the time, Pallas kernels for 18%

profile of v2, /device:TPU:1, one launch (start us, length us, event | category | flops | bytes accessed | tf_op | source)
XLA Modules:
  0.0 82.2 jit_solution(1264139720920436340)
XLA Ops:
  0.6 0.8 fusion.3
  1.4 0.0 copy-start
  1.4 0.0 copy-start.1
  1.4 1.2 %fusion.2 = (f32[2,64,512]{2,1,0:T(8,128)S(1)}, f32[2,64,512]{2,1,0:T(8,128)S(1)}) fusion(f32[2,256,512]{2,1,0:T(8,128)} %base.1), kind=kLoop, calls=%fused_computation.4 | loop fusion | bytes 1048576 | tf_op jit(solution)/shard_map/slice | solution.py:513
  2.6 0.1 fusion
  2.7 0.0 copy-start.4
  2.7 0.7 collective-permute-start.1
  3.4 0.0 copy-start.2
  3.4 0.0 copy-start.3
  3.4 4.6 %collective-permute-start = (f32[2,72,512]{2,1,0:T(8,128)S(1)}, f32[2,72,512]{2,1,0:T(8,128)S(1)}, u32[]{:S(2)}, u32[]{:S(2)}) collective-permute-start(f32[2,72,512]{2,1,0:T(8,128)S(1)} %get-tuple-element.27), channel_id=1, source_target_pairs={{0,1},{1,0},{2,3},{3,2},{4,5},{5,4},{6,7},{7,6},{8,9},{9,8},{10,11... | collective-permute-start | bytes 884744 | tf_op jit(solution)/shard_map/ppermute | solution.py:30
  8.0 0.0 copy-done.4
  8.0 0.1 copy.13.refs_2_.refs_8_.refs_5_.refs_9_
  8.1 0.0 copy-done
  8.1 0.0 copy-done.1
  8.1 0.0 copy-done.2
  8.1 0.0 copy-done.3
  8.1 5.8 %own_part.2.unused.refs_0_ = f32[2,256,512]{2,1,0:T(8,128)S(1)} custom-call(f32[2,256,512]{2,1,0:T(8,128)S(1)} %copy-done.1, f32[2,256,512]{2,1,0:T(8,128)S(1)} %copy-done, s32[6,2,2]{2,1,0:T(2,128)S(1)} %copy.13.refs_2_.refs_8_.refs_5_.refs_9_, f32[35]{0:T(128)S(1)} %copy-done.2, s32[2]{0:T(128)S(1)} %copy-done.3), custom_call_target="tpu_custom_call" | custom-call | bytes 18000000 | tf_op jit(solution)/shard_map/own_part/pallas_call | solution.py:468
  14.0 0.0 collective-permute-done.1.refs_3_.refs_4_.refs_6_
  14.0 0.4 collective-permute-done.refs_2_.refs_3_.refs_5_
  14.4 0.2 pack_columns.2
  14.7 5.0 %collective-permute-start.3 = (f32[640,128]{1,0:T(8,128)S(1)}, f32[640,128]{1,0:T(8,128)S(1)}, u32[]{:S(2)}, u32[]{:S(2)}) collective-permute-start(f32[640,128]{1,0:T(8,128)S(1)} %get-tuple-element.13), channel_id=1, source_target_pairs={{16,32},{32,16},{48,64},{64,48},{80,96},{96,80},{112,128},{128,112... | collective-permute-start | bytes 983048 | tf_op jit(solution)/shard_map/ppermute | solution.py:31
  19.7 0.1 collective-permute-start.2
  19.8 1.7 %rows_part.2.refs_0_ = f32[2,256,512]{2,1,0:T(8,128)S(1)} custom-call(f32[2,256,512]{2,1,0:T(8,128)S(1)} %own_part.2.unused.refs_0_, f32[2,256,512]{2,1,0:T(8,128)S(1)} %copy-done.1, f32[2,256,512]{2,1,0:T(8,128)S(1)} %copy-done, f32[2,72,512]{2,1,0:T(8,128)S(1)} %collective-permute-done.refs_2_.refs_3_.refs_5_, ...), custom_call_target="tpu_custom_call" | custom-call | bytes 9000000 | tf_op jit(solution)/shard_map/rows_part/pallas_call | solution.py:468
  21.5 2.9 %collective-permute-done.3.refs_4_.refs_7_ = f32[640,128]{1,0:T(8,128)S(1)} collective-permute-done((f32[640,128]{1,0:T(8,128)S(1)}, f32[640,128]{1,0:T(8,128)S(1)}, u32[]{:S(2)}, u32[]{:S(2)}) %collective-permute-start.3) | collective-permute-done | bytes 327712 | tf_op jit(solution)/shard_map/ppermute | solution.py:31
  24.4 0.0 collective-permute-done.2.refs_3_.refs_6_
  24.4 3.0 %first_apply.1 = (f32[2,256,512]{2,1,0:T(8,128)S(1)}, f32[3,8,128]{2,1,0:T(8,128)S(1)}, f32[2,64,512]{2,1,0:T(8,128)S(1)}, f32[2,64,512]{2,1,0:T(8,128)S(1)}) custom-call(f32[2,256,512]{2,1,0:T(8,128)S(1)} %rows_part.2.refs_0_, f32[2,256,512]{2,1,0:T(8,128)S(1)} %copy-done.1, f32[2,256,512]{2,1,0:T(8,128)S(1)} %copy-done, ...), custom_call_target="tpu_custom_call" | custom-call | bytes 9000000 | tf_op jit(solution)/shard_map/first_apply/pallas_call | solution.py:468
  27.4 1.5 %collective-permute-start.4 = (f32[2,64,512]{2,1,0:T(8,128)S(1)}, f32[2,64,512]{2,1,0:T(8,128)S(1)}, u32[]{:S(2)}, u32[]{:S(2)}) collective-permute-start(f32[2,64,512]{2,1,0:T(8,128)S(1)} %get-tuple-element.15), channel_id=1, source_target_pairs={{0,1},{1,0},{2,3},{3,2},{4,5},{5,4},{6,7},{7,6},{8,9},{9,8},{10,11... | collective-permute-start | bytes 786440 | tf_op jit(solution)/shard_map/ppermute | solution.py:30
  29.0 0.7 collective-permute-start.5
  29.6 5.9 %own_part.3.unused.refs_0_ = f32[2,256,512]{2,1,0:T(8,128)S(1)} custom-call(f32[2,256,512]{2,1,0:T(8,128)S(1)} %get-tuple-element.14.refs_0_.refs_1_.refs_2_.w_vec, f32[2,256,512]{2,1,0:T(8,128)S(1)} %copy-done, s32[6,2,2]{2,1,0:T(2,128)S(1)} %copy.13.refs_2_.refs_8_.refs_5_.refs_9_, f32[35]{0:T(128)S(1)} %copy-done.2, s32[2]{0:T(128)S(1)} %copy-done.3), custom_call_target="tpu_custom_call" | custom-call | bytes 18000000 | tf_op jit(solution)/shard_map/own_part/pallas_call | solution.py:468
  35.5 0.0 collective-permute-done.4.refs_1_.refs_3_
  35.5 0.0 collective-permute-done.5.refs_2_.refs_4_
  35.5 0.2 pack_columns.3
  35.7 4.1 %collective-permute-start.7 = (f32[384,128]{1,0:T(8,128)S(1)}, f32[384,128]{1,0:T(8,128)S(1)}, u32[]{:S(2)}, u32[]{:S(2)}) collective-permute-start(f32[384,128]{1,0:T(8,128)S(1)} %get-tuple-element.18), channel_id=1, source_target_pairs={{16,32},{32,16},{48,64},{64,48},{80,96},{96,80},{112,128},{128,112... | collective-permute-start | bytes 589832 | tf_op jit(solution)/shard_map/ppermute | solution.py:31
  39.9 0.1 collective-permute-start.6
  40.0 1.7 %rows_part.3.refs_1_ = f32[2,256,512]{2,1,0:T(8,128)S(1)} custom-call(f32[2,256,512]{2,1,0:T(8,128)S(1)} %own_part.3.unused.refs_0_, f32[2,256,512]{2,1,0:T(8,128)S(1)} %get-tuple-element.14.refs_0_.refs_1_.refs_2_.w_vec, f32[2,256,512]{2,1,0:T(8,128)S(1)} %copy-done, f32[2,64,512]{2,1,0:T(8,128)S(1)} %collective-permute-done.4.refs_1_.refs_3_, ...), custom_call_target="tpu_custom_call" | custom-call | bytes 9000000 | tf_op jit(solution)/shard_map/rows_part/pallas_call | solution.py:468
  41.7 1.5 %collective-permute-done.7.refs_5_ = f32[384,128]{1,0:T(8,128)S(1)} collective-permute-done((f32[384,128]{1,0:T(8,128)S(1)}, f32[384,128]{1,0:T(8,128)S(1)}, u32[]{:S(2)}, u32[]{:S(2)}) %collective-permute-start.7) | collective-permute-done | bytes 196640 | tf_op jit(solution)/shard_map/ppermute | solution.py:31
  43.2 0.0 collective-permute-done.6.refs_4_
  43.2 3.3 %second_apply.1 = (f32[2,256,512]{2,1,0:T(8,128)S(1)}, f32[256,128]{1,0:T(8,128)S(1)}) custom-call(f32[2,256,512]{2,1,0:T(8,128)S(1)} %copy-done.1, f32[2,256,512]{2,1,0:T(8,128)S(1)} %rows_part.3.refs_1_, f32[2,256,512]{2,1,0:T(8,128)S(1)} %get-tuple-element.14.refs_0_.refs_1_.refs_2_.w_vec, f32[2,256,512]{2,1,0:T(8,128)S(1)} %copy-done, ...), custom_call_target="tpu_custom_call" | custom-call | bytes 9000000 | tf_op jit(solution)/shard_map/second_apply/pallas_call | solution.py:468
  46.5 32.6 %all_to_all.11 = f32[256,1,128]{2,1,0:T(1,128)S(1)} all-to-all(f32[256,1,128]{2,1,0:T(1,128)S(1)} %bitcast.5), channel_id=1, replica_groups=mesh['gx'=16,'gy'=16] {'gx','gy'}, dimensions={0} | all-to-all | bytes 262144 | tf_op jit(solution)/shard_map/all_to_all | solution.py:534
  79.1 3.1 %last_update.1 = (f32[2,256,512]{2,1,0:T(8,128)}, f32[2,256,512]{2,1,0:T(8,128)}) custom-call(f32[256,128]{1,0:T(8,128)S(1)} %bitcast.4, f32[2,256,512]{2,1,0:T(8,128)S(1)} %copy-done.1, f32[2,256,512]{2,1,0:T(8,128)S(1)} %get-tuple-element.14.refs_0_.refs_1_.refs_2_.w_vec, f32[2,256,512]{2,1,0:T(8,128)S(1)} %get-tuple-element.21.n_vec), custom_call_target="tpu_custom_call" | custom-call | tf_op jit(solution)/shard_map/last_update/pallas_call | solution.py:537
Async XLA Ops:
  1.4 6.7 %copy-start = (f32[2,256,512]{2,1,0:T(8,128)S(1)}, f32[2,256,512]{2,1,0:T(8,128)}, u32[]{:S(2)}) copy-start(f32[2,256,512]{2,1,0:T(8,128)} %refs_3_.5) | copy-start | bytes 3145732
  1.4 6.7 %copy-start.1 = (f32[2,256,512]{2,1,0:T(8,128)S(1)}, f32[2,256,512]{2,1,0:T(8,128)}, u32[]{:S(2)}) copy-start(f32[2,256,512]{2,1,0:T(8,128)} %base.1) | copy-start | bytes 3145732
  2.7 5.3 %copy-start.4 = (s32[6,2,2]{0,2,1:T(2,128)S(1)}, s32[6,2,2]{0,2,1:T(2,128)}, u32[]{:S(2)}) copy-start(s32[6,2,2]{0,2,1:T(2,128)} %param.9) | copy-start | bytes 292
  2.7 11.3 %collective-permute-start.1 = (f32[2,72,512]{2,1,0:T(8,128)S(1)}, f32[2,72,512]{2,1,0:T(8,128)S(1)}, u32[]{:S(2)}, u32[]{:S(2)}) collective-permute-start(f32[2,72,512]{2,1,0:T(8,128)S(1)} %get-tuple-element.26), channel_id=1, source_target_pairs={{1,2},{2,1},{3,4},{4,3},{5,6},{6,5},{7,8},{8,7},{9,10},{10,9},{11,... | collective-permute-start | bytes 884744 | tf_op jit(solution)/shard_map/ppermute | solution.py:31
  3.4 4.7 %copy-start.2 = (f32[35]{0:T(128)S(1)}, f32[35]{0:T(128)}, u32[]{:S(2)}) copy-start(f32[35]{0:T(128)} %refs_10_.5) | copy-start | bytes 424
  3.4 4.7 %copy-start.3 = (s32[2]{0:T(128)S(1)}, s32[2]{0:T(128)}, u32[]{:S(2)}) copy-start(s32[2]{0:T(128)} %refs_11_.1) | copy-start | bytes 28
  3.4 11.0 %collective-permute-start = (f32[2,72,512]{2,1,0:T(8,128)S(1)}, f32[2,72,512]{2,1,0:T(8,128)S(1)}, u32[]{:S(2)}, u32[]{:S(2)}) collective-permute-start(f32[2,72,512]{2,1,0:T(8,128)S(1)} %get-tuple-element.27), channel_id=1, source_target_pairs={{0,1},{1,0},{2,3},{3,2},{4,5},{5,4},{6,7},{7,6},{8,9},{9,8},{10,11... | collective-permute-start | bytes 884744 | tf_op jit(solution)/shard_map/ppermute | solution.py:30
  14.7 9.7 %collective-permute-start.3 = (f32[640,128]{1,0:T(8,128)S(1)}, f32[640,128]{1,0:T(8,128)S(1)}, u32[]{:S(2)}, u32[]{:S(2)}) collective-permute-start(f32[640,128]{1,0:T(8,128)S(1)} %get-tuple-element.13), channel_id=1, source_target_pairs={{16,32},{32,16},{48,64},{64,48},{80,96},{96,80},{112,128},{128,112... | collective-permute-start | bytes 983048 | tf_op jit(solution)/shard_map/ppermute | solution.py:31
  19.7 4.7 %collective-permute-start.2 = (f32[640,128]{1,0:T(8,128)S(1)}, f32[640,128]{1,0:T(8,128)S(1)}, u32[]{:S(2)}, u32[]{:S(2)}) collective-permute-start(f32[640,128]{1,0:T(8,128)S(1)} %get-tuple-element.12.refs_7_), channel_id=1, source_target_pairs={{0,16},{16,0},{32,48},{48,32},{64,80},{80,64},{96,112},{112,96},{1... | collective-permute-start | bytes 983048 | tf_op jit(solution)/shard_map/ppermute | solution.py:30
  27.4 8.1 %collective-permute-start.4 = (f32[2,64,512]{2,1,0:T(8,128)S(1)}, f32[2,64,512]{2,1,0:T(8,128)S(1)}, u32[]{:S(2)}, u32[]{:S(2)}) collective-permute-start(f32[2,64,512]{2,1,0:T(8,128)S(1)} %get-tuple-element.15), channel_id=1, source_target_pairs={{0,1},{1,0},{2,3},{3,2},{4,5},{5,4},{6,7},{7,6},{8,9},{9,8},{10,11... | collective-permute-start | bytes 786440 | tf_op jit(solution)/shard_map/ppermute | solution.py:30
  29.0 6.5 %collective-permute-start.5 = (f32[2,64,512]{2,1,0:T(8,128)S(1)}, f32[2,64,512]{2,1,0:T(8,128)S(1)}, u32[]{:S(2)}, u32[]{:S(2)}) collective-permute-start(f32[2,64,512]{2,1,0:T(8,128)S(1)} %get-tuple-element.16), channel_id=1, source_target_pairs={{1,2},{2,1},{3,4},{4,3},{5,6},{6,5},{7,8},{8,7},{9,10},{10,9},{11,... | collective-permute-start | bytes 786440 | tf_op jit(solution)/shard_map/ppermute | solution.py:31
  35.7 7.5 %collective-permute-start.7 = (f32[384,128]{1,0:T(8,128)S(1)}, f32[384,128]{1,0:T(8,128)S(1)}, u32[]{:S(2)}, u32[]{:S(2)}) collective-permute-start(f32[384,128]{1,0:T(8,128)S(1)} %get-tuple-element.18), channel_id=1, source_target_pairs={{16,32},{32,16},{48,64},{64,48},{80,96},{96,80},{112,128},{128,112... | collective-permute-start | bytes 589832 | tf_op jit(solution)/shard_map/ppermute | solution.py:31
  39.9 3.3 %collective-permute-start.6 = (f32[384,128]{1,0:T(8,128)S(1)}, f32[384,128]{1,0:T(8,128)S(1)}, u32[]{:S(2)}, u32[]{:S(2)}) collective-permute-start(f32[384,128]{1,0:T(8,128)S(1)} %get-tuple-element.17.refs_7_), channel_id=1, source_target_pairs={{0,16},{16,0},{32,48},{48,32},{64,80},{80,64},{96,112},{112,96},{1... | collective-permute-start | bytes 589832 | tf_op jit(solution)/shard_map/ppermute | solution.py:30

commit v3 on v2

--- a/solution.py
+++ b/solution.py
@@ -9,7 +9,11 @@
 LANES = 128
 HALF = 64
 CHUNK = 32
+PIECES = 4
 VMEM_BYTES = 32 * 1024 * 1024
+EDGE_BYTES = 62 * 1024 * 1024
+VMEM_SPEC = pl.BlockSpec(memory_space=pltpu.VMEM)
+SMEM_SPEC = pl.BlockSpec(memory_space=pltpu.SMEM)
 
 
 def even_swap(count):
@@ -50,11 +54,7 @@
     odd_ref[start : start + rows, :] = jnp.where(odd, high, low)
 
 
-def pack_kernel(with_coeff, *refs):
-    if with_coeff:
-        field, coeff, even_rows, odd_rows, even_out, odd_out = refs
-    else:
-        field, even_rows, odd_rows, even_out, odd_out = refs
+def pack_kernel(field, even_rows, odd_rows, ends, even_out, odd_out):
     rows, cols = field.shape[1:]
     odd_x, odd_y = is_odd("gx"), is_odd("gy")
     edges = (slice(0, LANES), slice(cols - LANES, cols))
@@ -73,32 +73,59 @@
                 pair = [halo(layer, edge, part == "above") for layer in range(2)]
             packed.append(pack_columns(pair[0], pair[1], high))
         store_packed(even_out, odd_out, odd_x, start, packed[0], packed[1])
-    if with_coeff:
-        packed = [
-            pack_columns(coeff[0, :, edge], coeff[1, :, edge], high)
-            for high, edge in enumerate(edges)
-        ]
-        store_packed(even_out, odd_out, odd_x, 2 * REACH + rows, packed[0], packed[1])
-
-
-def pack(field, coeff, even_rows, odd_rows, after):
+    if ends is not None:
+        store_packed(even_out, odd_out, odd_x, 2 * REACH + rows, ends[0], ends[1])
+
+
+def pack(field, even_rows, odd_rows, after, with_ends):
     rows = field.shape[1]
-    total = rows + 2 * REACH + (0 if coeff is None else rows)
-    out = jax.ShapeDtypeStruct((total, LANES), jnp.float32)
-    operands = [after, field] + ([] if coeff is None else [coeff]) + [even_rows, odd_rows]
-
-    def kernel(unused, *refs):
-        del unused
-        pack_kernel(coeff is not None, *refs)
+    out = jax.ShapeDtypeStruct((rows + 2 * REACH + (8 if with_ends else 0), LANES), jnp.float32)
+
+    def kernel(field, even_rows, odd_rows, after, even_out, odd_out):
+        pack_kernel(field, even_rows, odd_rows, after if with_ends else None, even_out, odd_out)
 
     return pl.pallas_call(
         kernel,
         out_shape=(out, out),
-        in_specs=[pl.BlockSpec(memory_space=pltpu.VMEM)] * len(operands),
-        out_specs=(pl.BlockSpec(memory_space=pltpu.VMEM),) * 2,
+        in_specs=[VMEM_SPEC] * 4,
+        out_specs=(VMEM_SPEC,) * 2,
         compiler_params=pltpu.CompilerParams(vmem_limit_bytes=VMEM_BYTES),
         name="pack_columns",
-    )(*operands)
+    )(field, even_rows, odd_rows, after)
+
+
+def edge_kernel(field, coeff, even_out, odd_out, sems):
+    rows = field.shape[1]
+    odd_y = is_odd("gy")
+    copies = []
+    for index, (out, at_top) in enumerate(((even_out, odd_y), (odd_out, jnp.logical_not(odd_y)))):
+        for part, (source, place, depth) in enumerate(((field, 0, REACH), (coeff, REACH, 8))):
+            start = pl.multiple_of(jnp.where(at_top, 0, rows - depth), 8)
+            copies.append(
+                pltpu.make_async_copy(
+                    source.at[:, pl.ds(start, depth), :],
+                    out.at[:, pl.ds(place, depth), :],
+                    sems.at[index, part],
+                )
+            )
+    for copy in copies:
+        copy.start()
+    for copy in copies:
+        copy.wait()
+
+
+def edge_rows(field, coeff):
+    layers, _, cols = field.shape
+    out = jax.ShapeDtypeStruct((layers, REACH + 8, cols), jnp.float32)
+    return pl.pallas_call(
+        edge_kernel,
+        out_shape=(out, out),
+        in_specs=[pl.BlockSpec(memory_space=pltpu.HBM)] * 2,
+        out_specs=(pl.BlockSpec(memory_space=pltpu.HBM),) * 2,
+        scratch_shapes=[pltpu.SemaphoreType.DMA((2, 2))],
+        compiler_params=pltpu.CompilerParams(vmem_limit_bytes=EDGE_BYTES),
+        name="edge_rows",
+    )(field, coeff)
 
 
 def zero_rim(pad, depth, rows):
@@ -198,12 +225,29 @@
     return 0.5 * table[entry[layer]]
 
 
-def own_kernel(grid_shape, field, coeff, shifts, table, entry, out, pad, coeff_pad):
+def pack_ends(coeff, ends):
+    rows, cols = coeff.shape[1:]
+    lane = lane_of((8, LANES))
+    for high, edge in enumerate((slice(0, LANES), slice(cols - LANES, cols))):
+        packed = jnp.zeros((8, LANES), jnp.float32)
+        for layer in range(2):
+            for group in range(rows // 8):
+                at = layer * (rows // 8) + group
+                turn = (at + high) % LANES
+                value = coeff[layer, 8 * group : 8 * group + 8, edge]
+                value = pltpu.roll(value, turn, 1) if turn else value
+                packed = jnp.where(lane == at, value, packed)
+        ends[high] = packed
+
+
+def own_kernel(grid_shape, field, coeff, shifts, table, entry, out, ends, pad, coeff_pad):
     rows, cols = field.shape[1:]
     zero_rim(pad, REACH, rows)
     zero_rim(coeff_pad, 8, rows)
     fill_own(pad, REACH, field)
     fill_own(coeff_pad, 8, coeff)
+    if ends is not None:
+        pack_ends(coeff, ends)
     for layer in range(2):
         weight = weight_of(table, entry, layer)
 
@@ -219,11 +263,28 @@
         lax.fori_loop(0, rows // CHUNK, step, 0)
 
 
+def products_of(own, result, base, fit):
+    if base is None:
+        pairs = ((own, own), (own, result), (result, result))
+    else:
+        rest = [a - fit * b for a, b in zip(base, own, strict=True)]
+        slope = [a - fit * b for a, b in zip(own, result, strict=True)]
+        pairs = (
+            (rest, rest), (rest, own), (slope, rest), (result, rest), (slope, own), (result, own),
+        )
+    return tuple(dot_of(*pair) for pair in pairs)
+
+
+def fit_of(sums):
+    gamma, delta, omega = (jnp.sum(sums[index], keepdims=True) for index in range(3))
+    fit = jnp.where(omega > 0.0, delta / jnp.where(omega > 0.0, omega, 1.0), 0.0)
+    return gamma, delta, omega, jnp.clip(fit, -1.0, 1.0)
+
+
 def rows_kernel(
-    grid_shape, before, field, coeff, even_rows, odd_rows, even_edge, odd_edge, packed, shifts,
-    table, entry, out, pad,
+    grid_shape, field, coeff, even_rows, odd_rows, even_edge, odd_edge, base, sums, shifts,
+    table, entry, out, products, pad,
 ):
-    del packed
     rows, cols = field.shape[1:]
     tiles = cols // LANES
     odd_y = is_odd("gy")
@@ -243,7 +304,6 @@
             pad[layer, 0, 1 + tile, REACH:, :] = zeros
             pad[layer, 1, 1 + tile, 0:REACH, :] = zeros
             pad[layer, 1, 1 + tile, REACH:, :] = jnp.where(odd_y, other, even)
-    out[...] = before[...]
     lane = lane_of((CHUNK, LANES))
     row_at = lax.broadcasted_iota(jnp.int32, (CHUNK, LANES), 0)
     for layer in range(2):
@@ -308,27 +368,49 @@
             own_c = coeff[layer, start : start + 8, :]
             extra = weight * (edge_c * value - (own_c + edge_c) * edge_v)
             out[layer, start : start + 8, :] += jnp.where(at == spot, extra, 0.0)
-
-
-def finish_chunk(
-    grid_shape, layer, row, before, field, coeff, pad, coeff_pad, shifts, weight, odd_x,
-):
+    fit = None if base is None else fit_of(sums)[3]
+    carry = (jnp.zeros((8, LANES), jnp.float32),) * products.shape[0]
+    inner = [slice(tile * LANES, (tile + 1) * LANES) for tile in range(1, tiles - 1)]
+    for layer in range(2):
+
+        def add(i, carry, layer=layer):
+            chunk = pl.ds(pl.multiple_of(i * CHUNK, CHUNK), CHUNK)
+            start, own, result = (
+                None if ref is None else [ref[layer, chunk, lanes] for lanes in inner]
+                for ref in (base, field, out)
+            )
+            more = products_of(own, result, start, fit)
+            return tuple(a + b for a, b in zip(carry, more, strict=True))
+
+        carry = lax.fori_loop(0, rows // CHUNK, add, carry)
+    for index, value in enumerate(carry):
+        products[index] = value
+
+
+def finish_chunk(grid_shape, layer, row, field, coeff, out, pad, ends, shifts, weight):
     rows, cols = field.shape[1:]
     tiles = cols // LANES
     first_row = lax.axis_index("gy") * rows + row
     first_col = lax.axis_index("gx") * cols
     lane = lane_of((CHUNK, LANES))
     row_at = lax.broadcasted_iota(jnp.int32, (CHUNK, LANES), 0)
-    cut = [slice(tile * LANES, (tile + 1) * LANES) for tile in range(tiles)]
+    cut = (slice(0, LANES), slice(cols - LANES, cols))
     own = [field[layer, pl.ds(row, CHUNK), lanes] for lanes in cut]
-    result = [before[layer, pl.ds(row, CHUNK), lanes] for lanes in cut]
-    ends = []
-    for tile, side, turn, spot in ((0, 0, 1, 0), (tiles - 1, 1, LANES - 1, LANES - 1)):
-        edge_v = pltpu.roll(pad[layer, side, pl.ds(REACH + row, CHUNK), :], turn, 1)
-        edge_c = pltpu.roll(coeff_pad[layer, side, pl.ds(row, CHUNK), :], turn, 1)
-        own_c = coeff[layer, pl.ds(row, CHUNK), cut[tile]]
-        extra = weight * (edge_c * own[tile] - (own_c + edge_c) * edge_v)
-        ends.append(result[tile] + jnp.where(lane == spot, extra, 0.0))
+    result = []
+    for side, spot in ((0, 0), (1, LANES - 1)):
+        at = layer * (rows // 8) + lax.shift_right_logical(row, 3)
+        edge_c = jnp.concatenate(
+            [
+                pltpu.roll(ends[side], jnp.bitwise_and(LANES + spot - at - i, LANES - 1), 1)
+                for i in range(CHUNK // 8)
+            ]
+        )
+        edge_v = pad[layer, side, pl.ds(REACH + row, CHUNK), :]
+        edge_v = pltpu.roll(edge_v, LANES - 1 if side else 1, 1)
+        own_c = coeff[layer, pl.ds(row, CHUNK), cut[side]]
+        extra = weight * (edge_c * own[side] - (own_c + edge_c) * edge_v)
+        extra = jnp.where(lane == spot, extra, 0.0)
+        result.append(out[layer, pl.ds(row, CHUNK), cut[side]] + extra)
     for direction in range(shifts.shape[0]):
         shift_r, shift_c = shifts[direction, layer, 0], shifts[direction, layer, 1]
         start_r = REACH + row + shifts[direction, 1 - layer, 0] - shift_r
@@ -341,45 +423,55 @@
         low, low_end = shift_c - first_col, jnp.where(step_c < 0, -step_c, 0)
         high = jnp.where(step_c < 0, LANES, LANES - step_c)
         high_end = grid_shape[1] + shift_c - first_col - (tiles - 1) * LANES
-        ends[0] = ends[0] + jnp.where((lane >= low) & (lane < low_end), moved, 0.0)
-        ends[1] = ends[1] + jnp.where((lane >= high) & (lane < high_end), moved, 0.0)
-    return own, [ends[0]] + result[1:-1] + [ends[1]]
-
-
-def fill_sides(pad, coeff_pad, rows, even_cols, odd_cols, even_side, odd_side):
-    odd_x = is_odd("gx")
-    depth = rows + 2 * REACH
-    for target, even, other in (
-        (pad, even_cols[0:depth, :], odd_cols[0:depth, :]),
-        (coeff_pad, even_side[depth : depth + rows, :], odd_side[depth : depth + rows, :]),
-    ):
-        for side, packed in ((0, jnp.where(odd_x, even, other)), (1, jnp.where(odd_x, other, even))):
-            target[0, side] = packed
-            target[1, side] = pltpu.roll(packed, HALF, 1)
-
-
-def first_kernel(
-    grid_shape, before, field, coeff, even_cols, odd_cols, shifts, table, entry,
-    out, sums, even_out, odd_out, pad, coeff_pad,
+        result[0] = result[0] + jnp.where((lane >= low) & (lane < low_end), moved, 0.0)
+        result[1] = result[1] + jnp.where((lane >= high) & (lane < high_end), moved, 0.0)
+    for side in range(2):
+        out[layer, pl.ds(row, CHUNK), cut[side]] = result[side]
+    return own, result
+
+
+def finish(
+    grid_shape, base, fit, field, coeff, even_cols, odd_cols, even_ends, odd_ends, products, shifts,
+    table, entry, out, pad,
 ):
     rows, cols = field.shape[1:]
-    fill_sides(pad, coeff_pad, rows, even_cols, odd_cols, even_cols, odd_cols)
+    depth = rows + 2 * REACH
     odd_x = is_odd("gx")
-    carry = (jnp.zeros((8, LANES), jnp.float32),) * 3
+    even, other = even_cols[0:depth, :], odd_cols[0:depth, :]
+    for side, packed in ((0, jnp.where(odd_x, even, other)), (1, jnp.where(odd_x, other, even))):
+        pad[0, side] = packed
+        pad[1, side] = pltpu.roll(packed, HALF, 1)
+    even, other = even_ends[depth : depth + 8, :], odd_ends[depth : depth + 8, :]
+    ends = (jnp.where(odd_x, even, other), jnp.where(odd_x, other, even))
+    cut = (slice(0, LANES), slice(cols - LANES, cols))
+    carry = tuple(products[index] for index in range(products.shape[0]))
     for layer in range(2):
         weight = weight_of(table, entry, layer)
 
         def step(i, carry, layer=layer, weight=weight):
             row = pl.multiple_of(i * CHUNK, CHUNK)
             own, result = finish_chunk(
-                grid_shape, layer, row, before, field, coeff, pad, coeff_pad, shifts, weight, odd_x,
+                grid_shape, layer, row, field, coeff, out, pad, ends, shifts, weight
             )
-            for tile, value in enumerate(result):
-                out[layer, pl.ds(row, CHUNK), tile * LANES : (tile + 1) * LANES] = value
-            pairs = ((own, own), (own, result), (result, result))
-            return tuple(c + dot_of(*p) for c, p in zip(carry, pairs, strict=True))
+            chunk = pl.ds(row, CHUNK)
+            start = None if base is None else [base[layer, chunk, lanes] for lanes in cut]
+            more = products_of(own, result, start, fit)
+            return tuple(a + b for a, b in zip(carry, more, strict=True))
 
         carry = lax.fori_loop(0, rows // CHUNK, step, carry)
+    return carry
+
+
+def first_kernel(
+    grid_shape, before, field, coeff, even_cols, odd_cols, products, shifts, table, entry,
+    out, sums, even_out, odd_out, pad,
+):
+    del before
+    rows = field.shape[1]
+    carry = finish(
+        grid_shape, None, None, field, coeff, even_cols, odd_cols, even_cols, odd_cols, products,
+        shifts, table, entry, out, pad,
+    )
     for index, value in enumerate(carry):
         sums[index] = value
     odd_y = is_odd("gy")
@@ -389,36 +481,15 @@
 
 
 def second_kernel(
-    grid_shape, base, before, field, coeff, even_cols, odd_cols, even_side, odd_side, sums, shifts,
-    table, entry, out, parts, pad, coeff_pad,
+    grid_shape, before, base, field, coeff, even_cols, odd_cols, even_ends, odd_ends, products,
+    sums, shifts, table, entry, out, parts, pad,
 ):
-    rows, cols = field.shape[1:]
-    fill_sides(pad, coeff_pad, rows, even_cols, odd_cols, even_side, odd_side)
-    odd_x = is_odd("gx")
-    gamma, delta, omega = (jnp.sum(sums[index], keepdims=True) for index in range(3))
-    fit = jnp.where(omega > 0.0, delta / jnp.where(omega > 0.0, omega, 1.0), 0.0)
-    fit = jnp.clip(fit, -1.0, 1.0)
-    carry = (jnp.zeros((8, LANES), jnp.float32),) * 6
-    for layer in range(2):
-        weight = weight_of(table, entry, layer)
-
-        def step(i, carry, layer=layer, weight=weight):
-            row = pl.multiple_of(i * CHUNK, CHUNK)
-            own, result = finish_chunk(
-                grid_shape, layer, row, before, field, coeff, pad, coeff_pad, shifts, weight, odd_x,
-            )
-            rest, slope = [], []
-            for tile, value in enumerate(result):
-                lanes = slice(tile * LANES, (tile + 1) * LANES)
-                out[layer, pl.ds(row, CHUNK), lanes] = value
-                rest.append(base[layer, pl.ds(row, CHUNK), lanes] - fit * own[tile])
-                slope.append(own[tile] - fit * value)
-            pairs = (
-                (rest, rest), (rest, own), (slope, rest), (result, rest), (slope, own), (result, own),
-            )
-            return tuple(c + dot_of(*p) for c, p in zip(carry, pairs, strict=True))
-
-        carry = lax.fori_loop(0, rows // CHUNK, step, carry)
+    del before
+    gamma, delta, omega, fit = fit_of(sums)
+    carry = finish(
+        grid_shape, base, fit, field, coeff, even_cols, odd_cols, even_ends, odd_ends, products,
+        shifts, table, entry, out, pad,
+    )
     rest2, rest_w, slope_rest, n_rest, slope_w, n_w = (
         jnp.sum(value, keepdims=True) for value in carry
     )
@@ -437,7 +508,9 @@
     return jnp.sum(jnp.where(lane == at, row, 0.0), keepdims=True)
 
 
-def last_kernel(parts, base, w_vec, n_vec, solution_out, residual_out):
+def last_kernel(
+    parts, base, w_vec, n_vec, solution_out, residual_out, solution_part, residual_part, sems
+):
     gathered = parts[...]
     count = gathered.shape[0]
     lane = lane_of((8, LANES))
@@ -451,26 +524,39 @@
     gamma_next, delta_next = pick(total, lane, 0), pick(total, lane, 1)
     beta = gamma_next / gamma
     alpha_next = gamma_next / (delta_next - beta * gamma_next / alpha)
-    for layer in range(base.shape[0]):
-        start, w_start = base[layer], w_vec[layer]
-        residual = start - alpha * w_start
-        w_next = w_start - alpha * n_vec[layer]
-        solution_out[layer] = alpha * start + alpha_next * (residual + beta * start)
-        residual_out[layer] = residual - alpha_next * (w_next + beta * w_start)
-
-
-VMEM_SPEC = pl.BlockSpec(memory_space=pltpu.VMEM)
-SMEM_SPEC = pl.BlockSpec(memory_space=pltpu.SMEM)
-
-
-def on_tensor_core(kernel, name, operands, scalars, out_shape, scratch, microseconds):
-    many = isinstance(out_shape, tuple)
+    layers, rows = base.shape[:2]
+    depth = rows // PIECES
+    copies = []
+    for layer in range(layers):
+        for piece in range(PIECES):
+            part = pl.ds(piece * depth, depth)
+            start, w_start = base[layer, part, :], w_vec[layer, part, :]
+            residual = start - alpha * w_start
+            w_next = w_start - alpha * n_vec[layer, part, :]
+            solution_part[layer, part, :] = alpha * start + alpha_next * (residual + beta * start)
+            residual_part[layer, part, :] = residual - alpha_next * (w_next + beta * w_start)
+            for which, (source, target) in enumerate(
+                ((solution_part, solution_out), (residual_part, residual_out))
+            ):
+                copy = pltpu.make_async_copy(
+                    source.at[layer, part, :],
+                    target.at[layer, part, :],
+                    sems.at[which, layer, piece],
+                )
+                copy.start()
+                copies.append(copy)
+    for copy in copies:
+        copy.wait()
+
+
+def on_tensor_core(kernel, name, operands, scalars, out_shape, scratch, microseconds, in_place=False):
     return pl.pallas_call(
         kernel,
         out_shape=out_shape,
         in_specs=[VMEM_SPEC] * len(operands) + [SMEM_SPEC] * len(scalars),
-        out_specs=(VMEM_SPEC,) * len(out_shape) if many else VMEM_SPEC,
+        out_specs=(VMEM_SPEC,) * len(out_shape),
         scratch_shapes=[pltpu.VMEM(shape, jnp.float32) for shape in scratch],
+        input_output_aliases={0: 0} if in_place else {},
         compiler_params=pltpu.CompilerParams(vmem_limit_bytes=VMEM_BYTES),
         cost_estimate=pl.CostEstimate(
             flops=0, bytes_accessed=3_000_000 * microseconds, transcendentals=0
@@ -485,11 +571,15 @@
     devices = count_x * count_y
     tiles = cols // LANES
     grid_shape = (rows * count_y, cols * count_x)
-    params = pltpu.CompilerParams(vmem_limit_bytes=VMEM_BYTES)
     full = jax.ShapeDtypeStruct((layers, rows, cols), jnp.float32)
     edge = jax.ShapeDtypeStruct((layers, REACH, cols), jnp.float32)
     scalars = (shifts, strength_table, layer_entry)
-    sides = [(2, 2, rows + 2 * REACH, LANES), (2, 2, rows, LANES)]
+    own_pads = [(2, tiles + 2, rows + 2 * REACH, LANES), (2, tiles + 2, rows + 16, LANES)]
+    row_pads = [(2, 2, tiles + 2, 2 * REACH, LANES)]
+    side_pads = [(2, 2, rows + 2 * REACH, LANES)]
+
+    def sums_of(count):
+        return jax.ShapeDtypeStruct((count, 8, LANES), jnp.float32)
 
     def bind(kernel):
         def bound(*refs):
@@ -497,50 +587,62 @@
 
         return bound
 
-    def own_part(field):
-        return on_tensor_core(
-            bind(own_kernel), "own_part", (field, coefficient), scalars, full,
-            [(2, tiles + 2, rows + 2 * REACH, LANES), (2, tiles + 2, rows + 16, LANES)], 6,
-        )
-
-    def rows_part(before, field, around, edges, packed):
-        return on_tensor_core(
-            bind(rows_kernel), "rows_part", (before, field, coefficient, *around, *edges, packed),
-            scalars, full, [(2, 2, tiles + 2, 2 * REACH, LANES)], 3,
-        )
-
-    odd_y = is_odd("gy")
-    low = jnp.concatenate([right_side[:, :REACH], coefficient[:, :8]], axis=1)
-    high = jnp.concatenate([right_side[:, rows - REACH :], coefficient[:, rows - 8 :]], axis=1)
-    rows0 = swap(jnp.where(odd_y, low, high), jnp.where(odd_y, high, low), "gy")
-    w_own = own_part(right_side)
-    packed = pack(right_side, coefficient, *rows0, w_own)
+    def rows_first(before, field, coeff, even, odd, packed, *refs):
+        del before, packed
+        rows_kernel(grid_shape, field, coeff, even, odd, even, odd, None, None, *refs)
+
+    def rows_second(before, field, coeff, even, odd, even_edge, odd_edge, packed, *refs):
+        del before, packed
+        rows_kernel(grid_shape, field, coeff, even, odd, even_edge, odd_edge, *refs)
+
+    def own_first(field, coeff, shifts, table, entry, out, ends, *pads):
+        own_kernel(grid_shape, field, coeff, shifts, table, entry, out, ends, *pads)
+
+    def own_second(field, coeff, shifts, table, entry, out, *pads):
+        own_kernel(grid_shape, field, coeff, shifts, table, entry, out, None, *pads)
+
+    rows0 = swap(*edge_rows(right_side, coefficient), "gy")
+    w_own, ends = on_tensor_core(
+        own_first, "own_first", (right_side, coefficient), scalars, (full, sums_of(2)), own_pads, 6
+    )
+    packed = pack(right_side, *rows0, ends, True)
     cols0 = swap(*packed, "gx")
-    w_rows = rows_part(w_own, right_side, rows0, rows0, packed[0])
+    w_rows, products = on_tensor_core(
+        rows_first, "rows_first", (w_own, right_side, coefficient, *rows0, packed[0]), scalars,
+        (full, sums_of(3)), row_pads, 3, True,
+    )
     w_vec, sums, even, odd = on_tensor_core(
-        bind(first_kernel), "first_apply", (w_rows, right_side, coefficient, *cols0), scalars,
-        (full, jax.ShapeDtypeStruct((3, 8, LANES), jnp.float32), edge, edge), sides, 3,
+        bind(first_kernel), "first_apply", (w_rows, right_side, coefficient, *cols0, products),
+        scalars, (full, sums_of(3), edge, edge), side_pads, 3, True,
     )
     rows1 = swap(even, odd, "gy")
-    n_own = own_part(w_vec)
-    packed = pack(w_vec, None, *rows1, n_own)
+    (n_own,) = on_tensor_core(
+        own_second, "own_second", (w_vec, coefficient), scalars, (full,), own_pads, 6
+    )
+    packed = pack(w_vec, *rows1, n_own, False)
     cols1 = swap(*packed, "gx")
-    n_rows = rows_part(n_own, w_vec, rows1, rows0, packed[0])
+    n_rows, products = on_tensor_core(
+        rows_second, "rows_second",
+        (n_own, w_vec, coefficient, *rows1, *rows0, packed[0], right_side, sums), scalars,
+        (full, sums_of(6)), row_pads, 3, True,
+    )
     n_vec, parts = on_tensor_core(
         bind(second_kernel), "second_apply",
-        (right_side, n_rows, w_vec, coefficient, *cols1, *cols0, sums), scalars,
-        (full, jax.ShapeDtypeStruct((devices, LANES), jnp.float32)), sides, 3,
+        (n_rows, right_side, w_vec, coefficient, *cols1, *cols0, products, sums), scalars,
+        (full, jax.ShapeDtypeStruct((devices, LANES), jnp.float32)), side_pads, 3, True,
     )
     gathered = lax.all_to_all(parts, ("gx", "gy"), 0, 0, tiled=True)
-    steps = 4
-    block = pl.BlockSpec((layers, rows // steps, cols), lambda i: (0, i, 0))
     return pl.pallas_call(
         last_kernel,
-        grid=(steps,),
         out_shape=(full, full),
-        in_specs=[pl.BlockSpec((devices, LANES), lambda i: (0, 0))] + [block] * 3,
-        out_specs=(block, block),
-        compiler_params=params,
+        in_specs=[VMEM_SPEC] * 4,
+        out_specs=(pl.BlockSpec(memory_space=pltpu.HBM),) * 2,
+        scratch_shapes=[
+            pltpu.VMEM((layers, rows, cols), jnp.float32),
+            pltpu.VMEM((layers, rows, cols), jnp.float32),
+            pltpu.SemaphoreType.DMA((2, layers, PIECES)),
+        ],
+        compiler_params=pltpu.CompilerParams(vmem_limit_bytes=VMEM_BYTES),
         name="last_update",
     )(gathered, right_side, w_vec, n_vec)
 

time: 82.6 us -> 97.4 us (1.18)
  Pallas kernels: 25 us -> 43.3 us
  waiting for transfers between devices: 4.88 us -> 2.4 us
    pallas_call x3 -> x4, Pallas kernels: 3.52 us -> 21.2 us  [the longest x1 19 us: edge_rows(): pl.pallas_call(edge_kernel, out_shape=(out, out), in_specs=[pl.BlockSpec(...]
    ppermute x4, waiting for transfers between devices: 4.44 us -> 2.38 us  [swap(): lax.ppermute(odd, axis, odd_swap(count))]
    slice x2 -> x0, local copies, waits for them, and re-layouts: 2 us -> none  [on_device(): low = jnp.concatenate([right_side[:, :REACH], coefficient[:, :8]], axis=1)]
    unnamed x11 -> x13, local copies, waits for them, and re-layouts: 0.12 us -> 1.34 us
  transfers between devices with their start and end apart: 8 -> 8, of which waited for: 3 -> 2; matrix products, arithmetic and copies ran while one was open for 0% -> 0% of each run, Pallas kernels for 18% -> 17%
where the time goes in v3:
time: 97.4 us; the launch traced here: 97.2 us
  Pallas kernels  43.3 us (44%)
  blocking collectives  33.3 us (34%)
  starting transfers between devices  15.9 us (16%)
  waiting for transfers between devices  2.4 us (2%)
  local copies, waits for them, and re-layouts  1.34 us (1%)
    all_to_all x1, blocking collectives, on_device(): gathered = lax.all_to_all(parts, ('gx', 'gy'), 0, 0, tiled=True)  33.3 us
    pallas_call x6, Pallas kernels, on_tensor_core(): pl.pallas_call(kernel, out_shape=out_shape, in_specs=[VMEM_SPEC] * len(op...  22.1 us
    pallas_call x1, Pallas kernels, edge_rows(): pl.pallas_call(edge_kernel, out_shape=(out, out), in_specs=[pl.BlockSpec(...  19 us
    ppermute x4, starting transfers between devices, swap(): lax.ppermute(odd, axis, odd_swap(count))  9.91 us
    ppermute x4, starting transfers between devices, swap(): lax.ppermute(even, axis, even_swap(count))  6.04 us
    ppermute x4, waiting for transfers between devices, swap(): lax.ppermute(odd, axis, odd_swap(count))  2.38 us
  transfers between devices with their start and end apart: 8, of which 2 were waited for; matrix products, arithmetic and copies ran while one was open for 0% of the time, Pallas kernels for 17%

profile of v3, /device:TPU:1, one launch (start us, length us, event | category | flops | bytes accessed | tf_op | source)
XLA Modules:
  0.0 97.2 jit_solution(13382332499107827005)
XLA Ops:
  0.6 0.0 copy-start
  0.6 19.0 %edge_rows.1 = (f32[2,72,512]{2,1,0:T(8,128)}, f32[2,72,512]{2,1,0:T(8,128)}) custom-call(f32[2,256,512]{2,1,0:T(8,128)} %base.1, f32[2,256,512]{2,1,0:T(8,128)} %refs_3_.3), custom_call_target="tpu_custom_call" | custom-call | tf_op jit(solution)/shard_map/edge_rows/pallas_call | solution.py:120
  19.7 0.0 copy-start.5
  19.7 2.1 %collective-permute-start = (f32[2,72,512]{2,1,0:T(8,128)}, f32[2,72,512]{2,1,0:T(8,128)S(1)}, u32[]{:S(2)}, u32[]{:S(2)}) collective-permute-start(f32[2,72,512]{2,1,0:T(8,128)} %get-tuple-element.21), channel_id=1, source_target_pairs={{0,1},{1,0},{2,3},{3,2},{4,5},{5,4},{6,7},{7,6},{8,9},{9,8},{10,11... | collective-permute-start | bytes 884744 | tf_op jit(solution)/shard_map/ppermute | solution.py:34
  21.8 0.0 copy-start.3
  21.8 0.0 copy-start.4
  21.8 0.8 collective-permute-start.1
  22.6 0.0 copy-done.5
  22.6 0.1 copy.17.shifts.refs_0_.refs_6_.refs_2_.refs_10_
  22.7 0.0 copy-done
  22.7 0.0 copy-done.3
  22.7 0.0 copy-done.4
  22.7 0.0 copy-start.1
  22.7 1.2 %copy-done.1 = f32[2,256,512]{2,1,0:T(8,128)S(1)} copy-done((f32[2,256,512]{2,1,0:T(8,128)S(1)}, f32[2,256,512]{2,1,0:T(8,128)}, u32[]{:S(2)}) %copy-start.1) | copy-done | bytes 1048600
  24.0 6.0 %own_first.1 = (f32[2,256,512]{2,1,0:T(8,128)S(1)}, f32[2,8,128]{2,1,0:T(8,128)S(1)}) custom-call(f32[2,256,512]{2,1,0:T(8,128)S(1)} %copy-done, f32[2,256,512]{2,1,0:T(8,128)S(1)} %copy-done.1, s32[6,2,2]{2,1,0:T(2,128)S(1)} %copy.17.shifts.refs_0_.refs_6_.refs_2_.refs_10_, f32[35]{0:T(128)S(1)} %copy-done.3, s32[2]{0:T(128)S(1)} %copy-done.4), custom_call_target="tpu_custom_call" | custom-call | bytes 18000000 | tf_op jit(solution)/shard_map/own_first/pallas_call | solution.py:553
  30.0 0.0 collective-permute-done.even_rows.even.even_edge
  30.0 0.0 collective-permute-done.1.odd_rows.odd.odd_edge
  30.0 0.2 pack_columns.2
  30.2 4.4 %collective-permute-start.3 = (f32[392,128]{1,0:T(8,128)S(1)}, f32[392,128]{1,0:T(8,128)S(1)}, u32[]{:S(2)}, u32[]{:S(2)}) collective-permute-start(f32[392,128]{1,0:T(8,128)S(1)} %get-tuple-element.26), channel_id=1, source_target_pairs={{16,32},{32,16},{48,64},{64,48},{80,96},{96,80},{112,128},{128,112... | collective-permute-start | bytes 602120 | tf_op jit(solution)/shard_map/ppermute | solution.py:35
  34.6 0.1 collective-permute-start.2
  34.7 1.9 %rows_first.1 = (f32[2,256,512]{2,1,0:T(8,128)S(1)}, f32[3,8,128]{2,1,0:T(8,128)S(1)}) custom-call(f32[2,256,512]{2,1,0:T(8,128)S(1)} %get-tuple-element.20.before, f32[2,256,512]{2,1,0:T(8,128)S(1)} %copy-done, f32[2,256,512]{2,1,0:T(8,128)S(1)} %copy-done.1, ...), custom_call_target="tpu_custom_call", output_to_operand_aliasing={{0}: (0, {})} | custom-call | bytes 9000000 | tf_op jit(solution)/shard_map/rows_first/pallas_call | solution.py:553
  36.6 1.4 %collective-permute-done.3.refs_4_.refs_7_ = f32[392,128]{1,0:T(8,128)S(1)} collective-permute-done((f32[392,128]{1,0:T(8,128)S(1)}, f32[392,128]{1,0:T(8,128)S(1)}, u32[]{:S(2)}, u32[]{:S(2)}) %collective-permute-start.3) | collective-permute-done | bytes 200736 | tf_op jit(solution)/shard_map/ppermute | solution.py:35
  38.0 0.0 collective-permute-done.2.refs_3_.refs_6_
  38.0 0.0 copy-start.2
  38.0 2.9 %first_apply.1 = (f32[2,256,512]{2,1,0:T(8,128)S(1)}, f32[3,8,128]{2,1,0:T(8,128)S(1)}, f32[2,64,512]{2,1,0:T(8,128)S(1)}, f32[2,64,512]{2,1,0:T(8,128)S(1)}) custom-call(f32[2,256,512]{2,1,0:T(8,128)S(1)} %get-tuple-element.25.refs_0_, f32[2,256,512]{2,1,0:T(8,128)S(1)} %copy-done, f32[2,256,512]{2,1,0:T(8,128)S(1)} %copy-done.1, ...), custom_call_target="tpu_custom_call", output_to_operand_aliasing={{0}: (0, {})} | custom-call | bytes 9000000 | tf_op jit(solution)/shard_map/first_apply/pallas_call | solution.py:553
  40.9 3.7 %collective-permute-start.4 = (f32[2,64,512]{2,1,0:T(8,128)S(1)}, f32[2,64,512]{2,1,0:T(8,128)S(1)}, u32[]{:S(2)}, u32[]{:S(2)}) collective-permute-start(f32[2,64,512]{2,1,0:T(8,128)S(1)} %get-tuple-element.29), channel_id=1, source_target_pairs={{0,1},{1,0},{2,3},{3,2},{4,5},{5,4},{6,7},{7,6},{8,9},{9,8},{10,11... | collective-permute-start | bytes 786440 | tf_op jit(solution)/shard_map/ppermute | solution.py:34
  44.6 0.7 collective-permute-start.5
  45.3 0.0 copy-done.2
  45.3 5.9 %own_second.1.after.before = f32[2,256,512]{2,1,0:T(8,128)S(1)} custom-call(f32[2,256,512]{2,1,0:T(8,128)S(1)} %get-tuple-element.28.field.refs_2_.w_vec, f32[2,256,512]{2,1,0:T(8,128)S(1)} %copy-done.2, s32[6,2,2]{2,1,0:T(2,128)S(1)} %copy.17.shifts.refs_0_.refs_6_.refs_2_.refs_10_, f32[35]{0:T(128)S(1)} %copy-done.3, s32[2]{0:T(128)S(1)} %copy-done.4), custom_call_target="tpu_custom_call" | custom-call | bytes 18000000 | tf_op jit(solution)/shard_map/own_second/pallas_call | solution.py:553
  51.2 0.0 collective-permute-done.4.even_rows.even
  51.2 0.0 collective-permute-done.5.odd_rows.odd
  51.2 0.2 pack_columns.3
  51.4 4.1 %collective-permute-start.7 = (f32[384,128]{1,0:T(8,128)S(1)}, f32[384,128]{1,0:T(8,128)S(1)}, u32[]{:S(2)}, u32[]{:S(2)}) collective-permute-start(f32[384,128]{1,0:T(8,128)S(1)} %get-tuple-element.34), channel_id=1, source_target_pairs={{16,32},{32,16},{48,64},{64,48},{80,96},{96,80},{112,128},{128,112... | collective-permute-start | bytes 589832 | tf_op jit(solution)/shard_map/ppermute | solution.py:35
  55.5 0.1 collective-permute-start.6
  55.6 2.2 %rows_second.1 = (f32[2,256,512]{2,1,0:T(8,128)S(1)}, f32[6,8,128]{2,1,0:T(8,128)S(1)}) custom-call(f32[2,256,512]{2,1,0:T(8,128)S(1)} %own_second.1.after.before, f32[2,256,512]{2,1,0:T(8,128)S(1)} %get-tuple-element.28.field.refs_2_.w_vec, f32[2,256,512]{2,1,0:T(8,128)S(1)} %copy-done.2, ...), custom_call_target="tpu_custom_call", output_to_operand_aliasing={{0}: (0, {})} | custom-call | bytes 9000000 | tf_op jit(solution)/shard_map/rows_second/pallas_call | solution.py:553
  57.8 1.0 %collective-permute-done.7.refs_5_ = f32[384,128]{1,0:T(8,128)S(1)} collective-permute-done((f32[384,128]{1,0:T(8,128)S(1)}, f32[384,128]{1,0:T(8,128)S(1)}, u32[]{:S(2)}, u32[]{:S(2)}) %collective-permute-start.7) | collective-permute-done | bytes 196640 | tf_op jit(solution)/shard_map/ppermute | solution.py:35
  58.8 0.0 collective-permute-done.6.refs_4_
  58.8 3.1 %second_apply.1 = (f32[2,256,512]{2,1,0:T(8,128)S(1)}, f32[256,128]{1,0:T(8,128)S(1)}) custom-call(f32[2,256,512]{2,1,0:T(8,128)S(1)} %get-tuple-element.33.refs_0_, f32[2,256,512]{2,1,0:T(8,128)S(1)} %copy-done, f32[2,256,512]{2,1,0:T(8,128)S(1)} %get-tuple-element.28.field.refs_2_.w_vec, ...), custom_call_target="tpu_custom_call", output_to_operand_aliasing={{0}: (0, {})} | custom-call | bytes 9000000 | tf_op jit(solution)/shard_map/second_apply/pallas_call | solution.py:553
  61.9 33.3 %all_to_all.11 = f32[256,1,128]{2,1,0:T(1,128)S(1)} all-to-all(f32[256,1,128]{2,1,0:T(1,128)S(1)} %bitcast.5), channel_id=1, replica_groups=mesh['gx'=16,'gy'=16] {'gx','gy'}, dimensions={0} | all-to-all | bytes 262144 | tf_op jit(solution)/shard_map/all_to_all | solution.py:634
  95.3 1.9 %last_update.1 = (f32[2,256,512]{2,1,0:T(8,128)}, f32[2,256,512]{2,1,0:T(8,128)}) custom-call(f32[256,128]{1,0:T(8,128)S(1)} %bitcast.4, f32[2,256,512]{2,1,0:T(8,128)S(1)} %copy-done, f32[2,256,512]{2,1,0:T(8,128)S(1)} %get-tuple-element.28.field.refs_2_.w_vec, f32[2,256,512]{2,1,0:T(8,128)S(1)} %get-tuple-element.37.n_vec), custom_call_target="tpu_custom_call" | custom-call | tf_op jit(solution)/shard_map/last_update/pallas_call | solution.py:635
Async XLA Ops:
  0.6 22.1 %copy-start = (f32[2,256,512]{2,1,0:T(8,128)S(1)}, f32[2,256,512]{2,1,0:T(8,128)}, u32[]{:S(2)}) copy-start(f32[2,256,512]{2,1,0:T(8,128)} %base.1) | copy-start | bytes 3145732
  19.7 3.0 %copy-start.5 = (s32[6,2,2]{0,2,1:T(2,128)S(1)}, s32[6,2,2]{0,2,1:T(2,128)}, u32[]{:S(2)}) copy-start(s32[6,2,2]{0,2,1:T(2,128)} %param.9) | copy-start | bytes 292
  19.7 10.3 %collective-permute-start = (f32[2,72,512]{2,1,0:T(8,128)}, f32[2,72,512]{2,1,0:T(8,128)S(1)}, u32[]{:S(2)}, u32[]{:S(2)}) collective-permute-start(f32[2,72,512]{2,1,0:T(8,128)} %get-tuple-element.21), channel_id=1, source_target_pairs={{0,1},{1,0},{2,3},{3,2},{4,5},{5,4},{6,7},{7,6},{8,9},{9,8},{10,11... | collective-permute-start | bytes 884744 | tf_op jit(solution)/shard_map/ppermute | solution.py:34
  21.8 0.9 copy-start.3
  21.8 0.9 copy-start.4
  21.8 8.2 %collective-permute-start.1 = (f32[2,72,512]{2,1,0:T(8,128)}, f32[2,72,512]{2,1,0:T(8,128)S(1)}, u32[]{:S(2)}, u32[]{:S(2)}) collective-permute-start(f32[2,72,512]{2,1,0:T(8,128)} %get-tuple-element.22), channel_id=1, source_target_pairs={{1,2},{2,1},{3,4},{4,3},{5,6},{6,5},{7,8},{8,7},{9,10},{10,9},{11,... | collective-permute-start | bytes 884744 | tf_op jit(solution)/shard_map/ppermute | solution.py:35
  22.7 1.2 %copy-start.1 = (f32[2,256,512]{2,1,0:T(8,128)S(1)}, f32[2,256,512]{2,1,0:T(8,128)}, u32[]{:S(2)}) copy-start(f32[2,256,512]{2,1,0:T(8,128)} %refs_3_.3) | copy-start | bytes 3145732
  30.2 7.8 %collective-permute-start.3 = (f32[392,128]{1,0:T(8,128)S(1)}, f32[392,128]{1,0:T(8,128)S(1)}, u32[]{:S(2)}, u32[]{:S(2)}) collective-permute-start(f32[392,128]{1,0:T(8,128)S(1)} %get-tuple-element.26), channel_id=1, source_target_pairs={{16,32},{32,16},{48,64},{64,48},{80,96},{96,80},{112,128},{128,112... | collective-permute-start | bytes 602120 | tf_op jit(solution)/shard_map/ppermute | solution.py:35
  34.6 3.4 %collective-permute-start.2 = (f32[392,128]{1,0:T(8,128)S(1)}, f32[392,128]{1,0:T(8,128)S(1)}, u32[]{:S(2)}, u32[]{:S(2)}) collective-permute-start(f32[392,128]{1,0:T(8,128)S(1)} %get-tuple-element.24.packed), channel_id=1, source_target_pairs={{0,16},{16,0},{32,48},{48,32},{64,80},{80,64},{96,112},{112,96},{1... | collective-permute-start | bytes 602120 | tf_op jit(solution)/shard_map/ppermute | solution.py:34
  38.0 7.3 %copy-start.2 = (f32[2,256,512]{2,1,0:T(8,128)S(1)}, f32[2,256,512]{2,1,0:T(8,128)}, u32[]{:S(2)}) copy-start(f32[2,256,512]{2,1,0:T(8,128)} %refs_3_.3) | copy-start | bytes 3145732
  40.9 10.3 %collective-permute-start.4 = (f32[2,64,512]{2,1,0:T(8,128)S(1)}, f32[2,64,512]{2,1,0:T(8,128)S(1)}, u32[]{:S(2)}, u32[]{:S(2)}) collective-permute-start(f32[2,64,512]{2,1,0:T(8,128)S(1)} %get-tuple-element.29), channel_id=1, source_target_pairs={{0,1},{1,0},{2,3},{3,2},{4,5},{5,4},{6,7},{7,6},{8,9},{9,8},{10,11... | collective-permute-start | bytes 786440 | tf_op jit(solution)/shard_map/ppermute | solution.py:34
  44.6 6.6 %collective-permute-start.5 = (f32[2,64,512]{2,1,0:T(8,128)S(1)}, f32[2,64,512]{2,1,0:T(8,128)S(1)}, u32[]{:S(2)}, u32[]{:S(2)}) collective-permute-start(f32[2,64,512]{2,1,0:T(8,128)S(1)} %get-tuple-element.30), channel_id=1, source_target_pairs={{1,2},{2,1},{3,4},{4,3},{5,6},{6,5},{7,8},{8,7},{9,10},{10,9},{11,... | collective-permute-start | bytes 786440 | tf_op jit(solution)/shard_map/ppermute | solution.py:35
  51.4 7.4 %collective-permute-start.7 = (f32[384,128]{1,0:T(8,128)S(1)}, f32[384,128]{1,0:T(8,128)S(1)}, u32[]{:S(2)}, u32[]{:S(2)}) collective-permute-start(f32[384,128]{1,0:T(8,128)S(1)} %get-tuple-element.34), channel_id=1, source_target_pairs={{16,32},{32,16},{48,64},{64,48},{80,96},{96,80},{112,128},{128,112... | collective-permute-start | bytes 589832 | tf_op jit(solution)/shard_map/ppermute | solution.py:35
  55.5 3.3 %collective-permute-start.6 = (f32[384,128]{1,0:T(8,128)S(1)}, f32[384,128]{1,0:T(8,128)S(1)}, u32[]{:S(2)}, u32[]{:S(2)}) collective-permute-start(f32[384,128]{1,0:T(8,128)S(1)} %get-tuple-element.31.packed), channel_id=1, source_target_pairs={{0,16},{16,0},{32,48},{48,32},{64,80},{80,64},{96,112},{112,96},{1... | collective-permute-start | bytes 589832 | tf_op jit(solution)/shard_map/ppermute | solution.py:34

commit v4 on v3

--- a/solution.py
+++ b/solution.py
@@ -9,9 +9,10 @@
 LANES = 128
 HALF = 64
 CHUNK = 32
+UNROLL = 8
 PIECES = 4
 VMEM_BYTES = 32 * 1024 * 1024
-EDGE_BYTES = 62 * 1024 * 1024
+EDGE_BYTES = 60 * 1024 * 1024
 VMEM_SPEC = pl.BlockSpec(memory_space=pltpu.VMEM)
 SMEM_SPEC = pl.BlockSpec(memory_space=pltpu.SMEM)
 
@@ -121,7 +122,7 @@
         edge_kernel,
         out_shape=(out, out),
         in_specs=[pl.BlockSpec(memory_space=pltpu.HBM)] * 2,
-        out_specs=(pl.BlockSpec(memory_space=pltpu.HBM),) * 2,
+        out_specs=(VMEM_SPEC,) * 2,
         scratch_shapes=[pltpu.SemaphoreType.DMA((2, 2))],
         compiler_params=pltpu.CompilerParams(vmem_limit_bytes=EDGE_BYTES),
         name="edge_rows",
@@ -260,7 +261,7 @@
                 out[layer, pl.ds(row, CHUNK), tile * LANES : (tile + 1) * LANES] = value
             return carry
 
-        lax.fori_loop(0, rows // CHUNK, step, 0)
+        lax.fori_loop(0, rows // CHUNK, step, 0, unroll=UNROLL)
 
 
 def products_of(own, result, base, fit):
@@ -382,7 +383,7 @@
             more = products_of(own, result, start, fit)
             return tuple(a + b for a, b in zip(carry, more, strict=True))
 
-        carry = lax.fori_loop(0, rows // CHUNK, add, carry)
+        carry = lax.fori_loop(0, rows // CHUNK, add, carry, unroll=UNROLL)
     for index, value in enumerate(carry):
         products[index] = value
 
@@ -458,7 +459,7 @@
             more = products_of(own, result, start, fit)
             return tuple(a + b for a, b in zip(carry, more, strict=True))
 
-        carry = lax.fori_loop(0, rows // CHUNK, step, carry)
+        carry = lax.fori_loop(0, rows // CHUNK, step, carry, unroll=UNROLL)
     return carry
 
 

time: 97.4 us -> 78.6 us (0.81)
  Pallas kernels: 43.3 us -> 21.3 us
  starting transfers between devices: 15.9 us -> 19 us
  local copies, waits for them, and re-layouts: 1.34 us -> 0.12 us
    pallas_call x1, Pallas kernels: 19 us -> 2.05 us  [edge_rows(): pl.pallas_call(edge_kernel, out_shape=(out, out), in_specs=[pl.BlockSpec(...]
    pallas_call x6, Pallas kernels: 22.1 us -> 17 us  [on_tensor_core(): pl.pallas_call(kernel, out_shape=out_shape, in_specs=[VMEM_SPEC] * len(op...]
    ppermute x4, starting transfers between devices: 9.91 us -> 12.7 us  [swap(): lax.ppermute(odd, axis, odd_swap(count))]
    unnamed x13 -> x11, local copies, waits for them, and re-layouts: 1.34 us -> 0.12 us
  transfers between devices with their start and end apart: 8 -> 8, of which waited for: 2 -> 4; matrix products, arithmetic and copies ran while one was open for 0% -> 0% of each run, Pallas kernels for 17% -> 17%
where the time goes in v4:
time: 78.6 us; the launch traced here: 78.3 us
  blocking collectives  33.8 us (43%)
  Pallas kernels  21.3 us (27%)
  starting transfers between devices  19 us (24%)
  waiting for transfers between devices  3.13 us (4%)
  between operations  0.94 us (1%)
    all_to_all x1, blocking collectives, on_device(): gathered = lax.all_to_all(parts, ('gx', 'gy'), 0, 0, tiled=True)  33.8 us
    pallas_call x6, Pallas kernels, on_tensor_core(): pl.pallas_call(kernel, out_shape=out_shape, in_specs=[VMEM_SPEC] * len(op...  17 us
    ppermute x4, starting transfers between devices, swap(): lax.ppermute(odd, axis, odd_swap(count))  12.7 us
    ppermute x4, starting transfers between devices, swap(): lax.ppermute(even, axis, even_swap(count))  6.3 us
    ppermute x4, waiting for transfers between devices, swap(): lax.ppermute(odd, axis, odd_swap(count))  2.71 us
    pallas_call x1, Pallas kernels, edge_rows(): pl.pallas_call(edge_kernel, out_shape=(out, out), in_specs=[pl.BlockSpec(...  2.05 us
    pallas_call x1, Pallas kernels, on_device(): pl.pallas_call(last_kernel, out_shape=(full, full), in_specs=[VMEM_SPEC]...  1.87 us
  transfers between devices with their start and end apart: 8, of which 4 were waited for; matrix products, arithmetic and copies ran while one was open for 0% of the time, Pallas kernels for 17%

profile of v4, /device:TPU:1, one launch (start us, length us, event | category | flops | bytes accessed | tf_op | source)
XLA Modules:
  0.0 78.3 jit_solution(6153632212470139314)
XLA Ops:
  0.6 0.0 copy-start
  0.6 0.0 copy-start.1
  0.6 2.0 %edge_rows.1 = (f32[2,72,512]{2,1,0:T(8,128)}, f32[2,72,512]{2,1,0:T(8,128)}) custom-call(f32[2,256,512]{2,1,0:T(8,128)} %base.1, f32[2,256,512]{2,1,0:T(8,128)} %refs_3_.3), custom_call_target="tpu_custom_call" | custom-call | tf_op jit(solution)/shard_map/edge_rows/pallas_call | solution.py:121
  2.7 0.0 copy-start.4
  2.7 2.1 %collective-permute-start = (f32[2,72,512]{2,1,0:T(8,128)}, f32[2,72,512]{2,1,0:T(8,128)S(1)}, u32[]{:S(2)}, u32[]{:S(2)}) collective-permute-start(f32[2,72,512]{2,1,0:T(8,128)} %get-tuple-element.21), channel_id=1, source_target_pairs={{0,1},{1,0},{2,3},{3,2},{4,5},{5,4},{6,7},{7,6},{8,9},{9,8},{10,11... | collective-permute-start | bytes 884744 | tf_op jit(solution)/shard_map/ppermute | solution.py:35
  4.8 0.0 copy-start.2
  4.8 0.0 copy-start.3
  4.8 0.8 %collective-permute-start.1 = (f32[2,72,512]{2,1,0:T(8,128)}, f32[2,72,512]{2,1,0:T(8,128)S(1)}, u32[]{:S(2)}, u32[]{:S(2)}) collective-permute-start(f32[2,72,512]{2,1,0:T(8,128)} %get-tuple-element.22), channel_id=1, source_target_pairs={{1,2},{2,1},{3,4},{4,3},{5,6},{6,5},{7,8},{8,7},{9,10},{10,9},{11,... | collective-permute-start | bytes 884744 | tf_op jit(solution)/shard_map/ppermute | solution.py:36
  5.7 0.0 copy-done.4
  5.7 0.1 copy.17.shifts.refs_0_.refs_6_.refs_2_.refs_10_
  5.8 0.0 copy-done
  5.8 0.0 copy-done.1
  5.8 0.0 copy-done.2
  5.8 0.0 copy-done.3
  5.8 4.7 %own_first.1 = (f32[2,256,512]{2,1,0:T(8,128)S(1)}, f32[2,8,128]{2,1,0:T(8,128)S(1)}) custom-call(f32[2,256,512]{2,1,0:T(8,128)S(1)} %copy-done, f32[2,256,512]{2,1,0:T(8,128)S(1)} %copy-done.1, s32[6,2,2]{2,1,0:T(2,128)S(1)} %copy.17.shifts.refs_0_.refs_6_.refs_2_.refs_10_, f32[35]{0:T(128)S(1)} %copy-done.2, s32[2]{0:T(128)S(1)} %copy-done.3), custom_call_target="tpu_custom_call" | custom-call | bytes 18000000 | tf_op jit(solution)/shard_map/own_first/pallas_call | solution.py:554
  10.4 0.1 collective-permute-done.even_rows.even.even_edge
  10.6 0.0 collective-permute-done.1.odd_rows.odd.odd_edge
  10.6 0.2 pack_columns.2
  10.7 6.1 %collective-permute-start.3 = (f32[392,128]{1,0:T(8,128)S(1)}, f32[392,128]{1,0:T(8,128)S(1)}, u32[]{:S(2)}, u32[]{:S(2)}) collective-permute-start(f32[392,128]{1,0:T(8,128)S(1)} %get-tuple-element.26), channel_id=1, source_target_pairs={{16,32},{32,16},{48,64},{64,48},{80,96},{96,80},{112,128},{128,112... | collective-permute-start | bytes 602120 | tf_op jit(solution)/shard_map/ppermute | solution.py:36
  16.9 0.1 collective-permute-start.2
  17.0 1.8 %rows_first.1 = (f32[2,256,512]{2,1,0:T(8,128)S(1)}, f32[3,8,128]{2,1,0:T(8,128)S(1)}) custom-call(f32[2,256,512]{2,1,0:T(8,128)S(1)} %get-tuple-element.20.before, f32[2,256,512]{2,1,0:T(8,128)S(1)} %copy-done, f32[2,256,512]{2,1,0:T(8,128)S(1)} %copy-done.1, ...), custom_call_target="tpu_custom_call", output_to_operand_aliasing={{0}: (0, {})} | custom-call | bytes 9000000 | tf_op jit(solution)/shard_map/rows_first/pallas_call | solution.py:554
  18.8 1.5 %collective-permute-done.3.refs_4_.refs_7_ = f32[392,128]{1,0:T(8,128)S(1)} collective-permute-done((f32[392,128]{1,0:T(8,128)S(1)}, f32[392,128]{1,0:T(8,128)S(1)}, u32[]{:S(2)}, u32[]{:S(2)}) %collective-permute-start.3) | collective-permute-done | bytes 200736 | tf_op jit(solution)/shard_map/ppermute | solution.py:36
  20.3 0.0 collective-permute-done.2.refs_3_.refs_6_
  20.3 1.8 %first_apply.1 = (f32[2,256,512]{2,1,0:T(8,128)S(1)}, f32[3,8,128]{2,1,0:T(8,128)S(1)}, f32[2,64,512]{2,1,0:T(8,128)S(1)}, f32[2,64,512]{2,1,0:T(8,128)S(1)}) custom-call(f32[2,256,512]{2,1,0:T(8,128)S(1)} %get-tuple-element.25.refs_0_, f32[2,256,512]{2,1,0:T(8,128)S(1)} %copy-done, f32[2,256,512]{2,1,0:T(8,128)S(1)} %copy-done.1, ...), custom_call_target="tpu_custom_call", output_to_operand_aliasing={{0}: (0, {})} | custom-call | bytes 9000000 | tf_op jit(solution)/shard_map/first_apply/pallas_call | solution.py:554
  22.1 4.0 %collective-permute-start.4 = (f32[2,64,512]{2,1,0:T(8,128)S(1)}, f32[2,64,512]{2,1,0:T(8,128)S(1)}, u32[]{:S(2)}, u32[]{:S(2)}) collective-permute-start(f32[2,64,512]{2,1,0:T(8,128)S(1)} %get-tuple-element.29), channel_id=1, source_target_pairs={{0,1},{1,0},{2,3},{3,2},{4,5},{5,4},{6,7},{7,6},{8,9},{9,8},{10,11... | collective-permute-start | bytes 786440 | tf_op jit(solution)/shard_map/ppermute | solution.py:35
  26.1 0.8 %collective-permute-start.5 = (f32[2,64,512]{2,1,0:T(8,128)S(1)}, f32[2,64,512]{2,1,0:T(8,128)S(1)}, u32[]{:S(2)}, u32[]{:S(2)}) collective-permute-start(f32[2,64,512]{2,1,0:T(8,128)S(1)} %get-tuple-element.30), channel_id=1, source_target_pairs={{1,2},{2,1},{3,4},{4,3},{5,6},{6,5},{7,8},{8,7},{9,10},{10,9},{11,... | collective-permute-start | bytes 786440 | tf_op jit(solution)/shard_map/ppermute | solution.py:36
  27.0 4.6 %own_second.1.after.before = f32[2,256,512]{2,1,0:T(8,128)S(1)} custom-call(f32[2,256,512]{2,1,0:T(8,128)S(1)} %get-tuple-element.28.field.refs_2_.w_vec, f32[2,256,512]{2,1,0:T(8,128)S(1)} %copy-done.1, s32[6,2,2]{2,1,0:T(2,128)S(1)} %copy.17.shifts.refs_0_.refs_6_.refs_2_.refs_10_, f32[35]{0:T(128)S(1)} %copy-done.2, s32[2]{0:T(128)S(1)} %copy-done.3), custom_call_target="tpu_custom_call" | custom-call | bytes 18000000 | tf_op jit(solution)/shard_map/own_second/pallas_call | solution.py:554
  31.6 0.3 collective-permute-done.4.even_rows.even
  31.9 0.0 collective-permute-done.5.odd_rows.odd
  31.9 0.2 pack_columns.3
  32.1 4.9 %collective-permute-start.7 = (f32[384,128]{1,0:T(8,128)S(1)}, f32[384,128]{1,0:T(8,128)S(1)}, u32[]{:S(2)}, u32[]{:S(2)}) collective-permute-start(f32[384,128]{1,0:T(8,128)S(1)} %get-tuple-element.34), channel_id=1, source_target_pairs={{16,32},{32,16},{48,64},{64,48},{80,96},{96,80},{112,128},{128,112... | collective-permute-start | bytes 589832 | tf_op jit(solution)/shard_map/ppermute | solution.py:36
  37.0 0.1 collective-permute-start.6
  37.1 2.0 %rows_second.1 = (f32[2,256,512]{2,1,0:T(8,128)S(1)}, f32[6,8,128]{2,1,0:T(8,128)S(1)}) custom-call(f32[2,256,512]{2,1,0:T(8,128)S(1)} %own_second.1.after.before, f32[2,256,512]{2,1,0:T(8,128)S(1)} %get-tuple-element.28.field.refs_2_.w_vec, f32[2,256,512]{2,1,0:T(8,128)S(1)} %copy-done.1, ...), custom_call_target="tpu_custom_call", output_to_operand_aliasing={{0}: (0, {})} | custom-call | bytes 9000000 | tf_op jit(solution)/shard_map/rows_second/pallas_call | solution.py:554
  39.2 1.2 %collective-permute-done.7.refs_5_ = f32[384,128]{1,0:T(8,128)S(1)} collective-permute-done((f32[384,128]{1,0:T(8,128)S(1)}, f32[384,128]{1,0:T(8,128)S(1)}, u32[]{:S(2)}, u32[]{:S(2)}) %collective-permute-start.7) | collective-permute-done | bytes 196640 | tf_op jit(solution)/shard_map/ppermute | solution.py:36
  40.3 0.0 collective-permute-done.6.refs_4_
  40.3 2.1 %second_apply.1 = (f32[2,256,512]{2,1,0:T(8,128)S(1)}, f32[256,128]{1,0:T(8,128)S(1)}) custom-call(f32[2,256,512]{2,1,0:T(8,128)S(1)} %get-tuple-element.33.refs_0_, f32[2,256,512]{2,1,0:T(8,128)S(1)} %copy-done, f32[2,256,512]{2,1,0:T(8,128)S(1)} %get-tuple-element.28.field.refs_2_.w_vec, ...), custom_call_target="tpu_custom_call", output_to_operand_aliasing={{0}: (0, {})} | custom-call | bytes 9000000 | tf_op jit(solution)/shard_map/second_apply/pallas_call | solution.py:554
  42.5 33.8 %all_to_all.11 = f32[256,1,128]{2,1,0:T(1,128)S(1)} all-to-all(f32[256,1,128]{2,1,0:T(1,128)S(1)} %bitcast.5), channel_id=1, replica_groups=mesh['gx'=16,'gy'=16] {'gx','gy'}, dimensions={0} | all-to-all | bytes 262144 | tf_op jit(solution)/shard_map/all_to_all | solution.py:635
  76.3 1.9 %last_update.1 = (f32[2,256,512]{2,1,0:T(8,128)}, f32[2,256,512]{2,1,0:T(8,128)}) custom-call(f32[256,128]{1,0:T(8,128)S(1)} %bitcast.4, f32[2,256,512]{2,1,0:T(8,128)S(1)} %copy-done, f32[2,256,512]{2,1,0:T(8,128)S(1)} %get-tuple-element.28.field.refs_2_.w_vec, f32[2,256,512]{2,1,0:T(8,128)S(1)} %get-tuple-element.37.n_vec), custom_call_target="tpu_custom_call" | custom-call | tf_op jit(solution)/shard_map/last_update/pallas_call | solution.py:636
Async XLA Ops:
  0.6 5.1 %copy-start = (f32[2,256,512]{2,1,0:T(8,128)S(1)}, f32[2,256,512]{2,1,0:T(8,128)}, u32[]{:S(2)}) copy-start(f32[2,256,512]{2,1,0:T(8,128)} %base.1) | copy-start | bytes 3145732
  0.6 5.1 %copy-start.1 = (f32[2,256,512]{2,1,0:T(8,128)S(1)}, f32[2,256,512]{2,1,0:T(8,128)}, u32[]{:S(2)}) copy-start(f32[2,256,512]{2,1,0:T(8,128)} %refs_3_.3) | copy-start | bytes 3145732
  2.7 3.0 %copy-start.4 = (s32[6,2,2]{0,2,1:T(2,128)S(1)}, s32[6,2,2]{0,2,1:T(2,128)}, u32[]{:S(2)}) copy-start(s32[6,2,2]{0,2,1:T(2,128)} %param.9) | copy-start | bytes 292
  2.7 7.8 %collective-permute-start = (f32[2,72,512]{2,1,0:T(8,128)}, f32[2,72,512]{2,1,0:T(8,128)S(1)}, u32[]{:S(2)}, u32[]{:S(2)}) collective-permute-start(f32[2,72,512]{2,1,0:T(8,128)} %get-tuple-element.21), channel_id=1, source_target_pairs={{0,1},{1,0},{2,3},{3,2},{4,5},{5,4},{6,7},{7,6},{8,9},{9,8},{10,11... | collective-permute-start | bytes 884744 | tf_op jit(solution)/shard_map/ppermute | solution.py:35
  4.8 0.9 %copy-start.2 = (f32[35]{0:T(128)S(1)}, f32[35]{0:T(128)}, u32[]{:S(2)}) copy-start(f32[35]{0:T(128)} %refs_11_.1) | copy-start | bytes 424
  4.8 0.9 %copy-start.3 = (s32[2]{0:T(128)S(1)}, s32[2]{0:T(128)}, u32[]{:S(2)}) copy-start(s32[2]{0:T(128)} %refs_12_.1) | copy-start | bytes 28
  4.8 5.7 %collective-permute-start.1 = (f32[2,72,512]{2,1,0:T(8,128)}, f32[2,72,512]{2,1,0:T(8,128)S(1)}, u32[]{:S(2)}, u32[]{:S(2)}) collective-permute-start(f32[2,72,512]{2,1,0:T(8,128)} %get-tuple-element.22), channel_id=1, source_target_pairs={{1,2},{2,1},{3,4},{4,3},{5,6},{6,5},{7,8},{8,7},{9,10},{10,9},{11,... | collective-permute-start | bytes 884744 | tf_op jit(solution)/shard_map/ppermute | solution.py:36
  10.7 9.5 %collective-permute-start.3 = (f32[392,128]{1,0:T(8,128)S(1)}, f32[392,128]{1,0:T(8,128)S(1)}, u32[]{:S(2)}, u32[]{:S(2)}) collective-permute-start(f32[392,128]{1,0:T(8,128)S(1)} %get-tuple-element.26), channel_id=1, source_target_pairs={{16,32},{32,16},{48,64},{64,48},{80,96},{96,80},{112,128},{128,112... | collective-permute-start | bytes 602120 | tf_op jit(solution)/shard_map/ppermute | solution.py:36
  16.9 3.4 %collective-permute-start.2 = (f32[392,128]{1,0:T(8,128)S(1)}, f32[392,128]{1,0:T(8,128)S(1)}, u32[]{:S(2)}, u32[]{:S(2)}) collective-permute-start(f32[392,128]{1,0:T(8,128)S(1)} %get-tuple-element.24.packed), channel_id=1, source_target_pairs={{0,16},{16,0},{32,48},{48,32},{64,80},{80,64},{96,112},{112,96},{1... | collective-permute-start | bytes 602120 | tf_op jit(solution)/shard_map/ppermute | solution.py:35
  22.1 9.7 %collective-permute-start.4 = (f32[2,64,512]{2,1,0:T(8,128)S(1)}, f32[2,64,512]{2,1,0:T(8,128)S(1)}, u32[]{:S(2)}, u32[]{:S(2)}) collective-permute-start(f32[2,64,512]{2,1,0:T(8,128)S(1)} %get-tuple-element.29), channel_id=1, source_target_pairs={{0,1},{1,0},{2,3},{3,2},{4,5},{5,4},{6,7},{7,6},{8,9},{9,8},{10,11... | collective-permute-start | bytes 786440 | tf_op jit(solution)/shard_map/ppermute | solution.py:35
  26.1 5.8 %collective-permute-start.5 = (f32[2,64,512]{2,1,0:T(8,128)S(1)}, f32[2,64,512]{2,1,0:T(8,128)S(1)}, u32[]{:S(2)}, u32[]{:S(2)}) collective-permute-start(f32[2,64,512]{2,1,0:T(8,128)S(1)} %get-tuple-element.30), channel_id=1, source_target_pairs={{1,2},{2,1},{3,4},{4,3},{5,6},{6,5},{7,8},{8,7},{9,10},{10,9},{11,... | collective-permute-start | bytes 786440 | tf_op jit(solution)/shard_map/ppermute | solution.py:36
  32.1 8.3 %collective-permute-start.7 = (f32[384,128]{1,0:T(8,128)S(1)}, f32[384,128]{1,0:T(8,128)S(1)}, u32[]{:S(2)}, u32[]{:S(2)}) collective-permute-start(f32[384,128]{1,0:T(8,128)S(1)} %get-tuple-element.34), channel_id=1, source_target_pairs={{16,32},{32,16},{48,64},{64,48},{80,96},{96,80},{112,128},{128,112... | collective-permute-start | bytes 589832 | tf_op jit(solution)/shard_map/ppermute | solution.py:36
  37.0 3.3 %collective-permute-start.6 = (f32[384,128]{1,0:T(8,128)S(1)}, f32[384,128]{1,0:T(8,128)S(1)}, u32[]{:S(2)}, u32[]{:S(2)}) collective-permute-start(f32[384,128]{1,0:T(8,128)S(1)} %get-tuple-element.31.packed), channel_id=1, source_target_pairs={{0,16},{16,0},{32,48},{48,32},{64,80},{80,64},{96,112},{112,96},{1... | collective-permute-start | bytes 589832 | tf_op jit(solution)/shard_map/ppermute | solution.py:35

commit v5 on v4

--- a/solution.py
+++ b/solution.py
@@ -49,50 +49,60 @@
     return jnp.where(low_lanes, first, turned)
 
 
-def store_packed(even_ref, odd_ref, odd, start, low, high):
+def packed_edges(load, cols):
+    edges = (slice(0, LANES), slice(cols - LANES, cols))
+    return [pack_columns(load(0, edge), load(1, edge), high) for high, edge in enumerate(edges)]
+
+
+def store_packed(even_ref, odd_ref, start, low, high):
+    odd = is_odd("gx")
     rows = low.shape[0]
     even_ref[start : start + rows, :] = jnp.where(odd, low, high)
     odd_ref[start : start + rows, :] = jnp.where(odd, high, low)
 
 
-def pack_kernel(field, even_rows, odd_rows, ends, even_out, odd_out):
+def pack_sides_kernel(with_ends, field, after, even_out, odd_out):
     rows, cols = field.shape[1:]
-    odd_x, odd_y = is_odd("gx"), is_odd("gy")
-    edges = (slice(0, LANES), slice(cols - LANES, cols))
-
-    def halo(layer, edge, before):
-        even = even_rows[layer, 0:REACH, edge]
-        other = odd_rows[layer, 0:REACH, edge]
-        return jnp.where(odd_y == before, even, other)
-
-    for start, part in ((0, "above"), (REACH, "own"), (REACH + rows, "below")):
-        packed = []
-        for high, edge in enumerate(edges):
-            if part == "own":
-                pair = [field[layer, :, edge] for layer in range(2)]
-            else:
-                pair = [halo(layer, edge, part == "above") for layer in range(2)]
-            packed.append(pack_columns(pair[0], pair[1], high))
-        store_packed(even_out, odd_out, odd_x, start, packed[0], packed[1])
-    if ends is not None:
-        store_packed(even_out, odd_out, odd_x, 2 * REACH + rows, ends[0], ends[1])
-
-
-def pack(field, even_rows, odd_rows, after, with_ends):
-    rows = field.shape[1]
-    out = jax.ShapeDtypeStruct((rows + 2 * REACH + (8 if with_ends else 0), LANES), jnp.float32)
-
-    def kernel(field, even_rows, odd_rows, after, even_out, odd_out):
-        pack_kernel(field, even_rows, odd_rows, after if with_ends else None, even_out, odd_out)
-
+    low, high = packed_edges(lambda layer, edge: field[layer, :, edge], cols)
+    store_packed(even_out, odd_out, 0, low, high)
+    if with_ends:
+        store_packed(even_out, odd_out, rows, after[0], after[1])
+
+
+def pack_corners_kernel(even_rows, odd_rows, even_out, odd_out):
+    cols = even_rows.shape[2]
+    odd_y = is_odd("gy")
+    for start, above in ((0, True), (REACH, False)):
+
+        def halo(layer, edge, above=above):
+            even = even_rows[layer, 0:REACH, edge]
+            other = odd_rows[layer, 0:REACH, edge]
+            return jnp.where(odd_y == above, even, other)
+
+        store_packed(even_out, odd_out, start, *packed_edges(halo, cols))
+
+
+def pack(kernel, operands, rows, name):
+    out = jax.ShapeDtypeStruct((rows, LANES), jnp.float32)
     return pl.pallas_call(
         kernel,
         out_shape=(out, out),
-        in_specs=[VMEM_SPEC] * 4,
+        in_specs=[VMEM_SPEC] * len(operands),
         out_specs=(VMEM_SPEC,) * 2,
         compiler_params=pltpu.CompilerParams(vmem_limit_bytes=VMEM_BYTES),
-        name="pack_columns",
-    )(field, even_rows, odd_rows, after)
+        name=name,
+    )(*operands)
+
+
+def pack_sides(field, after, with_ends):
+    def kernel(*refs):
+        pack_sides_kernel(with_ends, *refs)
+
+    return pack(kernel, (field, after), field.shape[1] + (8 if with_ends else 0), "pack_sides")
+
+
+def pack_corners(even_rows, odd_rows):
+    return pack(pack_corners_kernel, (even_rows, odd_rows), 2 * REACH, "pack_corners")
 
 
 def edge_kernel(field, coeff, even_out, odd_out, sems):
@@ -432,17 +442,21 @@
 
 
 def finish(
-    grid_shape, base, fit, field, coeff, even_cols, odd_cols, even_ends, odd_ends, products, shifts,
-    table, entry, out, pad,
+    grid_shape, base, fit, field, coeff, even_cols, odd_cols, even_corners, odd_corners, even_ends,
+    odd_ends, products, shifts, table, entry, out, pad,
 ):
     rows, cols = field.shape[1:]
-    depth = rows + 2 * REACH
     odd_x = is_odd("gx")
-    even, other = even_cols[0:depth, :], odd_cols[0:depth, :]
-    for side, packed in ((0, jnp.where(odd_x, even, other)), (1, jnp.where(odd_x, other, even))):
-        pad[0, side] = packed
-        pad[1, side] = pltpu.roll(packed, HALF, 1)
-    even, other = even_ends[depth : depth + 8, :], odd_ends[depth : depth + 8, :]
+    for even_ref, odd_ref, start, place, depth in (
+        (even_cols, odd_cols, 0, REACH, rows),
+        (even_corners, odd_corners, 0, 0, REACH),
+        (even_corners, odd_corners, REACH, REACH + rows, REACH),
+    ):
+        even, other = even_ref[start : start + depth, :], odd_ref[start : start + depth, :]
+        for side, packed in ((0, jnp.where(odd_x, even, other)), (1, jnp.where(odd_x, other, even))):
+            pad[0, side, place : place + depth, :] = packed
+            pad[1, side, place : place + depth, :] = pltpu.roll(packed, HALF, 1)
+    even, other = even_ends[rows : rows + 8, :], odd_ends[rows : rows + 8, :]
     ends = (jnp.where(odd_x, even, other), jnp.where(odd_x, other, even))
     cut = (slice(0, LANES), slice(cols - LANES, cols))
     carry = tuple(products[index] for index in range(products.shape[0]))
@@ -464,14 +478,14 @@
 
 
 def first_kernel(
-    grid_shape, before, field, coeff, even_cols, odd_cols, products, shifts, table, entry,
-    out, sums, even_out, odd_out, pad,
+    grid_shape, before, field, coeff, even_cols, odd_cols, even_corners, odd_corners, products,
+    shifts, table, entry, out, sums, even_out, odd_out, pad,
 ):
     del before
     rows = field.shape[1]
     carry = finish(
-        grid_shape, None, None, field, coeff, even_cols, odd_cols, even_cols, odd_cols, products,
-        shifts, table, entry, out, pad,
+        grid_shape, None, None, field, coeff, even_cols, odd_cols, even_corners, odd_corners, even_cols,
+        odd_cols, products, shifts, table, entry, out, pad,
     )
     for index, value in enumerate(carry):
         sums[index] = value
@@ -482,14 +496,14 @@
 
 
 def second_kernel(
-    grid_shape, before, base, field, coeff, even_cols, odd_cols, even_ends, odd_ends, products,
-    sums, shifts, table, entry, out, parts, pad,
+    grid_shape, before, base, field, coeff, even_cols, odd_cols, even_corners, odd_corners, even_ends,
+    odd_ends, products, sums, shifts, table, entry, out, parts, pad,
 ):
     del before
     gamma, delta, omega, fit = fit_of(sums)
     carry = finish(
-        grid_shape, base, fit, field, coeff, even_cols, odd_cols, even_ends, odd_ends, products,
-        shifts, table, entry, out, pad,
+        grid_shape, base, fit, field, coeff, even_cols, odd_cols, even_corners, odd_corners, even_ends,
+        odd_ends, products, shifts, table, entry, out, pad,
     )
     rest2, rest_w, slope_rest, n_rest, slope_w, n_w = (
         jnp.sum(value, keepdims=True) for value in carry
@@ -606,22 +620,25 @@
     w_own, ends = on_tensor_core(
         own_first, "own_first", (right_side, coefficient), scalars, (full, sums_of(2)), own_pads, 6
     )
-    packed = pack(right_side, *rows0, ends, True)
-    cols0 = swap(*packed, "gx")
+    cols0 = swap(*pack_sides(right_side, ends, True), "gx")
+    packed = pack_corners(*rows0)
+    corners0 = swap(*packed, "gx")
     w_rows, products = on_tensor_core(
         rows_first, "rows_first", (w_own, right_side, coefficient, *rows0, packed[0]), scalars,
         (full, sums_of(3)), row_pads, 3, True,
     )
     w_vec, sums, even, odd = on_tensor_core(
-        bind(first_kernel), "first_apply", (w_rows, right_side, coefficient, *cols0, products),
-        scalars, (full, sums_of(3), edge, edge), side_pads, 3, True,
+        bind(first_kernel), "first_apply",
+        (w_rows, right_side, coefficient, *cols0, *corners0, products), scalars,
+        (full, sums_of(3), edge, edge), side_pads, 3, True,
     )
     rows1 = swap(even, odd, "gy")
     (n_own,) = on_tensor_core(
         own_second, "own_second", (w_vec, coefficient), scalars, (full,), own_pads, 6
     )
-    packed = pack(w_vec, *rows1, n_own, False)
-    cols1 = swap(*packed, "gx")
+    cols1 = swap(*pack_sides(w_vec, n_own, False), "gx")
+    packed = pack_corners(*rows1)
+    corners1 = swap(*packed, "gx")
     n_rows, products = on_tensor_core(
         rows_second, "rows_second",
         (n_own, w_vec, coefficient, *rows1, *rows0, packed[0], right_side, sums), scalars,
@@ -629,7 +646,7 @@
     )
     n_vec, parts = on_tensor_core(
         bind(second_kernel), "second_apply",
-        (n_rows, right_side, w_vec, coefficient, *cols1, *cols0, products, sums), scalars,
+        (n_rows, right_side, w_vec, coefficient, *cols1, *corners1, *cols0, products, sums), scalars,
         (full, jax.ShapeDtypeStruct((devices, LANES), jnp.float32)), side_pads, 3, True,
     )
     gathered = lax.all_to_all(parts, ("gx", "gy"), 0, 0, tiled=True)

time: 78.6 us -> 77.2 us (0.982)
  starting transfers between devices: 19 us -> 25.2 us
  blocking collectives: 33.8 us -> 28.8 us
  waiting for transfers between devices: 3.13 us -> 0.16 us
    ppermute x4 -> x6, starting transfers between devices: 12.7 us -> 17.9 us  [swap(): lax.ppermute(odd, axis, odd_swap(count))]
    all_to_all x1, blocking collectives: 33.8 us -> 28.8 us  [on_device(): gathered = lax.all_to_all(parts, ('gx', 'gy'), 0, 0, tiled=True)]
    ppermute x4 -> x6, waiting for transfers between devices: 2.71 us -> 0.15 us  [swap(): lax.ppermute(odd, axis, odd_swap(count))]
    ppermute x4 -> x6, starting transfers between devices: 6.3 us -> 7.33 us  [swap(): lax.ppermute(even, axis, even_swap(count))]
  transfers between devices with their start and end apart: 8 -> 12, of which waited for: 4 -> 1; matrix products, arithmetic and copies ran while one was open for 0% -> 0% of each run, Pallas kernels for 17% -> 18%
where the time goes in v5:
time: 77.2 us; the launch traced here: 76.9 us
  blocking collectives  28.8 us (37%)
  starting transfers between devices  25.2 us (33%)
  Pallas kernels  21.5 us (28%)
  between operations  1.07 us (1%)
    all_to_all x1, blocking collectives, on_device(): gathered = lax.all_to_all(parts, ('gx', 'gy'), 0, 0, tiled=True)  28.8 us
    ppermute x6, starting transfers between devices, swap(): lax.ppermute(odd, axis, odd_swap(count))  17.9 us
    pallas_call x6, Pallas kernels, on_tensor_core(): pl.pallas_call(kernel, out_shape=out_shape, in_specs=[VMEM_SPEC] * len(op...  17.1 us
    ppermute x6, starting transfers between devices, swap(): lax.ppermute(even, axis, even_swap(count))  7.33 us
    pallas_call x1, Pallas kernels, edge_rows(): pl.pallas_call(edge_kernel, out_shape=(out, out), in_specs=[pl.BlockSpec(...  2.05 us
    pallas_call x1, Pallas kernels, on_device(): pl.pallas_call(last_kernel, out_shape=(full, full), in_specs=[VMEM_SPEC]...  1.87 us
  transfers between devices with their start and end apart: 12, of which 1 were waited for; matrix products, arithmetic and copies ran while one was open for 0% of the time, Pallas kernels for 18%

profile of v5, /device:TPU:1, one launch (start us, length us, event | category | flops | bytes accessed | tf_op | source)
XLA Modules:
  0.0 76.9 jit_solution(5463151545262000670)
XLA Ops:
  0.6 0.0 copy-start
  0.6 0.0 copy-start.1
  0.6 2.0 %edge_rows.1 = (f32[2,72,512]{2,1,0:T(8,128)}, f32[2,72,512]{2,1,0:T(8,128)}) custom-call(f32[2,256,512]{2,1,0:T(8,128)} %base.1, f32[2,256,512]{2,1,0:T(8,128)} %refs_3_.3), custom_call_target="tpu_custom_call" | custom-call | tf_op jit(solution)/shard_map/edge_rows/pallas_call | solution.py:131
  2.7 0.0 copy-start.4
  2.7 2.1 %collective-permute-start = (f32[2,72,512]{2,1,0:T(8,128)}, f32[2,72,512]{2,1,0:T(8,128)S(1)}, u32[]{:S(2)}, u32[]{:S(2)}) collective-permute-start(f32[2,72,512]{2,1,0:T(8,128)} %get-tuple-element.25), channel_id=1, source_target_pairs={{0,1},{1,0},{2,3},{3,2},{4,5},{5,4},{6,7},{7,6},{8,9},{9,8},{10,11... | collective-permute-start | bytes 884744 | tf_op jit(solution)/shard_map/ppermute | solution.py:35
  4.8 0.0 copy-start.2
  4.8 0.0 copy-start.3
  4.8 0.8 %collective-permute-start.1 = (f32[2,72,512]{2,1,0:T(8,128)}, f32[2,72,512]{2,1,0:T(8,128)S(1)}, u32[]{:S(2)}, u32[]{:S(2)}) collective-permute-start(f32[2,72,512]{2,1,0:T(8,128)} %get-tuple-element.26), channel_id=1, source_target_pairs={{1,2},{2,1},{3,4},{4,3},{5,6},{6,5},{7,8},{8,7},{9,10},{10,9},{11,... | collective-permute-start | bytes 884744 | tf_op jit(solution)/shard_map/ppermute | solution.py:36
  5.7 0.0 copy-done.4
  5.7 0.1 copy.17.shifts.refs_0_.refs_8_.refs_2_.refs_12_
  5.8 0.0 copy-done
  5.8 0.0 copy-done.1
  5.8 0.0 copy-done.2
  5.8 0.0 copy-done.3
  5.8 4.7 %own_first.1 = (f32[2,256,512]{2,1,0:T(8,128)S(1)}, f32[2,8,128]{2,1,0:T(8,128)S(1)}) custom-call(f32[2,256,512]{2,1,0:T(8,128)S(1)} %copy-done, f32[2,256,512]{2,1,0:T(8,128)S(1)} %copy-done.1, s32[6,2,2]{2,1,0:T(2,128)S(1)} %copy.17.shifts.refs_0_.refs_8_.refs_2_.refs_12_, f32[35]{0:T(128)S(1)} %copy-done.2, s32[2]{0:T(128)S(1)} %copy-done.3), custom_call_target="tpu_custom_call" | custom-call | bytes 18000000 | tf_op jit(solution)/shard_map/own_first/pallas_call | solution.py:568
  10.5 0.1 pack_sides.2
  10.6 1.2 %collective-permute-start.2 = (f32[264,128]{1,0:T(8,128)S(1)}, f32[264,128]{1,0:T(8,128)S(1)}, u32[]{:S(2)}, u32[]{:S(2)}) collective-permute-start(f32[264,128]{1,0:T(8,128)S(1)} %get-tuple-element.30), channel_id=1, source_target_pairs={{0,16},{16,0},{32,48},{48,32},{64,80},{80,64},{96,112},{112,96},{1... | collective-permute-start | bytes 405512 | tf_op jit(solution)/shard_map/ppermute | solution.py:35
  11.8 3.3 %collective-permute-start.3 = (f32[264,128]{1,0:T(8,128)S(1)}, f32[264,128]{1,0:T(8,128)S(1)}, u32[]{:S(2)}, u32[]{:S(2)}) collective-permute-start(f32[264,128]{1,0:T(8,128)S(1)} %get-tuple-element.31), channel_id=1, source_target_pairs={{16,32},{32,16},{48,64},{64,48},{80,96},{96,80},{112,128},{128,112... | collective-permute-start | bytes 405512 | tf_op jit(solution)/shard_map/ppermute | solution.py:36
  15.1 0.0 collective-permute-done.even_rows.even.even_edge
  15.1 0.0 collective-permute-done.1.odd_rows.odd.odd_edge
  15.1 0.1 pack_corners.2
  15.2 0.1 collective-permute-start.4
  15.3 3.9 %collective-permute-start.5 = (f32[128,128]{1,0:T(8,128)S(1)}, f32[128,128]{1,0:T(8,128)S(1)}, u32[]{:S(2)}, u32[]{:S(2)}) collective-permute-start(f32[128,128]{1,0:T(8,128)S(1)} %get-tuple-element.32), channel_id=1, source_target_pairs={{16,32},{32,16},{48,64},{64,48},{80,96},{96,80},{112,128},{128,112... | collective-permute-start | bytes 196616 | tf_op jit(solution)/shard_map/ppermute | solution.py:36
  19.3 1.8 %rows_first.1 = (f32[2,256,512]{2,1,0:T(8,128)S(1)}, f32[3,8,128]{2,1,0:T(8,128)S(1)}) custom-call(f32[2,256,512]{2,1,0:T(8,128)S(1)} %get-tuple-element.24.before, f32[2,256,512]{2,1,0:T(8,128)S(1)} %copy-done, f32[2,256,512]{2,1,0:T(8,128)S(1)} %copy-done.1, ...), custom_call_target="tpu_custom_call", output_to_operand_aliasing={{0}: (0, {})} | custom-call | bytes 9000000 | tf_op jit(solution)/shard_map/rows_first/pallas_call | solution.py:568
  21.0 0.0 collective-permute-done.2.refs_3_.refs_8_
  21.1 0.0 collective-permute-done.3.refs_4_.refs_9_
  21.1 0.0 collective-permute-done.4.refs_5_
  21.1 0.1 collective-permute-done.5.refs_6_
  21.2 1.8 %first_apply.1 = (f32[2,256,512]{2,1,0:T(8,128)S(1)}, f32[3,8,128]{2,1,0:T(8,128)S(1)}, f32[2,64,512]{2,1,0:T(8,128)S(1)}, f32[2,64,512]{2,1,0:T(8,128)S(1)}) custom-call(f32[2,256,512]{2,1,0:T(8,128)S(1)} %get-tuple-element.28.refs_0_, f32[2,256,512]{2,1,0:T(8,128)S(1)} %copy-done, f32[2,256,512]{2,1,0:T(8,128)S(1)} %copy-done.1, ...), custom_call_target="tpu_custom_call", output_to_operand_aliasing={{0}: (0, {})} | custom-call | bytes 9000000 | tf_op jit(solution)/shard_map/first_apply/pallas_call | solution.py:568
  23.1 3.7 %collective-permute-start.6 = (f32[2,64,512]{2,1,0:T(8,128)S(1)}, f32[2,64,512]{2,1,0:T(8,128)S(1)}, u32[]{:S(2)}, u32[]{:S(2)}) collective-permute-start(f32[2,64,512]{2,1,0:T(8,128)S(1)} %get-tuple-element.35), channel_id=1, source_target_pairs={{0,1},{1,0},{2,3},{3,2},{4,5},{5,4},{6,7},{7,6},{8,9},{9,8},{10,11... | collective-permute-start | bytes 786440 | tf_op jit(solution)/shard_map/ppermute | solution.py:35
  26.8 0.8 %collective-permute-start.7 = (f32[2,64,512]{2,1,0:T(8,128)S(1)}, f32[2,64,512]{2,1,0:T(8,128)S(1)}, u32[]{:S(2)}, u32[]{:S(2)}) collective-permute-start(f32[2,64,512]{2,1,0:T(8,128)S(1)} %get-tuple-element.36), channel_id=1, source_target_pairs={{1,2},{2,1},{3,4},{4,3},{5,6},{6,5},{7,8},{8,7},{9,10},{10,9},{11,... | collective-permute-start | bytes 786440 | tf_op jit(solution)/shard_map/ppermute | solution.py:36
  27.6 4.6 %own_second.1.before.refs_1_ = f32[2,256,512]{2,1,0:T(8,128)S(1)} custom-call(f32[2,256,512]{2,1,0:T(8,128)S(1)} %get-tuple-element.34.field.refs_0_.refs_2_.w_vec, f32[2,256,512]{2,1,0:T(8,128)S(1)} %copy-done.1, s32[6,2,2]{2,1,0:T(2,128)S(1)} %copy.17.shifts.refs_0_.refs_8_.refs_2_.refs_12_, f32[35]{0:T(128)S(1)} %copy-done.2, s32[2]{0:T(128)S(1)} %copy-done.3), custom_call_target="tpu_custom_call" | custom-call | bytes 18000000 | tf_op jit(solution)/shard_map/own_second/pallas_call | solution.py:568
  32.2 0.1 pack_sides.3
  32.4 0.1 collective-permute-start.8
  32.5 3.9 %collective-permute-start.9 = (f32[256,128]{1,0:T(8,128)S(1)}, f32[256,128]{1,0:T(8,128)S(1)}, u32[]{:S(2)}, u32[]{:S(2)}) collective-permute-start(f32[256,128]{1,0:T(8,128)S(1)} %get-tuple-element.41), channel_id=1, source_target_pairs={{16,32},{32,16},{48,64},{64,48},{80,96},{96,80},{112,128},{128,112... | collective-permute-start | bytes 393224 | tf_op jit(solution)/shard_map/ppermute | solution.py:36
  36.4 0.0 collective-permute-done.6.even_rows.even
  36.4 0.0 collective-permute-done.7.odd_rows.odd
  36.4 0.1 pack_corners.3
  36.6 0.1 collective-permute-start.10
  36.7 5.1 %collective-permute-start.11 = (f32[128,128]{1,0:T(8,128)S(1)}, f32[128,128]{1,0:T(8,128)S(1)}, u32[]{:S(2)}, u32[]{:S(2)}) collective-permute-start(f32[128,128]{1,0:T(8,128)S(1)} %get-tuple-element.42), channel_id=1, source_target_pairs={{16,32},{32,16},{48,64},{64,48},{80,96},{96,80},{112,128},{128,112... | collective-permute-start | bytes 196616 | tf_op jit(solution)/shard_map/ppermute | solution.py:36
  41.8 2.1 %rows_second.1 = (f32[2,256,512]{2,1,0:T(8,128)S(1)}, f32[6,8,128]{2,1,0:T(8,128)S(1)}) custom-call(f32[2,256,512]{2,1,0:T(8,128)S(1)} %own_second.1.before.refs_1_, f32[2,256,512]{2,1,0:T(8,128)S(1)} %get-tuple-element.34.field.refs_0_.refs_2_.w_vec, f32[2,256,512]{2,1,0:T(8,128)S(1)} %copy-done.1, ...), custom_call_target="tpu_custom_call", output_to_operand_aliasing={{0}: (0, {})} | custom-call | bytes 9000000 | tf_op jit(solution)/shard_map/rows_second/pallas_call | solution.py:568
  43.9 0.0 collective-permute-done.8.refs_4_
  43.9 0.0 collective-permute-done.9.refs_5_
  43.9 0.0 collective-permute-done.10.refs_6_
  43.9 0.0 collective-permute-done.11.refs_7_
  43.9 2.1 %second_apply.1 = (f32[2,256,512]{2,1,0:T(8,128)S(1)}, f32[256,128]{1,0:T(8,128)S(1)}) custom-call(f32[2,256,512]{2,1,0:T(8,128)S(1)} %get-tuple-element.39.refs_0_, f32[2,256,512]{2,1,0:T(8,128)S(1)} %copy-done, f32[2,256,512]{2,1,0:T(8,128)S(1)} %get-tuple-element.34.field.refs_0_.refs_2_.w_vec, ...), custom_call_target="tpu_custom_call", output_to_operand_aliasing={{0}: (0, {})} | custom-call | bytes 9000000 | tf_op jit(solution)/shard_map/second_apply/pallas_call | solution.py:568
  46.0 28.8 %all_to_all.11 = f32[256,1,128]{2,1,0:T(1,128)S(1)} all-to-all(f32[256,1,128]{2,1,0:T(1,128)S(1)} %bitcast.5), channel_id=1, replica_groups=mesh['gx'=16,'gy'=16] {'gx','gy'}, dimensions={0} | all-to-all | bytes 262144 | tf_op jit(solution)/shard_map/all_to_all | solution.py:652
  74.8 1.9 %last_update.1 = (f32[2,256,512]{2,1,0:T(8,128)}, f32[2,256,512]{2,1,0:T(8,128)}) custom-call(f32[256,128]{1,0:T(8,128)S(1)} %bitcast.4, f32[2,256,512]{2,1,0:T(8,128)S(1)} %copy-done, f32[2,256,512]{2,1,0:T(8,128)S(1)} %get-tuple-element.34.field.refs_0_.refs_2_.w_vec, f32[2,256,512]{2,1,0:T(8,128)S(1)} %get-tuple-element.45.n_vec), custom_call_target="tpu_custom_call" | custom-call | tf_op jit(solution)/shard_map/last_update/pallas_call | solution.py:653
Async XLA Ops:
  0.6 5.1 %copy-start = (f32[2,256,512]{2,1,0:T(8,128)S(1)}, f32[2,256,512]{2,1,0:T(8,128)}, u32[]{:S(2)}) copy-start(f32[2,256,512]{2,1,0:T(8,128)} %base.1) | copy-start | bytes 3145732
  0.6 5.1 %copy-start.1 = (f32[2,256,512]{2,1,0:T(8,128)S(1)}, f32[2,256,512]{2,1,0:T(8,128)}, u32[]{:S(2)}) copy-start(f32[2,256,512]{2,1,0:T(8,128)} %refs_3_.3) | copy-start | bytes 3145732
  2.7 3.0 %copy-start.4 = (s32[6,2,2]{0,2,1:T(2,128)S(1)}, s32[6,2,2]{0,2,1:T(2,128)}, u32[]{:S(2)}) copy-start(s32[6,2,2]{0,2,1:T(2,128)} %param.9) | copy-start | bytes 292
  2.7 12.4 %collective-permute-start = (f32[2,72,512]{2,1,0:T(8,128)}, f32[2,72,512]{2,1,0:T(8,128)S(1)}, u32[]{:S(2)}, u32[]{:S(2)}) collective-permute-start(f32[2,72,512]{2,1,0:T(8,128)} %get-tuple-element.25), channel_id=1, source_target_pairs={{0,1},{1,0},{2,3},{3,2},{4,5},{5,4},{6,7},{7,6},{8,9},{9,8},{10,11... | collective-permute-start | bytes 884744 | tf_op jit(solution)/shard_map/ppermute | solution.py:35
  4.8 0.9 %copy-start.2 = (f32[35]{0:T(128)S(1)}, f32[35]{0:T(128)}, u32[]{:S(2)}) copy-start(f32[35]{0:T(128)} %refs_13_.1) | copy-start | bytes 424
  4.8 0.9 %copy-start.3 = (s32[2]{0:T(128)S(1)}, s32[2]{0:T(128)}, u32[]{:S(2)}) copy-start(s32[2]{0:T(128)} %refs_14_.1) | copy-start | bytes 28
  4.8 10.3 %collective-permute-start.1 = (f32[2,72,512]{2,1,0:T(8,128)}, f32[2,72,512]{2,1,0:T(8,128)S(1)}, u32[]{:S(2)}, u32[]{:S(2)}) collective-permute-start(f32[2,72,512]{2,1,0:T(8,128)} %get-tuple-element.26), channel_id=1, source_target_pairs={{1,2},{2,1},{3,4},{4,3},{5,6},{6,5},{7,8},{8,7},{9,10},{10,9},{11,... | collective-permute-start | bytes 884744 | tf_op jit(solution)/shard_map/ppermute | solution.py:36
  10.6 10.4 %collective-permute-start.2 = (f32[264,128]{1,0:T(8,128)S(1)}, f32[264,128]{1,0:T(8,128)S(1)}, u32[]{:S(2)}, u32[]{:S(2)}) collective-permute-start(f32[264,128]{1,0:T(8,128)S(1)} %get-tuple-element.30), channel_id=1, source_target_pairs={{0,16},{16,0},{32,48},{48,32},{64,80},{80,64},{96,112},{112,96},{1... | collective-permute-start | bytes 405512 | tf_op jit(solution)/shard_map/ppermute | solution.py:35
  11.8 9.2 %collective-permute-start.3 = (f32[264,128]{1,0:T(8,128)S(1)}, f32[264,128]{1,0:T(8,128)S(1)}, u32[]{:S(2)}, u32[]{:S(2)}) collective-permute-start(f32[264,128]{1,0:T(8,128)S(1)} %get-tuple-element.31), channel_id=1, source_target_pairs={{16,32},{32,16},{48,64},{64,48},{80,96},{96,80},{112,128},{128,112... | collective-permute-start | bytes 405512 | tf_op jit(solution)/shard_map/ppermute | solution.py:36
  15.2 5.8 %collective-permute-start.4 = (f32[128,128]{1,0:T(8,128)S(1)}, f32[128,128]{1,0:T(8,128)S(1)}, u32[]{:S(2)}, u32[]{:S(2)}) collective-permute-start(f32[128,128]{1,0:T(8,128)S(1)} %get-tuple-element.27.packed), channel_id=1, source_target_pairs={{0,16},{16,0},{32,48},{48,32},{64,80},{80,64},{96,112},{112,96},{1... | collective-permute-start | bytes 196616 | tf_op jit(solution)/shard_map/ppermute | solution.py:35
  15.3 5.9 %collective-permute-start.5 = (f32[128,128]{1,0:T(8,128)S(1)}, f32[128,128]{1,0:T(8,128)S(1)}, u32[]{:S(2)}, u32[]{:S(2)}) collective-permute-start(f32[128,128]{1,0:T(8,128)S(1)} %get-tuple-element.32), channel_id=1, source_target_pairs={{16,32},{32,16},{48,64},{64,48},{80,96},{96,80},{112,128},{128,112... | collective-permute-start | bytes 196616 | tf_op jit(solution)/shard_map/ppermute | solution.py:36
  23.1 13.4 %collective-permute-start.6 = (f32[2,64,512]{2,1,0:T(8,128)S(1)}, f32[2,64,512]{2,1,0:T(8,128)S(1)}, u32[]{:S(2)}, u32[]{:S(2)}) collective-permute-start(f32[2,64,512]{2,1,0:T(8,128)S(1)} %get-tuple-element.35), channel_id=1, source_target_pairs={{0,1},{1,0},{2,3},{3,2},{4,5},{5,4},{6,7},{7,6},{8,9},{9,8},{10,11... | collective-permute-start | bytes 786440 | tf_op jit(solution)/shard_map/ppermute | solution.py:35
  26.8 9.7 %collective-permute-start.7 = (f32[2,64,512]{2,1,0:T(8,128)S(1)}, f32[2,64,512]{2,1,0:T(8,128)S(1)}, u32[]{:S(2)}, u32[]{:S(2)}) collective-permute-start(f32[2,64,512]{2,1,0:T(8,128)S(1)} %get-tuple-element.36), channel_id=1, source_target_pairs={{1,2},{2,1},{3,4},{4,3},{5,6},{6,5},{7,8},{8,7},{9,10},{10,9},{11,... | collective-permute-start | bytes 786440 | tf_op jit(solution)/shard_map/ppermute | solution.py:36
  32.4 11.5 %collective-permute-start.8 = (f32[256,128]{1,0:T(8,128)S(1)}, f32[256,128]{1,0:T(8,128)S(1)}, u32[]{:S(2)}, u32[]{:S(2)}) collective-permute-start(f32[256,128]{1,0:T(8,128)S(1)} %get-tuple-element.40), channel_id=1, source_target_pairs={{0,16},{16,0},{32,48},{48,32},{64,80},{80,64},{96,112},{112,96},{1... | collective-permute-start | bytes 393224 | tf_op jit(solution)/shard_map/ppermute | solution.py:35
  32.5 11.4 %collective-permute-start.9 = (f32[256,128]{1,0:T(8,128)S(1)}, f32[256,128]{1,0:T(8,128)S(1)}, u32[]{:S(2)}, u32[]{:S(2)}) collective-permute-start(f32[256,128]{1,0:T(8,128)S(1)} %get-tuple-element.41), channel_id=1, source_target_pairs={{16,32},{32,16},{48,64},{64,48},{80,96},{96,80},{112,128},{128,112... | collective-permute-start | bytes 393224 | tf_op jit(solution)/shard_map/ppermute | solution.py:36
  36.6 7.3 %collective-permute-start.10 = (f32[128,128]{1,0:T(8,128)S(1)}, f32[128,128]{1,0:T(8,128)S(1)}, u32[]{:S(2)}, u32[]{:S(2)}) collective-permute-start(f32[128,128]{1,0:T(8,128)S(1)} %get-tuple-element.37.packed), channel_id=1, source_target_pairs={{0,16},{16,0},{32,48},{48,32},{64,80},{80,64},{96,112},{112,96},{1... | collective-permute-start | bytes 196616 | tf_op jit(solution)/shard_map/ppermute | solution.py:35
  36.7 7.2 %collective-permute-start.11 = (f32[128,128]{1,0:T(8,128)S(1)}, f32[128,128]{1,0:T(8,128)S(1)}, u32[]{:S(2)}, u32[]{:S(2)}) collective-permute-start(f32[128,128]{1,0:T(8,128)S(1)} %get-tuple-element.42), channel_id=1, source_target_pairs={{16,32},{32,16},{48,64},{64,48},{80,96},{96,80},{112,128},{128,112... | collective-permute-start | bytes 196616 | tf_op jit(solution)/shard_map/ppermute | solution.py:36

commit v6 on v5

--- a/solution.py
+++ b/solution.py
@@ -12,7 +12,7 @@
 UNROLL = 8
 PIECES = 4
 VMEM_BYTES = 32 * 1024 * 1024
-EDGE_BYTES = 60 * 1024 * 1024
+EDGE_BYTES = 53 * 1024 * 1024
 VMEM_SPEC = pl.BlockSpec(memory_space=pltpu.VMEM)
 SMEM_SPEC = pl.BlockSpec(memory_space=pltpu.SMEM)
 
@@ -293,8 +293,8 @@
 
 
 def rows_kernel(
-    grid_shape, field, coeff, even_rows, odd_rows, even_edge, odd_edge, base, sums, shifts,
-    table, entry, out, products, pad,
+    grid_shape, field, coeff, even_rows, odd_rows, even_edge, odd_edge, even_cols, odd_cols, even_ends,
+    odd_ends, base, sums, shifts, table, entry, out, products, side_pad, pad,
 ):
     rows, cols = field.shape[1:]
     tiles = cols // LANES
@@ -394,6 +394,11 @@
             return tuple(a + b for a, b in zip(carry, more, strict=True))
 
         carry = lax.fori_loop(0, rows // CHUNK, add, carry, unroll=UNROLL)
+    fill_sides(side_pad, even_cols, odd_cols, 0, REACH, rows)
+    carry = finish(
+        range(REACH // CHUNK, (rows - REACH) // CHUNK), carry, grid_shape, base, fit, field, coeff,
+        even_ends, odd_ends, shifts, table, entry, out, side_pad,
+    )
     for index, value in enumerate(carry):
         products[index] = value
 
@@ -409,10 +414,10 @@
     own = [field[layer, pl.ds(row, CHUNK), lanes] for lanes in cut]
     result = []
     for side, spot in ((0, 0), (1, LANES - 1)):
-        at = layer * (rows // 8) + lax.shift_right_logical(row, 3)
+        at = layer * (rows // 8) + row // 8
         edge_c = jnp.concatenate(
             [
-                pltpu.roll(ends[side], jnp.bitwise_and(LANES + spot - at - i, LANES - 1), 1)
+                pltpu.roll(ends[side], (spot - at - i) % LANES, 1)
                 for i in range(CHUNK // 8)
             ]
         )
@@ -441,51 +446,55 @@
     return own, result
 
 
+def fill_sides(pad, even_ref, odd_ref, start, place, depth):
+    odd_x = is_odd("gx")
+    even, other = even_ref[start : start + depth, :], odd_ref[start : start + depth, :]
+    for side, packed in ((0, jnp.where(odd_x, even, other)), (1, jnp.where(odd_x, other, even))):
+        pad[0, side, place : place + depth, :] = packed
+        pad[1, side, place : place + depth, :] = pltpu.roll(packed, HALF, 1)
+
+
 def finish(
-    grid_shape, base, fit, field, coeff, even_cols, odd_cols, even_corners, odd_corners, even_ends,
-    odd_ends, products, shifts, table, entry, out, pad,
+    chunks, carry, grid_shape, base, fit, field, coeff, even_ends, odd_ends, shifts, table, entry, out,
+    pad,
 ):
     rows, cols = field.shape[1:]
     odd_x = is_odd("gx")
-    for even_ref, odd_ref, start, place, depth in (
-        (even_cols, odd_cols, 0, REACH, rows),
-        (even_corners, odd_corners, 0, 0, REACH),
-        (even_corners, odd_corners, REACH, REACH + rows, REACH),
-    ):
-        even, other = even_ref[start : start + depth, :], odd_ref[start : start + depth, :]
-        for side, packed in ((0, jnp.where(odd_x, even, other)), (1, jnp.where(odd_x, other, even))):
-            pad[0, side, place : place + depth, :] = packed
-            pad[1, side, place : place + depth, :] = pltpu.roll(packed, HALF, 1)
     even, other = even_ends[rows : rows + 8, :], odd_ends[rows : rows + 8, :]
     ends = (jnp.where(odd_x, even, other), jnp.where(odd_x, other, even))
     cut = (slice(0, LANES), slice(cols - LANES, cols))
-    carry = tuple(products[index] for index in range(products.shape[0]))
     for layer in range(2):
         weight = weight_of(table, entry, layer)
-
-        def step(i, carry, layer=layer, weight=weight):
-            row = pl.multiple_of(i * CHUNK, CHUNK)
+        for row in (chunk * CHUNK for chunk in chunks):
             own, result = finish_chunk(
                 grid_shape, layer, row, field, coeff, out, pad, ends, shifts, weight
             )
-            chunk = pl.ds(row, CHUNK)
-            start = None if base is None else [base[layer, chunk, lanes] for lanes in cut]
+            start = None if base is None else [base[layer, row : row + CHUNK, x] for x in cut]
             more = products_of(own, result, start, fit)
-            return tuple(a + b for a, b in zip(carry, more, strict=True))
-
-        carry = lax.fori_loop(0, rows // CHUNK, step, carry, unroll=UNROLL)
+            carry = tuple(a + b for a, b in zip(carry, more, strict=True))
     return carry
 
 
+def finish_ends(grid_shape, even_corners, odd_corners, products, pad, field, *rest):
+    rows = field.shape[1]
+    fill_sides(pad, even_corners, odd_corners, 0, 0, REACH)
+    fill_sides(pad, even_corners, odd_corners, REACH, REACH + rows, REACH)
+    depth = REACH // CHUNK
+    chunks = [*range(depth), *range(rows // CHUNK - depth, rows // CHUNK)]
+    carry = tuple(products[index] for index in range(products.shape[0]))
+    base, fit, *others = rest
+    return finish(chunks, carry, grid_shape, base, fit, field, *others, pad)
+
+
 def first_kernel(
-    grid_shape, before, field, coeff, even_cols, odd_cols, even_corners, odd_corners, products,
-    shifts, table, entry, out, sums, even_out, odd_out, pad,
+    grid_shape, before, pad_before, field, coeff, even_ends, odd_ends, even_corners, odd_corners,
+    products, shifts, table, entry, out, pad, sums, even_out, odd_out,
 ):
-    del before
+    del before, pad_before
     rows = field.shape[1]
-    carry = finish(
-        grid_shape, None, None, field, coeff, even_cols, odd_cols, even_corners, odd_corners, even_cols,
-        odd_cols, products, shifts, table, entry, out, pad,
+    carry = finish_ends(
+        grid_shape, even_corners, odd_corners, products, pad, field, None, None, coeff, even_ends,
+        odd_ends, shifts, table, entry, out,
     )
     for index, value in enumerate(carry):
         sums[index] = value
@@ -496,14 +505,14 @@
 
 
 def second_kernel(
-    grid_shape, before, base, field, coeff, even_cols, odd_cols, even_corners, odd_corners, even_ends,
-    odd_ends, products, sums, shifts, table, entry, out, parts, pad,
+    grid_shape, before, pad_before, base, field, coeff, even_ends, odd_ends, even_corners, odd_corners,
+    products, sums, shifts, table, entry, out, pad, parts,
 ):
-    del before
+    del before, pad_before
     gamma, delta, omega, fit = fit_of(sums)
-    carry = finish(
-        grid_shape, base, fit, field, coeff, even_cols, odd_cols, even_corners, odd_corners, even_ends,
-        odd_ends, products, shifts, table, entry, out, pad,
+    carry = finish_ends(
+        grid_shape, even_corners, odd_corners, products, pad, field, base, fit, coeff, even_ends,
+        odd_ends, shifts, table, entry, out,
     )
     rest2, rest_w, slope_rest, n_rest, slope_w, n_w = (
         jnp.sum(value, keepdims=True) for value in carry
@@ -564,14 +573,14 @@
         copy.wait()
 
 
-def on_tensor_core(kernel, name, operands, scalars, out_shape, scratch, microseconds, in_place=False):
+def on_tensor_core(kernel, name, operands, scalars, out_shape, scratch, microseconds, in_place=0):
     return pl.pallas_call(
         kernel,
         out_shape=out_shape,
         in_specs=[VMEM_SPEC] * len(operands) + [SMEM_SPEC] * len(scalars),
         out_specs=(VMEM_SPEC,) * len(out_shape),
         scratch_shapes=[pltpu.VMEM(shape, jnp.float32) for shape in scratch],
-        input_output_aliases={0: 0} if in_place else {},
+        input_output_aliases={index: index for index in range(in_place)},
         compiler_params=pltpu.CompilerParams(vmem_limit_bytes=VMEM_BYTES),
         cost_estimate=pl.CostEstimate(
             flops=0, bytes_accessed=3_000_000 * microseconds, transcendentals=0
@@ -591,7 +600,7 @@
     scalars = (shifts, strength_table, layer_entry)
     own_pads = [(2, tiles + 2, rows + 2 * REACH, LANES), (2, tiles + 2, rows + 16, LANES)]
     row_pads = [(2, 2, tiles + 2, 2 * REACH, LANES)]
-    side_pads = [(2, 2, rows + 2 * REACH, LANES)]
+    side_pad = jax.ShapeDtypeStruct((2, 2, rows + 2 * REACH, LANES), jnp.float32)
 
     def sums_of(count):
         return jax.ShapeDtypeStruct((count, 8, LANES), jnp.float32)
@@ -602,13 +611,16 @@
 
         return bound
 
-    def rows_first(before, field, coeff, even, odd, packed, *refs):
+    def rows_first(before, packed, field, coeff, even, odd, even_cols, odd_cols, *refs):
         del before, packed
-        rows_kernel(grid_shape, field, coeff, even, odd, even, odd, None, None, *refs)
-
-    def rows_second(before, field, coeff, even, odd, even_edge, odd_edge, packed, *refs):
+        rows_kernel(
+            grid_shape, field, coeff, even, odd, even, odd, even_cols, odd_cols, even_cols, odd_cols,
+            None, None, *refs,
+        )
+
+    def rows_second(before, packed, *refs):
         del before, packed
-        rows_kernel(grid_shape, field, coeff, even, odd, even_edge, odd_edge, *refs)
+        rows_kernel(grid_shape, *refs)
 
     def own_first(field, coeff, shifts, table, entry, out, ends, *pads):
         own_kernel(grid_shape, field, coeff, shifts, table, entry, out, ends, *pads)
@@ -623,14 +635,14 @@
     cols0 = swap(*pack_sides(right_side, ends, True), "gx")
     packed = pack_corners(*rows0)
     corners0 = swap(*packed, "gx")
-    w_rows, products = on_tensor_core(
-        rows_first, "rows_first", (w_own, right_side, coefficient, *rows0, packed[0]), scalars,
-        (full, sums_of(3)), row_pads, 3, True,
-    )
-    w_vec, sums, even, odd = on_tensor_core(
+    w_rows, products, sides = on_tensor_core(
+        rows_first, "rows_first", (w_own, packed[0], right_side, coefficient, *rows0, *cols0), scalars,
+        (full, sums_of(3), side_pad), row_pads, 3, 1,
+    )
+    w_vec, _, sums, even, odd = on_tensor_core(
         bind(first_kernel), "first_apply",
-        (w_rows, right_side, coefficient, *cols0, *corners0, products), scalars,
-        (full, sums_of(3), edge, edge), side_pads, 3, True,
+        (w_rows, sides, right_side, coefficient, *cols0, *corners0, products), scalars,
+        (full, side_pad, sums_of(3), edge, edge), [], 3, 2,
     )
     rows1 = swap(even, odd, "gy")
     (n_own,) = on_tensor_core(
@@ -639,15 +651,15 @@
     cols1 = swap(*pack_sides(w_vec, n_own, False), "gx")
     packed = pack_corners(*rows1)
     corners1 = swap(*packed, "gx")
-    n_rows, products = on_tensor_core(
+    n_rows, products, sides = on_tensor_core(
         rows_second, "rows_second",
-        (n_own, w_vec, coefficient, *rows1, *rows0, packed[0], right_side, sums), scalars,
-        (full, sums_of(6)), row_pads, 3, True,
-    )
-    n_vec, parts = on_tensor_core(
+        (n_own, packed[0], w_vec, coefficient, *rows1, *rows0, *cols1, *cols0, right_side, sums),
+        scalars, (full, sums_of(6), side_pad), row_pads, 3, 1,
+    )
+    n_vec, _, parts = on_tensor_core(
         bind(second_kernel), "second_apply",
-        (n_rows, right_side, w_vec, coefficient, *cols1, *corners1, *cols0, products, sums), scalars,
-        (full, jax.ShapeDtypeStruct((devices, LANES), jnp.float32)), side_pads, 3, True,
+        (n_rows, sides, right_side, w_vec, coefficient, *cols0, *corners1, products, sums), scalars,
+        (full, side_pad, jax.ShapeDtypeStruct((devices, LANES), jnp.float32)), [], 3, 2,
     )
     gathered = lax.all_to_all(parts, ("gx", "gy"), 0, 0, tiled=True)
     return pl.pallas_call(

time: 77.2 us -> 75.2 us (0.974)
  blocking collectives: 28.8 us -> 27.7 us
  Pallas kernels: 21.5 us -> 20.7 us
    all_to_all x1, blocking collectives: 28.8 us -> 27.7 us  [on_device(): gathered = lax.all_to_all(parts, ('gx', 'gy'), 0, 0, tiled=True)]
    pallas_call x1, Pallas kernels: 2.05 us -> 1.24 us  [edge_rows(): pl.pallas_call(edge_kernel, out_shape=(out, out), in_specs=[pl.BlockSpec(...]
  transfers between devices with their start and end apart: 12 -> 12, of which waited for: 1 -> 0; matrix products, arithmetic and copies ran while one was open for 0% -> 0% of each run, Pallas kernels for 18% -> 20%
where the time goes in v6:
time: 75.2 us; the launch traced here: 74.9 us
  blocking collectives  27.7 us (37%)
  starting transfers between devices  25.2 us (34%)
  Pallas kernels  20.7 us (28%)
  between operations  1.08 us (1%)
    all_to_all x1, blocking collectives, on_device(): gathered = lax.all_to_all(parts, ('gx', 'gy'), 0, 0, tiled=True)  27.7 us
    ppermute x6, starting transfers between devices, swap(): lax.ppermute(odd, axis, odd_swap(count))  17.9 us
    pallas_call x6, Pallas kernels, on_tensor_core(): pl.pallas_call(kernel, out_shape=out_shape, in_specs=[VMEM_SPEC] * len(op...  17.1 us
    ppermute x6, starting transfers between devices, swap(): lax.ppermute(even, axis, even_swap(count))  7.32 us
    pallas_call x1, Pallas kernels, on_device(): pl.pallas_call(last_kernel, out_shape=(full, full), in_specs=[VMEM_SPEC]...  1.87 us
  transfers between devices with their start and end apart: 12, of which 0 were waited for; matrix products, arithmetic and copies ran while one was open for 0% of the time, Pallas kernels for 20%

profile of v6, /device:TPU:1, one launch (start us, length us, event | category | flops | bytes accessed | tf_op | source)
XLA Modules:
  0.0 74.9 jit_solution(13920381960970116715)
XLA Ops:
  0.6 0.0 copy-start
  0.6 0.0 copy-start.1
  0.6 1.2 %edge_rows.1 = (f32[2,72,512]{2,1,0:T(8,128)S(1)}, f32[2,72,512]{2,1,0:T(8,128)S(1)}) custom-call(f32[2,256,512]{2,1,0:T(8,128)} %base.1, f32[2,256,512]{2,1,0:T(8,128)} %refs_4_.1), custom_call_target="tpu_custom_call" | custom-call | tf_op jit(solution)/shard_map/edge_rows/pallas_call | solution.py:131
  1.9 0.0 copy-start.4
  1.9 2.1 %collective-permute-start = (f32[2,72,512]{2,1,0:T(8,128)S(1)}, f32[2,72,512]{2,1,0:T(8,128)S(1)}, u32[]{:S(2)}, u32[]{:S(2)}) collective-permute-start(f32[2,72,512]{2,1,0:T(8,128)S(1)} %get-tuple-element.27), channel_id=1, source_target_pairs={{0,1},{1,0},{2,3},{3,2},{4,5},{5,4},{6,7},{7,6},{8,9},{9,8},{10,11... | collective-permute-start | bytes 884744 | tf_op jit(solution)/shard_map/ppermute | solution.py:35
  4.0 0.0 copy-start.2
  4.0 0.0 copy-start.3
  4.0 0.8 %collective-permute-start.1 = (f32[2,72,512]{2,1,0:T(8,128)S(1)}, f32[2,72,512]{2,1,0:T(8,128)S(1)}, u32[]{:S(2)}, u32[]{:S(2)}) collective-permute-start(f32[2,72,512]{2,1,0:T(8,128)S(1)} %get-tuple-element.28), channel_id=1, source_target_pairs={{1,2},{2,1},{3,4},{4,3},{5,6},{6,5},{7,8},{8,7},{9,10},{10,9},{11,... | collective-permute-start | bytes 884744 | tf_op jit(solution)/shard_map/ppermute | solution.py:36
  4.8 0.0 copy-done.4
  4.9 0.1 copy.19.shifts.refs_0_.refs_9_.refs_12_.refs_11_
  5.0 0.0 copy-done
  5.0 0.0 copy-done.1
  5.0 0.0 copy-done.2
  5.0 0.0 copy-done.3
  5.0 4.7 %own_first.1 = (f32[2,256,512]{2,1,0:T(8,128)S(1)}, f32[2,8,128]{2,1,0:T(8,128)S(1)}) custom-call(f32[2,256,512]{2,1,0:T(8,128)S(1)} %copy-done, f32[2,256,512]{2,1,0:T(8,128)S(1)} %copy-done.1, s32[6,2,2]{2,1,0:T(2,128)S(1)} %copy.19.shifts.refs_0_.refs_9_.refs_12_.refs_11_, f32[35]{0:T(128)S(1)} %copy-done.2, s32[2]{0:T(128)S(1)} %copy-done.3), custom_call_target="tpu_custom_call" | custom-call | bytes 18000000 | tf_op jit(solution)/shard_map/own_first/pallas_call | solution.py:577
  9.7 0.1 pack_sides.2
  9.8 1.2 %collective-permute-start.2 = (f32[264,128]{1,0:T(8,128)S(1)}, f32[264,128]{1,0:T(8,128)S(1)}, u32[]{:S(2)}, u32[]{:S(2)}) collective-permute-start(f32[264,128]{1,0:T(8,128)S(1)} %get-tuple-element.31), channel_id=1, source_target_pairs={{0,16},{16,0},{32,48},{48,32},{64,80},{80,64},{96,112},{112,96},{1... | collective-permute-start | bytes 405512 | tf_op jit(solution)/shard_map/ppermute | solution.py:35
  11.0 3.3 %collective-permute-start.3 = (f32[264,128]{1,0:T(8,128)S(1)}, f32[264,128]{1,0:T(8,128)S(1)}, u32[]{:S(2)}, u32[]{:S(2)}) collective-permute-start(f32[264,128]{1,0:T(8,128)S(1)} %get-tuple-element.32), channel_id=1, source_target_pairs={{16,32},{32,16},{48,64},{64,48},{80,96},{96,80},{112,128},{128,112... | collective-permute-start | bytes 405512 | tf_op jit(solution)/shard_map/ppermute | solution.py:36
  14.3 0.0 collective-permute-done.even_rows.even.refs_4_
  14.3 0.0 collective-permute-done.1.odd_rows.odd.refs_5_
  14.3 0.1 pack_corners.2
  14.5 0.1 collective-permute-start.4
  14.6 3.9 %collective-permute-start.5 = (f32[128,128]{1,0:T(8,128)S(1)}, f32[128,128]{1,0:T(8,128)S(1)}, u32[]{:S(2)}, u32[]{:S(2)}) collective-permute-start(f32[128,128]{1,0:T(8,128)S(1)} %get-tuple-element.35), channel_id=1, source_target_pairs={{16,32},{32,16},{48,64},{64,48},{80,96},{96,80},{112,128},{128,112... | collective-permute-start | bytes 196616 | tf_op jit(solution)/shard_map/ppermute | solution.py:36
  18.5 0.0 collective-permute-done.2.even_cols.refs_4_.refs_8_.refs_5_
  18.5 0.0 collective-permute-done.3.odd_cols.refs_5_.refs_9_.refs_6_
  18.5 2.4 %rows_first.1 = (f32[2,256,512]{2,1,0:T(8,128)S(1)}, f32[3,8,128]{2,1,0:T(8,128)S(1)}, f32[2,2,384,128]{3,2,1,0:T(8,128)S(1)}) custom-call(f32[2,256,512]{2,1,0:T(8,128)S(1)} %get-tuple-element.26.before, f32[128,128]{1,0:T(8,128)S(1)} %get-tuple-element.29.packed, f32[2,256,512]{2,1,0:T(8,128)S(1)} %copy-done, ...), custom_call_target="tpu_custom_call", output_to_operand_aliasing={{0}: (0, {})} | custom-call | bytes 9000000 | tf_op jit(solution)/shard_map/rows_first/pallas_call | solution.py:577
  20.9 0.0 collective-permute-done.4.refs_6_
  20.9 0.0 collective-permute-done.5.refs_7_
  20.9 1.3 %first_apply.1 = (f32[2,256,512]{2,1,0:T(8,128)S(1)}, f32[2,2,384,128]{3,2,1,0:T(8,128)S(1)}, f32[3,8,128]{2,1,0:T(8,128)S(1)}, f32[2,64,512]{2,1,0:T(8,128)S(1)}, f32[2,64,512]{2,1,0:T(8,128)S(1)}) custom-call(f32[2,256,512]{2,1,0:T(8,128)S(1)} %get-tuple-element.33.refs_0_, ...), custom_call_target="tpu_custom_call", output_to_operand_aliasing={{0}: (0, {}), {1}: (1, {})} | custom-call | bytes 9000000 | tf_op jit(solution)/shard_map/first_apply/pallas_call | solution.py:577
  22.2 3.7 %collective-permute-start.6 = (f32[2,64,512]{2,1,0:T(8,128)S(1)}, f32[2,64,512]{2,1,0:T(8,128)S(1)}, u32[]{:S(2)}, u32[]{:S(2)}) collective-permute-start(f32[2,64,512]{2,1,0:T(8,128)S(1)} %get-tuple-element.38), channel_id=1, source_target_pairs={{0,1},{1,0},{2,3},{3,2},{4,5},{5,4},{6,7},{7,6},{8,9},{9,8},{10,11... | collective-permute-start | bytes 786440 | tf_op jit(solution)/shard_map/ppermute | solution.py:35
  25.9 0.8 %collective-permute-start.7 = (f32[2,64,512]{2,1,0:T(8,128)S(1)}, f32[2,64,512]{2,1,0:T(8,128)S(1)}, u32[]{:S(2)}, u32[]{:S(2)}) collective-permute-start(f32[2,64,512]{2,1,0:T(8,128)S(1)} %get-tuple-element.39), channel_id=1, source_target_pairs={{1,2},{2,1},{3,4},{4,3},{5,6},{6,5},{7,8},{8,7},{9,10},{10,9},{11,... | collective-permute-start | bytes 786440 | tf_op jit(solution)/shard_map/ppermute | solution.py:36
  26.8 4.6 %own_second.1.refs_1_.before = f32[2,256,512]{2,1,0:T(8,128)S(1)} custom-call(f32[2,256,512]{2,1,0:T(8,128)S(1)} %get-tuple-element.37.field.refs_0_.refs_3_.w_vec, f32[2,256,512]{2,1,0:T(8,128)S(1)} %copy-done.1, s32[6,2,2]{2,1,0:T(2,128)S(1)} %copy.19.shifts.refs_0_.refs_9_.refs_12_.refs_11_, f32[35]{0:T(128)S(1)} %copy-done.2, s32[2]{0:T(128)S(1)} %copy-done.3), custom_call_target="tpu_custom_call" | custom-call | bytes 18000000 | tf_op jit(solution)/shard_map/own_second/pallas_call | solution.py:577
  31.4 0.1 pack_sides.3
  31.6 0.1 collective-permute-start.8
  31.7 3.9 %collective-permute-start.9 = (f32[256,128]{1,0:T(8,128)S(1)}, f32[256,128]{1,0:T(8,128)S(1)}, u32[]{:S(2)}, u32[]{:S(2)}) collective-permute-start(f32[256,128]{1,0:T(8,128)S(1)} %get-tuple-element.42), channel_id=1, source_target_pairs={{16,32},{32,16},{48,64},{64,48},{80,96},{96,80},{112,128},{128,112... | collective-permute-start | bytes 393224 | tf_op jit(solution)/shard_map/ppermute | solution.py:36
  35.6 0.0 collective-permute-done.6.even_rows.refs_2_
  35.6 0.0 collective-permute-done.7.odd_rows.refs_3_
  35.6 0.1 pack_corners.3
  35.7 0.1 collective-permute-start.10
  35.8 5.1 %collective-permute-start.11 = (f32[128,128]{1,0:T(8,128)S(1)}, f32[128,128]{1,0:T(8,128)S(1)}, u32[]{:S(2)}, u32[]{:S(2)}) collective-permute-start(f32[128,128]{1,0:T(8,128)S(1)} %get-tuple-element.46), channel_id=1, source_target_pairs={{16,32},{32,16},{48,64},{64,48},{80,96},{96,80},{112,128},{128,112... | collective-permute-start | bytes 196616 | tf_op jit(solution)/shard_map/ppermute | solution.py:36
  41.0 0.0 collective-permute-done.8.refs_6_
  41.0 0.0 collective-permute-done.9.refs_7_
  41.0 2.6 %rows_second.1 = (f32[2,256,512]{2,1,0:T(8,128)S(1)}, f32[6,8,128]{2,1,0:T(8,128)S(1)}, f32[2,2,384,128]{3,2,1,0:T(8,128)S(1)}) custom-call(f32[2,256,512]{2,1,0:T(8,128)S(1)} %own_second.1.refs_1_.before, f32[128,128]{1,0:T(8,128)S(1)} %get-tuple-element.40.packed, ...), custom_call_target="tpu_custom_call", output_to_operand_aliasing={{0}: (0, {})} | custom-call | bytes 9000000 | tf_op jit(solution)/shard_map/rows_second/pallas_call | solution.py:577
  43.6 0.0 collective-permute-done.10.refs_7_
  43.6 0.0 collective-permute-done.11.refs_8_
  43.6 1.5 %second_apply.1 = (f32[2,256,512]{2,1,0:T(8,128)S(1)}, f32[2,2,384,128]{3,2,1,0:T(8,128)S(1)}, f32[256,128]{1,0:T(8,128)S(1)}) custom-call(f32[2,256,512]{2,1,0:T(8,128)S(1)} %get-tuple-element.44.refs_0_, f32[2,2,384,128]{3,2,1,0:T(8,128)S(1)} %get-tuple-element.45.refs_1_, ...), custom_call_target="tpu_custom_call", output_to_operand_aliasing={{0}: (0, {}), {1}: (1, {})} | custom-call | bytes 9000000 | tf_op jit(solution)/shard_map/second_apply/pallas_call | solution.py:577
  45.2 27.7 %all_to_all.11 = f32[256,1,128]{2,1,0:T(1,128)S(1)} all-to-all(f32[256,1,128]{2,1,0:T(1,128)S(1)} %bitcast.5), channel_id=1, replica_groups=mesh['gx'=16,'gy'=16] {'gx','gy'}, dimensions={0} | all-to-all | bytes 262144 | tf_op jit(solution)/shard_map/all_to_all | solution.py:664
  72.9 1.9 %last_update.1 = (f32[2,256,512]{2,1,0:T(8,128)}, f32[2,256,512]{2,1,0:T(8,128)}) custom-call(f32[256,128]{1,0:T(8,128)S(1)} %bitcast.4, f32[2,256,512]{2,1,0:T(8,128)S(1)} %copy-done, f32[2,256,512]{2,1,0:T(8,128)S(1)} %get-tuple-element.37.field.refs_0_.refs_3_.w_vec, f32[2,256,512]{2,1,0:T(8,128)S(1)} %get-tuple-element.49.n_vec), custom_call_target="tpu_custom_call" | custom-call | tf_op jit(solution)/shard_map/last_update/pallas_call | solution.py:665
Async XLA Ops:
  0.6 4.3 %copy-start = (f32[2,256,512]{2,1,0:T(8,128)S(1)}, f32[2,256,512]{2,1,0:T(8,128)}, u32[]{:S(2)}) copy-start(f32[2,256,512]{2,1,0:T(8,128)} %base.1) | copy-start | bytes 3145732
  0.6 4.3 %copy-start.1 = (f32[2,256,512]{2,1,0:T(8,128)S(1)}, f32[2,256,512]{2,1,0:T(8,128)}, u32[]{:S(2)}) copy-start(f32[2,256,512]{2,1,0:T(8,128)} %refs_4_.1) | copy-start | bytes 3145732
  1.9 3.0 %copy-start.4 = (s32[6,2,2]{0,2,1:T(2,128)S(1)}, s32[6,2,2]{0,2,1:T(2,128)}, u32[]{:S(2)}) copy-start(s32[6,2,2]{0,2,1:T(2,128)} %param.9) | copy-start | bytes 292
  1.9 12.4 %collective-permute-start = (f32[2,72,512]{2,1,0:T(8,128)S(1)}, f32[2,72,512]{2,1,0:T(8,128)S(1)}, u32[]{:S(2)}, u32[]{:S(2)}) collective-permute-start(f32[2,72,512]{2,1,0:T(8,128)S(1)} %get-tuple-element.27), channel_id=1, source_target_pairs={{0,1},{1,0},{2,3},{3,2},{4,5},{5,4},{6,7},{7,6},{8,9},{9,8},{10,11... | collective-permute-start | bytes 884744 | tf_op jit(solution)/shard_map/ppermute | solution.py:35
  4.0 0.9 %copy-start.2 = (f32[35]{0:T(128)S(1)}, f32[35]{0:T(128)}, u32[]{:S(2)}) copy-start(f32[35]{0:T(128)} %refs_12_.2) | copy-start | bytes 424
  4.0 0.9 %copy-start.3 = (s32[2]{0:T(128)S(1)}, s32[2]{0:T(128)}, u32[]{:S(2)}) copy-start(s32[2]{0:T(128)} %refs_13_.3) | copy-start | bytes 28
  4.0 10.3 %collective-permute-start.1 = (f32[2,72,512]{2,1,0:T(8,128)S(1)}, f32[2,72,512]{2,1,0:T(8,128)S(1)}, u32[]{:S(2)}, u32[]{:S(2)}) collective-permute-start(f32[2,72,512]{2,1,0:T(8,128)S(1)} %get-tuple-element.28), channel_id=1, source_target_pairs={{1,2},{2,1},{3,4},{4,3},{5,6},{6,5},{7,8},{8,7},{9,10},{10,9},{11,... | collective-permute-start | bytes 884744 | tf_op jit(solution)/shard_map/ppermute | solution.py:36
  9.8 8.7 %collective-permute-start.2 = (f32[264,128]{1,0:T(8,128)S(1)}, f32[264,128]{1,0:T(8,128)S(1)}, u32[]{:S(2)}, u32[]{:S(2)}) collective-permute-start(f32[264,128]{1,0:T(8,128)S(1)} %get-tuple-element.31), channel_id=1, source_target_pairs={{0,16},{16,0},{32,48},{48,32},{64,80},{80,64},{96,112},{112,96},{1... | collective-permute-start | bytes 405512 | tf_op jit(solution)/shard_map/ppermute | solution.py:35
  11.0 7.5 %collective-permute-start.3 = (f32[264,128]{1,0:T(8,128)S(1)}, f32[264,128]{1,0:T(8,128)S(1)}, u32[]{:S(2)}, u32[]{:S(2)}) collective-permute-start(f32[264,128]{1,0:T(8,128)S(1)} %get-tuple-element.32), channel_id=1, source_target_pairs={{16,32},{32,16},{48,64},{64,48},{80,96},{96,80},{112,128},{128,112... | collective-permute-start | bytes 405512 | tf_op jit(solution)/shard_map/ppermute | solution.py:36
  14.5 6.5 %collective-permute-start.4 = (f32[128,128]{1,0:T(8,128)S(1)}, f32[128,128]{1,0:T(8,128)S(1)}, u32[]{:S(2)}, u32[]{:S(2)}) collective-permute-start(f32[128,128]{1,0:T(8,128)S(1)} %get-tuple-element.29.packed), channel_id=1, source_target_pairs={{0,16},{16,0},{32,48},{48,32},{64,80},{80,64},{96,112},{112,96},{1... | collective-permute-start | bytes 196616 | tf_op jit(solution)/shard_map/ppermute | solution.py:35
  14.6 6.4 %collective-permute-start.5 = (f32[128,128]{1,0:T(8,128)S(1)}, f32[128,128]{1,0:T(8,128)S(1)}, u32[]{:S(2)}, u32[]{:S(2)}) collective-permute-start(f32[128,128]{1,0:T(8,128)S(1)} %get-tuple-element.35), channel_id=1, source_target_pairs={{16,32},{32,16},{48,64},{64,48},{80,96},{96,80},{112,128},{128,112... | collective-permute-start | bytes 196616 | tf_op jit(solution)/shard_map/ppermute | solution.py:36
  22.2 13.4 %collective-permute-start.6 = (f32[2,64,512]{2,1,0:T(8,128)S(1)}, f32[2,64,512]{2,1,0:T(8,128)S(1)}, u32[]{:S(2)}, u32[]{:S(2)}) collective-permute-start(f32[2,64,512]{2,1,0:T(8,128)S(1)} %get-tuple-element.38), channel_id=1, source_target_pairs={{0,1},{1,0},{2,3},{3,2},{4,5},{5,4},{6,7},{7,6},{8,9},{9,8},{10,11... | collective-permute-start | bytes 786440 | tf_op jit(solution)/shard_map/ppermute | solution.py:35
  25.9 9.7 %collective-permute-start.7 = (f32[2,64,512]{2,1,0:T(8,128)S(1)}, f32[2,64,512]{2,1,0:T(8,128)S(1)}, u32[]{:S(2)}, u32[]{:S(2)}) collective-permute-start(f32[2,64,512]{2,1,0:T(8,128)S(1)} %get-tuple-element.39), channel_id=1, source_target_pairs={{1,2},{2,1},{3,4},{4,3},{5,6},{6,5},{7,8},{8,7},{9,10},{10,9},{11,... | collective-permute-start | bytes 786440 | tf_op jit(solution)/shard_map/ppermute | solution.py:36
  31.6 9.4 %collective-permute-start.8 = (f32[256,128]{1,0:T(8,128)S(1)}, f32[256,128]{1,0:T(8,128)S(1)}, u32[]{:S(2)}, u32[]{:S(2)}) collective-permute-start(f32[256,128]{1,0:T(8,128)S(1)} %get-tuple-element.41), channel_id=1, source_target_pairs={{0,16},{16,0},{32,48},{48,32},{64,80},{80,64},{96,112},{112,96},{1... | collective-permute-start | bytes 393224 | tf_op jit(solution)/shard_map/ppermute | solution.py:35
  31.7 9.3 %collective-permute-start.9 = (f32[256,128]{1,0:T(8,128)S(1)}, f32[256,128]{1,0:T(8,128)S(1)}, u32[]{:S(2)}, u32[]{:S(2)}) collective-permute-start(f32[256,128]{1,0:T(8,128)S(1)} %get-tuple-element.42), channel_id=1, source_target_pairs={{16,32},{32,16},{48,64},{64,48},{80,96},{96,80},{112,128},{128,112... | collective-permute-start | bytes 393224 | tf_op jit(solution)/shard_map/ppermute | solution.py:36
  35.7 7.9 %collective-permute-start.10 = (f32[128,128]{1,0:T(8,128)S(1)}, f32[128,128]{1,0:T(8,128)S(1)}, u32[]{:S(2)}, u32[]{:S(2)}) collective-permute-start(f32[128,128]{1,0:T(8,128)S(1)} %get-tuple-element.40.packed), channel_id=1, source_target_pairs={{0,16},{16,0},{32,48},{48,32},{64,80},{80,64},{96,112},{112,96},{1... | collective-permute-start | bytes 196616 | tf_op jit(solution)/shard_map/ppermute | solution.py:35
  35.8 7.8 %collective-permute-start.11 = (f32[128,128]{1,0:T(8,128)S(1)}, f32[128,128]{1,0:T(8,128)S(1)}, u32[]{:S(2)}, u32[]{:S(2)}) collective-permute-start(f32[128,128]{1,0:T(8,128)S(1)} %get-tuple-element.46), channel_id=1, source_target_pairs={{16,32},{32,16},{48,64},{64,48},{80,96},{96,80},{112,128},{128,112... | collective-permute-start | bytes 196616 | tf_op jit(solution)/shard_map/ppermute | solution.py:36

commit v7 on v6

--- a/solution.py
+++ b/solution.py
@@ -140,14 +140,11 @@
 
 
 def zero_rim(pad, depth, rows):
-    tiles = pad.shape[1]
+    zeros = jnp.zeros((depth, LANES), jnp.float32)
     for layer in range(2):
-        for tile in range(tiles):
-            if tile in (0, tiles - 1):
-                pad[layer, tile] = jnp.zeros(pad.shape[2:], jnp.float32)
-            else:
-                pad[layer, tile, 0:depth, :] = jnp.zeros((depth, LANES), jnp.float32)
-                pad[layer, tile, depth + rows :, :] = jnp.zeros((depth, LANES), jnp.float32)
+        for tile in range(pad.shape[1]):
+            pad[layer, tile, 0:depth, :] = zeros
+            pad[layer, tile, depth + rows :, :] = zeros
 
 
 def fill_own(pad, depth, field):
@@ -155,21 +152,32 @@
     for layer in range(2):
         for tile in range(cols // LANES):
             lanes = slice(tile * LANES, (tile + 1) * LANES)
-            pad[layer, 1 + tile, depth : depth + rows, :] = field[layer, :, lanes]
-
-
-def neighbours_across(load, tiles):
-    lane = lane_of((CHUNK, LANES))
-    values = [load(tile) for tile in range(tiles + 2)]
-    back = [pltpu.roll(value, 1, 1) for value in values[:-1]]
-    ahead = [pltpu.roll(value, LANES - 1, 1) for value in values[1:]]
-    left = [jnp.where(lane == 0, back[i], back[i + 1]) for i in range(tiles)]
-    right = [jnp.where(lane == LANES - 1, ahead[i + 1], ahead[i]) for i in range(tiles)]
-    return values[1:-1], left, right
-
-
-def apply_chunk(layer, row, pad, coeff_pad, shifts, weight, grid_shape, tile_shape):
-    dirs = shifts.shape[0]
+            pad[layer, tile, depth : depth + rows, :] = field[layer, :, lanes]
+
+
+def move_across(tiles, step_c, lane):
+    count = len(tiles)
+    back = jnp.bitwise_and(LANES - step_c, LANES - 1)
+    from_left = lane < jnp.where(step_c < 0, -step_c, 0)
+    from_right = lane >= jnp.where(step_c < 0, LANES, LANES - step_c)
+    turned = [0.0] + [pltpu.roll(tile, back, 1) for tile in tiles] + [0.0]
+    return [
+        jnp.where(from_left, turned[i], jnp.where(from_right, turned[i + 2], turned[i + 1]))
+        for i in range(count)
+    ]
+
+
+def from_the_right(tiles, lane, last):
+    ahead = [pltpu.roll(tile, LANES - 1, 1) for tile in tiles]
+    return [
+        jnp.where(lane == LANES - 1, after, tile)
+        for tile, after in zip(ahead, [*ahead[1:], last], strict=True)
+    ]
+
+
+def apply_chunk(
+    layer, row, pad, coeff_pad, across, across_out, shifts, weight, grid_shape, tile_shape
+):
     rows, cols = tile_shape
     tiles = cols // LANES
     other = 1 - layer
@@ -177,38 +185,36 @@
     row_at = lax.broadcasted_iota(jnp.int32, (CHUNK, LANES), 0)
     first_row = lax.axis_index("gy") * rows + row
     first_col = lax.axis_index("gx") * cols
-
-    def field_at(tile):
-        return pad[layer, tile, pl.ds(REACH + row, CHUNK), :]
-
-    def coeff_at(tile):
-        return coeff_pad[layer, tile, pl.ds(8 + row, CHUNK), :]
-
-    own, left, right = neighbours_across(field_at, tiles)
-    own_c, left_c, right_c = neighbours_across(coeff_at, tiles)
+    cut = [slice(tile * LANES, (tile + 1) * LANES) for tile in range(tiles)]
+
+    def at(ref, tile, start):
+        return ref[layer, tile, pl.ds(start, CHUNK), :]
+
+    own = [at(pad, tile, REACH + row) for tile in range(tiles)]
+    own_c = [at(coeff_pad, tile, 8 + row) for tile in range(tiles)]
+    if across is None:
+        right_c = from_the_right(own_c, lane, 0.0)
+        both = [a + b for a, b in zip(own_c, right_c, strict=True)]
+        for value, lanes in zip(both, cut, strict=True):
+            across_out[layer, pl.ds(row, CHUNK), lanes] = value
+    else:
+        both = [across[layer, pl.ds(row, CHUNK), lanes] for lanes in cut]
+    right = from_the_right(own, lane, own[-1])
+    flow = [c * (a - b) for c, a, b in zip(both, own, right, strict=True)]
+    turned = [pltpu.roll(value, 1, 1) for value in flow]
     result = []
     for tile in range(tiles):
         value, coeff = own[tile], own_c[tile]
-        above = pad[layer, 1 + tile, pl.ds(REACH - 1 + row, CHUNK), :]
-        below = pad[layer, 1 + tile, pl.ds(REACH + 1 + row, CHUNK), :]
-        above_c = coeff_pad[layer, 1 + tile, pl.ds(7 + row, CHUNK), :]
-        below_c = coeff_pad[layer, 1 + tile, pl.ds(9 + row, CHUNK), :]
+        above, below = at(pad, tile, REACH - 1 + row), at(pad, tile, REACH + 1 + row)
+        above_c, below_c = at(coeff_pad, tile, 7 + row), at(coeff_pad, tile, 9 + row)
         total = (coeff + above_c) * (value - above) + (coeff + below_c) * (value - below)
-        total += (coeff + left_c[tile]) * (value - left[tile])
-        total += (coeff + right_c[tile]) * (value - right[tile])
-        result.append(weight * total)
-    for direction in range(dirs):
+        inflow = jnp.where(lane == 0, turned[tile - 1] if tile else 0.0, turned[tile])
+        result.append(weight * (total + flow[tile] - inflow))
+    for direction in range(shifts.shape[0]):
         shift_r, shift_c = shifts[direction, layer, 0], shifts[direction, layer, 1]
         start_r = REACH + row + shifts[direction, other, 0] - shift_r
-        start_c = LANES + shifts[direction, other, 1] - shift_c
-        skip = lax.shift_right_logical(start_c, 7)
-        turn = jnp.bitwise_and(start_c, LANES - 1)
-        back = jnp.bitwise_and(LANES - turn, LANES - 1)
-        moved = [
-            pltpu.roll(pad[other, skip + tile, pl.ds(start_r, CHUNK), :], back, 1)
-            for tile in range(tiles + 1)
-        ]
-        here = lane < LANES - turn
+        source = [pad[other, tile, pl.ds(start_r, CHUNK), :] for tile in range(tiles)]
+        moved = move_across(source, shifts[direction, other, 1] - shift_c, lane)
         image_row = row_at + (first_row - shift_r)
         inside = (image_row >= 0) & (image_row < grid_shape[0])
         for tile in range(tiles):
@@ -217,8 +223,7 @@
                 mask = mask & (lane >= shift_c - first_col)
             if tile == tiles - 1:
                 mask = mask & (lane < grid_shape[1] + shift_c - first_col - tile * LANES)
-            value = own[tile] + jnp.where(here, moved[tile], moved[tile + 1])
-            result[tile] = result[tile] + jnp.where(mask, value, 0.0)
+            result[tile] = result[tile] + jnp.where(mask, own[tile] + moved[tile], 0.0)
     return result
 
 
@@ -251,7 +256,9 @@
         ends[high] = packed
 
 
-def own_kernel(grid_shape, field, coeff, shifts, table, entry, out, ends, pad, coeff_pad):
+def own_kernel(
+    grid_shape, field, coeff, across, shifts, table, entry, out, ends, across_out, pad, coeff_pad
+):
     rows, cols = field.shape[1:]
     zero_rim(pad, REACH, rows)
     zero_rim(coeff_pad, 8, rows)
@@ -265,7 +272,7 @@
         def step(i, carry, layer=layer, weight=weight):
             row = pl.multiple_of(i * CHUNK, CHUNK)
             result = apply_chunk(
-                layer, row, pad, coeff_pad, shifts, weight, grid_shape, (rows, cols)
+                layer, row, pad, coeff_pad, across, across_out, shifts, weight, grid_shape, (rows, cols)
             )
             for tile, value in enumerate(result):
                 out[layer, pl.ds(row, CHUNK), tile * LANES : (tile + 1) * LANES] = value
@@ -303,18 +310,14 @@
     first_col = lax.axis_index("gx") * cols
     zeros = jnp.zeros((REACH, LANES), jnp.float32)
     for layer in range(2):
-        for side in range(2):
-            for tile in (0, tiles + 1):
-                pad[layer, side, tile, 0:REACH, :] = zeros
-                pad[layer, side, tile, REACH:, :] = zeros
         for tile in range(tiles):
             lanes = slice(tile * LANES, (tile + 1) * LANES)
             even = even_rows[layer, 0:REACH, lanes]
             other = odd_rows[layer, 0:REACH, lanes]
-            pad[layer, 0, 1 + tile, 0:REACH, :] = jnp.where(odd_y, even, other)
-            pad[layer, 0, 1 + tile, REACH:, :] = zeros
-            pad[layer, 1, 1 + tile, 0:REACH, :] = zeros
-            pad[layer, 1, 1 + tile, REACH:, :] = jnp.where(odd_y, other, even)
+            pad[layer, 0, tile, 0:REACH, :] = jnp.where(odd_y, even, other)
+            pad[layer, 0, tile, REACH:, :] = zeros
+            pad[layer, 1, tile, 0:REACH, :] = zeros
+            pad[layer, 1, tile, REACH:, :] = jnp.where(odd_y, other, even)
     lane = lane_of((CHUNK, LANES))
     row_at = lax.broadcasted_iota(jnp.int32, (CHUNK, LANES), 0)
     for layer in range(2):
@@ -326,26 +329,19 @@
             for direction in range(shifts.shape[0]):
                 shift_r, shift_c = shifts[direction, layer, 0], shifts[direction, layer, 1]
                 step_r = shifts[direction, other_layer, 0] - shift_r
-                start_c = LANES + shifts[direction, other_layer, 1] - shift_c
                 side = jnp.where(step_r < 0, 0, 1)
                 start_r = part + step_r + jnp.where(step_r < 0, REACH, 0)
                 row = part + jnp.where(step_r < 0, 0, rows - REACH)
-                skip = lax.shift_right_logical(start_c, 7)
-                turn = jnp.bitwise_and(start_c, LANES - 1)
-                back = jnp.bitwise_and(LANES - turn, LANES - 1)
-                moved = [
-                    pltpu.roll(
-                        pad[other_layer, side, skip + tile, pl.ds(start_r, CHUNK), :], back, 1
-                    )
-                    for tile in range(tiles + 1)
+                source = [
+                    pad[other_layer, side, tile, pl.ds(start_r, CHUNK), :] for tile in range(tiles)
                 ]
-                here = lane < LANES - turn
+                moved = move_across(source, shifts[direction, other_layer, 1] - shift_c, lane)
                 image_row = row_at + (first_row + row - shift_r)
                 inside = (image_row >= 0) & (image_row < grid_shape[0])
                 upper = inside & (jnp.full((CHUNK, LANES), side, jnp.int32) == 0)
                 lower = inside & (jnp.full((CHUNK, LANES), side, jnp.int32) == 1)
                 for tile in range(tiles):
-                    value = jnp.where(here, moved[tile], moved[tile + 1])
+                    value = moved[tile]
                     if tile == 0:
                         value = jnp.where(lane >= shift_c - first_col, value, 0.0)
                     if tile == tiles - 1:
@@ -359,7 +355,7 @@
                     out[layer, pl.ds(base + part, CHUNK), lanes] += totals[side][tile]
             return carry
 
-        lax.fori_loop(0, REACH // CHUNK, step, 0)
+        lax.fori_loop(0, REACH // CHUNK, step, 0, unroll=True)
         weight = weight_of(table, entry, layer)
         at = lax.broadcasted_iota(jnp.int32, (8, cols), 0)
         even = even_edge[layer, REACH : REACH + 8, :]
@@ -424,7 +420,7 @@
         edge_v = pad[layer, side, pl.ds(REACH + row, CHUNK), :]
         edge_v = pltpu.roll(edge_v, LANES - 1 if side else 1, 1)
         own_c = coeff[layer, pl.ds(row, CHUNK), cut[side]]
-        extra = weight * (edge_c * own[side] - (own_c + edge_c) * edge_v)
+        extra = weight * ((own_c + edge_c) * (own[side] - edge_v))
         extra = jnp.where(lane == spot, extra, 0.0)
         result.append(out[layer, pl.ds(row, CHUNK), cut[side]] + extra)
     for direction in range(shifts.shape[0]):
@@ -598,8 +594,8 @@
     full = jax.ShapeDtypeStruct((layers, rows, cols), jnp.float32)
     edge = jax.ShapeDtypeStruct((layers, REACH, cols), jnp.float32)
     scalars = (shifts, strength_table, layer_entry)
-    own_pads = [(2, tiles + 2, rows + 2 * REACH, LANES), (2, tiles + 2, rows + 16, LANES)]
-    row_pads = [(2, 2, tiles + 2, 2 * REACH, LANES)]
+    own_pads = [(2, tiles, rows + 2 * REACH, LANES), (2, tiles, rows + 16, LANES)]
+    row_pads = [(2, 2, tiles, 2 * REACH, LANES)]
     side_pad = jax.ShapeDtypeStruct((2, 2, rows + 2 * REACH, LANES), jnp.float32)
 
     def sums_of(count):
@@ -622,15 +618,16 @@
         del before, packed
         rows_kernel(grid_shape, *refs)
 
-    def own_first(field, coeff, shifts, table, entry, out, ends, *pads):
-        own_kernel(grid_shape, field, coeff, shifts, table, entry, out, ends, *pads)
-
-    def own_second(field, coeff, shifts, table, entry, out, *pads):
-        own_kernel(grid_shape, field, coeff, shifts, table, entry, out, None, *pads)
+    def own_first(field, coeff, *refs):
+        own_kernel(grid_shape, field, coeff, None, *refs)
+
+    def own_second(field, coeff, across, shifts, table, entry, out, *pads):
+        own_kernel(grid_shape, field, coeff, across, shifts, table, entry, out, None, None, *pads)
 
     rows0 = swap(*edge_rows(right_side, coefficient), "gy")
-    w_own, ends = on_tensor_core(
-        own_first, "own_first", (right_side, coefficient), scalars, (full, sums_of(2)), own_pads, 6
+    w_own, ends, across = on_tensor_core(
+        own_first, "own_first", (right_side, coefficient), scalars, (full, sums_of(2), full), own_pads,
+        6,
     )
     cols0 = swap(*pack_sides(right_side, ends, True), "gx")
     packed = pack_corners(*rows0)
@@ -646,7 +643,7 @@
     )
     rows1 = swap(even, odd, "gy")
     (n_own,) = on_tensor_core(
-        own_second, "own_second", (w_vec, coefficient), scalars, (full,), own_pads, 6
+        own_second, "own_second", (w_vec, coefficient, across), scalars, (full,), own_pads, 6
     )
     cols1 = swap(*pack_sides(w_vec, n_own, False), "gx")
     packed = pack_corners(*rows1)

time: 75.2 us -> 73.9 us (0.983)
  starting transfers between devices: 25.2 us -> 20.4 us
  blocking collectives: 27.7 us -> 30.8 us
  waiting for transfers between devices: 0.03 us -> 2.66 us
  Pallas kernels: 20.7 us -> 18.6 us
    ppermute x6, starting transfers between devices: 17.9 us -> 13 us  [swap(): lax.ppermute(odd, axis, odd_swap(count))]
    all_to_all x1, blocking collectives: 27.7 us -> 30.8 us  [on_device(): gathered = lax.all_to_all(parts, ('gx', 'gy'), 0, 0, tiled=True)]
    ppermute x6, waiting for transfers between devices: 0.02 us -> 2.64 us  [swap(): lax.ppermute(odd, axis, odd_swap(count))]
    pallas_call x6, Pallas kernels: 17.1 us -> 15 us  [on_tensor_core(): pl.pallas_call(kernel, out_shape=out_shape, in_specs=[VMEM_SPEC] * len(op...]
  transfers between devices with their start and end apart: 12 -> 12, of which waited for: 0 -> 4; matrix products, arithmetic and copies ran while one was open for 0% -> 0% of each run, Pallas kernels for 20% -> 17%
where the time goes in v7:
time: 73.9 us; the launch traced here: 73.6 us
  blocking collectives  30.8 us (42%)
  starting transfers between devices  20.4 us (28%)
  Pallas kernels  18.6 us (25%)
  waiting for transfers between devices  2.66 us (4%)
  between operations  1.03 us (1%)
    all_to_all x1, blocking collectives, on_device(): gathered = lax.all_to_all(parts, ('gx', 'gy'), 0, 0, tiled=True)  30.8 us
    pallas_call x6, Pallas kernels, on_tensor_core(): pl.pallas_call(kernel, out_shape=out_shape, in_specs=[VMEM_SPEC] * len(op...  15 us
    ppermute x6, starting transfers between devices, swap(): lax.ppermute(odd, axis, odd_swap(count))  13 us
    ppermute x6, starting transfers between devices, swap(): lax.ppermute(even, axis, even_swap(count))  7.33 us
    ppermute x6, waiting for transfers between devices, swap(): lax.ppermute(odd, axis, odd_swap(count))  2.64 us
    pallas_call x1, Pallas kernels, on_device(): pl.pallas_call(last_kernel, out_shape=(full, full), in_specs=[VMEM_SPEC]...  1.87 us
  transfers between devices with their start and end apart: 12, of which 4 were waited for; matrix products, arithmetic and copies ran while one was open for 0% of the time, Pallas kernels for 17%

profile of v7, /device:TPU:1, one launch (start us, length us, event | category | flops | bytes accessed | tf_op | source)
XLA Modules:
  0.0 73.6 jit_solution(8116798158816378164)
XLA Ops:
  0.6 0.0 copy-start
  0.6 0.0 copy-start.1
  0.6 1.2 %edge_rows.1 = (f32[2,72,512]{2,1,0:T(8,128)S(1)}, f32[2,72,512]{2,1,0:T(8,128)S(1)}) custom-call(f32[2,256,512]{2,1,0:T(8,128)} %base.1, f32[2,256,512]{2,1,0:T(8,128)} %refs_4_.1), custom_call_target="tpu_custom_call" | custom-call | tf_op jit(solution)/shard_map/edge_rows/pallas_call | solution.py:131
  1.9 0.0 copy-start.4
  1.9 2.1 %collective-permute-start = (f32[2,72,512]{2,1,0:T(8,128)S(1)}, f32[2,72,512]{2,1,0:T(8,128)S(1)}, u32[]{:S(2)}, u32[]{:S(2)}) collective-permute-start(f32[2,72,512]{2,1,0:T(8,128)S(1)} %get-tuple-element.28), channel_id=1, source_target_pairs={{0,1},{1,0},{2,3},{3,2},{4,5},{5,4},{6,7},{7,6},{8,9},{9,8},{10,11... | collective-permute-start | bytes 884744 | tf_op jit(solution)/shard_map/ppermute | solution.py:35
  4.0 0.0 copy-start.2
  4.0 0.0 copy-start.3
  4.0 0.8 %collective-permute-start.1 = (f32[2,72,512]{2,1,0:T(8,128)S(1)}, f32[2,72,512]{2,1,0:T(8,128)S(1)}, u32[]{:S(2)}, u32[]{:S(2)}) collective-permute-start(f32[2,72,512]{2,1,0:T(8,128)S(1)} %get-tuple-element.29), channel_id=1, source_target_pairs={{1,2},{2,1},{3,4},{4,3},{5,6},{6,5},{7,8},{8,7},{9,10},{10,9},{11,... | collective-permute-start | bytes 884744 | tf_op jit(solution)/shard_map/ppermute | solution.py:36
  4.8 0.0 copy-done.4
  4.9 0.1 copy.19.refs_0_.refs_9_.shifts.refs_12_.refs_11_
  5.0 0.0 copy-done
  5.0 0.0 copy-done.1
  5.0 0.0 copy-done.2
  5.0 0.0 copy-done.3
  5.0 4.3 %own_first.1 = (f32[2,256,512]{2,1,0:T(8,128)S(1)}, f32[2,8,128]{2,1,0:T(8,128)S(1)}, f32[2,256,512]{2,1,0:T(8,128)S(1)}) custom-call(f32[2,256,512]{2,1,0:T(8,128)S(1)} %copy-done, f32[2,256,512]{2,1,0:T(8,128)S(1)} %copy-done.1, s32[6,2,2]{2,1,0:T(2,128)S(1)} %copy.19.refs_0_.refs_9_.shifts.refs_12_.refs_11_, f32[35]{0:T(128)S(1)} %copy-done.2, s32[2]{0:T(128)S(1)} %copy-done.3), custom_call_target="tpu_custom_call" | custom-call | bytes 18000000 | tf_op jit(solution)/shard_map/own_first/pallas_call | solution.py:573
  9.3 0.1 pack_sides.2
  9.4 1.2 %collective-permute-start.2 = (f32[264,128]{1,0:T(8,128)S(1)}, f32[264,128]{1,0:T(8,128)S(1)}, u32[]{:S(2)}, u32[]{:S(2)}) collective-permute-start(f32[264,128]{1,0:T(8,128)S(1)} %get-tuple-element.32), channel_id=1, source_target_pairs={{0,16},{16,0},{32,48},{48,32},{64,80},{80,64},{96,112},{112,96},{1... | collective-permute-start | bytes 405512 | tf_op jit(solution)/shard_map/ppermute | solution.py:35
  10.6 3.3 %collective-permute-start.3 = (f32[264,128]{1,0:T(8,128)S(1)}, f32[264,128]{1,0:T(8,128)S(1)}, u32[]{:S(2)}, u32[]{:S(2)}) collective-permute-start(f32[264,128]{1,0:T(8,128)S(1)} %get-tuple-element.33), channel_id=1, source_target_pairs={{16,32},{32,16},{48,64},{64,48},{80,96},{96,80},{112,128},{128,112... | collective-permute-start | bytes 405512 | tf_op jit(solution)/shard_map/ppermute | solution.py:36
  13.9 0.0 collective-permute-done.even_rows.even.refs_4_
  13.9 0.0 collective-permute-done.1.odd_rows.odd.refs_5_
  13.9 0.1 pack_corners.2
  14.1 2.3 %collective-permute-start.5 = (f32[128,128]{1,0:T(8,128)S(1)}, f32[128,128]{1,0:T(8,128)S(1)}, u32[]{:S(2)}, u32[]{:S(2)}) collective-permute-start(f32[128,128]{1,0:T(8,128)S(1)} %get-tuple-element.36), channel_id=1, source_target_pairs={{16,32},{32,16},{48,64},{64,48},{80,96},{96,80},{112,128},{128,112... | collective-permute-start | bytes 196616 | tf_op jit(solution)/shard_map/ppermute | solution.py:36
  16.3 0.1 collective-permute-start.4
  16.4 0.0 collective-permute-done.2.even_cols.refs_4_.refs_8_.refs_5_
  16.4 0.5 collective-permute-done.3.odd_cols.refs_5_.refs_9_.refs_6_
  16.9 1.9 %rows_first.1 = (f32[2,256,512]{2,1,0:T(8,128)S(1)}, f32[3,8,128]{2,1,0:T(8,128)S(1)}, f32[2,2,384,128]{3,2,1,0:T(8,128)S(1)}) custom-call(f32[2,256,512]{2,1,0:T(8,128)S(1)} %get-tuple-element.27.before, f32[128,128]{1,0:T(8,128)S(1)} %get-tuple-element.30.packed, f32[2,256,512]{2,1,0:T(8,128)S(1)} %copy-done, ...), custom_call_target="tpu_custom_call", output_to_operand_aliasing={{0}: (0, {})} | custom-call | bytes 9000000 | tf_op jit(solution)/shard_map/rows_first/pallas_call | solution.py:573
  18.9 0.8 %collective-permute-done.5.refs_7_ = f32[128,128]{1,0:T(8,128)S(1)} collective-permute-done((f32[128,128]{1,0:T(8,128)S(1)}, f32[128,128]{1,0:T(8,128)S(1)}, u32[]{:S(2)}, u32[]{:S(2)}) %collective-permute-start.5) | collective-permute-done | bytes 65568 | tf_op jit(solution)/shard_map/ppermute | solution.py:36
  19.6 0.0 collective-permute-done.4.refs_6_
  19.6 1.3 %first_apply.1 = (f32[2,256,512]{2,1,0:T(8,128)S(1)}, f32[2,2,384,128]{3,2,1,0:T(8,128)S(1)}, f32[3,8,128]{2,1,0:T(8,128)S(1)}, f32[2,64,512]{2,1,0:T(8,128)S(1)}, f32[2,64,512]{2,1,0:T(8,128)S(1)}) custom-call(f32[2,256,512]{2,1,0:T(8,128)S(1)} %get-tuple-element.34.refs_0_, ...), custom_call_target="tpu_custom_call", output_to_operand_aliasing={{0}: (0, {}), {1}: (1, {})} | custom-call | bytes 9000000 | tf_op jit(solution)/shard_map/first_apply/pallas_call | solution.py:573
  20.9 3.7 %collective-permute-start.6 = (f32[2,64,512]{2,1,0:T(8,128)S(1)}, f32[2,64,512]{2,1,0:T(8,128)S(1)}, u32[]{:S(2)}, u32[]{:S(2)}) collective-permute-start(f32[2,64,512]{2,1,0:T(8,128)S(1)} %get-tuple-element.40), channel_id=1, source_target_pairs={{0,1},{1,0},{2,3},{3,2},{4,5},{5,4},{6,7},{7,6},{8,9},{9,8},{10,11... | collective-permute-start | bytes 786440 | tf_op jit(solution)/shard_map/ppermute | solution.py:35
  24.6 0.7 collective-permute-start.7
  25.3 3.9 %own_second.1.refs_1_.before = f32[2,256,512]{2,1,0:T(8,128)S(1)} custom-call(f32[2,256,512]{2,1,0:T(8,128)S(1)} %get-tuple-element.38.field.refs_0_.refs_3_.w_vec, f32[2,256,512]{2,1,0:T(8,128)S(1)} %copy-done.1, f32[2,256,512]{2,1,0:T(8,128)S(1)} %get-tuple-element.39.across, s32[6,2,2]{2,1,0:T(2,128)S(1)} %copy.19.refs_0_.refs_9_.shifts.refs_12_.refs_11_, ...), custom_call_target="tpu_custom_call" | custom-call | bytes 18000000 | tf_op jit(solution)/shard_map/own_second/pallas_call | solution.py:573
  29.2 0.1 pack_sides.3
  29.3 0.1 collective-permute-start.8
  29.4 4.1 %collective-permute-start.9 = (f32[256,128]{1,0:T(8,128)S(1)}, f32[256,128]{1,0:T(8,128)S(1)}, u32[]{:S(2)}, u32[]{:S(2)}) collective-permute-start(f32[256,128]{1,0:T(8,128)S(1)} %get-tuple-element.44), channel_id=1, source_target_pairs={{16,32},{32,16},{48,64},{64,48},{80,96},{96,80},{112,128},{128,112... | collective-permute-start | bytes 393224 | tf_op jit(solution)/shard_map/ppermute | solution.py:36
  33.5 0.0 collective-permute-done.6.even_rows.refs_2_
  33.5 0.0 collective-permute-done.7.odd_rows.refs_3_
  33.6 0.1 pack_corners.3
  33.7 1.9 %collective-permute-start.11 = (f32[128,128]{1,0:T(8,128)S(1)}, f32[128,128]{1,0:T(8,128)S(1)}, u32[]{:S(2)}, u32[]{:S(2)}) collective-permute-start(f32[128,128]{1,0:T(8,128)S(1)} %get-tuple-element.48), channel_id=1, source_target_pairs={{16,32},{32,16},{48,64},{64,48},{80,96},{96,80},{112,128},{128,112... | collective-permute-start | bytes 196616 | tf_op jit(solution)/shard_map/ppermute | solution.py:36
  35.6 0.1 collective-permute-start.10
  35.7 0.0 collective-permute-done.8.refs_6_
  35.7 0.5 collective-permute-done.9.refs_7_
  36.2 2.2 %rows_second.1 = (f32[2,256,512]{2,1,0:T(8,128)S(1)}, f32[6,8,128]{2,1,0:T(8,128)S(1)}, f32[2,2,384,128]{3,2,1,0:T(8,128)S(1)}) custom-call(f32[2,256,512]{2,1,0:T(8,128)S(1)} %own_second.1.refs_1_.before, f32[128,128]{1,0:T(8,128)S(1)} %get-tuple-element.42.packed, ...), custom_call_target="tpu_custom_call", output_to_operand_aliasing={{0}: (0, {})} | custom-call | bytes 9000000 | tf_op jit(solution)/shard_map/rows_second/pallas_call | solution.py:573
  38.4 0.9 %collective-permute-done.11.refs_8_ = f32[128,128]{1,0:T(8,128)S(1)} collective-permute-done((f32[128,128]{1,0:T(8,128)S(1)}, f32[128,128]{1,0:T(8,128)S(1)}, u32[]{:S(2)}, u32[]{:S(2)}) %collective-permute-start.11) | collective-permute-done | bytes 65568 | tf_op jit(solution)/shard_map/ppermute | solution.py:36
  39.3 0.0 collective-permute-done.10.refs_7_
  39.3 1.5 %second_apply.1 = (f32[2,256,512]{2,1,0:T(8,128)S(1)}, f32[2,2,384,128]{3,2,1,0:T(8,128)S(1)}, f32[256,128]{1,0:T(8,128)S(1)}) custom-call(f32[2,256,512]{2,1,0:T(8,128)S(1)} %get-tuple-element.46.refs_0_, f32[2,2,384,128]{3,2,1,0:T(8,128)S(1)} %get-tuple-element.47.refs_1_, ...), custom_call_target="tpu_custom_call", output_to_operand_aliasing={{0}: (0, {}), {1}: (1, {})} | custom-call | bytes 9000000 | tf_op jit(solution)/shard_map/second_apply/pallas_call | solution.py:573
  40.7 30.8 %all_to_all.11 = f32[256,1,128]{2,1,0:T(1,128)S(1)} all-to-all(f32[256,1,128]{2,1,0:T(1,128)S(1)} %bitcast.5), channel_id=1, replica_groups=mesh['gx'=16,'gy'=16] {'gx','gy'}, dimensions={0} | all-to-all | bytes 262144 | tf_op jit(solution)/shard_map/all_to_all | solution.py:661
  71.5 1.9 %last_update.1 = (f32[2,256,512]{2,1,0:T(8,128)}, f32[2,256,512]{2,1,0:T(8,128)}) custom-call(f32[256,128]{1,0:T(8,128)S(1)} %bitcast.4, f32[2,256,512]{2,1,0:T(8,128)S(1)} %copy-done, f32[2,256,512]{2,1,0:T(8,128)S(1)} %get-tuple-element.38.field.refs_0_.refs_3_.w_vec, f32[2,256,512]{2,1,0:T(8,128)S(1)} %get-tuple-element.51.n_vec), custom_call_target="tpu_custom_call" | custom-call | tf_op jit(solution)/shard_map/last_update/pallas_call | solution.py:662
Async XLA Ops:
  0.6 4.3 %copy-start = (f32[2,256,512]{2,1,0:T(8,128)S(1)}, f32[2,256,512]{2,1,0:T(8,128)}, u32[]{:S(2)}) copy-start(f32[2,256,512]{2,1,0:T(8,128)} %base.1) | copy-start | bytes 3145732
  0.6 4.3 %copy-start.1 = (f32[2,256,512]{2,1,0:T(8,128)S(1)}, f32[2,256,512]{2,1,0:T(8,128)}, u32[]{:S(2)}) copy-start(f32[2,256,512]{2,1,0:T(8,128)} %refs_4_.1) | copy-start | bytes 3145732
  1.9 3.0 %copy-start.4 = (s32[6,2,2]{0,2,1:T(2,128)S(1)}, s32[6,2,2]{0,2,1:T(2,128)}, u32[]{:S(2)}) copy-start(s32[6,2,2]{0,2,1:T(2,128)} %param.9) | copy-start | bytes 292
  1.9 12.0 %collective-permute-start = (f32[2,72,512]{2,1,0:T(8,128)S(1)}, f32[2,72,512]{2,1,0:T(8,128)S(1)}, u32[]{:S(2)}, u32[]{:S(2)}) collective-permute-start(f32[2,72,512]{2,1,0:T(8,128)S(1)} %get-tuple-element.28), channel_id=1, source_target_pairs={{0,1},{1,0},{2,3},{3,2},{4,5},{5,4},{6,7},{7,6},{8,9},{9,8},{10,11... | collective-permute-start | bytes 884744 | tf_op jit(solution)/shard_map/ppermute | solution.py:35
  4.0 0.9 %copy-start.2 = (f32[35]{0:T(128)S(1)}, f32[35]{0:T(128)}, u32[]{:S(2)}) copy-start(f32[35]{0:T(128)} %refs_12_.2) | copy-start | bytes 424
  4.0 0.9 %copy-start.3 = (s32[2]{0:T(128)S(1)}, s32[2]{0:T(128)}, u32[]{:S(2)}) copy-start(s32[2]{0:T(128)} %refs_13_.3) | copy-start | bytes 28
  4.0 9.9 %collective-permute-start.1 = (f32[2,72,512]{2,1,0:T(8,128)S(1)}, f32[2,72,512]{2,1,0:T(8,128)S(1)}, u32[]{:S(2)}, u32[]{:S(2)}) collective-permute-start(f32[2,72,512]{2,1,0:T(8,128)S(1)} %get-tuple-element.29), channel_id=1, source_target_pairs={{1,2},{2,1},{3,4},{4,3},{5,6},{6,5},{7,8},{8,7},{9,10},{10,9},{11,... | collective-permute-start | bytes 884744 | tf_op jit(solution)/shard_map/ppermute | solution.py:36
  9.4 7.0 %collective-permute-start.2 = (f32[264,128]{1,0:T(8,128)S(1)}, f32[264,128]{1,0:T(8,128)S(1)}, u32[]{:S(2)}, u32[]{:S(2)}) collective-permute-start(f32[264,128]{1,0:T(8,128)S(1)} %get-tuple-element.32), channel_id=1, source_target_pairs={{0,16},{16,0},{32,48},{48,32},{64,80},{80,64},{96,112},{112,96},{1... | collective-permute-start | bytes 405512 | tf_op jit(solution)/shard_map/ppermute | solution.py:35
  10.6 6.3 %collective-permute-start.3 = (f32[264,128]{1,0:T(8,128)S(1)}, f32[264,128]{1,0:T(8,128)S(1)}, u32[]{:S(2)}, u32[]{:S(2)}) collective-permute-start(f32[264,128]{1,0:T(8,128)S(1)} %get-tuple-element.33), channel_id=1, source_target_pairs={{16,32},{32,16},{48,64},{64,48},{80,96},{96,80},{112,128},{128,112... | collective-permute-start | bytes 405512 | tf_op jit(solution)/shard_map/ppermute | solution.py:36
  14.1 5.6 %collective-permute-start.5 = (f32[128,128]{1,0:T(8,128)S(1)}, f32[128,128]{1,0:T(8,128)S(1)}, u32[]{:S(2)}, u32[]{:S(2)}) collective-permute-start(f32[128,128]{1,0:T(8,128)S(1)} %get-tuple-element.36), channel_id=1, source_target_pairs={{16,32},{32,16},{48,64},{64,48},{80,96},{96,80},{112,128},{128,112... | collective-permute-start | bytes 196616 | tf_op jit(solution)/shard_map/ppermute | solution.py:36
  16.3 3.3 %collective-permute-start.4 = (f32[128,128]{1,0:T(8,128)S(1)}, f32[128,128]{1,0:T(8,128)S(1)}, u32[]{:S(2)}, u32[]{:S(2)}) collective-permute-start(f32[128,128]{1,0:T(8,128)S(1)} %get-tuple-element.30.packed), channel_id=1, source_target_pairs={{0,16},{16,0},{32,48},{48,32},{64,80},{80,64},{96,112},{112,96},{1... | collective-permute-start | bytes 196616 | tf_op jit(solution)/shard_map/ppermute | solution.py:35
  20.9 12.6 %collective-permute-start.6 = (f32[2,64,512]{2,1,0:T(8,128)S(1)}, f32[2,64,512]{2,1,0:T(8,128)S(1)}, u32[]{:S(2)}, u32[]{:S(2)}) collective-permute-start(f32[2,64,512]{2,1,0:T(8,128)S(1)} %get-tuple-element.40), channel_id=1, source_target_pairs={{0,1},{1,0},{2,3},{3,2},{4,5},{5,4},{6,7},{7,6},{8,9},{9,8},{10,11... | collective-permute-start | bytes 786440 | tf_op jit(solution)/shard_map/ppermute | solution.py:35
  24.6 8.9 %collective-permute-start.7 = (f32[2,64,512]{2,1,0:T(8,128)S(1)}, f32[2,64,512]{2,1,0:T(8,128)S(1)}, u32[]{:S(2)}, u32[]{:S(2)}) collective-permute-start(f32[2,64,512]{2,1,0:T(8,128)S(1)} %get-tuple-element.41), channel_id=1, source_target_pairs={{1,2},{2,1},{3,4},{4,3},{5,6},{6,5},{7,8},{8,7},{9,10},{10,9},{11,... | collective-permute-start | bytes 786440 | tf_op jit(solution)/shard_map/ppermute | solution.py:36
  29.3 6.4 %collective-permute-start.8 = (f32[256,128]{1,0:T(8,128)S(1)}, f32[256,128]{1,0:T(8,128)S(1)}, u32[]{:S(2)}, u32[]{:S(2)}) collective-permute-start(f32[256,128]{1,0:T(8,128)S(1)} %get-tuple-element.43), channel_id=1, source_target_pairs={{0,16},{16,0},{32,48},{48,32},{64,80},{80,64},{96,112},{112,96},{1... | collective-permute-start | bytes 393224 | tf_op jit(solution)/shard_map/ppermute | solution.py:35
  29.4 6.7 %collective-permute-start.9 = (f32[256,128]{1,0:T(8,128)S(1)}, f32[256,128]{1,0:T(8,128)S(1)}, u32[]{:S(2)}, u32[]{:S(2)}) collective-permute-start(f32[256,128]{1,0:T(8,128)S(1)} %get-tuple-element.44), channel_id=1, source_target_pairs={{16,32},{32,16},{48,64},{64,48},{80,96},{96,80},{112,128},{128,112... | collective-permute-start | bytes 393224 | tf_op jit(solution)/shard_map/ppermute | solution.py:36
  33.7 5.6 %collective-permute-start.11 = (f32[128,128]{1,0:T(8,128)S(1)}, f32[128,128]{1,0:T(8,128)S(1)}, u32[]{:S(2)}, u32[]{:S(2)}) collective-permute-start(f32[128,128]{1,0:T(8,128)S(1)} %get-tuple-element.48), channel_id=1, source_target_pairs={{16,32},{32,16},{48,64},{64,48},{80,96},{96,80},{112,128},{128,112... | collective-permute-start | bytes 196616 | tf_op jit(solution)/shard_map/ppermute | solution.py:36
  35.6 3.7 %collective-permute-start.10 = (f32[128,128]{1,0:T(8,128)S(1)}, f32[128,128]{1,0:T(8,128)S(1)}, u32[]{:S(2)}, u32[]{:S(2)}) collective-permute-start(f32[128,128]{1,0:T(8,128)S(1)} %get-tuple-element.42.packed), channel_id=1, source_target_pairs={{0,16},{16,0},{32,48},{48,32},{64,80},{80,64},{96,112},{112,96},{1... | collective-permute-start | bytes 196616 | tf_op jit(solution)/shard_map/ppermute | solution.py:35

commit v8 on v7

--- a/solution.py
+++ b/solution.py
@@ -1,3 +1,5 @@
+import functools
+
 import jax
 import jax.numpy as jnp
 from jax import lax
@@ -5,7 +7,8 @@
 from jax.experimental.pallas import tpu as pltpu
 from jax.sharding import PartitionSpec as P
 
-REACH = 64
+SMAX = 32
+REACH = 2 * SMAX
 LANES = 128
 HALF = 64
 CHUNK = 32
@@ -59,14 +62,6 @@
     rows = low.shape[0]
     even_ref[start : start + rows, :] = jnp.where(odd, low, high)
     odd_ref[start : start + rows, :] = jnp.where(odd, high, low)
-
-
-def pack_sides_kernel(with_ends, field, after, even_out, odd_out):
-    rows, cols = field.shape[1:]
-    low, high = packed_edges(lambda layer, edge: field[layer, :, edge], cols)
-    store_packed(even_out, odd_out, 0, low, high)
-    if with_ends:
-        store_packed(even_out, odd_out, rows, after[0], after[1])
 
 
 def pack_corners_kernel(even_rows, odd_rows, even_out, odd_out):
@@ -92,13 +87,6 @@
         compiler_params=pltpu.CompilerParams(vmem_limit_bytes=VMEM_BYTES),
         name=name,
     )(*operands)
-
-
-def pack_sides(field, after, with_ends):
-    def kernel(*refs):
-        pack_sides_kernel(with_ends, *refs)
-
-    return pack(kernel, (field, after), field.shape[1] + (8 if with_ends else 0), "pack_sides")
 
 
 def pack_corners(even_rows, odd_rows):
@@ -173,6 +161,10 @@
         jnp.where(lane == LANES - 1, after, tile)
         for tile, after in zip(ahead, [*ahead[1:], last], strict=True)
     ]
+
+
+def near_end(row, rows):
+    return row < SMAX or row + CHUNK > rows - SMAX
 
 
 def apply_chunk(
@@ -210,20 +202,24 @@
         total = (coeff + above_c) * (value - above) + (coeff + below_c) * (value - below)
         inflow = jnp.where(lane == 0, turned[tile - 1] if tile else 0.0, turned[tile])
         result.append(weight * (total + flow[tile] - inflow))
-    for direction in range(shifts.shape[0]):
-        shift_r, shift_c = shifts[direction, layer, 0], shifts[direction, layer, 1]
-        start_r = REACH + row + shifts[direction, other, 0] - shift_r
+    for direction in range(shifts.shape[2]):
+        shift_r, shift_c = shifts[layer, 0, direction], shifts[layer, 1, direction]
+        start_r = REACH + row + shifts[other, 0, direction] - shift_r
         source = [pad[other, tile, pl.ds(start_r, CHUNK), :] for tile in range(tiles)]
-        moved = move_across(source, shifts[direction, other, 1] - shift_c, lane)
-        image_row = row_at + (first_row - shift_r)
-        inside = (image_row >= 0) & (image_row < grid_shape[0])
+        moved = move_across(source, shifts[other, 1, direction] - shift_c, lane)
+        masks = [[] for _ in range(tiles)]
+        masks[0].append(lane >= shift_c - first_col)
+        masks[-1].append(lane < grid_shape[1] + shift_c - first_col - (tiles - 1) * LANES)
+        if near_end(row, rows):
+            image_row = row_at + (first_row - shift_r)
+            inside = (image_row >= 0) & (image_row < grid_shape[0])
+            for mask in masks:
+                mask.append(inside)
         for tile in range(tiles):
-            mask = inside
-            if tile == 0:
-                mask = mask & (lane >= shift_c - first_col)
-            if tile == tiles - 1:
-                mask = mask & (lane < grid_shape[1] + shift_c - first_col - tile * LANES)
-            result[tile] = result[tile] + jnp.where(mask, own[tile] + moved[tile], 0.0)
+            value = own[tile] + moved[tile]
+            if masks[tile]:
+                value = jnp.where(functools.reduce(jnp.logical_and, masks[tile]), value, 0.0)
+            result[tile] = result[tile] + value
     return result
 
 
@@ -241,7 +237,8 @@
     return 0.5 * table[entry[layer]]
 
 
-def pack_ends(coeff, ends):
+def packed_ends(coeff):
+    ends = []
     rows, cols = coeff.shape[1:]
     lane = lane_of((8, LANES))
     for high, edge in enumerate((slice(0, LANES), slice(cols - LANES, cols))):
@@ -253,32 +250,31 @@
                 value = coeff[layer, 8 * group : 8 * group + 8, edge]
                 value = pltpu.roll(value, turn, 1) if turn else value
                 packed = jnp.where(lane == at, value, packed)
-        ends[high] = packed
+        ends.append(packed)
+    return ends
 
 
 def own_kernel(
-    grid_shape, field, coeff, across, shifts, table, entry, out, ends, across_out, pad, coeff_pad
+    grid_shape, field, coeff, across, shifts, table, entry, out, even_side, odd_side, across_out, pad,
+    coeff_pad,
 ):
     rows, cols = field.shape[1:]
     zero_rim(pad, REACH, rows)
     zero_rim(coeff_pad, 8, rows)
     fill_own(pad, REACH, field)
     fill_own(coeff_pad, 8, coeff)
-    if ends is not None:
-        pack_ends(coeff, ends)
+    low, high = packed_edges(lambda layer, edge: field[layer, :, edge], cols)
+    store_packed(even_side, odd_side, 0, low, high)
+    if across is None:
+        store_packed(even_side, odd_side, rows, *packed_ends(coeff))
     for layer in range(2):
         weight = weight_of(table, entry, layer)
-
-        def step(i, carry, layer=layer, weight=weight):
-            row = pl.multiple_of(i * CHUNK, CHUNK)
+        for row in range(0, rows, CHUNK):
             result = apply_chunk(
                 layer, row, pad, coeff_pad, across, across_out, shifts, weight, grid_shape, (rows, cols)
             )
             for tile, value in enumerate(result):
-                out[layer, pl.ds(row, CHUNK), tile * LANES : (tile + 1) * LANES] = value
-            return carry
-
-        lax.fori_loop(0, rows // CHUNK, step, 0, unroll=UNROLL)
+                out[layer, row : row + CHUNK, tile * LANES : (tile + 1) * LANES] = value
 
 
 def products_of(own, result, base, fit):
@@ -326,16 +322,16 @@
         def step(i, carry, layer=layer, other_layer=other_layer):
             part = pl.multiple_of(i * CHUNK, CHUNK)
             totals = [[jnp.zeros((CHUNK, LANES), jnp.float32)] * tiles for _ in range(2)]
-            for direction in range(shifts.shape[0]):
-                shift_r, shift_c = shifts[direction, layer, 0], shifts[direction, layer, 1]
-                step_r = shifts[direction, other_layer, 0] - shift_r
+            for direction in range(shifts.shape[2]):
+                shift_r, shift_c = shifts[layer, 0, direction], shifts[layer, 1, direction]
+                step_r = shifts[other_layer, 0, direction] - shift_r
                 side = jnp.where(step_r < 0, 0, 1)
                 start_r = part + step_r + jnp.where(step_r < 0, REACH, 0)
                 row = part + jnp.where(step_r < 0, 0, rows - REACH)
                 source = [
                     pad[other_layer, side, tile, pl.ds(start_r, CHUNK), :] for tile in range(tiles)
                 ]
-                moved = move_across(source, shifts[direction, other_layer, 1] - shift_c, lane)
+                moved = move_across(source, shifts[other_layer, 1, direction] - shift_c, lane)
                 image_row = row_at + (first_row + row - shift_r)
                 inside = (image_row >= 0) & (image_row < grid_shape[0])
                 upper = inside & (jnp.full((CHUNK, LANES), side, jnp.int32) == 0)
@@ -423,15 +419,16 @@
         extra = weight * ((own_c + edge_c) * (own[side] - edge_v))
         extra = jnp.where(lane == spot, extra, 0.0)
         result.append(out[layer, pl.ds(row, CHUNK), cut[side]] + extra)
-    for direction in range(shifts.shape[0]):
-        shift_r, shift_c = shifts[direction, layer, 0], shifts[direction, layer, 1]
-        start_r = REACH + row + shifts[direction, 1 - layer, 0] - shift_r
-        step_c = shifts[direction, 1 - layer, 1] - shift_c
+    for direction in range(shifts.shape[2]):
+        shift_r, shift_c = shifts[layer, 0, direction], shifts[layer, 1, direction]
+        start_r = REACH + row + shifts[1 - layer, 0, direction] - shift_r
+        step_c = shifts[1 - layer, 1, direction] - shift_c
         side = jnp.where(step_c < 0, 0, 1)
         back = jnp.bitwise_and(LANES - step_c, LANES - 1)
         moved = pltpu.roll(pad[1 - layer, side, pl.ds(start_r, CHUNK), :], back, 1)
-        image_row = row_at + (first_row - shift_r)
-        moved = jnp.where((image_row >= 0) & (image_row < grid_shape[0]), moved, 0.0)
+        if near_end(row, rows):
+            image_row = row_at + (first_row - shift_r)
+            moved = jnp.where((image_row >= 0) & (image_row < grid_shape[0]), moved, 0.0)
         low, low_end = shift_c - first_col, jnp.where(step_c < 0, -step_c, 0)
         high = jnp.where(step_c < 0, LANES, LANES - step_c)
         high_end = grid_shape[1] + shift_c - first_col - (tiles - 1) * LANES
@@ -593,10 +590,13 @@
     grid_shape = (rows * count_y, cols * count_x)
     full = jax.ShapeDtypeStruct((layers, rows, cols), jnp.float32)
     edge = jax.ShapeDtypeStruct((layers, REACH, cols), jnp.float32)
-    scalars = (shifts, strength_table, layer_entry)
+    scalars = (jnp.transpose(shifts, (1, 2, 0)), strength_table, layer_entry)
     own_pads = [(2, tiles, rows + 2 * REACH, LANES), (2, tiles, rows + 16, LANES)]
     row_pads = [(2, 2, tiles, 2 * REACH, LANES)]
     side_pad = jax.ShapeDtypeStruct((2, 2, rows + 2 * REACH, LANES), jnp.float32)
+
+    def side_of(count):
+        return jax.ShapeDtypeStruct((count, LANES), jnp.float32)
 
     def sums_of(count):
         return jax.ShapeDtypeStruct((count, 8, LANES), jnp.float32)
@@ -621,15 +621,15 @@
     def own_first(field, coeff, *refs):
         own_kernel(grid_shape, field, coeff, None, *refs)
 
-    def own_second(field, coeff, across, shifts, table, entry, out, *pads):
-        own_kernel(grid_shape, field, coeff, across, shifts, table, entry, out, None, None, *pads)
+    def own_second(field, coeff, across, shifts, table, entry, out, even, odd, *pads):
+        own_kernel(grid_shape, field, coeff, across, shifts, table, entry, out, even, odd, None, *pads)
 
     rows0 = swap(*edge_rows(right_side, coefficient), "gy")
-    w_own, ends, across = on_tensor_core(
-        own_first, "own_first", (right_side, coefficient), scalars, (full, sums_of(2), full), own_pads,
-        6,
-    )
-    cols0 = swap(*pack_sides(right_side, ends, True), "gx")
+    w_own, *columns, across = on_tensor_core(
+        own_first, "own_first", (right_side, coefficient), scalars,
+        (full, side_of(rows + 8), side_of(rows + 8), full), own_pads, 6,
+    )
+    cols0 = swap(*columns, "gx")
     packed = pack_corners(*rows0)
     corners0 = swap(*packed, "gx")
     w_rows, products, sides = on_tensor_core(
@@ -642,10 +642,11 @@
         (full, side_pad, sums_of(3), edge, edge), [], 3, 2,
     )
     rows1 = swap(even, odd, "gy")
-    (n_own,) = on_tensor_core(
-        own_second, "own_second", (w_vec, coefficient, across), scalars, (full,), own_pads, 6
-    )
-    cols1 = swap(*pack_sides(w_vec, n_own, False), "gx")
+    n_own, *columns = on_tensor_core(
+        own_second, "own_second", (w_vec, coefficient, across), scalars,
+        (full, side_of(rows), side_of(rows)), own_pads, 6,
+    )
+    cols1 = swap(*columns, "gx")
     packed = pack_corners(*rows1)
     corners1 = swap(*packed, "gx")
     n_rows, products, sides = on_tensor_core(

time: 73.9 us -> 73.3 us (level)
  no operation moved by 1% of the time
where the time goes in v8:
time: 73.3 us; the launch traced here: 73 us
  blocking collectives  30.8 us (42%)
  starting transfers between devices  20.4 us (28%)
  Pallas kernels  17.9 us (24%)
  waiting for transfers between devices  2.84 us (4%)
  between operations  1.04 us (1%)
    all_to_all x1, blocking collectives, on_device(): gathered = lax.all_to_all(parts, ('gx', 'gy'), 0, 0, tiled=True)  30.8 us
    pallas_call x6, Pallas kernels, on_tensor_core(): pl.pallas_call(kernel, out_shape=out_shape, in_specs=[VMEM_SPEC] * len(op...  14.6 us
    ppermute x6, starting transfers between devices, swap(): lax.ppermute(odd, axis, odd_swap(count))  12.9 us
    ppermute x6, starting transfers between devices, swap(): lax.ppermute(even, axis, even_swap(count))  7.51 us
    ppermute x6, waiting for transfers between devices, swap(): lax.ppermute(odd, axis, odd_swap(count))  2.82 us
    pallas_call x1, Pallas kernels, on_device(): pl.pallas_call(last_kernel, out_shape=(full, full), in_specs=[VMEM_SPEC]...  1.88 us
  transfers between devices with their start and end apart: 12, of which 4 were waited for; matrix products, arithmetic and copies ran while one was open for 0% of the time, Pallas kernels for 17%

profile of v8, /device:TPU:1, one launch (start us, length us, event | category | flops | bytes accessed | tf_op | source)
XLA Modules:
  0.0 73.0 jit_solution(75435409455814313)
XLA Ops:
  0.6 0.0 copy-start
  0.6 0.0 copy-start.1
  0.6 1.2 %edge_rows.1 = (f32[2,72,512]{2,1,0:T(8,128)S(1)}, f32[2,72,512]{2,1,0:T(8,128)S(1)}) custom-call(f32[2,256,512]{2,1,0:T(8,128)} %base.1, f32[2,256,512]{2,1,0:T(8,128)} %refs_4_.1), custom_call_target="tpu_custom_call" | custom-call | tf_op jit(solution)/shard_map/edge_rows/pallas_call | solution.py:119
  1.9 0.0 copy-start.2
  1.9 2.1 %collective-permute-start = (f32[2,72,512]{2,1,0:T(8,128)S(1)}, f32[2,72,512]{2,1,0:T(8,128)S(1)}, u32[]{:S(2)}, u32[]{:S(2)}) collective-permute-start(f32[2,72,512]{2,1,0:T(8,128)S(1)} %get-tuple-element.28), channel_id=1, source_target_pairs={{0,1},{1,0},{2,3},{3,2},{4,5},{5,4},{6,7},{7,6},{8,9},{9,8},{10,11... | collective-permute-start | bytes 884744 | tf_op jit(solution)/shard_map/ppermute | solution.py:38
  4.0 0.0 copy-start.3
  4.0 0.0 copy-start.4
  4.0 0.8 %collective-permute-start.1 = (f32[2,72,512]{2,1,0:T(8,128)S(1)}, f32[2,72,512]{2,1,0:T(8,128)S(1)}, u32[]{:S(2)}, u32[]{:S(2)}) collective-permute-start(f32[2,72,512]{2,1,0:T(8,128)S(1)} %get-tuple-element.29), channel_id=1, source_target_pairs={{1,2},{2,1},{3,4},{4,3},{5,6},{6,5},{7,8},{8,7},{9,10},{10,9},{11,... | collective-permute-start | bytes 884744 | tf_op jit(solution)/shard_map/ppermute | solution.py:39
  4.8 0.0 copy-done
  4.9 0.0 copy-done.1
  4.9 0.0 copy-done.2
  4.9 0.0 copy-done.3
  4.9 0.0 copy-done.4
  4.9 4.4 %own_first.1 = (f32[2,256,512]{2,1,0:T(8,128)S(1)}, f32[264,128]{1,0:T(8,128)S(1)}, f32[264,128]{1,0:T(8,128)S(1)}, f32[2,256,512]{2,1,0:T(8,128)S(1)}) custom-call(f32[2,256,512]{2,1,0:T(8,128)S(1)} %copy-done.1, f32[2,256,512]{2,1,0:T(8,128)S(1)} %copy-done, s32[2,2,6]{2,1,0:T(2,128)S(1)} %bitcast.7, f32[35]{0:T(128)S(1)} %copy-done.3, s32[2]{0:T(128)S(1)} %copy-done.4), custom_call_target="tpu_custom_call" | custom-call | bytes 18000000 | tf_op jit(solution)/shard_map/own_first/pallas_call | solution.py:570
  9.3 1.2 %collective-permute-start.2 = (f32[264,128]{1,0:T(8,128)S(1)}, f32[264,128]{1,0:T(8,128)S(1)}, u32[]{:S(2)}, u32[]{:S(2)}) collective-permute-start(f32[264,128]{1,0:T(8,128)S(1)} %get-tuple-element.31), channel_id=1, source_target_pairs={{0,16},{16,0},{32,48},{48,32},{64,80},{80,64},{96,112},{112,96},{1... | collective-permute-start | bytes 405512 | tf_op jit(solution)/shard_map/ppermute | solution.py:38
  10.5 3.3 %collective-permute-start.3 = (f32[264,128]{1,0:T(8,128)S(1)}, f32[264,128]{1,0:T(8,128)S(1)}, u32[]{:S(2)}, u32[]{:S(2)}) collective-permute-start(f32[264,128]{1,0:T(8,128)S(1)} %get-tuple-element.32), channel_id=1, source_target_pairs={{16,32},{32,16},{48,64},{64,48},{80,96},{96,80},{112,128},{128,112... | collective-permute-start | bytes 405512 | tf_op jit(solution)/shard_map/ppermute | solution.py:39
  13.8 0.0 collective-permute-done.even_rows.even.refs_4_
  13.8 0.0 collective-permute-done.1.odd_rows.odd.refs_5_
  13.8 0.1 pack_corners.2
  13.9 2.3 %collective-permute-start.5 = (f32[128,128]{1,0:T(8,128)S(1)}, f32[128,128]{1,0:T(8,128)S(1)}, u32[]{:S(2)}, u32[]{:S(2)}) collective-permute-start(f32[128,128]{1,0:T(8,128)S(1)} %get-tuple-element.35), channel_id=1, source_target_pairs={{16,32},{32,16},{48,64},{64,48},{80,96},{96,80},{112,128},{128,112... | collective-permute-start | bytes 196616 | tf_op jit(solution)/shard_map/ppermute | solution.py:39
  16.2 0.1 collective-permute-start.4
  16.3 0.0 collective-permute-done.2.even_cols.refs_4_.refs_8_.refs_5_
  16.3 0.5 collective-permute-done.3.odd_cols.refs_5_.refs_9_.refs_6_
  16.8 1.8 %rows_first.1 = (f32[2,256,512]{2,1,0:T(8,128)S(1)}, f32[3,8,128]{2,1,0:T(8,128)S(1)}, f32[2,2,384,128]{3,2,1,0:T(8,128)S(1)}) custom-call(f32[2,256,512]{2,1,0:T(8,128)S(1)} %get-tuple-element.27.before, f32[128,128]{1,0:T(8,128)S(1)} %get-tuple-element.30.packed, f32[2,256,512]{2,1,0:T(8,128)S(1)} %copy-done.1, ...), custom_call_target="tpu_custom_call", output_to_operand_aliasing={{0}: (0, {})} | custom-call | bytes 9000000 | tf_op jit(solution)/shard_map/rows_first/pallas_call | solution.py:570
  18.6 0.9 %collective-permute-done.5.refs_7_ = f32[128,128]{1,0:T(8,128)S(1)} collective-permute-done((f32[128,128]{1,0:T(8,128)S(1)}, f32[128,128]{1,0:T(8,128)S(1)}, u32[]{:S(2)}, u32[]{:S(2)}) %collective-permute-start.5) | collective-permute-done | bytes 65568 | tf_op jit(solution)/shard_map/ppermute | solution.py:39
  19.5 0.0 collective-permute-done.4.refs_6_
  19.5 1.2 %first_apply.1 = (f32[2,256,512]{2,1,0:T(8,128)S(1)}, f32[2,2,384,128]{3,2,1,0:T(8,128)S(1)}, f32[3,8,128]{2,1,0:T(8,128)S(1)}, f32[2,64,512]{2,1,0:T(8,128)S(1)}, f32[2,64,512]{2,1,0:T(8,128)S(1)}) custom-call(f32[2,256,512]{2,1,0:T(8,128)S(1)} %get-tuple-element.33.refs_0_, ...), custom_call_target="tpu_custom_call", output_to_operand_aliasing={{0}: (0, {}), {1}: (1, {})} | custom-call | bytes 9000000 | tf_op jit(solution)/shard_map/first_apply/pallas_call | solution.py:570
  20.7 3.7 %collective-permute-start.6 = (f32[2,64,512]{2,1,0:T(8,128)S(1)}, f32[2,64,512]{2,1,0:T(8,128)S(1)}, u32[]{:S(2)}, u32[]{:S(2)}) collective-permute-start(f32[2,64,512]{2,1,0:T(8,128)S(1)} %get-tuple-element.40), channel_id=1, source_target_pairs={{0,1},{1,0},{2,3},{3,2},{4,5},{5,4},{6,7},{7,6},{8,9},{9,8},{10,11... | collective-permute-start | bytes 786440 | tf_op jit(solution)/shard_map/ppermute | solution.py:38
  24.4 0.7 collective-permute-start.7
  25.1 4.0 %own_second.1 = (f32[2,256,512]{2,1,0:T(8,128)S(1)}, f32[256,128]{1,0:T(8,128)S(1)}, f32[256,128]{1,0:T(8,128)S(1)}) custom-call(f32[2,256,512]{2,1,0:T(8,128)S(1)} %get-tuple-element.37.field.refs_0_.refs_3_.w_vec, f32[2,256,512]{2,1,0:T(8,128)S(1)} %copy-done, f32[2,256,512]{2,1,0:T(8,128)S(1)} %get-tuple-element.38.across, s32[2,2,6]{2,1,0:T(2,128)S(1)} %bitcast.10, ...), custom_call_target="tpu_custom_call" | custom-call | bytes 18000000 | tf_op jit(solution)/shard_map/own_second/pallas_call | solution.py:570
  29.0 0.1 collective-permute-start.8
  29.1 3.9 %collective-permute-start.9 = (f32[256,128]{1,0:T(8,128)S(1)}, f32[256,128]{1,0:T(8,128)S(1)}, u32[]{:S(2)}, u32[]{:S(2)}) collective-permute-start(f32[256,128]{1,0:T(8,128)S(1)} %get-tuple-element.44), channel_id=1, source_target_pairs={{16,32},{32,16},{48,64},{64,48},{80,96},{96,80},{112,128},{128,112... | collective-permute-start | bytes 393224 | tf_op jit(solution)/shard_map/ppermute | solution.py:39
  33.1 0.0 collective-permute-done.6.even_rows.refs_2_
  33.1 0.0 collective-permute-done.7.odd_rows.refs_3_
  33.1 0.1 pack_corners.3
  33.2 1.9 %collective-permute-start.11 = (f32[128,128]{1,0:T(8,128)S(1)}, f32[128,128]{1,0:T(8,128)S(1)}, u32[]{:S(2)}, u32[]{:S(2)}) collective-permute-start(f32[128,128]{1,0:T(8,128)S(1)} %get-tuple-element.48), channel_id=1, source_target_pairs={{16,32},{32,16},{48,64},{64,48},{80,96},{96,80},{112,128},{128,112... | collective-permute-start | bytes 196616 | tf_op jit(solution)/shard_map/ppermute | solution.py:39
  35.1 0.3 collective-permute-start.10
  35.4 0.0 collective-permute-done.8.refs_6_
  35.4 0.3 collective-permute-done.9.refs_7_
  35.7 2.0 %rows_second.1 = (f32[2,256,512]{2,1,0:T(8,128)S(1)}, f32[6,8,128]{2,1,0:T(8,128)S(1)}, f32[2,2,384,128]{3,2,1,0:T(8,128)S(1)}) custom-call(f32[2,256,512]{2,1,0:T(8,128)S(1)} %get-tuple-element.39.before, f32[128,128]{1,0:T(8,128)S(1)} %get-tuple-element.42.packed, ...), custom_call_target="tpu_custom_call", output_to_operand_aliasing={{0}: (0, {})} | custom-call | bytes 9000000 | tf_op jit(solution)/shard_map/rows_second/pallas_call | solution.py:570
  37.7 1.1 %collective-permute-done.11.refs_8_ = f32[128,128]{1,0:T(8,128)S(1)} collective-permute-done((f32[128,128]{1,0:T(8,128)S(1)}, f32[128,128]{1,0:T(8,128)S(1)}, u32[]{:S(2)}, u32[]{:S(2)}) %collective-permute-start.11) | collective-permute-done | bytes 65568 | tf_op jit(solution)/shard_map/ppermute | solution.py:39
  38.8 0.0 collective-permute-done.10.refs_7_
  38.8 1.3 %second_apply.1 = (f32[2,256,512]{2,1,0:T(8,128)S(1)}, f32[2,2,384,128]{3,2,1,0:T(8,128)S(1)}, f32[256,128]{1,0:T(8,128)S(1)}) custom-call(f32[2,256,512]{2,1,0:T(8,128)S(1)} %get-tuple-element.46.refs_0_, f32[2,2,384,128]{3,2,1,0:T(8,128)S(1)} %get-tuple-element.47.refs_1_, ...), custom_call_target="tpu_custom_call", output_to_operand_aliasing={{0}: (0, {}), {1}: (1, {})} | custom-call | bytes 9000000 | tf_op jit(solution)/shard_map/second_apply/pallas_call | solution.py:570
  40.1 30.8 %all_to_all.11 = f32[256,1,128]{2,1,0:T(1,128)S(1)} all-to-all(f32[256,1,128]{2,1,0:T(1,128)S(1)} %bitcast.6), channel_id=1, replica_groups=mesh['gx'=16,'gy'=16] {'gx','gy'}, dimensions={0} | all-to-all | bytes 262144 | tf_op jit(solution)/shard_map/all_to_all | solution.py:662
  70.9 1.9 %last_update.1 = (f32[2,256,512]{2,1,0:T(8,128)}, f32[2,256,512]{2,1,0:T(8,128)}) custom-call(f32[256,128]{1,0:T(8,128)S(1)} %bitcast.5, f32[2,256,512]{2,1,0:T(8,128)S(1)} %copy-done.1, f32[2,256,512]{2,1,0:T(8,128)S(1)} %get-tuple-element.37.field.refs_0_.refs_3_.w_vec, f32[2,256,512]{2,1,0:T(8,128)S(1)} %get-tuple-element.51.n_vec), custom_call_target="tpu_custom_call" | custom-call | tf_op jit(solution)/shard_map/last_update/pallas_call | solution.py:663
Async XLA Ops:
  0.6 4.2 %copy-start = (f32[2,256,512]{2,1,0:T(8,128)S(1)}, f32[2,256,512]{2,1,0:T(8,128)}, u32[]{:S(2)}) copy-start(f32[2,256,512]{2,1,0:T(8,128)} %refs_4_.1) | copy-start | bytes 3145732
  0.6 4.2 %copy-start.1 = (f32[2,256,512]{2,1,0:T(8,128)S(1)}, f32[2,256,512]{2,1,0:T(8,128)}, u32[]{:S(2)}) copy-start(f32[2,256,512]{2,1,0:T(8,128)} %base.1) | copy-start | bytes 3145732
  1.9 3.0 %copy-start.2 = (s32[6,2,2]{0,2,1:T(2,128)S(1)}, s32[6,2,2]{0,2,1:T(2,128)}, u32[]{:S(2)}) copy-start(s32[6,2,2]{0,2,1:T(2,128)} %param.9) | copy-start | bytes 292
  1.9 11.9 %collective-permute-start = (f32[2,72,512]{2,1,0:T(8,128)S(1)}, f32[2,72,512]{2,1,0:T(8,128)S(1)}, u32[]{:S(2)}, u32[]{:S(2)}) collective-permute-start(f32[2,72,512]{2,1,0:T(8,128)S(1)} %get-tuple-element.28), channel_id=1, source_target_pairs={{0,1},{1,0},{2,3},{3,2},{4,5},{5,4},{6,7},{7,6},{8,9},{9,8},{10,11... | collective-permute-start | bytes 884744 | tf_op jit(solution)/shard_map/ppermute | solution.py:38
  4.0 0.8 %copy-start.3 = (f32[35]{0:T(128)S(1)}, f32[35]{0:T(128)}, u32[]{:S(2)}) copy-start(f32[35]{0:T(128)} %refs_12_.1) | copy-start | bytes 424
  4.0 0.9 %copy-start.4 = (s32[2]{0:T(128)S(1)}, s32[2]{0:T(128)}, u32[]{:S(2)}) copy-start(s32[2]{0:T(128)} %refs_13_.3) | copy-start | bytes 28
  4.0 9.8 %collective-permute-start.1 = (f32[2,72,512]{2,1,0:T(8,128)S(1)}, f32[2,72,512]{2,1,0:T(8,128)S(1)}, u32[]{:S(2)}, u32[]{:S(2)}) collective-permute-start(f32[2,72,512]{2,1,0:T(8,128)S(1)} %get-tuple-element.29), channel_id=1, source_target_pairs={{1,2},{2,1},{3,4},{4,3},{5,6},{6,5},{7,8},{8,7},{9,10},{10,9},{11,... | collective-permute-start | bytes 884744 | tf_op jit(solution)/shard_map/ppermute | solution.py:39
  9.3 7.0 %collective-permute-start.2 = (f32[264,128]{1,0:T(8,128)S(1)}, f32[264,128]{1,0:T(8,128)S(1)}, u32[]{:S(2)}, u32[]{:S(2)}) collective-permute-start(f32[264,128]{1,0:T(8,128)S(1)} %get-tuple-element.31), channel_id=1, source_target_pairs={{0,16},{16,0},{32,48},{48,32},{64,80},{80,64},{96,112},{112,96},{1... | collective-permute-start | bytes 405512 | tf_op jit(solution)/shard_map/ppermute | solution.py:38
  10.5 6.3 %collective-permute-start.3 = (f32[264,128]{1,0:T(8,128)S(1)}, f32[264,128]{1,0:T(8,128)S(1)}, u32[]{:S(2)}, u32[]{:S(2)}) collective-permute-start(f32[264,128]{1,0:T(8,128)S(1)} %get-tuple-element.32), channel_id=1, source_target_pairs={{16,32},{32,16},{48,64},{64,48},{80,96},{96,80},{112,128},{128,112... | collective-permute-start | bytes 405512 | tf_op jit(solution)/shard_map/ppermute | solution.py:39
  13.9 5.6 %collective-permute-start.5 = (f32[128,128]{1,0:T(8,128)S(1)}, f32[128,128]{1,0:T(8,128)S(1)}, u32[]{:S(2)}, u32[]{:S(2)}) collective-permute-start(f32[128,128]{1,0:T(8,128)S(1)} %get-tuple-element.35), channel_id=1, source_target_pairs={{16,32},{32,16},{48,64},{64,48},{80,96},{96,80},{112,128},{128,112... | collective-permute-start | bytes 196616 | tf_op jit(solution)/shard_map/ppermute | solution.py:39
  16.2 3.3 %collective-permute-start.4 = (f32[128,128]{1,0:T(8,128)S(1)}, f32[128,128]{1,0:T(8,128)S(1)}, u32[]{:S(2)}, u32[]{:S(2)}) collective-permute-start(f32[128,128]{1,0:T(8,128)S(1)} %get-tuple-element.30.packed), channel_id=1, source_target_pairs={{0,16},{16,0},{32,48},{48,32},{64,80},{80,64},{96,112},{112,96},{1... | collective-permute-start | bytes 196616 | tf_op jit(solution)/shard_map/ppermute | solution.py:38
  20.7 12.4 %collective-permute-start.6 = (f32[2,64,512]{2,1,0:T(8,128)S(1)}, f32[2,64,512]{2,1,0:T(8,128)S(1)}, u32[]{:S(2)}, u32[]{:S(2)}) collective-permute-start(f32[2,64,512]{2,1,0:T(8,128)S(1)} %get-tuple-element.40), channel_id=1, source_target_pairs={{0,1},{1,0},{2,3},{3,2},{4,5},{5,4},{6,7},{7,6},{8,9},{9,8},{10,11... | collective-permute-start | bytes 786440 | tf_op jit(solution)/shard_map/ppermute | solution.py:38
  24.4 8.7 %collective-permute-start.7 = (f32[2,64,512]{2,1,0:T(8,128)S(1)}, f32[2,64,512]{2,1,0:T(8,128)S(1)}, u32[]{:S(2)}, u32[]{:S(2)}) collective-permute-start(f32[2,64,512]{2,1,0:T(8,128)S(1)} %get-tuple-element.41), channel_id=1, source_target_pairs={{1,2},{2,1},{3,4},{4,3},{5,6},{6,5},{7,8},{8,7},{9,10},{10,9},{11,... | collective-permute-start | bytes 786440 | tf_op jit(solution)/shard_map/ppermute | solution.py:39
  29.0 6.4 %collective-permute-start.8 = (f32[256,128]{1,0:T(8,128)S(1)}, f32[256,128]{1,0:T(8,128)S(1)}, u32[]{:S(2)}, u32[]{:S(2)}) collective-permute-start(f32[256,128]{1,0:T(8,128)S(1)} %get-tuple-element.43), channel_id=1, source_target_pairs={{0,16},{16,0},{32,48},{48,32},{64,80},{80,64},{96,112},{112,96},{1... | collective-permute-start | bytes 393224 | tf_op jit(solution)/shard_map/ppermute | solution.py:38
  29.1 6.6 %collective-permute-start.9 = (f32[256,128]{1,0:T(8,128)S(1)}, f32[256,128]{1,0:T(8,128)S(1)}, u32[]{:S(2)}, u32[]{:S(2)}) collective-permute-start(f32[256,128]{1,0:T(8,128)S(1)} %get-tuple-element.44), channel_id=1, source_target_pairs={{16,32},{32,16},{48,64},{64,48},{80,96},{96,80},{112,128},{128,112... | collective-permute-start | bytes 393224 | tf_op jit(solution)/shard_map/ppermute | solution.py:39
  33.2 5.6 %collective-permute-start.11 = (f32[128,128]{1,0:T(8,128)S(1)}, f32[128,128]{1,0:T(8,128)S(1)}, u32[]{:S(2)}, u32[]{:S(2)}) collective-permute-start(f32[128,128]{1,0:T(8,128)S(1)} %get-tuple-element.48), channel_id=1, source_target_pairs={{16,32},{32,16},{48,64},{64,48},{80,96},{96,80},{112,128},{128,112... | collective-permute-start | bytes 196616 | tf_op jit(solution)/shard_map/ppermute | solution.py:39
  35.1 3.7 %collective-permute-start.10 = (f32[128,128]{1,0:T(8,128)S(1)}, f32[128,128]{1,0:T(8,128)S(1)}, u32[]{:S(2)}, u32[]{:S(2)}) collective-permute-start(f32[128,128]{1,0:T(8,128)S(1)} %get-tuple-element.42.packed), channel_id=1, source_target_pairs={{0,16},{16,0},{32,48},{48,32},{64,80},{80,64},{96,112},{112,96},{1... | collective-permute-start | bytes 196616 | tf_op jit(solution)/shard_map/ppermute | solution.py:38

commit v9 on v8

--- a/solution.py
+++ b/solution.py
@@ -12,6 +12,7 @@
 LANES = 128
 HALF = 64
 CHUNK = 32
+OWN_CHUNK = 64
 UNROLL = 8
 PIECES = 4
 VMEM_BYTES = 32 * 1024 * 1024
@@ -20,23 +21,23 @@
 SMEM_SPEC = pl.BlockSpec(memory_space=pltpu.SMEM)
 
 
-def even_swap(count):
-    return [(i, i ^ 1) for i in range(count)]
-
-
-def odd_swap(count):
-    return [(i, i + 1 if i % 2 else i - 1) for i in range(1, count - 1)]
+def pairs_from(start, count):
+    low = range(start, count - 1, 2)
+    return [(i, i + 1) for i in low] + [(i + 1, i) for i in low]
+
+
+FIRST = {"gy": 1, "gx": 0}
 
 
 def is_odd(axis):
-    return lax.rem(lax.axis_index(axis), 2) == 1
+    return lax.rem(lax.axis_index(axis) + FIRST[axis], 2) == 1
 
 
 def swap(even, odd, axis):
     count = lax.axis_size(axis)
     return (
-        lax.ppermute(even, axis, even_swap(count)),
-        lax.ppermute(odd, axis, odd_swap(count)),
+        lax.ppermute(even, axis, pairs_from(FIRST[axis], count)),
+        lax.ppermute(odd, axis, pairs_from(1 - FIRST[axis], count)),
     )
 
 
@@ -163,8 +164,8 @@
     ]
 
 
-def near_end(row, rows):
-    return row < SMAX or row + CHUNK > rows - SMAX
+def near_end(row, depth, rows):
+    return row < SMAX or row + depth > rows - SMAX
 
 
 def apply_chunk(
@@ -173,14 +174,14 @@
     rows, cols = tile_shape
     tiles = cols // LANES
     other = 1 - layer
-    lane = lane_of((CHUNK, LANES))
-    row_at = lax.broadcasted_iota(jnp.int32, (CHUNK, LANES), 0)
+    lane = lane_of((OWN_CHUNK, LANES))
+    row_at = lax.broadcasted_iota(jnp.int32, (OWN_CHUNK, LANES), 0)
     first_row = lax.axis_index("gy") * rows + row
     first_col = lax.axis_index("gx") * cols
     cut = [slice(tile * LANES, (tile + 1) * LANES) for tile in range(tiles)]
 
     def at(ref, tile, start):
-        return ref[layer, tile, pl.ds(start, CHUNK), :]
+        return ref[layer, tile, pl.ds(start, OWN_CHUNK), :]
 
     own = [at(pad, tile, REACH + row) for tile in range(tiles)]
     own_c = [at(coeff_pad, tile, 8 + row) for tile in range(tiles)]
@@ -188,9 +189,9 @@
         right_c = from_the_right(own_c, lane, 0.0)
         both = [a + b for a, b in zip(own_c, right_c, strict=True)]
         for value, lanes in zip(both, cut, strict=True):
-            across_out[layer, pl.ds(row, CHUNK), lanes] = value
+            across_out[layer, pl.ds(row, OWN_CHUNK), lanes] = value
     else:
-        both = [across[layer, pl.ds(row, CHUNK), lanes] for lanes in cut]
+        both = [across[layer, pl.ds(row, OWN_CHUNK), lanes] for lanes in cut]
     right = from_the_right(own, lane, own[-1])
     flow = [c * (a - b) for c, a, b in zip(both, own, right, strict=True)]
     turned = [pltpu.roll(value, 1, 1) for value in flow]
@@ -205,12 +206,12 @@
     for direction in range(shifts.shape[2]):
         shift_r, shift_c = shifts[layer, 0, direction], shifts[layer, 1, direction]
         start_r = REACH + row + shifts[other, 0, direction] - shift_r
-        source = [pad[other, tile, pl.ds(start_r, CHUNK), :] for tile in range(tiles)]
+        source = [pad[other, tile, pl.ds(start_r, OWN_CHUNK), :] for tile in range(tiles)]
         moved = move_across(source, shifts[other, 1, direction] - shift_c, lane)
         masks = [[] for _ in range(tiles)]
         masks[0].append(lane >= shift_c - first_col)
         masks[-1].append(lane < grid_shape[1] + shift_c - first_col - (tiles - 1) * LANES)
-        if near_end(row, rows):
+        if near_end(row, OWN_CHUNK, rows):
             image_row = row_at + (first_row - shift_r)
             inside = (image_row >= 0) & (image_row < grid_shape[0])
             for mask in masks:
@@ -255,26 +256,26 @@
 
 
 def own_kernel(
-    grid_shape, field, coeff, across, shifts, table, entry, out, even_side, odd_side, across_out, pad,
-    coeff_pad,
+    grid_shape, field, coeff, across, shifts, table, entry, out, even_side, odd_side, across_out,
+    coeff_pad, pad,
 ):
     rows, cols = field.shape[1:]
     zero_rim(pad, REACH, rows)
-    zero_rim(coeff_pad, 8, rows)
     fill_own(pad, REACH, field)
-    fill_own(coeff_pad, 8, coeff)
     low, high = packed_edges(lambda layer, edge: field[layer, :, edge], cols)
     store_packed(even_side, odd_side, 0, low, high)
     if across is None:
+        zero_rim(coeff_pad, 8, rows)
+        fill_own(coeff_pad, 8, coeff)
         store_packed(even_side, odd_side, rows, *packed_ends(coeff))
     for layer in range(2):
         weight = weight_of(table, entry, layer)
-        for row in range(0, rows, CHUNK):
+        for row in range(0, rows, OWN_CHUNK):
             result = apply_chunk(
                 layer, row, pad, coeff_pad, across, across_out, shifts, weight, grid_shape, (rows, cols)
             )
             for tile, value in enumerate(result):
-                out[layer, row : row + CHUNK, tile * LANES : (tile + 1) * LANES] = value
+                out[layer, row : row + OWN_CHUNK, tile * LANES : (tile + 1) * LANES] = value
 
 
 def products_of(own, result, base, fit):
@@ -426,7 +427,7 @@
         side = jnp.where(step_c < 0, 0, 1)
         back = jnp.bitwise_and(LANES - step_c, LANES - 1)
         moved = pltpu.roll(pad[1 - layer, side, pl.ds(start_r, CHUNK), :], back, 1)
-        if near_end(row, rows):
+        if near_end(row, CHUNK, rows):
             image_row = row_at + (first_row - shift_r)
             moved = jnp.where((image_row >= 0) & (image_row < grid_shape[0]), moved, 0.0)
         low, low_end = shift_c - first_col, jnp.where(step_c < 0, -step_c, 0)
@@ -591,7 +592,8 @@
     full = jax.ShapeDtypeStruct((layers, rows, cols), jnp.float32)
     edge = jax.ShapeDtypeStruct((layers, REACH, cols), jnp.float32)
     scalars = (jnp.transpose(shifts, (1, 2, 0)), strength_table, layer_entry)
-    own_pads = [(2, tiles, rows + 2 * REACH, LANES), (2, tiles, rows + 16, LANES)]
+    own_pads = [(2, tiles, rows + 2 * REACH, LANES)]
+    coeff_room = jax.ShapeDtypeStruct((2, tiles, rows + 16, LANES), jnp.float32)
     row_pads = [(2, 2, tiles, 2 * REACH, LANES)]
     side_pad = jax.ShapeDtypeStruct((2, 2, rows + 2 * REACH, LANES), jnp.float32)
 
@@ -621,13 +623,15 @@
     def own_first(field, coeff, *refs):
         own_kernel(grid_shape, field, coeff, None, *refs)
 
-    def own_second(field, coeff, across, shifts, table, entry, out, even, odd, *pads):
-        own_kernel(grid_shape, field, coeff, across, shifts, table, entry, out, even, odd, None, *pads)
+    def own_second(field, coeff_pad, across, shifts, table, entry, out, even, odd, pad):
+        own_kernel(
+            grid_shape, field, None, across, shifts, table, entry, out, even, odd, None, coeff_pad, pad
+        )
 
     rows0 = swap(*edge_rows(right_side, coefficient), "gy")
-    w_own, *columns, across = on_tensor_core(
+    w_own, *columns, across, coeff_pad = on_tensor_core(
         own_first, "own_first", (right_side, coefficient), scalars,
-        (full, side_of(rows + 8), side_of(rows + 8), full), own_pads, 6,
+        (full, side_of(rows + 8), side_of(rows + 8), full, coeff_room), own_pads, 6,
     )
     cols0 = swap(*columns, "gx")
     packed = pack_corners(*rows0)
@@ -643,7 +647,7 @@
     )
     rows1 = swap(even, odd, "gy")
     n_own, *columns = on_tensor_core(
-        own_second, "own_second", (w_vec, coefficient, across), scalars,
+        own_second, "own_second", (w_vec, coeff_pad, across), scalars,
         (full, side_of(rows), side_of(rows)), own_pads, 6,
     )
     cols1 = swap(*columns, "gx")

time: 73.3 us -> 73.4 us (level)
  starting transfers between devices: 20.4 us -> 23.1 us
  blocking collectives: 30.8 us -> 29 us
    ppermute x12, starting transfers between devices: 20.4 us -> 23.1 us  [the longest x6 20 us: swap(): lax.ppermute(odd, axis, pairs_from(1 - FIRST[axis], count))]
    all_to_all x1, blocking collectives: 30.8 us -> 29 us  [on_device(): gathered = lax.all_to_all(parts, ('gx', 'gy'), 0, 0, tiled=True)]
  transfers between devices with their start and end apart: 12 -> 12, of which waited for: 4 -> 3; matrix products, arithmetic and copies ran while one was open for 0% -> 0% of each run, Pallas kernels for 17% -> 16%
where the time goes in v9:
time: 73.4 us; the launch traced here: 73.1 us
  blocking collectives  29 us (40%)
  starting transfers between devices  23.1 us (31%)
  Pallas kernels  17.6 us (24%)
  waiting for transfers between devices  2.42 us (3%)
  between operations  1.04 us (1%)
    all_to_all x1, blocking collectives, on_device(): gathered = lax.all_to_all(parts, ('gx', 'gy'), 0, 0, tiled=True)  29 us
    ppermute x6, starting transfers between devices, swap(): lax.ppermute(odd, axis, pairs_from(1 - FIRST[axis], count))  20 us
    pallas_call x6, Pallas kernels, on_tensor_core(): pl.pallas_call(kernel, out_shape=out_shape, in_specs=[VMEM_SPEC] * len(op...  14.2 us
    ppermute x6, starting transfers between devices, swap(): lax.ppermute(even, axis, pairs_from(FIRST[axis], count))  3.14 us
    ppermute x6, waiting for transfers between devices, swap(): lax.ppermute(odd, axis, pairs_from(1 - FIRST[axis], count))  2.4 us
    pallas_call x1, Pallas kernels, on_device(): pl.pallas_call(last_kernel, out_shape=(full, full), in_specs=[VMEM_SPEC]...  1.88 us
  transfers between devices with their start and end apart: 12, of which 3 were waited for; matrix products, arithmetic and copies ran while one was open for 0% of the time, Pallas kernels for 16%

profile of v9, /device:TPU:1, one launch (start us, length us, event | category | flops | bytes accessed | tf_op | source)
XLA Modules:
  0.0 73.1 jit_solution(1889005897443492971)
XLA Ops:
  0.6 0.0 copy-start
  0.6 0.0 copy-start.1
  0.7 0.0 copy-start.4
  0.7 0.0 copy-start.3
  0.7 0.0 copy-start.2
  0.7 1.2 %edge_rows.1 = (f32[2,72,512]{2,1,0:T(8,128)S(1)}, f32[2,72,512]{2,1,0:T(8,128)S(1)}) custom-call(f32[2,256,512]{2,1,0:T(8,128)} %base.1, f32[2,256,512]{2,1,0:T(8,128)} %refs_4_.1), custom_call_target="tpu_custom_call" | custom-call | tf_op jit(solution)/shard_map/edge_rows/pallas_call | solution.py:120
  1.9 0.7 collective-permute-start
  2.6 4.6 %collective-permute-start.1 = (f32[2,72,512]{2,1,0:T(8,128)S(1)}, f32[2,72,512]{2,1,0:T(8,128)S(1)}, u32[]{:S(2)}, u32[]{:S(2)}) collective-permute-start(f32[2,72,512]{2,1,0:T(8,128)S(1)} %get-tuple-element.30), channel_id=1, source_target_pairs={{0,1},{2,3},{4,5},{6,7},{8,9},{10,11},{12,13},{14,15},{1,0},{3,2},... | collective-permute-start | bytes 884744 | tf_op jit(solution)/shard_map/ppermute | solution.py:40
  7.2 0.0 copy-done
  7.2 0.0 copy-done.1
  7.2 0.0 copy-done.4
  7.2 0.0 copy-done.3
  7.2 0.0 copy-done.2
  7.2 4.2 %own_first.1 = (f32[2,256,512]{2,1,0:T(8,128)S(1)}, f32[264,128]{1,0:T(8,128)S(1)}, f32[264,128]{1,0:T(8,128)S(1)}, f32[2,256,512]{2,1,0:T(8,128)S(1)}, f32[2,4,272,128]{3,2,1,0:T(8,128)S(1)}) custom-call(f32[2,256,512]{2,1,0:T(8,128)S(1)} %copy-done, f32[2,256,512]{2,1,0:T(8,128)S(1)} %copy-done.1, s32[2,2,6]{2,1,0:T(2,128)S(1)} %bitcast.7, ...), custom_call_target="tpu_custom_call" | custom-call | bytes 18000000 | tf_op jit(solution)/shard_map/own_first/pallas_call | solution.py:571
  11.4 1.3 %collective-permute-start.2 = (f32[264,128]{1,0:T(8,128)S(1)}, f32[264,128]{1,0:T(8,128)S(1)}, u32[]{:S(2)}, u32[]{:S(2)}) collective-permute-start(f32[264,128]{1,0:T(8,128)S(1)} %get-tuple-element.32), channel_id=1, source_target_pairs={{0,16},{32,48},{64,80},{96,112},{128,144},{160,176},{192,208},{224... | collective-permute-start | bytes 405512 | tf_op jit(solution)/shard_map/ppermute | solution.py:39
  12.7 3.4 %collective-permute-start.3 = (f32[264,128]{1,0:T(8,128)S(1)}, f32[264,128]{1,0:T(8,128)S(1)}, u32[]{:S(2)}, u32[]{:S(2)}) collective-permute-start(f32[264,128]{1,0:T(8,128)S(1)} %get-tuple-element.33), channel_id=1, source_target_pairs={{16,32},{48,64},{80,96},{112,128},{144,160},{176,192},{208,224},{3... | collective-permute-start | bytes 405512 | tf_op jit(solution)/shard_map/ppermute | solution.py:40
  16.2 0.0 collective-permute-done.even_rows.even.refs_4_
  16.2 0.0 collective-permute-done.1.odd_rows.odd.refs_5_
  16.2 0.1 pack_corners.2
  16.3 2.4 %collective-permute-start.5 = (f32[128,128]{1,0:T(8,128)S(1)}, f32[128,128]{1,0:T(8,128)S(1)}, u32[]{:S(2)}, u32[]{:S(2)}) collective-permute-start(f32[128,128]{1,0:T(8,128)S(1)} %get-tuple-element.36), channel_id=1, source_target_pairs={{16,32},{48,64},{80,96},{112,128},{144,160},{176,192},{208,224},{3... | collective-permute-start | bytes 196616 | tf_op jit(solution)/shard_map/ppermute | solution.py:40
  18.7 0.1 collective-permute-start.4
  18.8 0.0 collective-permute-done.2.even_cols.refs_4_.refs_8_.refs_5_
  18.8 0.2 collective-permute-done.3.odd_cols.refs_5_.refs_9_.refs_6_
  19.1 1.8 %rows_first.1 = (f32[2,256,512]{2,1,0:T(8,128)S(1)}, f32[3,8,128]{2,1,0:T(8,128)S(1)}, f32[2,2,384,128]{3,2,1,0:T(8,128)S(1)}) custom-call(f32[2,256,512]{2,1,0:T(8,128)S(1)} %get-tuple-element.28.before, f32[128,128]{1,0:T(8,128)S(1)} %get-tuple-element.31.packed, f32[2,256,512]{2,1,0:T(8,128)S(1)} %copy-done, ...), custom_call_target="tpu_custom_call", output_to_operand_aliasing={{0}: (0, {})} | custom-call | bytes 9000000 | tf_op jit(solution)/shard_map/rows_first/pallas_call | solution.py:571
  20.8 1.1 %collective-permute-done.5.refs_7_ = f32[128,128]{1,0:T(8,128)S(1)} collective-permute-done((f32[128,128]{1,0:T(8,128)S(1)}, f32[128,128]{1,0:T(8,128)S(1)}, u32[]{:S(2)}, u32[]{:S(2)}) %collective-permute-start.5) | collective-permute-done | bytes 65568 | tf_op jit(solution)/shard_map/ppermute | solution.py:40
  21.9 0.0 collective-permute-done.4.refs_6_
  21.9 1.2 %first_apply.1 = (f32[2,256,512]{2,1,0:T(8,128)S(1)}, f32[2,2,384,128]{3,2,1,0:T(8,128)S(1)}, f32[3,8,128]{2,1,0:T(8,128)S(1)}, f32[2,64,512]{2,1,0:T(8,128)S(1)}, f32[2,64,512]{2,1,0:T(8,128)S(1)}) custom-call(f32[2,256,512]{2,1,0:T(8,128)S(1)} %get-tuple-element.34.refs_0_, ...), custom_call_target="tpu_custom_call", output_to_operand_aliasing={{0}: (0, {}), {1}: (1, {})} | custom-call | bytes 9000000 | tf_op jit(solution)/shard_map/first_apply/pallas_call | solution.py:571
  23.1 0.7 collective-permute-start.6
  23.8 3.4 %collective-permute-start.7 = (f32[2,64,512]{2,1,0:T(8,128)S(1)}, f32[2,64,512]{2,1,0:T(8,128)S(1)}, u32[]{:S(2)}, u32[]{:S(2)}) collective-permute-start(f32[2,64,512]{2,1,0:T(8,128)S(1)} %get-tuple-element.43), channel_id=1, source_target_pairs={{0,1},{2,3},{4,5},{6,7},{8,9},{10,11},{12,13},{14,15},{1,0},{3,2},... | collective-permute-start | bytes 786440 | tf_op jit(solution)/shard_map/ppermute | solution.py:40
  27.2 3.8 %own_second.1 = (f32[2,256,512]{2,1,0:T(8,128)S(1)}, f32[256,128]{1,0:T(8,128)S(1)}, f32[256,128]{1,0:T(8,128)S(1)}) custom-call(f32[2,256,512]{2,1,0:T(8,128)S(1)} %get-tuple-element.38.field.refs_0_.refs_3_.w_vec, f32[2,4,272,128]{3,2,1,0:T(8,128)S(1)} %get-tuple-element.39.coeff_pad, f32[2,256,512]{2,1,0:T(8,128)S(1)} %get-tuple-element.40.across, ...), custom_call_target="tpu_custom_call" | custom-call | bytes 18000000 | tf_op jit(solution)/shard_map/own_second/pallas_call | solution.py:571
  31.0 0.1 collective-permute-start.8
  31.1 3.9 %collective-permute-start.9 = (f32[256,128]{1,0:T(8,128)S(1)}, f32[256,128]{1,0:T(8,128)S(1)}, u32[]{:S(2)}, u32[]{:S(2)}) collective-permute-start(f32[256,128]{1,0:T(8,128)S(1)} %get-tuple-element.46), channel_id=1, source_target_pairs={{16,32},{48,64},{80,96},{112,128},{144,160},{176,192},{208,224},{3... | collective-permute-start | bytes 393224 | tf_op jit(solution)/shard_map/ppermute | solution.py:40
  35.0 0.0 collective-permute-done.6.even_rows.refs_2_
  35.0 0.0 collective-permute-done.7.odd_rows.refs_3_
  35.1 0.1 pack_corners.3
  35.2 2.2 %collective-permute-start.11 = (f32[128,128]{1,0:T(8,128)S(1)}, f32[128,128]{1,0:T(8,128)S(1)}, u32[]{:S(2)}, u32[]{:S(2)}) collective-permute-start(f32[128,128]{1,0:T(8,128)S(1)} %get-tuple-element.50), channel_id=1, source_target_pairs={{16,32},{48,64},{80,96},{112,128},{144,160},{176,192},{208,224},{3... | collective-permute-start | bytes 196616 | tf_op jit(solution)/shard_map/ppermute | solution.py:40
  37.4 0.3 collective-permute-start.10
  37.7 0.0 collective-permute-done.8.refs_6_
  37.7 0.0 collective-permute-done.9.refs_7_
  37.7 2.0 %rows_second.1 = (f32[2,256,512]{2,1,0:T(8,128)S(1)}, f32[6,8,128]{2,1,0:T(8,128)S(1)}, f32[2,2,384,128]{3,2,1,0:T(8,128)S(1)}) custom-call(f32[2,256,512]{2,1,0:T(8,128)S(1)} %get-tuple-element.41.before, f32[128,128]{1,0:T(8,128)S(1)} %get-tuple-element.44.packed, ...), custom_call_target="tpu_custom_call", output_to_operand_aliasing={{0}: (0, {})} | custom-call | bytes 9000000 | tf_op jit(solution)/shard_map/rows_second/pallas_call | solution.py:571
  39.7 1.1 %collective-permute-done.11.refs_8_ = f32[128,128]{1,0:T(8,128)S(1)} collective-permute-done((f32[128,128]{1,0:T(8,128)S(1)}, f32[128,128]{1,0:T(8,128)S(1)}, u32[]{:S(2)}, u32[]{:S(2)}) %collective-permute-start.11) | collective-permute-done | bytes 65568 | tf_op jit(solution)/shard_map/ppermute | solution.py:40
  40.8 0.0 collective-permute-done.10.refs_7_
  40.8 1.3 %second_apply.1 = (f32[2,256,512]{2,1,0:T(8,128)S(1)}, f32[2,2,384,128]{3,2,1,0:T(8,128)S(1)}, f32[256,128]{1,0:T(8,128)S(1)}) custom-call(f32[2,256,512]{2,1,0:T(8,128)S(1)} %get-tuple-element.48.refs_0_, f32[2,2,384,128]{3,2,1,0:T(8,128)S(1)} %get-tuple-element.49.refs_1_, ...), custom_call_target="tpu_custom_call", output_to_operand_aliasing={{0}: (0, {}), {1}: (1, {})} | custom-call | bytes 9000000 | tf_op jit(solution)/shard_map/second_apply/pallas_call | solution.py:571
  42.1 29.0 %all_to_all.11 = f32[256,1,128]{2,1,0:T(1,128)S(1)} all-to-all(f32[256,1,128]{2,1,0:T(1,128)S(1)} %bitcast.6), channel_id=1, replica_groups=mesh['gx'=16,'gy'=16] {'gx','gy'}, dimensions={0} | all-to-all | bytes 262144 | tf_op jit(solution)/shard_map/all_to_all | solution.py:666
  71.1 1.9 %last_update.1 = (f32[2,256,512]{2,1,0:T(8,128)}, f32[2,256,512]{2,1,0:T(8,128)}) custom-call(f32[256,128]{1,0:T(8,128)S(1)} %bitcast.5, f32[2,256,512]{2,1,0:T(8,128)S(1)} %copy-done, f32[2,256,512]{2,1,0:T(8,128)S(1)} %get-tuple-element.38.field.refs_0_.refs_3_.w_vec, f32[2,256,512]{2,1,0:T(8,128)S(1)} %get-tuple-element.53.n_vec), custom_call_target="tpu_custom_call" | custom-call | tf_op jit(solution)/shard_map/last_update/pallas_call | solution.py:667
Async XLA Ops:
  0.6 6.5 %copy-start = (f32[2,256,512]{2,1,0:T(8,128)S(1)}, f32[2,256,512]{2,1,0:T(8,128)}, u32[]{:S(2)}) copy-start(f32[2,256,512]{2,1,0:T(8,128)} %base.1) | copy-start | bytes 3145732
  0.6 6.5 %copy-start.1 = (f32[2,256,512]{2,1,0:T(8,128)S(1)}, f32[2,256,512]{2,1,0:T(8,128)}, u32[]{:S(2)}) copy-start(f32[2,256,512]{2,1,0:T(8,128)} %refs_4_.1) | copy-start | bytes 3145732
  0.7 6.5 %copy-start.4 = (s32[2]{0:T(128)S(1)}, s32[2]{0:T(128)}, u32[]{:S(2)}) copy-start(s32[2]{0:T(128)} %refs_13_.3) | copy-start | bytes 28
  0.7 6.5 %copy-start.3 = (f32[35]{0:T(128)S(1)}, f32[35]{0:T(128)}, u32[]{:S(2)}) copy-start(f32[35]{0:T(128)} %refs_12_.1) | copy-start | bytes 424
  0.7 6.5 %copy-start.2 = (s32[6,2,2]{0,2,1:T(2,128)S(1)}, s32[6,2,2]{0,2,1:T(2,128)}, u32[]{:S(2)}) copy-start(s32[6,2,2]{0,2,1:T(2,128)} %param.9) | copy-start | bytes 292
  1.9 14.3 %collective-permute-start = (f32[2,72,512]{2,1,0:T(8,128)S(1)}, f32[2,72,512]{2,1,0:T(8,128)S(1)}, u32[]{:S(2)}, u32[]{:S(2)}) collective-permute-start(f32[2,72,512]{2,1,0:T(8,128)S(1)} %get-tuple-element.29), channel_id=1, source_target_pairs={{1,2},{3,4},{5,6},{7,8},{9,10},{11,12},{13,14},{2,1},{4,3},{6,5},{... | collective-permute-start | bytes 884744 | tf_op jit(solution)/shard_map/ppermute | solution.py:39
  2.6 13.6 %collective-permute-start.1 = (f32[2,72,512]{2,1,0:T(8,128)S(1)}, f32[2,72,512]{2,1,0:T(8,128)S(1)}, u32[]{:S(2)}, u32[]{:S(2)}) collective-permute-start(f32[2,72,512]{2,1,0:T(8,128)S(1)} %get-tuple-element.30), channel_id=1, source_target_pairs={{0,1},{2,3},{4,5},{6,7},{8,9},{10,11},{12,13},{14,15},{1,0},{3,2},... | collective-permute-start | bytes 884744 | tf_op jit(solution)/shard_map/ppermute | solution.py:40
  11.4 7.4 %collective-permute-start.2 = (f32[264,128]{1,0:T(8,128)S(1)}, f32[264,128]{1,0:T(8,128)S(1)}, u32[]{:S(2)}, u32[]{:S(2)}) collective-permute-start(f32[264,128]{1,0:T(8,128)S(1)} %get-tuple-element.32), channel_id=1, source_target_pairs={{0,16},{32,48},{64,80},{96,112},{128,144},{160,176},{192,208},{224... | collective-permute-start | bytes 405512 | tf_op jit(solution)/shard_map/ppermute | solution.py:39
  12.7 6.3 %collective-permute-start.3 = (f32[264,128]{1,0:T(8,128)S(1)}, f32[264,128]{1,0:T(8,128)S(1)}, u32[]{:S(2)}, u32[]{:S(2)}) collective-permute-start(f32[264,128]{1,0:T(8,128)S(1)} %get-tuple-element.33), channel_id=1, source_target_pairs={{16,32},{48,64},{80,96},{112,128},{144,160},{176,192},{208,224},{3... | collective-permute-start | bytes 405512 | tf_op jit(solution)/shard_map/ppermute | solution.py:40
  16.3 5.6 %collective-permute-start.5 = (f32[128,128]{1,0:T(8,128)S(1)}, f32[128,128]{1,0:T(8,128)S(1)}, u32[]{:S(2)}, u32[]{:S(2)}) collective-permute-start(f32[128,128]{1,0:T(8,128)S(1)} %get-tuple-element.36), channel_id=1, source_target_pairs={{16,32},{48,64},{80,96},{112,128},{144,160},{176,192},{208,224},{3... | collective-permute-start | bytes 196616 | tf_op jit(solution)/shard_map/ppermute | solution.py:40
  18.7 3.2 %collective-permute-start.4 = (f32[128,128]{1,0:T(8,128)S(1)}, f32[128,128]{1,0:T(8,128)S(1)}, u32[]{:S(2)}, u32[]{:S(2)}) collective-permute-start(f32[128,128]{1,0:T(8,128)S(1)} %get-tuple-element.31.packed), channel_id=1, source_target_pairs={{0,16},{32,48},{64,80},{96,112},{128,144},{160,176},{192,208},{224... | collective-permute-start | bytes 196616 | tf_op jit(solution)/shard_map/ppermute | solution.py:39
  23.1 11.9 %collective-permute-start.6 = (f32[2,64,512]{2,1,0:T(8,128)S(1)}, f32[2,64,512]{2,1,0:T(8,128)S(1)}, u32[]{:S(2)}, u32[]{:S(2)}) collective-permute-start(f32[2,64,512]{2,1,0:T(8,128)S(1)} %get-tuple-element.42), channel_id=1, source_target_pairs={{1,2},{3,4},{5,6},{7,8},{9,10},{11,12},{13,14},{2,1},{4,3},{6,5},{... | collective-permute-start | bytes 786440 | tf_op jit(solution)/shard_map/ppermute | solution.py:39
  23.8 11.3 %collective-permute-start.7 = (f32[2,64,512]{2,1,0:T(8,128)S(1)}, f32[2,64,512]{2,1,0:T(8,128)S(1)}, u32[]{:S(2)}, u32[]{:S(2)}) collective-permute-start(f32[2,64,512]{2,1,0:T(8,128)S(1)} %get-tuple-element.43), channel_id=1, source_target_pairs={{0,1},{2,3},{4,5},{6,7},{8,9},{10,11},{12,13},{14,15},{1,0},{3,2},... | collective-permute-start | bytes 786440 | tf_op jit(solution)/shard_map/ppermute | solution.py:40
  31.0 6.7 %collective-permute-start.8 = (f32[256,128]{1,0:T(8,128)S(1)}, f32[256,128]{1,0:T(8,128)S(1)}, u32[]{:S(2)}, u32[]{:S(2)}) collective-permute-start(f32[256,128]{1,0:T(8,128)S(1)} %get-tuple-element.45), channel_id=1, source_target_pairs={{0,16},{32,48},{64,80},{96,112},{128,144},{160,176},{192,208},{224... | collective-permute-start | bytes 393224 | tf_op jit(solution)/shard_map/ppermute | solution.py:39
  31.1 6.6 %collective-permute-start.9 = (f32[256,128]{1,0:T(8,128)S(1)}, f32[256,128]{1,0:T(8,128)S(1)}, u32[]{:S(2)}, u32[]{:S(2)}) collective-permute-start(f32[256,128]{1,0:T(8,128)S(1)} %get-tuple-element.46), channel_id=1, source_target_pairs={{16,32},{48,64},{80,96},{112,128},{144,160},{176,192},{208,224},{3... | collective-permute-start | bytes 393224 | tf_op jit(solution)/shard_map/ppermute | solution.py:40
  35.2 5.6 %collective-permute-start.11 = (f32[128,128]{1,0:T(8,128)S(1)}, f32[128,128]{1,0:T(8,128)S(1)}, u32[]{:S(2)}, u32[]{:S(2)}) collective-permute-start(f32[128,128]{1,0:T(8,128)S(1)} %get-tuple-element.50), channel_id=1, source_target_pairs={{16,32},{48,64},{80,96},{112,128},{144,160},{176,192},{208,224},{3... | collective-permute-start | bytes 196616 | tf_op jit(solution)/shard_map/ppermute | solution.py:40
  37.4 3.3 %collective-permute-start.10 = (f32[128,128]{1,0:T(8,128)S(1)}, f32[128,128]{1,0:T(8,128)S(1)}, u32[]{:S(2)}, u32[]{:S(2)}) collective-permute-start(f32[128,128]{1,0:T(8,128)S(1)} %get-tuple-element.44.packed), channel_id=1, source_target_pairs={{0,16},{32,48},{64,80},{96,112},{128,144},{160,176},{192,208},{224... | collective-permute-start | bytes 196616 | tf_op jit(solution)/shard_map/ppermute | solution.py:39

commit v10 on v9

--- a/solution.py
+++ b/solution.py
@@ -33,12 +33,16 @@
     return lax.rem(lax.axis_index(axis) + FIRST[axis], 2) == 1
 
 
+def swap_even(even, axis):
+    return lax.ppermute(even, axis, pairs_from(FIRST[axis], lax.axis_size(axis)))
+
+
+def swap_odd(odd, axis):
+    return lax.ppermute(odd, axis, pairs_from(1 - FIRST[axis], lax.axis_size(axis)))
+
+
 def swap(even, odd, axis):
-    count = lax.axis_size(axis)
-    return (
-        lax.ppermute(even, axis, pairs_from(FIRST[axis], count)),
-        lax.ppermute(odd, axis, pairs_from(1 - FIRST[axis], count)),
-    )
+    return swap_even(even, axis), swap_odd(odd, axis)
 
 
 def lane_of(shape):
@@ -65,8 +69,9 @@
     odd_ref[start : start + rows, :] = jnp.where(odd, high, low)
 
 
-def pack_corners_kernel(even_rows, odd_rows, even_out, odd_out):
+def pack_corners_kernel(even_rows, odd_rows, even_side, even_out, odd_out):
     cols = even_rows.shape[2]
+    even_out[2 * REACH :, :] = even_side[...]
     odd_y = is_odd("gy")
     for start, above in ((0, True), (REACH, False)):
 
@@ -78,20 +83,47 @@
         store_packed(even_out, odd_out, start, *packed_edges(halo, cols))
 
 
-def pack(kernel, operands, rows, name):
-    out = jax.ShapeDtypeStruct((rows, LANES), jnp.float32)
+def pack_corners(even_rows, odd_rows, even_side, *after):
+    def side_of(rows):
+        return jax.ShapeDtypeStruct((rows, LANES), jnp.float32)
+
+    def kernel(even_rows, odd_rows, even_side, *refs):
+        pack_corners_kernel(even_rows, odd_rows, even_side, *refs[len(after) :])
+
+    return pl.pallas_call(
+        kernel,
+        out_shape=(side_of(2 * REACH + even_side.shape[0]), side_of(2 * REACH)),
+        in_specs=[VMEM_SPEC] * (3 + len(after)),
+        out_specs=(VMEM_SPEC,) * 2,
+        compiler_params=pltpu.CompilerParams(vmem_limit_bytes=VMEM_BYTES),
+        name="pack_corners",
+    )(even_rows, odd_rows, even_side, *after)
+
+
+def pack_sides(field, coeff):
+    rows, cols = field.shape[1:]
+
+    def kernel(*refs):
+        field, *ends, even_out, odd_out = refs
+        low, high = packed_edges(lambda layer, edge: field[layer, :, edge], cols)
+        store_packed(even_out, odd_out, 0, low, high)
+        if ends:
+            store_packed(even_out, odd_out, rows, *packed_ends(ends[0]))
+
+    operands = [field] + ([] if coeff is None else [coeff])
+    out = jax.ShapeDtypeStruct((rows + (0 if coeff is None else 8), LANES), jnp.float32)
     return pl.pallas_call(
         kernel,
         out_shape=(out, out),
         in_specs=[VMEM_SPEC] * len(operands),
         out_specs=(VMEM_SPEC,) * 2,
         compiler_params=pltpu.CompilerParams(vmem_limit_bytes=VMEM_BYTES),
-        name=name,
+        name="pack_sides",
     )(*operands)
 
 
-def pack_corners(even_rows, odd_rows):
-    return pack(pack_corners_kernel, (even_rows, odd_rows), 2 * REACH, "pack_corners")
+def own_rows(side):
+    return side.at[pl.ds(2 * REACH, side.shape[0] - 2 * REACH), :]
 
 
 def edge_kernel(field, coeff, even_out, odd_out, sems):
@@ -256,18 +288,14 @@
 
 
 def own_kernel(
-    grid_shape, field, coeff, across, shifts, table, entry, out, even_side, odd_side, across_out,
-    coeff_pad, pad,
+    grid_shape, field, coeff, across, shifts, table, entry, out, across_out, coeff_pad, pad
 ):
     rows, cols = field.shape[1:]
     zero_rim(pad, REACH, rows)
     fill_own(pad, REACH, field)
-    low, high = packed_edges(lambda layer, edge: field[layer, :, edge], cols)
-    store_packed(even_side, odd_side, 0, low, high)
     if across is None:
         zero_rim(coeff_pad, 8, rows)
         fill_own(coeff_pad, 8, coeff)
-        store_packed(even_side, odd_side, rows, *packed_ends(coeff))
     for layer in range(2):
         weight = weight_of(table, entry, layer)
         for row in range(0, rows, OWN_CHUNK):
@@ -300,6 +328,7 @@
     grid_shape, field, coeff, even_rows, odd_rows, even_edge, odd_edge, even_cols, odd_cols, even_ends,
     odd_ends, base, sums, shifts, table, entry, out, products, side_pad, pad,
 ):
+    even_cols, even_ends = own_rows(even_cols), own_rows(even_ends)
     rows, cols = field.shape[1:]
     tiles = cols // LANES
     odd_y = is_odd("gy")
@@ -477,7 +506,10 @@
     chunks = [*range(depth), *range(rows // CHUNK - depth, rows // CHUNK)]
     carry = tuple(products[index] for index in range(products.shape[0]))
     base, fit, *others = rest
-    return finish(chunks, carry, grid_shape, base, fit, field, *others, pad)
+    coeff, even_ends, *others = others
+    return finish(
+        chunks, carry, grid_shape, base, fit, field, coeff, own_rows(even_ends), *others, pad
+    )
 
 
 def first_kernel(
@@ -620,24 +652,26 @@
         del before, packed
         rows_kernel(grid_shape, *refs)
 
-    def own_first(field, coeff, *refs):
+    def own_first(field, coeff, side, *refs):
+        del side
         own_kernel(grid_shape, field, coeff, None, *refs)
 
-    def own_second(field, coeff_pad, across, shifts, table, entry, out, even, odd, pad):
-        own_kernel(
-            grid_shape, field, None, across, shifts, table, entry, out, even, odd, None, coeff_pad, pad
-        )
+    def own_second(field, coeff_pad, across, side, shifts, table, entry, out, pad):
+        del side
+        own_kernel(grid_shape, field, None, across, shifts, table, entry, out, None, coeff_pad, pad)
 
     rows0 = swap(*edge_rows(right_side, coefficient), "gy")
-    w_own, *columns, across, coeff_pad = on_tensor_core(
-        own_first, "own_first", (right_side, coefficient), scalars,
-        (full, side_of(rows + 8), side_of(rows + 8), full, coeff_room), own_pads, 6,
-    )
-    cols0 = swap(*columns, "gx")
-    packed = pack_corners(*rows0)
-    corners0 = swap(*packed, "gx")
+    even_side, odd_side = pack_sides(right_side, coefficient)
+    odd_cols = swap_odd(odd_side, "gx")
+    w_own, across, coeff_pad = on_tensor_core(
+        own_first, "own_first", (right_side, coefficient, odd_side), scalars, (full, full, coeff_room),
+        own_pads, 6,
+    )
+    packed = pack_corners(*rows0, even_side, odd_cols, w_own)
+    cols0 = (swap_even(packed[0], "gx"), odd_cols)
+    corners0 = (cols0[0], swap_odd(packed[1], "gx"))
     w_rows, products, sides = on_tensor_core(
-        rows_first, "rows_first", (w_own, packed[0], right_side, coefficient, *rows0, *cols0), scalars,
+        rows_first, "rows_first", (w_own, packed[1], right_side, coefficient, *rows0, *cols0), scalars,
         (full, sums_of(3), side_pad), row_pads, 3, 1,
     )
     w_vec, _, sums, even, odd = on_tensor_core(
@@ -646,16 +680,17 @@
         (full, side_pad, sums_of(3), edge, edge), [], 3, 2,
     )
     rows1 = swap(even, odd, "gy")
-    n_own, *columns = on_tensor_core(
-        own_second, "own_second", (w_vec, coeff_pad, across), scalars,
-        (full, side_of(rows), side_of(rows)), own_pads, 6,
-    )
-    cols1 = swap(*columns, "gx")
-    packed = pack_corners(*rows1)
-    corners1 = swap(*packed, "gx")
+    even_side, odd_side = pack_sides(w_vec, None)
+    odd_cols = swap_odd(odd_side, "gx")
+    (n_own,) = on_tensor_core(
+        own_second, "own_second", (w_vec, coeff_pad, across, odd_side), scalars, (full,), own_pads, 6
+    )
+    packed = pack_corners(*rows1, even_side, odd_cols, n_own)
+    cols1 = (swap_even(packed[0], "gx"), odd_cols)
+    corners1 = (cols1[0], swap_odd(packed[1], "gx"))
     n_rows, products, sides = on_tensor_core(
         rows_second, "rows_second",
-        (n_own, packed[0], w_vec, coefficient, *rows1, *rows0, *cols1, *cols0, right_side, sums),
+        (n_own, packed[1], w_vec, coefficient, *rows1, *rows0, *cols1, *cols0, right_side, sums),
         scalars, (full, sums_of(6), side_pad), row_pads, 3, 1,
     )
     n_vec, _, parts = on_tensor_core(

time: 73.4 us -> 74.9 us (1.020)
  starting transfers between devices: 23.1 us -> 26.6 us
  waiting for transfers between devices: 2.42 us -> 0.16 us
    ppermute x12 -> x10, starting transfers between devices: 23.1 us -> 26.6 us  [the longest x6 24.9 us: swap_odd(): lax.ppermute(odd, axis, pairs_from(1 - FIRST[axis], lax.axis_size(axis)))]
    ppermute x12 -> x10, waiting for transfers between devices: 2.42 us -> 0.16 us  [the longest x6 0.15 us: swap_odd(): lax.ppermute(odd, axis, pairs_from(1 - FIRST[axis], lax.axis_size(axis)))]
  transfers between devices with their start and end apart: 12 -> 10, of which waited for: 3 -> 1; matrix products, arithmetic and copies ran while one was open for 0% -> 0% of each run, Pallas kernels for 16% -> 16%
where the time goes in v10:
time: 74.9 us; the launch traced here: 74.6 us
  blocking collectives  29.3 us (39%)
  starting transfers between devices  26.6 us (36%)
  Pallas kernels  17.5 us (23%)
  between operations  1.07 us (1%)
    all_to_all x1, blocking collectives, on_device(): gathered = lax.all_to_all(parts, ('gx', 'gy'), 0, 0, tiled=True)  29.3 us
    ppermute x6, starting transfers between devices, swap_odd(): lax.ppermute(odd, axis, pairs_from(1 - FIRST[axis], lax.axis_size(axis)))  24.9 us
    pallas_call x6, Pallas kernels, on_tensor_core(): pl.pallas_call(kernel, out_shape=out_shape, in_specs=[VMEM_SPEC] * len(op...  13.7 us
    pallas_call x1, Pallas kernels, on_device(): pl.pallas_call(last_kernel, out_shape=(full, full), in_specs=[VMEM_SPEC]...  1.88 us
    ppermute x4, starting transfers between devices, swap_even(): lax.ppermute(even, axis, pairs_from(FIRST[axis], lax.axis_size(axis)))  1.67 us
  transfers between devices with their start and end apart: 10, of which 1 were waited for; matrix products, arithmetic and copies ran while one was open for 0% of the time, Pallas kernels for 16%

profile of v10, /device:TPU:1, one launch (start us, length us, event | category | flops | bytes accessed | tf_op | source)
XLA Modules:
  0.0 74.6 jit_solution(5334403592250217983)
XLA Ops:
  0.6 0.0 copy-start
  0.6 0.0 copy-start.1
  0.6 1.2 %edge_rows.1 = (f32[2,72,512]{2,1,0:T(8,128)S(1)}, f32[2,72,512]{2,1,0:T(8,128)S(1)}) custom-call(f32[2,256,512]{2,1,0:T(8,128)} %base.1, f32[2,256,512]{2,1,0:T(8,128)} %refs_4_.1), custom_call_target="tpu_custom_call" | custom-call | tf_op jit(solution)/shard_map/edge_rows/pallas_call | solution.py:152
  1.9 0.0 copy-start.2
  1.9 0.0 copy-start.3
  1.9 0.0 copy-start.4
  1.9 0.8 %collective-permute-start = (f32[2,72,512]{2,1,0:T(8,128)S(1)}, f32[2,72,512]{2,1,0:T(8,128)S(1)}, u32[]{:S(2)}, u32[]{:S(2)}) collective-permute-start(f32[2,72,512]{2,1,0:T(8,128)S(1)} %get-tuple-element.29), channel_id=1, source_target_pairs={{1,2},{3,4},{5,6},{7,8},{9,10},{11,12},{13,14},{2,1},{4,3},{6,5},{... | collective-permute-start | bytes 884744 | tf_op jit(solution)/shard_map/ppermute | solution.py:37
  2.8 4.6 %collective-permute-start.1 = (f32[2,72,512]{2,1,0:T(8,128)S(1)}, f32[2,72,512]{2,1,0:T(8,128)S(1)}, u32[]{:S(2)}, u32[]{:S(2)}) collective-permute-start(f32[2,72,512]{2,1,0:T(8,128)S(1)} %get-tuple-element.30), channel_id=1, source_target_pairs={{0,1},{2,3},{4,5},{6,7},{8,9},{10,11},{12,13},{14,15},{1,0},{3,2},... | collective-permute-start | bytes 884744 | tf_op jit(solution)/shard_map/ppermute | solution.py:41
  7.3 0.0 copy-done
  7.3 0.0 copy-done.1
  7.3 0.3 pack_sides.2
  7.6 4.7 %collective-permute-start.2 = (f32[264,128]{1,0:T(8,128)S(1)}, f32[264,128]{1,0:T(8,128)S(1)}, u32[]{:S(2)}, u32[]{:S(2)}) collective-permute-start(f32[264,128]{1,0:T(8,128)S(1)} %get-tuple-element.27.side), channel_id=1, source_target_pairs={{16,32},{48,64},{80,96},{112,128},{144,160},{176,192},{208,224},{3... | collective-permute-start | bytes 405512 | tf_op jit(solution)/shard_map/ppermute | solution.py:41
  12.3 0.0 copy-done.2
  12.3 0.0 copy-done.3
  12.3 0.0 copy-done.4
  12.3 3.9 %own_first.1 = (f32[2,256,512]{2,1,0:T(8,128)S(1)}, f32[2,256,512]{2,1,0:T(8,128)S(1)}, f32[2,4,272,128]{3,2,1,0:T(8,128)S(1)}) custom-call(f32[2,256,512]{2,1,0:T(8,128)S(1)} %copy-done, f32[2,256,512]{2,1,0:T(8,128)S(1)} %copy-done.1, f32[264,128]{1,0:T(8,128)S(1)} %get-tuple-element.27.side, s32[2,2,6]{2,1,0:T(2,128)S(1)} %bitcast.7, f32[35]{0:T(128)S(1)} %copy-done.3, ...), custom_call_target="tpu_custom_call" | custom-call | bytes 18000000 | tf_op jit(solution)/shard_map/own_first/pallas_call | solution.py:603
  16.2 0.0 collective-permute-done.2.refs_0_.odd_cols.refs_5_.refs_9_.refs_6_
  16.2 0.0 collective-permute-done.even_rows.even.refs_4_
  16.2 0.0 collective-permute-done.1.odd_rows.odd.refs_5_
  16.2 0.1 pack_corners.2
  16.4 0.1 collective-permute-start.3
  16.5 3.9 %collective-permute-start.4 = (f32[128,128]{1,0:T(8,128)S(1)}, f32[128,128]{1,0:T(8,128)S(1)}, u32[]{:S(2)}, u32[]{:S(2)}) collective-permute-start(f32[128,128]{1,0:T(8,128)S(1)} %get-tuple-element.32.packed), channel_id=1, source_target_pairs={{16,32},{48,64},{80,96},{112,128},{144,160},{176,192},{208,224},{3... | collective-permute-start | bytes 196616 | tf_op jit(solution)/shard_map/ppermute | solution.py:41
  20.4 0.0 collective-permute-done.3.even_cols.refs_4_.refs_6_.refs_8_.refs_5_
  20.4 1.8 %rows_first.1 = (f32[2,256,512]{2,1,0:T(8,128)S(1)}, f32[3,8,128]{2,1,0:T(8,128)S(1)}, f32[2,2,384,128]{3,2,1,0:T(8,128)S(1)}) custom-call(f32[2,256,512]{2,1,0:T(8,128)S(1)} %get-tuple-element.28.refs_1_.before, f32[128,128]{1,0:T(8,128)S(1)} %get-tuple-element.32.packed, f32[2,256,512]{2,1,0:T(8,128)S(1)} %copy-done, ...), custom_call_target="tpu_custom_call", output_to_operand_aliasing={{0}: (0, {})} | custom-call | bytes 9000000 | tf_op jit(solution)/shard_map/rows_first/pallas_call | solution.py:603
  22.2 0.1 collective-permute-done.4.refs_7_
  22.3 1.2 %first_apply.1 = (f32[2,256,512]{2,1,0:T(8,128)S(1)}, f32[2,2,384,128]{3,2,1,0:T(8,128)S(1)}, f32[3,8,128]{2,1,0:T(8,128)S(1)}, f32[2,64,512]{2,1,0:T(8,128)S(1)}, f32[2,64,512]{2,1,0:T(8,128)S(1)}) custom-call(f32[2,256,512]{2,1,0:T(8,128)S(1)} %get-tuple-element.34.refs_0_, ...), custom_call_target="tpu_custom_call", output_to_operand_aliasing={{0}: (0, {}), {1}: (1, {})} | custom-call | bytes 9000000 | tf_op jit(solution)/shard_map/first_apply/pallas_call | solution.py:603
  23.5 0.7 collective-permute-start.5
  24.2 3.4 %collective-permute-start.6 = (f32[2,64,512]{2,1,0:T(8,128)S(1)}, f32[2,64,512]{2,1,0:T(8,128)S(1)}, u32[]{:S(2)}, u32[]{:S(2)}) collective-permute-start(f32[2,64,512]{2,1,0:T(8,128)S(1)} %get-tuple-element.42), channel_id=1, source_target_pairs={{0,1},{2,3},{4,5},{6,7},{8,9},{10,11},{12,13},{14,15},{1,0},{3,2},... | collective-permute-start | bytes 786440 | tf_op jit(solution)/shard_map/ppermute | solution.py:41
  27.6 0.1 pack_sides.3
  27.8 4.2 %collective-permute-start.7 = (f32[256,128]{1,0:T(8,128)S(1)}, f32[256,128]{1,0:T(8,128)S(1)}, u32[]{:S(2)}, u32[]{:S(2)}) collective-permute-start(f32[256,128]{1,0:T(8,128)S(1)} %get-tuple-element.40.side), channel_id=1, source_target_pairs={{16,32},{48,64},{80,96},{112,128},{144,160},{176,192},{208,224},{3... | collective-permute-start | bytes 393224 | tf_op jit(solution)/shard_map/ppermute | solution.py:41
  32.0 3.6 %own_second.1.refs_1_.before = f32[2,256,512]{2,1,0:T(8,128)S(1)} custom-call(f32[2,256,512]{2,1,0:T(8,128)S(1)} %get-tuple-element.37.refs_0_.field.refs_3_.w_vec, f32[2,4,272,128]{3,2,1,0:T(8,128)S(1)} %get-tuple-element.38.coeff_pad, f32[2,256,512]{2,1,0:T(8,128)S(1)} %get-tuple-element.39.across, f32[256,128]{1,0:T(8,128)S(1)} %get-tuple-element.40.side, ...), custom_call_target="tpu_custom_call" | custom-call | bytes 18000000 | tf_op jit(solution)/shard_map/own_second/pallas_call | solution.py:603
  35.5 0.0 collective-permute-done.7.refs_0_.refs_7_
  35.5 0.0 collective-permute-done.5.even_rows.refs_2_
  35.6 0.0 collective-permute-done.6.odd_rows.refs_3_
  35.6 0.1 pack_corners.3
  35.7 0.1 collective-permute-start.8
  35.8 4.1 %collective-permute-start.9 = (f32[128,128]{1,0:T(8,128)S(1)}, f32[128,128]{1,0:T(8,128)S(1)}, u32[]{:S(2)}, u32[]{:S(2)}) collective-permute-start(f32[128,128]{1,0:T(8,128)S(1)} %get-tuple-element.44.packed), channel_id=1, source_target_pairs={{16,32},{48,64},{80,96},{112,128},{144,160},{176,192},{208,224},{3... | collective-permute-start | bytes 196616 | tf_op jit(solution)/shard_map/ppermute | solution.py:41
  39.9 0.0 collective-permute-done.8.refs_6_.refs_7_
  39.9 2.0 %rows_second.1 = (f32[2,256,512]{2,1,0:T(8,128)S(1)}, f32[6,8,128]{2,1,0:T(8,128)S(1)}, f32[2,2,384,128]{3,2,1,0:T(8,128)S(1)}) custom-call(f32[2,256,512]{2,1,0:T(8,128)S(1)} %own_second.1.refs_1_.before, f32[128,128]{1,0:T(8,128)S(1)} %get-tuple-element.44.packed, ...), custom_call_target="tpu_custom_call", output_to_operand_aliasing={{0}: (0, {})} | custom-call | bytes 9000000 | tf_op jit(solution)/shard_map/rows_second/pallas_call | solution.py:603
  41.9 0.0 collective-permute-done.9.refs_8_
  41.9 1.3 %second_apply.1 = (f32[2,256,512]{2,1,0:T(8,128)S(1)}, f32[2,2,384,128]{3,2,1,0:T(8,128)S(1)}, f32[256,128]{1,0:T(8,128)S(1)}) custom-call(f32[2,256,512]{2,1,0:T(8,128)S(1)} %get-tuple-element.47.refs_0_, f32[2,2,384,128]{3,2,1,0:T(8,128)S(1)} %get-tuple-element.48.refs_1_, ...), custom_call_target="tpu_custom_call", output_to_operand_aliasing={{0}: (0, {}), {1}: (1, {})} | custom-call | bytes 9000000 | tf_op jit(solution)/shard_map/second_apply/pallas_call | solution.py:603
  43.3 29.3 %all_to_all.11 = f32[256,1,128]{2,1,0:T(1,128)S(1)} all-to-all(f32[256,1,128]{2,1,0:T(1,128)S(1)} %bitcast.6), channel_id=1, replica_groups=mesh['gx'=16,'gy'=16] {'gx','gy'}, dimensions={0} | all-to-all | bytes 262144 | tf_op jit(solution)/shard_map/all_to_all | solution.py:701
  72.6 1.9 %last_update.1 = (f32[2,256,512]{2,1,0:T(8,128)}, f32[2,256,512]{2,1,0:T(8,128)}) custom-call(f32[256,128]{1,0:T(8,128)S(1)} %bitcast.5, f32[2,256,512]{2,1,0:T(8,128)S(1)} %copy-done, f32[2,256,512]{2,1,0:T(8,128)S(1)} %get-tuple-element.37.refs_0_.field.refs_3_.w_vec, f32[2,256,512]{2,1,0:T(8,128)S(1)} %get-tuple-element.51.n_vec), custom_call_target="tpu_custom_call" | custom-call | tf_op jit(solution)/shard_map/last_update/pallas_call | solution.py:702
Async XLA Ops:
  0.6 6.7 %copy-start = (f32[2,256,512]{2,1,0:T(8,128)S(1)}, f32[2,256,512]{2,1,0:T(8,128)}, u32[]{:S(2)}) copy-start(f32[2,256,512]{2,1,0:T(8,128)} %base.1) | copy-start | bytes 3145732
  0.6 6.7 %copy-start.1 = (f32[2,256,512]{2,1,0:T(8,128)S(1)}, f32[2,256,512]{2,1,0:T(8,128)}, u32[]{:S(2)}) copy-start(f32[2,256,512]{2,1,0:T(8,128)} %refs_4_.1) | copy-start | bytes 3145732
  1.9 10.4 %copy-start.2 = (s32[6,2,2]{0,2,1:T(2,128)S(1)}, s32[6,2,2]{0,2,1:T(2,128)}, u32[]{:S(2)}) copy-start(s32[6,2,2]{0,2,1:T(2,128)} %param.9) | copy-start | bytes 292
  1.9 10.4 %copy-start.3 = (f32[35]{0:T(128)S(1)}, f32[35]{0:T(128)}, u32[]{:S(2)}) copy-start(f32[35]{0:T(128)} %refs_12_.1) | copy-start | bytes 424
  1.9 10.4 %copy-start.4 = (s32[2]{0:T(128)S(1)}, s32[2]{0:T(128)}, u32[]{:S(2)}) copy-start(s32[2]{0:T(128)} %refs_13_.3) | copy-start | bytes 28
  1.9 14.3 %collective-permute-start = (f32[2,72,512]{2,1,0:T(8,128)S(1)}, f32[2,72,512]{2,1,0:T(8,128)S(1)}, u32[]{:S(2)}, u32[]{:S(2)}) collective-permute-start(f32[2,72,512]{2,1,0:T(8,128)S(1)} %get-tuple-element.29), channel_id=1, source_target_pairs={{1,2},{3,4},{5,6},{7,8},{9,10},{11,12},{13,14},{2,1},{4,3},{6,5},{... | collective-permute-start | bytes 884744 | tf_op jit(solution)/shard_map/ppermute | solution.py:37
  2.8 13.5 %collective-permute-start.1 = (f32[2,72,512]{2,1,0:T(8,128)S(1)}, f32[2,72,512]{2,1,0:T(8,128)S(1)}, u32[]{:S(2)}, u32[]{:S(2)}) collective-permute-start(f32[2,72,512]{2,1,0:T(8,128)S(1)} %get-tuple-element.30), channel_id=1, source_target_pairs={{0,1},{2,3},{4,5},{6,7},{8,9},{10,11},{12,13},{14,15},{1,0},{3,2},... | collective-permute-start | bytes 884744 | tf_op jit(solution)/shard_map/ppermute | solution.py:41
  7.6 8.6 %collective-permute-start.2 = (f32[264,128]{1,0:T(8,128)S(1)}, f32[264,128]{1,0:T(8,128)S(1)}, u32[]{:S(2)}, u32[]{:S(2)}) collective-permute-start(f32[264,128]{1,0:T(8,128)S(1)} %get-tuple-element.27.side), channel_id=1, source_target_pairs={{16,32},{48,64},{80,96},{112,128},{144,160},{176,192},{208,224},{3... | collective-permute-start | bytes 405512 | tf_op jit(solution)/shard_map/ppermute | solution.py:41
  16.4 4.0 %collective-permute-start.3 = (f32[392,128]{1,0:T(8,128)S(1)}, f32[392,128]{1,0:T(8,128)S(1)}, u32[]{:S(2)}, u32[]{:S(2)}) collective-permute-start(f32[392,128]{1,0:T(8,128)S(1)} %get-tuple-element.33), channel_id=1, source_target_pairs={{0,16},{32,48},{64,80},{96,112},{128,144},{160,176},{192,208},{224... | collective-permute-start | bytes 602120 | tf_op jit(solution)/shard_map/ppermute | solution.py:37
  16.5 5.9 %collective-permute-start.4 = (f32[128,128]{1,0:T(8,128)S(1)}, f32[128,128]{1,0:T(8,128)S(1)}, u32[]{:S(2)}, u32[]{:S(2)}) collective-permute-start(f32[128,128]{1,0:T(8,128)S(1)} %get-tuple-element.32.packed), channel_id=1, source_target_pairs={{16,32},{48,64},{80,96},{112,128},{144,160},{176,192},{208,224},{3... | collective-permute-start | bytes 196616 | tf_op jit(solution)/shard_map/ppermute | solution.py:41
  23.5 12.1 %collective-permute-start.5 = (f32[2,64,512]{2,1,0:T(8,128)S(1)}, f32[2,64,512]{2,1,0:T(8,128)S(1)}, u32[]{:S(2)}, u32[]{:S(2)}) collective-permute-start(f32[2,64,512]{2,1,0:T(8,128)S(1)} %get-tuple-element.41), channel_id=1, source_target_pairs={{1,2},{3,4},{5,6},{7,8},{9,10},{11,12},{13,14},{2,1},{4,3},{6,5},{... | collective-permute-start | bytes 786440 | tf_op jit(solution)/shard_map/ppermute | solution.py:37
  24.2 11.4 %collective-permute-start.6 = (f32[2,64,512]{2,1,0:T(8,128)S(1)}, f32[2,64,512]{2,1,0:T(8,128)S(1)}, u32[]{:S(2)}, u32[]{:S(2)}) collective-permute-start(f32[2,64,512]{2,1,0:T(8,128)S(1)} %get-tuple-element.42), channel_id=1, source_target_pairs={{0,1},{2,3},{4,5},{6,7},{8,9},{10,11},{12,13},{14,15},{1,0},{3,2},... | collective-permute-start | bytes 786440 | tf_op jit(solution)/shard_map/ppermute | solution.py:41
  27.8 7.8 %collective-permute-start.7 = (f32[256,128]{1,0:T(8,128)S(1)}, f32[256,128]{1,0:T(8,128)S(1)}, u32[]{:S(2)}, u32[]{:S(2)}) collective-permute-start(f32[256,128]{1,0:T(8,128)S(1)} %get-tuple-element.40.side), channel_id=1, source_target_pairs={{16,32},{48,64},{80,96},{112,128},{144,160},{176,192},{208,224},{3... | collective-permute-start | bytes 393224 | tf_op jit(solution)/shard_map/ppermute | solution.py:41
  35.7 4.2 %collective-permute-start.8 = (f32[384,128]{1,0:T(8,128)S(1)}, f32[384,128]{1,0:T(8,128)S(1)}, u32[]{:S(2)}, u32[]{:S(2)}) collective-permute-start(f32[384,128]{1,0:T(8,128)S(1)} %get-tuple-element.45), channel_id=1, source_target_pairs={{0,16},{32,48},{64,80},{96,112},{128,144},{160,176},{192,208},{224... | collective-permute-start | bytes 589832 | tf_op jit(solution)/shard_map/ppermute | solution.py:37
  35.8 6.1 %collective-permute-start.9 = (f32[128,128]{1,0:T(8,128)S(1)}, f32[128,128]{1,0:T(8,128)S(1)}, u32[]{:S(2)}, u32[]{:S(2)}) collective-permute-start(f32[128,128]{1,0:T(8,128)S(1)} %get-tuple-element.44.packed), channel_id=1, source_target_pairs={{16,32},{48,64},{80,96},{112,128},{144,160},{176,192},{208,224},{3... | collective-permute-start | bytes 196616 | tf_op jit(solution)/shard_map/ppermute | solution.py:41

commit v11 on v9

--- a/solution.py
+++ b/solution.py
@@ -26,7 +26,7 @@
     return [(i, i + 1) for i in low] + [(i + 1, i) for i in low]
 
 
-FIRST = {"gy": 1, "gx": 0}
+FIRST = {"gy": 1, "gx": 1}
 
 
 def is_odd(axis):
@@ -239,24 +239,23 @@
 
 
 def packed_ends(coeff):
-    ends = []
     rows, cols = coeff.shape[1:]
     lane = lane_of((8, LANES))
-    for high, edge in enumerate((slice(0, LANES), slice(cols - LANES, cols))):
-        packed = jnp.zeros((8, LANES), jnp.float32)
-        for layer in range(2):
-            for group in range(rows // 8):
-                at = layer * (rows // 8) + group
-                turn = (at + high) % LANES
-                value = coeff[layer, 8 * group : 8 * group + 8, edge]
-                value = pltpu.roll(value, turn, 1) if turn else value
-                packed = jnp.where(lane == at, value, packed)
-        ends.append(packed)
-    return ends
+    low = high = jnp.zeros((8, LANES), jnp.float32)
+    for layer in range(2):
+        for group in range(rows // 8):
+            at = layer * (rows // 8) + group
+            part = slice(8 * group, 8 * group + 8)
+            first, last = coeff[layer, part, 0:LANES], coeff[layer, part, cols - LANES : cols]
+            value = jnp.where(lane == 0, first, last)
+            value = pltpu.roll(value, at, 1) if at else value
+            low = jnp.where(lane == at, value, low)
+            high = jnp.where(lane == (at - 1) % LANES, value, high)
+    return low, pltpu.roll(high, 1, 1)
 
 
 def own_kernel(
-    grid_shape, field, coeff, across, shifts, table, entry, out, even_side, odd_side, across_out,
+    grid_shape, field, coeff, across, shifts, table, entry, out, odd_side, even_side, across_out,
     coeff_pad, pad,
 ):
     rows, cols = field.shape[1:]
@@ -623,9 +622,9 @@
     def own_first(field, coeff, *refs):
         own_kernel(grid_shape, field, coeff, None, *refs)
 
-    def own_second(field, coeff_pad, across, shifts, table, entry, out, even, odd, pad):
+    def own_second(field, coeff_pad, across, shifts, table, entry, out, odd, even, pad):
         own_kernel(
-            grid_shape, field, None, across, shifts, table, entry, out, even, odd, None, coeff_pad, pad
+            grid_shape, field, None, across, shifts, table, entry, out, odd, even, None, coeff_pad, pad
         )
 
     rows0 = swap(*edge_rows(right_side, coefficient), "gy")
@@ -633,11 +632,11 @@
         own_first, "own_first", (right_side, coefficient), scalars,
         (full, side_of(rows + 8), side_of(rows + 8), full, coeff_room), own_pads, 6,
     )
-    cols0 = swap(*columns, "gx")
+    cols0 = swap(*columns[::-1], "gx")
     packed = pack_corners(*rows0)
     corners0 = swap(*packed, "gx")
     w_rows, products, sides = on_tensor_core(
-        rows_first, "rows_first", (w_own, packed[0], right_side, coefficient, *rows0, *cols0), scalars,
+        rows_first, "rows_first", (w_own, packed[1], right_side, coefficient, *rows0, *cols0), scalars,
         (full, sums_of(3), side_pad), row_pads, 3, 1,
     )
     w_vec, _, sums, even, odd = on_tensor_core(
@@ -650,12 +649,12 @@
         own_second, "own_second", (w_vec, coeff_pad, across), scalars,
         (full, side_of(rows), side_of(rows)), own_pads, 6,
     )
-    cols1 = swap(*columns, "gx")
+    cols1 = swap(*columns[::-1], "gx")
     packed = pack_corners(*rows1)
     corners1 = swap(*packed, "gx")
     n_rows, products, sides = on_tensor_core(
         rows_second, "rows_second",
-        (n_own, packed[0], w_vec, coefficient, *rows1, *rows0, *cols1, *cols0, right_side, sums),
+        (n_own, packed[1], w_vec, coefficient, *rows1, *rows0, *cols1, *cols0, right_side, sums),
         scalars, (full, sums_of(6), side_pad), row_pads, 3, 1,
     )
     n_vec, _, parts = on_tensor_core(

time: 73.4 us -> 73.2 us (level)
  starting transfers between devices: 23.1 us -> 28.1 us
  blocking collectives: 29 us -> 26 us
  waiting for transfers between devices: 2.42 us -> 0.06 us
    ppermute x6, starting transfers between devices: 3.14 us -> 19.5 us  [swap(): lax.ppermute(even, axis, pairs_from(FIRST[axis], count))]
    ppermute x6, starting transfers between devices: 20 us -> 8.57 us  [swap(): lax.ppermute(odd, axis, pairs_from(1 - FIRST[axis], count))]
    all_to_all x1, blocking collectives: 29 us -> 26 us  [on_device(): gathered = lax.all_to_all(parts, ('gx', 'gy'), 0, 0, tiled=True)]
    ppermute x6, waiting for transfers between devices: 2.4 us -> 0.02 us  [swap(): lax.ppermute(odd, axis, pairs_from(1 - FIRST[axis], count))]
  transfers between devices with their start and end apart: 12 -> 12, of which waited for: 3 -> 0; matrix products, arithmetic and copies ran while one was open for 0% -> 0% of each run, Pallas kernels for 16% -> 17%
where the time goes in v11:
time: 73.2 us; the launch traced here: 73 us
  starting transfers between devices  28.1 us (38%)
  blocking collectives  26 us (36%)
  Pallas kernels  17.7 us (24%)
  between operations  1.07 us (1%)
    all_to_all x1, blocking collectives, on_device(): gathered = lax.all_to_all(parts, ('gx', 'gy'), 0, 0, tiled=True)  26 us
    ppermute x6, starting transfers between devices, swap(): lax.ppermute(even, axis, pairs_from(FIRST[axis], count))  19.5 us
    pallas_call x6, Pallas kernels, on_tensor_core(): pl.pallas_call(kernel, out_shape=out_shape, in_specs=[VMEM_SPEC] * len(op...  14.4 us
    ppermute x6, starting transfers between devices, swap(): lax.ppermute(odd, axis, pairs_from(1 - FIRST[axis], count))  8.57 us
    pallas_call x1, Pallas kernels, on_device(): pl.pallas_call(last_kernel, out_shape=(full, full), in_specs=[VMEM_SPEC]...  1.88 us
  transfers between devices with their start and end apart: 12, of which 0 were waited for; matrix products, arithmetic and copies ran while one was open for 0% of the time, Pallas kernels for 17%

profile of v11, /device:TPU:1, one launch (start us, length us, event | category | flops | bytes accessed | tf_op | source)
XLA Modules:
  0.0 73.0 jit_solution(3918754734411817189)
XLA Ops:
  0.6 0.0 copy-start
  0.6 0.0 copy-start.1
  0.7 0.0 copy-start.4
  0.7 0.0 copy-start.3
  0.7 0.0 copy-start.2
  0.7 1.2 %edge_rows.1 = (f32[2,72,512]{2,1,0:T(8,128)S(1)}, f32[2,72,512]{2,1,0:T(8,128)S(1)}) custom-call(f32[2,256,512]{2,1,0:T(8,128)} %base.1, f32[2,256,512]{2,1,0:T(8,128)} %refs_4_.1), custom_call_target="tpu_custom_call" | custom-call | tf_op jit(solution)/shard_map/edge_rows/pallas_call | solution.py:120
  1.9 0.7 collective-permute-start
  2.6 4.6 %collective-permute-start.1 = (f32[2,72,512]{2,1,0:T(8,128)S(1)}, f32[2,72,512]{2,1,0:T(8,128)S(1)}, u32[]{:S(2)}, u32[]{:S(2)}) collective-permute-start(f32[2,72,512]{2,1,0:T(8,128)S(1)} %get-tuple-element.30), channel_id=1, source_target_pairs={{0,1},{2,3},{4,5},{6,7},{8,9},{10,11},{12,13},{14,15},{1,0},{3,2},... | collective-permute-start | bytes 884744 | tf_op jit(solution)/shard_map/ppermute | solution.py:40
  7.2 0.0 copy-done
  7.2 0.0 copy-done.1
  7.2 0.0 copy-done.4
  7.2 0.0 copy-done.3
  7.2 0.0 copy-done.2
  7.2 4.4 %own_first.1 = (f32[2,256,512]{2,1,0:T(8,128)S(1)}, f32[264,128]{1,0:T(8,128)S(1)}, f32[264,128]{1,0:T(8,128)S(1)}, f32[2,256,512]{2,1,0:T(8,128)S(1)}, f32[2,4,272,128]{3,2,1,0:T(8,128)S(1)}) custom-call(f32[2,256,512]{2,1,0:T(8,128)S(1)} %copy-done, f32[2,256,512]{2,1,0:T(8,128)S(1)} %copy-done.1, s32[2,2,6]{2,1,0:T(2,128)S(1)} %bitcast.7, ...), custom_call_target="tpu_custom_call" | custom-call | bytes 18000000 | tf_op jit(solution)/shard_map/own_first/pallas_call | solution.py:570
  11.6 4.7 %collective-permute-start.2 = (f32[264,128]{1,0:T(8,128)S(1)}, f32[264,128]{1,0:T(8,128)S(1)}, u32[]{:S(2)}, u32[]{:S(2)}) collective-permute-start(f32[264,128]{1,0:T(8,128)S(1)} %get-tuple-element.32), channel_id=1, source_target_pairs={{16,32},{48,64},{80,96},{112,128},{144,160},{176,192},{208,224},{3... | collective-permute-start | bytes 405512 | tf_op jit(solution)/shard_map/ppermute | solution.py:39
  16.3 0.1 collective-permute-start.3
  16.4 0.0 collective-permute-done.even_rows.even.refs_4_
  16.4 0.0 collective-permute-done.1.odd_rows.odd.refs_5_
  16.4 0.1 pack_corners.2
  16.5 3.9 %collective-permute-start.4 = (f32[128,128]{1,0:T(8,128)S(1)}, f32[128,128]{1,0:T(8,128)S(1)}, u32[]{:S(2)}, u32[]{:S(2)}) collective-permute-start(f32[128,128]{1,0:T(8,128)S(1)} %get-tuple-element.36), channel_id=1, source_target_pairs={{16,32},{48,64},{80,96},{112,128},{144,160},{176,192},{208,224},{3... | collective-permute-start | bytes 196616 | tf_op jit(solution)/shard_map/ppermute | solution.py:39
  20.4 0.1 collective-permute-start.5
  20.5 0.0 collective-permute-done.2.even_cols.refs_4_.refs_8_.refs_5_
  20.5 0.0 collective-permute-done.3.odd_cols.refs_5_.refs_9_.refs_6_
  20.6 1.8 %rows_first.1 = (f32[2,256,512]{2,1,0:T(8,128)S(1)}, f32[3,8,128]{2,1,0:T(8,128)S(1)}, f32[2,2,384,128]{3,2,1,0:T(8,128)S(1)}) custom-call(f32[2,256,512]{2,1,0:T(8,128)S(1)} %get-tuple-element.28.before, f32[128,128]{1,0:T(8,128)S(1)} %get-tuple-element.31.packed, f32[2,256,512]{2,1,0:T(8,128)S(1)} %copy-done, ...), custom_call_target="tpu_custom_call", output_to_operand_aliasing={{0}: (0, {})} | custom-call | bytes 9000000 | tf_op jit(solution)/shard_map/rows_first/pallas_call | solution.py:570
  22.3 0.0 collective-permute-done.4.refs_6_
  22.4 0.0 collective-permute-done.5.refs_7_
  22.4 1.2 %first_apply.1 = (f32[2,256,512]{2,1,0:T(8,128)S(1)}, f32[2,2,384,128]{3,2,1,0:T(8,128)S(1)}, f32[3,8,128]{2,1,0:T(8,128)S(1)}, f32[2,64,512]{2,1,0:T(8,128)S(1)}, f32[2,64,512]{2,1,0:T(8,128)S(1)}) custom-call(f32[2,256,512]{2,1,0:T(8,128)S(1)} %get-tuple-element.34.refs_0_, ...), custom_call_target="tpu_custom_call", output_to_operand_aliasing={{0}: (0, {}), {1}: (1, {})} | custom-call | bytes 9000000 | tf_op jit(solution)/shard_map/first_apply/pallas_call | solution.py:570
  23.5 0.7 collective-permute-start.6
  24.2 3.4 %collective-permute-start.7 = (f32[2,64,512]{2,1,0:T(8,128)S(1)}, f32[2,64,512]{2,1,0:T(8,128)S(1)}, u32[]{:S(2)}, u32[]{:S(2)}) collective-permute-start(f32[2,64,512]{2,1,0:T(8,128)S(1)} %get-tuple-element.43), channel_id=1, source_target_pairs={{0,1},{2,3},{4,5},{6,7},{8,9},{10,11},{12,13},{14,15},{1,0},{3,2},... | collective-permute-start | bytes 786440 | tf_op jit(solution)/shard_map/ppermute | solution.py:40
  27.7 3.7 %own_second.1 = (f32[2,256,512]{2,1,0:T(8,128)S(1)}, f32[256,128]{1,0:T(8,128)S(1)}, f32[256,128]{1,0:T(8,128)S(1)}) custom-call(f32[2,256,512]{2,1,0:T(8,128)S(1)} %get-tuple-element.38.field.refs_0_.refs_3_.w_vec, f32[2,4,272,128]{3,2,1,0:T(8,128)S(1)} %get-tuple-element.39.coeff_pad, f32[2,256,512]{2,1,0:T(8,128)S(1)} %get-tuple-element.40.across, ...), custom_call_target="tpu_custom_call" | custom-call | bytes 18000000 | tf_op jit(solution)/shard_map/own_second/pallas_call | solution.py:570
  31.4 4.5 %collective-permute-start.8 = (f32[256,128]{1,0:T(8,128)S(1)}, f32[256,128]{1,0:T(8,128)S(1)}, u32[]{:S(2)}, u32[]{:S(2)}) collective-permute-start(f32[256,128]{1,0:T(8,128)S(1)} %get-tuple-element.45), channel_id=1, source_target_pairs={{16,32},{48,64},{80,96},{112,128},{144,160},{176,192},{208,224},{3... | collective-permute-start | bytes 393224 | tf_op jit(solution)/shard_map/ppermute | solution.py:39
  35.9 0.1 collective-permute-start.9
  36.0 0.0 collective-permute-done.6.even_rows.refs_2_
  36.0 0.0 collective-permute-done.7.odd_rows.refs_3_
  36.0 0.1 pack_corners.3
  36.1 5.1 %collective-permute-start.10 = (f32[128,128]{1,0:T(8,128)S(1)}, f32[128,128]{1,0:T(8,128)S(1)}, u32[]{:S(2)}, u32[]{:S(2)}) collective-permute-start(f32[128,128]{1,0:T(8,128)S(1)} %get-tuple-element.50), channel_id=1, source_target_pairs={{16,32},{48,64},{80,96},{112,128},{144,160},{176,192},{208,224},{3... | collective-permute-start | bytes 196616 | tf_op jit(solution)/shard_map/ppermute | solution.py:39
  41.3 0.3 collective-permute-start.11
  41.5 0.0 collective-permute-done.8.refs_6_
  41.5 0.0 collective-permute-done.9.refs_7_
  41.6 2.0 %rows_second.1 = (f32[2,256,512]{2,1,0:T(8,128)S(1)}, f32[6,8,128]{2,1,0:T(8,128)S(1)}, f32[2,2,384,128]{3,2,1,0:T(8,128)S(1)}) custom-call(f32[2,256,512]{2,1,0:T(8,128)S(1)} %get-tuple-element.41.before, f32[128,128]{1,0:T(8,128)S(1)} %get-tuple-element.44.packed, ...), custom_call_target="tpu_custom_call", output_to_operand_aliasing={{0}: (0, {})} | custom-call | bytes 9000000 | tf_op jit(solution)/shard_map/rows_second/pallas_call | solution.py:570
  43.5 0.0 collective-permute-done.10.refs_7_
  43.6 0.0 collective-permute-done.11.refs_8_
  43.6 1.3 %second_apply.1 = (f32[2,256,512]{2,1,0:T(8,128)S(1)}, f32[2,2,384,128]{3,2,1,0:T(8,128)S(1)}, f32[256,128]{1,0:T(8,128)S(1)}) custom-call(f32[2,256,512]{2,1,0:T(8,128)S(1)} %get-tuple-element.48.refs_0_, f32[2,2,384,128]{3,2,1,0:T(8,128)S(1)} %get-tuple-element.49.refs_1_, ...), custom_call_target="tpu_custom_call", output_to_operand_aliasing={{0}: (0, {}), {1}: (1, {})} | custom-call | bytes 9000000 | tf_op jit(solution)/shard_map/second_apply/pallas_call | solution.py:570
  44.9 26.0 %all_to_all.11 = f32[256,1,128]{2,1,0:T(1,128)S(1)} all-to-all(f32[256,1,128]{2,1,0:T(1,128)S(1)} %bitcast.6), channel_id=1, replica_groups=mesh['gx'=16,'gy'=16] {'gx','gy'}, dimensions={0} | all-to-all | bytes 262144 | tf_op jit(solution)/shard_map/all_to_all | solution.py:665
  70.9 1.9 %last_update.1 = (f32[2,256,512]{2,1,0:T(8,128)}, f32[2,256,512]{2,1,0:T(8,128)}) custom-call(f32[256,128]{1,0:T(8,128)S(1)} %bitcast.5, f32[2,256,512]{2,1,0:T(8,128)S(1)} %copy-done, f32[2,256,512]{2,1,0:T(8,128)S(1)} %get-tuple-element.38.field.refs_0_.refs_3_.w_vec, f32[2,256,512]{2,1,0:T(8,128)S(1)} %get-tuple-element.53.n_vec), custom_call_target="tpu_custom_call" | custom-call | tf_op jit(solution)/shard_map/last_update/pallas_call | solution.py:666
Async XLA Ops:
  0.6 6.5 %copy-start = (f32[2,256,512]{2,1,0:T(8,128)S(1)}, f32[2,256,512]{2,1,0:T(8,128)}, u32[]{:S(2)}) copy-start(f32[2,256,512]{2,1,0:T(8,128)} %base.1) | copy-start | bytes 3145732
  0.6 6.5 %copy-start.1 = (f32[2,256,512]{2,1,0:T(8,128)S(1)}, f32[2,256,512]{2,1,0:T(8,128)}, u32[]{:S(2)}) copy-start(f32[2,256,512]{2,1,0:T(8,128)} %refs_4_.1) | copy-start | bytes 3145732
  0.7 6.5 %copy-start.4 = (s32[2]{0:T(128)S(1)}, s32[2]{0:T(128)}, u32[]{:S(2)}) copy-start(s32[2]{0:T(128)} %refs_13_.3) | copy-start | bytes 28
  0.7 6.5 %copy-start.3 = (f32[35]{0:T(128)S(1)}, f32[35]{0:T(128)}, u32[]{:S(2)}) copy-start(f32[35]{0:T(128)} %refs_12_.1) | copy-start | bytes 424
  0.7 6.5 %copy-start.2 = (s32[6,2,2]{0,2,1:T(2,128)S(1)}, s32[6,2,2]{0,2,1:T(2,128)}, u32[]{:S(2)}) copy-start(s32[6,2,2]{0,2,1:T(2,128)} %param.9) | copy-start | bytes 292
  1.9 14.4 %collective-permute-start = (f32[2,72,512]{2,1,0:T(8,128)S(1)}, f32[2,72,512]{2,1,0:T(8,128)S(1)}, u32[]{:S(2)}, u32[]{:S(2)}) collective-permute-start(f32[2,72,512]{2,1,0:T(8,128)S(1)} %get-tuple-element.29), channel_id=1, source_target_pairs={{1,2},{3,4},{5,6},{7,8},{9,10},{11,12},{13,14},{2,1},{4,3},{6,5},{... | collective-permute-start | bytes 884744 | tf_op jit(solution)/shard_map/ppermute | solution.py:39
  2.6 13.8 %collective-permute-start.1 = (f32[2,72,512]{2,1,0:T(8,128)S(1)}, f32[2,72,512]{2,1,0:T(8,128)S(1)}, u32[]{:S(2)}, u32[]{:S(2)}) collective-permute-start(f32[2,72,512]{2,1,0:T(8,128)S(1)} %get-tuple-element.30), channel_id=1, source_target_pairs={{0,1},{2,3},{4,5},{6,7},{8,9},{10,11},{12,13},{14,15},{1,0},{3,2},... | collective-permute-start | bytes 884744 | tf_op jit(solution)/shard_map/ppermute | solution.py:40
  11.6 8.9 %collective-permute-start.2 = (f32[264,128]{1,0:T(8,128)S(1)}, f32[264,128]{1,0:T(8,128)S(1)}, u32[]{:S(2)}, u32[]{:S(2)}) collective-permute-start(f32[264,128]{1,0:T(8,128)S(1)} %get-tuple-element.32), channel_id=1, source_target_pairs={{16,32},{48,64},{80,96},{112,128},{144,160},{176,192},{208,224},{3... | collective-permute-start | bytes 405512 | tf_op jit(solution)/shard_map/ppermute | solution.py:39
  16.3 4.3 %collective-permute-start.3 = (f32[264,128]{1,0:T(8,128)S(1)}, f32[264,128]{1,0:T(8,128)S(1)}, u32[]{:S(2)}, u32[]{:S(2)}) collective-permute-start(f32[264,128]{1,0:T(8,128)S(1)} %get-tuple-element.33), channel_id=1, source_target_pairs={{0,16},{32,48},{64,80},{96,112},{128,144},{160,176},{192,208},{224... | collective-permute-start | bytes 405512 | tf_op jit(solution)/shard_map/ppermute | solution.py:40
  16.5 5.9 %collective-permute-start.4 = (f32[128,128]{1,0:T(8,128)S(1)}, f32[128,128]{1,0:T(8,128)S(1)}, u32[]{:S(2)}, u32[]{:S(2)}) collective-permute-start(f32[128,128]{1,0:T(8,128)S(1)} %get-tuple-element.36), channel_id=1, source_target_pairs={{16,32},{48,64},{80,96},{112,128},{144,160},{176,192},{208,224},{3... | collective-permute-start | bytes 196616 | tf_op jit(solution)/shard_map/ppermute | solution.py:39
  20.4 1.9 %collective-permute-start.5 = (f32[128,128]{1,0:T(8,128)S(1)}, f32[128,128]{1,0:T(8,128)S(1)}, u32[]{:S(2)}, u32[]{:S(2)}) collective-permute-start(f32[128,128]{1,0:T(8,128)S(1)} %get-tuple-element.31.packed), channel_id=1, source_target_pairs={{0,16},{32,48},{64,80},{96,112},{128,144},{160,176},{192,208},{224... | collective-permute-start | bytes 196616 | tf_op jit(solution)/shard_map/ppermute | solution.py:40
  23.5 12.4 %collective-permute-start.6 = (f32[2,64,512]{2,1,0:T(8,128)S(1)}, f32[2,64,512]{2,1,0:T(8,128)S(1)}, u32[]{:S(2)}, u32[]{:S(2)}) collective-permute-start(f32[2,64,512]{2,1,0:T(8,128)S(1)} %get-tuple-element.42), channel_id=1, source_target_pairs={{1,2},{3,4},{5,6},{7,8},{9,10},{11,12},{13,14},{2,1},{4,3},{6,5},{... | collective-permute-start | bytes 786440 | tf_op jit(solution)/shard_map/ppermute | solution.py:39
  24.2 11.8 %collective-permute-start.7 = (f32[2,64,512]{2,1,0:T(8,128)S(1)}, f32[2,64,512]{2,1,0:T(8,128)S(1)}, u32[]{:S(2)}, u32[]{:S(2)}) collective-permute-start(f32[2,64,512]{2,1,0:T(8,128)S(1)} %get-tuple-element.43), channel_id=1, source_target_pairs={{0,1},{2,3},{4,5},{6,7},{8,9},{10,11},{12,13},{14,15},{1,0},{3,2},... | collective-permute-start | bytes 786440 | tf_op jit(solution)/shard_map/ppermute | solution.py:40
  31.4 10.1 %collective-permute-start.8 = (f32[256,128]{1,0:T(8,128)S(1)}, f32[256,128]{1,0:T(8,128)S(1)}, u32[]{:S(2)}, u32[]{:S(2)}) collective-permute-start(f32[256,128]{1,0:T(8,128)S(1)} %get-tuple-element.45), channel_id=1, source_target_pairs={{16,32},{48,64},{80,96},{112,128},{144,160},{176,192},{208,224},{3... | collective-permute-start | bytes 393224 | tf_op jit(solution)/shard_map/ppermute | solution.py:39
  35.9 5.7 %collective-permute-start.9 = (f32[256,128]{1,0:T(8,128)S(1)}, f32[256,128]{1,0:T(8,128)S(1)}, u32[]{:S(2)}, u32[]{:S(2)}) collective-permute-start(f32[256,128]{1,0:T(8,128)S(1)} %get-tuple-element.46), channel_id=1, source_target_pairs={{0,16},{32,48},{64,80},{96,112},{128,144},{160,176},{192,208},{224... | collective-permute-start | bytes 393224 | tf_op jit(solution)/shard_map/ppermute | solution.py:40
  36.1 7.4 %collective-permute-start.10 = (f32[128,128]{1,0:T(8,128)S(1)}, f32[128,128]{1,0:T(8,128)S(1)}, u32[]{:S(2)}, u32[]{:S(2)}) collective-permute-start(f32[128,128]{1,0:T(8,128)S(1)} %get-tuple-element.50), channel_id=1, source_target_pairs={{16,32},{48,64},{80,96},{112,128},{144,160},{176,192},{208,224},{3... | collective-permute-start | bytes 196616 | tf_op jit(solution)/shard_map/ppermute | solution.py:39
  41.3 2.3 %collective-permute-start.11 = (f32[128,128]{1,0:T(8,128)S(1)}, f32[128,128]{1,0:T(8,128)S(1)}, u32[]{:S(2)}, u32[]{:S(2)}) collective-permute-start(f32[128,128]{1,0:T(8,128)S(1)} %get-tuple-element.44.packed), channel_id=1, source_target_pairs={{0,16},{32,48},{64,80},{96,112},{128,144},{160,176},{192,208},{224... | collective-permute-start | bytes 196616 | tf_op jit(solution)/shard_map/ppermute | solution.py:40

commit v12 on v9

--- a/solution.py
+++ b/solution.py
@@ -14,7 +14,7 @@
 CHUNK = 32
 OWN_CHUNK = 64
 UNROLL = 8
-PIECES = 4
+PIECES = 8
 VMEM_BYTES = 32 * 1024 * 1024
 EDGE_BYTES = 53 * 1024 * 1024
 VMEM_SPEC = pl.BlockSpec(memory_space=pltpu.VMEM)

time: 73.4 us -> 73.5 us (level)
  no operation moved by 1% of the time
where the time goes in v12:
time: 73.5 us; the launch traced here: 73.2 us
  blocking collectives  29 us (39%)
  starting transfers between devices  23.2 us (32%)
  Pallas kernels  17.6 us (24%)
  waiting for transfers between devices  2.28 us (3%)
  between operations  1.04 us (1%)
    all_to_all x1, blocking collectives, on_device(): gathered = lax.all_to_all(parts, ('gx', 'gy'), 0, 0, tiled=True)  29 us
    ppermute x6, starting transfers between devices, swap(): lax.ppermute(odd, axis, pairs_from(1 - FIRST[axis], count))  20.1 us
    pallas_call x6, Pallas kernels, on_tensor_core(): pl.pallas_call(kernel, out_shape=out_shape, in_specs=[VMEM_SPEC] * len(op...  14.1 us
    ppermute x6, starting transfers between devices, swap(): lax.ppermute(even, axis, pairs_from(FIRST[axis], count))  3.14 us
    ppermute x6, waiting for transfers between devices, swap(): lax.ppermute(odd, axis, pairs_from(1 - FIRST[axis], count))  2.26 us
    pallas_call x1, Pallas kernels, on_device(): pl.pallas_call(last_kernel, out_shape=(full, full), in_specs=[VMEM_SPEC]...  2.01 us
  transfers between devices with their start and end apart: 12, of which 3 were waited for; matrix products, arithmetic and copies ran while one was open for 0% of the time, Pallas kernels for 16%

profile of v12, /device:TPU:1, one launch (start us, length us, event | category | flops | bytes accessed | tf_op | source)
XLA Modules:
  0.0 73.2 jit_solution(1092004004060348473)
XLA Ops:
  0.6 0.0 copy-start
  0.6 0.0 copy-start.1
  0.7 0.0 copy-start.4
  0.7 0.0 copy-start.3
  0.7 0.0 copy-start.2
  0.7 1.2 %edge_rows.1 = (f32[2,72,512]{2,1,0:T(8,128)S(1)}, f32[2,72,512]{2,1,0:T(8,128)S(1)}) custom-call(f32[2,256,512]{2,1,0:T(8,128)} %base.1, f32[2,256,512]{2,1,0:T(8,128)} %refs_4_.1), custom_call_target="tpu_custom_call" | custom-call | tf_op jit(solution)/shard_map/edge_rows/pallas_call | solution.py:120
  1.9 0.7 collective-permute-start
  2.6 4.6 %collective-permute-start.1 = (f32[2,72,512]{2,1,0:T(8,128)S(1)}, f32[2,72,512]{2,1,0:T(8,128)S(1)}, u32[]{:S(2)}, u32[]{:S(2)}) collective-permute-start(f32[2,72,512]{2,1,0:T(8,128)S(1)} %get-tuple-element.30), channel_id=1, source_target_pairs={{0,1},{2,3},{4,5},{6,7},{8,9},{10,11},{12,13},{14,15},{1,0},{3,2},... | collective-permute-start | bytes 884744 | tf_op jit(solution)/shard_map/ppermute | solution.py:40
  7.2 0.0 copy-done
  7.2 0.0 copy-done.1
  7.2 0.0 copy-done.4
  7.2 0.0 copy-done.3
  7.2 0.0 copy-done.2
  7.2 4.2 %own_first.1 = (f32[2,256,512]{2,1,0:T(8,128)S(1)}, f32[264,128]{1,0:T(8,128)S(1)}, f32[264,128]{1,0:T(8,128)S(1)}, f32[2,256,512]{2,1,0:T(8,128)S(1)}, f32[2,4,272,128]{3,2,1,0:T(8,128)S(1)}) custom-call(f32[2,256,512]{2,1,0:T(8,128)S(1)} %copy-done, f32[2,256,512]{2,1,0:T(8,128)S(1)} %copy-done.1, s32[2,2,6]{2,1,0:T(2,128)S(1)} %bitcast.7, ...), custom_call_target="tpu_custom_call" | custom-call | bytes 18000000 | tf_op jit(solution)/shard_map/own_first/pallas_call | solution.py:571
  11.4 1.3 %collective-permute-start.2 = (f32[264,128]{1,0:T(8,128)S(1)}, f32[264,128]{1,0:T(8,128)S(1)}, u32[]{:S(2)}, u32[]{:S(2)}) collective-permute-start(f32[264,128]{1,0:T(8,128)S(1)} %get-tuple-element.32), channel_id=1, source_target_pairs={{0,16},{32,48},{64,80},{96,112},{128,144},{160,176},{192,208},{224... | collective-permute-start | bytes 405512 | tf_op jit(solution)/shard_map/ppermute | solution.py:39
  12.7 3.4 %collective-permute-start.3 = (f32[264,128]{1,0:T(8,128)S(1)}, f32[264,128]{1,0:T(8,128)S(1)}, u32[]{:S(2)}, u32[]{:S(2)}) collective-permute-start(f32[264,128]{1,0:T(8,128)S(1)} %get-tuple-element.33), channel_id=1, source_target_pairs={{16,32},{48,64},{80,96},{112,128},{144,160},{176,192},{208,224},{3... | collective-permute-start | bytes 405512 | tf_op jit(solution)/shard_map/ppermute | solution.py:40
  16.1 0.0 collective-permute-done.even_rows.even.refs_4_
  16.2 0.0 collective-permute-done.1.odd_rows.odd.refs_5_
  16.2 0.1 pack_corners.2
  16.3 2.4 %collective-permute-start.5 = (f32[128,128]{1,0:T(8,128)S(1)}, f32[128,128]{1,0:T(8,128)S(1)}, u32[]{:S(2)}, u32[]{:S(2)}) collective-permute-start(f32[128,128]{1,0:T(8,128)S(1)} %get-tuple-element.36), channel_id=1, source_target_pairs={{16,32},{48,64},{80,96},{112,128},{144,160},{176,192},{208,224},{3... | collective-permute-start | bytes 196616 | tf_op jit(solution)/shard_map/ppermute | solution.py:40
  18.7 0.1 collective-permute-start.4
  18.8 0.0 collective-permute-done.2.even_cols.refs_4_.refs_8_.refs_5_
  18.8 0.2 collective-permute-done.3.odd_cols.refs_5_.refs_9_.refs_6_
  19.0 1.8 %rows_first.1 = (f32[2,256,512]{2,1,0:T(8,128)S(1)}, f32[3,8,128]{2,1,0:T(8,128)S(1)}, f32[2,2,384,128]{3,2,1,0:T(8,128)S(1)}) custom-call(f32[2,256,512]{2,1,0:T(8,128)S(1)} %get-tuple-element.28.before, f32[128,128]{1,0:T(8,128)S(1)} %get-tuple-element.31.packed, f32[2,256,512]{2,1,0:T(8,128)S(1)} %copy-done, ...), custom_call_target="tpu_custom_call", output_to_operand_aliasing={{0}: (0, {})} | custom-call | bytes 9000000 | tf_op jit(solution)/shard_map/rows_first/pallas_call | solution.py:571
  20.8 1.1 %collective-permute-done.5.refs_7_ = f32[128,128]{1,0:T(8,128)S(1)} collective-permute-done((f32[128,128]{1,0:T(8,128)S(1)}, f32[128,128]{1,0:T(8,128)S(1)}, u32[]{:S(2)}, u32[]{:S(2)}) %collective-permute-start.5) | collective-permute-done | bytes 65568 | tf_op jit(solution)/shard_map/ppermute | solution.py:40
  21.9 0.0 collective-permute-done.4.refs_6_
  21.9 1.2 %first_apply.1 = (f32[2,256,512]{2,1,0:T(8,128)S(1)}, f32[2,2,384,128]{3,2,1,0:T(8,128)S(1)}, f32[3,8,128]{2,1,0:T(8,128)S(1)}, f32[2,64,512]{2,1,0:T(8,128)S(1)}, f32[2,64,512]{2,1,0:T(8,128)S(1)}) custom-call(f32[2,256,512]{2,1,0:T(8,128)S(1)} %get-tuple-element.34.refs_0_, ...), custom_call_target="tpu_custom_call", output_to_operand_aliasing={{0}: (0, {}), {1}: (1, {})} | custom-call | bytes 9000000 | tf_op jit(solution)/shard_map/first_apply/pallas_call | solution.py:571
  23.1 0.7 collective-permute-start.6
  23.7 3.4 %collective-permute-start.7 = (f32[2,64,512]{2,1,0:T(8,128)S(1)}, f32[2,64,512]{2,1,0:T(8,128)S(1)}, u32[]{:S(2)}, u32[]{:S(2)}) collective-permute-start(f32[2,64,512]{2,1,0:T(8,128)S(1)} %get-tuple-element.43), channel_id=1, source_target_pairs={{0,1},{2,3},{4,5},{6,7},{8,9},{10,11},{12,13},{14,15},{1,0},{3,2},... | collective-permute-start | bytes 786440 | tf_op jit(solution)/shard_map/ppermute | solution.py:40
  27.2 3.7 %own_second.1 = (f32[2,256,512]{2,1,0:T(8,128)S(1)}, f32[256,128]{1,0:T(8,128)S(1)}, f32[256,128]{1,0:T(8,128)S(1)}) custom-call(f32[2,256,512]{2,1,0:T(8,128)S(1)} %get-tuple-element.38.field.refs_0_.refs_3_.w_vec, f32[2,4,272,128]{3,2,1,0:T(8,128)S(1)} %get-tuple-element.39.coeff_pad, f32[2,256,512]{2,1,0:T(8,128)S(1)} %get-tuple-element.40.across, ...), custom_call_target="tpu_custom_call" | custom-call | bytes 18000000 | tf_op jit(solution)/shard_map/own_second/pallas_call | solution.py:571
  30.9 0.1 collective-permute-start.8
  31.0 3.9 %collective-permute-start.9 = (f32[256,128]{1,0:T(8,128)S(1)}, f32[256,128]{1,0:T(8,128)S(1)}, u32[]{:S(2)}, u32[]{:S(2)}) collective-permute-start(f32[256,128]{1,0:T(8,128)S(1)} %get-tuple-element.46), channel_id=1, source_target_pairs={{16,32},{48,64},{80,96},{112,128},{144,160},{176,192},{208,224},{3... | collective-permute-start | bytes 393224 | tf_op jit(solution)/shard_map/ppermute | solution.py:40
  34.9 0.0 collective-permute-done.6.even_rows.refs_2_
  34.9 0.0 collective-permute-done.7.odd_rows.refs_3_
  34.9 0.1 pack_corners.3
  35.1 2.3 %collective-permute-start.11 = (f32[128,128]{1,0:T(8,128)S(1)}, f32[128,128]{1,0:T(8,128)S(1)}, u32[]{:S(2)}, u32[]{:S(2)}) collective-permute-start(f32[128,128]{1,0:T(8,128)S(1)} %get-tuple-element.50), channel_id=1, source_target_pairs={{16,32},{48,64},{80,96},{112,128},{144,160},{176,192},{208,224},{3... | collective-permute-start | bytes 196616 | tf_op jit(solution)/shard_map/ppermute | solution.py:40
  37.4 0.3 collective-permute-start.10
  37.7 0.0 collective-permute-done.8.refs_6_
  37.7 0.0 collective-permute-done.9.refs_7_
  37.7 2.0 %rows_second.1 = (f32[2,256,512]{2,1,0:T(8,128)S(1)}, f32[6,8,128]{2,1,0:T(8,128)S(1)}, f32[2,2,384,128]{3,2,1,0:T(8,128)S(1)}) custom-call(f32[2,256,512]{2,1,0:T(8,128)S(1)} %get-tuple-element.41.before, f32[128,128]{1,0:T(8,128)S(1)} %get-tuple-element.44.packed, ...), custom_call_target="tpu_custom_call", output_to_operand_aliasing={{0}: (0, {})} | custom-call | bytes 9000000 | tf_op jit(solution)/shard_map/rows_second/pallas_call | solution.py:571
  39.7 1.0 %collective-permute-done.11.refs_8_ = f32[128,128]{1,0:T(8,128)S(1)} collective-permute-done((f32[128,128]{1,0:T(8,128)S(1)}, f32[128,128]{1,0:T(8,128)S(1)}, u32[]{:S(2)}, u32[]{:S(2)}) %collective-permute-start.11) | collective-permute-done | bytes 65568 | tf_op jit(solution)/shard_map/ppermute | solution.py:40
  40.6 0.0 collective-permute-done.10.refs_7_
  40.6 1.3 %second_apply.1 = (f32[2,256,512]{2,1,0:T(8,128)S(1)}, f32[2,2,384,128]{3,2,1,0:T(8,128)S(1)}, f32[256,128]{1,0:T(8,128)S(1)}) custom-call(f32[2,256,512]{2,1,0:T(8,128)S(1)} %get-tuple-element.48.refs_0_, f32[2,2,384,128]{3,2,1,0:T(8,128)S(1)} %get-tuple-element.49.refs_1_, ...), custom_call_target="tpu_custom_call", output_to_operand_aliasing={{0}: (0, {}), {1}: (1, {})} | custom-call | bytes 9000000 | tf_op jit(solution)/shard_map/second_apply/pallas_call | solution.py:571
  42.0 29.0 %all_to_all.11 = f32[256,1,128]{2,1,0:T(1,128)S(1)} all-to-all(f32[256,1,128]{2,1,0:T(1,128)S(1)} %bitcast.6), channel_id=1, replica_groups=mesh['gx'=16,'gy'=16] {'gx','gy'}, dimensions={0} | all-to-all | bytes 262144 | tf_op jit(solution)/shard_map/all_to_all | solution.py:666
  71.0 2.0 %last_update.1 = (f32[2,256,512]{2,1,0:T(8,128)}, f32[2,256,512]{2,1,0:T(8,128)}) custom-call(f32[256,128]{1,0:T(8,128)S(1)} %bitcast.5, f32[2,256,512]{2,1,0:T(8,128)S(1)} %copy-done, f32[2,256,512]{2,1,0:T(8,128)S(1)} %get-tuple-element.38.field.refs_0_.refs_3_.w_vec, f32[2,256,512]{2,1,0:T(8,128)S(1)} %get-tuple-element.53.n_vec), custom_call_target="tpu_custom_call" | custom-call | tf_op jit(solution)/shard_map/last_update/pallas_call | solution.py:667
Async XLA Ops:
  0.6 6.5 %copy-start = (f32[2,256,512]{2,1,0:T(8,128)S(1)}, f32[2,256,512]{2,1,0:T(8,128)}, u32[]{:S(2)}) copy-start(f32[2,256,512]{2,1,0:T(8,128)} %base.1) | copy-start | bytes 3145732
  0.6 6.5 %copy-start.1 = (f32[2,256,512]{2,1,0:T(8,128)S(1)}, f32[2,256,512]{2,1,0:T(8,128)}, u32[]{:S(2)}) copy-start(f32[2,256,512]{2,1,0:T(8,128)} %refs_4_.1) | copy-start | bytes 3145732
  0.7 6.5 %copy-start.4 = (s32[2]{0:T(128)S(1)}, s32[2]{0:T(128)}, u32[]{:S(2)}) copy-start(s32[2]{0:T(128)} %refs_13_.3) | copy-start | bytes 28
  0.7 6.5 %copy-start.3 = (f32[35]{0:T(128)S(1)}, f32[35]{0:T(128)}, u32[]{:S(2)}) copy-start(f32[35]{0:T(128)} %refs_12_.1) | copy-start | bytes 424
  0.7 6.5 %copy-start.2 = (s32[6,2,2]{0,2,1:T(2,128)S(1)}, s32[6,2,2]{0,2,1:T(2,128)}, u32[]{:S(2)}) copy-start(s32[6,2,2]{0,2,1:T(2,128)} %param.9) | copy-start | bytes 292
  1.9 14.2 %collective-permute-start = (f32[2,72,512]{2,1,0:T(8,128)S(1)}, f32[2,72,512]{2,1,0:T(8,128)S(1)}, u32[]{:S(2)}, u32[]{:S(2)}) collective-permute-start(f32[2,72,512]{2,1,0:T(8,128)S(1)} %get-tuple-element.29), channel_id=1, source_target_pairs={{1,2},{3,4},{5,6},{7,8},{9,10},{11,12},{13,14},{2,1},{4,3},{6,5},{... | collective-permute-start | bytes 884744 | tf_op jit(solution)/shard_map/ppermute | solution.py:39
  2.6 13.6 %collective-permute-start.1 = (f32[2,72,512]{2,1,0:T(8,128)S(1)}, f32[2,72,512]{2,1,0:T(8,128)S(1)}, u32[]{:S(2)}, u32[]{:S(2)}) collective-permute-start(f32[2,72,512]{2,1,0:T(8,128)S(1)} %get-tuple-element.30), channel_id=1, source_target_pairs={{0,1},{2,3},{4,5},{6,7},{8,9},{10,11},{12,13},{14,15},{1,0},{3,2},... | collective-permute-start | bytes 884744 | tf_op jit(solution)/shard_map/ppermute | solution.py:40
  11.4 7.4 %collective-permute-start.2 = (f32[264,128]{1,0:T(8,128)S(1)}, f32[264,128]{1,0:T(8,128)S(1)}, u32[]{:S(2)}, u32[]{:S(2)}) collective-permute-start(f32[264,128]{1,0:T(8,128)S(1)} %get-tuple-element.32), channel_id=1, source_target_pairs={{0,16},{32,48},{64,80},{96,112},{128,144},{160,176},{192,208},{224... | collective-permute-start | bytes 405512 | tf_op jit(solution)/shard_map/ppermute | solution.py:39
  12.7 6.3 %collective-permute-start.3 = (f32[264,128]{1,0:T(8,128)S(1)}, f32[264,128]{1,0:T(8,128)S(1)}, u32[]{:S(2)}, u32[]{:S(2)}) collective-permute-start(f32[264,128]{1,0:T(8,128)S(1)} %get-tuple-element.33), channel_id=1, source_target_pairs={{16,32},{48,64},{80,96},{112,128},{144,160},{176,192},{208,224},{3... | collective-permute-start | bytes 405512 | tf_op jit(solution)/shard_map/ppermute | solution.py:40
  16.3 5.6 %collective-permute-start.5 = (f32[128,128]{1,0:T(8,128)S(1)}, f32[128,128]{1,0:T(8,128)S(1)}, u32[]{:S(2)}, u32[]{:S(2)}) collective-permute-start(f32[128,128]{1,0:T(8,128)S(1)} %get-tuple-element.36), channel_id=1, source_target_pairs={{16,32},{48,64},{80,96},{112,128},{144,160},{176,192},{208,224},{3... | collective-permute-start | bytes 196616 | tf_op jit(solution)/shard_map/ppermute | solution.py:40
  18.7 3.2 %collective-permute-start.4 = (f32[128,128]{1,0:T(8,128)S(1)}, f32[128,128]{1,0:T(8,128)S(1)}, u32[]{:S(2)}, u32[]{:S(2)}) collective-permute-start(f32[128,128]{1,0:T(8,128)S(1)} %get-tuple-element.31.packed), channel_id=1, source_target_pairs={{0,16},{32,48},{64,80},{96,112},{128,144},{160,176},{192,208},{224... | collective-permute-start | bytes 196616 | tf_op jit(solution)/shard_map/ppermute | solution.py:39
  23.1 11.9 %collective-permute-start.6 = (f32[2,64,512]{2,1,0:T(8,128)S(1)}, f32[2,64,512]{2,1,0:T(8,128)S(1)}, u32[]{:S(2)}, u32[]{:S(2)}) collective-permute-start(f32[2,64,512]{2,1,0:T(8,128)S(1)} %get-tuple-element.42), channel_id=1, source_target_pairs={{1,2},{3,4},{5,6},{7,8},{9,10},{11,12},{13,14},{2,1},{4,3},{6,5},{... | collective-permute-start | bytes 786440 | tf_op jit(solution)/shard_map/ppermute | solution.py:39
  23.7 11.2 %collective-permute-start.7 = (f32[2,64,512]{2,1,0:T(8,128)S(1)}, f32[2,64,512]{2,1,0:T(8,128)S(1)}, u32[]{:S(2)}, u32[]{:S(2)}) collective-permute-start(f32[2,64,512]{2,1,0:T(8,128)S(1)} %get-tuple-element.43), channel_id=1, source_target_pairs={{0,1},{2,3},{4,5},{6,7},{8,9},{10,11},{12,13},{14,15},{1,0},{3,2},... | collective-permute-start | bytes 786440 | tf_op jit(solution)/shard_map/ppermute | solution.py:40
  30.9 6.8 %collective-permute-start.8 = (f32[256,128]{1,0:T(8,128)S(1)}, f32[256,128]{1,0:T(8,128)S(1)}, u32[]{:S(2)}, u32[]{:S(2)}) collective-permute-start(f32[256,128]{1,0:T(8,128)S(1)} %get-tuple-element.45), channel_id=1, source_target_pairs={{0,16},{32,48},{64,80},{96,112},{128,144},{160,176},{192,208},{224... | collective-permute-start | bytes 393224 | tf_op jit(solution)/shard_map/ppermute | solution.py:39
  31.0 6.7 %collective-permute-start.9 = (f32[256,128]{1,0:T(8,128)S(1)}, f32[256,128]{1,0:T(8,128)S(1)}, u32[]{:S(2)}, u32[]{:S(2)}) collective-permute-start(f32[256,128]{1,0:T(8,128)S(1)} %get-tuple-element.46), channel_id=1, source_target_pairs={{16,32},{48,64},{80,96},{112,128},{144,160},{176,192},{208,224},{3... | collective-permute-start | bytes 393224 | tf_op jit(solution)/shard_map/ppermute | solution.py:40
  35.1 5.6 %collective-permute-start.11 = (f32[128,128]{1,0:T(8,128)S(1)}, f32[128,128]{1,0:T(8,128)S(1)}, u32[]{:S(2)}, u32[]{:S(2)}) collective-permute-start(f32[128,128]{1,0:T(8,128)S(1)} %get-tuple-element.50), channel_id=1, source_target_pairs={{16,32},{48,64},{80,96},{112,128},{144,160},{176,192},{208,224},{3... | collective-permute-start | bytes 196616 | tf_op jit(solution)/shard_map/ppermute | solution.py:40
  37.4 3.3 %collective-permute-start.10 = (f32[128,128]{1,0:T(8,128)S(1)}, f32[128,128]{1,0:T(8,128)S(1)}, u32[]{:S(2)}, u32[]{:S(2)}) collective-permute-start(f32[128,128]{1,0:T(8,128)S(1)} %get-tuple-element.44.packed), channel_id=1, source_target_pairs={{0,16},{32,48},{64,80},{96,112},{128,144},{160,176},{192,208},{224... | collective-permute-start | bytes 196616 | tf_op jit(solution)/shard_map/ppermute | solution.py:39

commit v13 on v12

--- a/solution.py
+++ b/solution.py
@@ -14,7 +14,7 @@
 CHUNK = 32
 OWN_CHUNK = 64
 UNROLL = 8
-PIECES = 8
+PIECES = 2
 VMEM_BYTES = 32 * 1024 * 1024
 EDGE_BYTES = 53 * 1024 * 1024
 VMEM_SPEC = pl.BlockSpec(memory_space=pltpu.VMEM)

time: 73.5 us -> 73.4 us (level)
  no operation moved by 1% of the time
where the time goes in v13:
time: 73.4 us; the launch traced here: 73.1 us
  blocking collectives  29 us (40%)
  starting transfers between devices  23.2 us (32%)
  Pallas kernels  17.5 us (24%)
  waiting for transfers between devices  2.34 us (3%)
  between operations  1.04 us (1%)
    all_to_all x1, blocking collectives, on_device(): gathered = lax.all_to_all(parts, ('gx', 'gy'), 0, 0, tiled=True)  29 us
    ppermute x6, starting transfers between devices, swap(): lax.ppermute(odd, axis, pairs_from(1 - FIRST[axis], count))  20 us
    pallas_call x6, Pallas kernels, on_tensor_core(): pl.pallas_call(kernel, out_shape=out_shape, in_specs=[VMEM_SPEC] * len(op...  14.1 us
    ppermute x6, starting transfers between devices, swap(): lax.ppermute(even, axis, pairs_from(FIRST[axis], count))  3.14 us
    ppermute x6, waiting for transfers between devices, swap(): lax.ppermute(odd, axis, pairs_from(1 - FIRST[axis], count))  2.32 us
    pallas_call x1, Pallas kernels, on_device(): pl.pallas_call(last_kernel, out_shape=(full, full), in_specs=[VMEM_SPEC]...  1.89 us
  transfers between devices with their start and end apart: 12, of which 3 were waited for; matrix products, arithmetic and copies ran while one was open for 0% of the time, Pallas kernels for 16%

profile of v13, /device:TPU:1, one launch (start us, length us, event | category | flops | bytes accessed | tf_op | source)
XLA Modules:
  0.0 73.1 jit_solution(85387294246311268)
XLA Ops:
  0.6 0.0 copy-start
  0.6 0.0 copy-start.1
  0.7 0.0 copy-start.4
  0.7 0.0 copy-start.3
  0.7 0.0 copy-start.2
  0.7 1.2 %edge_rows.1 = (f32[2,72,512]{2,1,0:T(8,128)S(1)}, f32[2,72,512]{2,1,0:T(8,128)S(1)}) custom-call(f32[2,256,512]{2,1,0:T(8,128)} %base.1, f32[2,256,512]{2,1,0:T(8,128)} %refs_4_.1), custom_call_target="tpu_custom_call" | custom-call | tf_op jit(solution)/shard_map/edge_rows/pallas_call | solution.py:120
  1.9 0.7 collective-permute-start
  2.6 4.6 %collective-permute-start.1 = (f32[2,72,512]{2,1,0:T(8,128)S(1)}, f32[2,72,512]{2,1,0:T(8,128)S(1)}, u32[]{:S(2)}, u32[]{:S(2)}) collective-permute-start(f32[2,72,512]{2,1,0:T(8,128)S(1)} %get-tuple-element.30), channel_id=1, source_target_pairs={{0,1},{2,3},{4,5},{6,7},{8,9},{10,11},{12,13},{14,15},{1,0},{3,2},... | collective-permute-start | bytes 884744 | tf_op jit(solution)/shard_map/ppermute | solution.py:40
  7.2 0.0 copy-done
  7.2 0.0 copy-done.1
  7.2 0.0 copy-done.4
  7.2 0.0 copy-done.3
  7.2 0.0 copy-done.2
  7.2 4.2 %own_first.1 = (f32[2,256,512]{2,1,0:T(8,128)S(1)}, f32[264,128]{1,0:T(8,128)S(1)}, f32[264,128]{1,0:T(8,128)S(1)}, f32[2,256,512]{2,1,0:T(8,128)S(1)}, f32[2,4,272,128]{3,2,1,0:T(8,128)S(1)}) custom-call(f32[2,256,512]{2,1,0:T(8,128)S(1)} %copy-done, f32[2,256,512]{2,1,0:T(8,128)S(1)} %copy-done.1, s32[2,2,6]{2,1,0:T(2,128)S(1)} %bitcast.7, ...), custom_call_target="tpu_custom_call" | custom-call | bytes 18000000 | tf_op jit(solution)/shard_map/own_first/pallas_call | solution.py:571
  11.4 1.3 %collective-permute-start.2 = (f32[264,128]{1,0:T(8,128)S(1)}, f32[264,128]{1,0:T(8,128)S(1)}, u32[]{:S(2)}, u32[]{:S(2)}) collective-permute-start(f32[264,128]{1,0:T(8,128)S(1)} %get-tuple-element.32), channel_id=1, source_target_pairs={{0,16},{32,48},{64,80},{96,112},{128,144},{160,176},{192,208},{224... | collective-permute-start | bytes 405512 | tf_op jit(solution)/shard_map/ppermute | solution.py:39
  12.7 3.4 %collective-permute-start.3 = (f32[264,128]{1,0:T(8,128)S(1)}, f32[264,128]{1,0:T(8,128)S(1)}, u32[]{:S(2)}, u32[]{:S(2)}) collective-permute-start(f32[264,128]{1,0:T(8,128)S(1)} %get-tuple-element.33), channel_id=1, source_target_pairs={{16,32},{48,64},{80,96},{112,128},{144,160},{176,192},{208,224},{3... | collective-permute-start | bytes 405512 | tf_op jit(solution)/shard_map/ppermute | solution.py:40
  16.2 0.0 collective-permute-done.even_rows.even.refs_4_
  16.2 0.0 collective-permute-done.1.odd_rows.odd.refs_5_
  16.2 0.1 pack_corners.2
  16.3 2.4 %collective-permute-start.5 = (f32[128,128]{1,0:T(8,128)S(1)}, f32[128,128]{1,0:T(8,128)S(1)}, u32[]{:S(2)}, u32[]{:S(2)}) collective-permute-start(f32[128,128]{1,0:T(8,128)S(1)} %get-tuple-element.36), channel_id=1, source_target_pairs={{16,32},{48,64},{80,96},{112,128},{144,160},{176,192},{208,224},{3... | collective-permute-start | bytes 196616 | tf_op jit(solution)/shard_map/ppermute | solution.py:40
  18.7 0.1 collective-permute-start.4
  18.8 0.0 collective-permute-done.2.even_cols.refs_4_.refs_8_.refs_5_
  18.8 0.2 collective-permute-done.3.odd_cols.refs_5_.refs_9_.refs_6_
  19.0 1.8 %rows_first.1 = (f32[2,256,512]{2,1,0:T(8,128)S(1)}, f32[3,8,128]{2,1,0:T(8,128)S(1)}, f32[2,2,384,128]{3,2,1,0:T(8,128)S(1)}) custom-call(f32[2,256,512]{2,1,0:T(8,128)S(1)} %get-tuple-element.28.before, f32[128,128]{1,0:T(8,128)S(1)} %get-tuple-element.31.packed, f32[2,256,512]{2,1,0:T(8,128)S(1)} %copy-done, ...), custom_call_target="tpu_custom_call", output_to_operand_aliasing={{0}: (0, {})} | custom-call | bytes 9000000 | tf_op jit(solution)/shard_map/rows_first/pallas_call | solution.py:571
  20.8 1.1 %collective-permute-done.5.refs_7_ = f32[128,128]{1,0:T(8,128)S(1)} collective-permute-done((f32[128,128]{1,0:T(8,128)S(1)}, f32[128,128]{1,0:T(8,128)S(1)}, u32[]{:S(2)}, u32[]{:S(2)}) %collective-permute-start.5) | collective-permute-done | bytes 65568 | tf_op jit(solution)/shard_map/ppermute | solution.py:40
  21.9 0.0 collective-permute-done.4.refs_6_
  21.9 1.2 %first_apply.1 = (f32[2,256,512]{2,1,0:T(8,128)S(1)}, f32[2,2,384,128]{3,2,1,0:T(8,128)S(1)}, f32[3,8,128]{2,1,0:T(8,128)S(1)}, f32[2,64,512]{2,1,0:T(8,128)S(1)}, f32[2,64,512]{2,1,0:T(8,128)S(1)}) custom-call(f32[2,256,512]{2,1,0:T(8,128)S(1)} %get-tuple-element.34.refs_0_, ...), custom_call_target="tpu_custom_call", output_to_operand_aliasing={{0}: (0, {}), {1}: (1, {})} | custom-call | bytes 9000000 | tf_op jit(solution)/shard_map/first_apply/pallas_call | solution.py:571
  23.1 0.7 collective-permute-start.6
  23.7 3.4 %collective-permute-start.7 = (f32[2,64,512]{2,1,0:T(8,128)S(1)}, f32[2,64,512]{2,1,0:T(8,128)S(1)}, u32[]{:S(2)}, u32[]{:S(2)}) collective-permute-start(f32[2,64,512]{2,1,0:T(8,128)S(1)} %get-tuple-element.43), channel_id=1, source_target_pairs={{0,1},{2,3},{4,5},{6,7},{8,9},{10,11},{12,13},{14,15},{1,0},{3,2},... | collective-permute-start | bytes 786440 | tf_op jit(solution)/shard_map/ppermute | solution.py:40
  27.2 3.7 %own_second.1 = (f32[2,256,512]{2,1,0:T(8,128)S(1)}, f32[256,128]{1,0:T(8,128)S(1)}, f32[256,128]{1,0:T(8,128)S(1)}) custom-call(f32[2,256,512]{2,1,0:T(8,128)S(1)} %get-tuple-element.38.field.refs_0_.refs_3_.w_vec, f32[2,4,272,128]{3,2,1,0:T(8,128)S(1)} %get-tuple-element.39.coeff_pad, f32[2,256,512]{2,1,0:T(8,128)S(1)} %get-tuple-element.40.across, ...), custom_call_target="tpu_custom_call" | custom-call | bytes 18000000 | tf_op jit(solution)/shard_map/own_second/pallas_call | solution.py:571
  30.9 0.1 collective-permute-start.8
  31.0 3.9 %collective-permute-start.9 = (f32[256,128]{1,0:T(8,128)S(1)}, f32[256,128]{1,0:T(8,128)S(1)}, u32[]{:S(2)}, u32[]{:S(2)}) collective-permute-start(f32[256,128]{1,0:T(8,128)S(1)} %get-tuple-element.46), channel_id=1, source_target_pairs={{16,32},{48,64},{80,96},{112,128},{144,160},{176,192},{208,224},{3... | collective-permute-start | bytes 393224 | tf_op jit(solution)/shard_map/ppermute | solution.py:40
  34.9 0.0 collective-permute-done.6.even_rows.refs_2_
  35.0 0.0 collective-permute-done.7.odd_rows.refs_3_
  35.0 0.1 pack_corners.3
  35.1 2.3 %collective-permute-start.11 = (f32[128,128]{1,0:T(8,128)S(1)}, f32[128,128]{1,0:T(8,128)S(1)}, u32[]{:S(2)}, u32[]{:S(2)}) collective-permute-start(f32[128,128]{1,0:T(8,128)S(1)} %get-tuple-element.50), channel_id=1, source_target_pairs={{16,32},{48,64},{80,96},{112,128},{144,160},{176,192},{208,224},{3... | collective-permute-start | bytes 196616 | tf_op jit(solution)/shard_map/ppermute | solution.py:40
  37.4 0.3 collective-permute-start.10
  37.7 0.0 collective-permute-done.8.refs_6_
  37.7 0.0 collective-permute-done.9.refs_7_
  37.7 2.0 %rows_second.1 = (f32[2,256,512]{2,1,0:T(8,128)S(1)}, f32[6,8,128]{2,1,0:T(8,128)S(1)}, f32[2,2,384,128]{3,2,1,0:T(8,128)S(1)}) custom-call(f32[2,256,512]{2,1,0:T(8,128)S(1)} %get-tuple-element.41.before, f32[128,128]{1,0:T(8,128)S(1)} %get-tuple-element.44.packed, ...), custom_call_target="tpu_custom_call", output_to_operand_aliasing={{0}: (0, {})} | custom-call | bytes 9000000 | tf_op jit(solution)/shard_map/rows_second/pallas_call | solution.py:571
  39.7 1.0 %collective-permute-done.11.refs_8_ = f32[128,128]{1,0:T(8,128)S(1)} collective-permute-done((f32[128,128]{1,0:T(8,128)S(1)}, f32[128,128]{1,0:T(8,128)S(1)}, u32[]{:S(2)}, u32[]{:S(2)}) %collective-permute-start.11) | collective-permute-done | bytes 65568 | tf_op jit(solution)/shard_map/ppermute | solution.py:40
  40.7 0.0 collective-permute-done.10.refs_7_
  40.7 1.3 %second_apply.1 = (f32[2,256,512]{2,1,0:T(8,128)S(1)}, f32[2,2,384,128]{3,2,1,0:T(8,128)S(1)}, f32[256,128]{1,0:T(8,128)S(1)}) custom-call(f32[2,256,512]{2,1,0:T(8,128)S(1)} %get-tuple-element.48.refs_0_, f32[2,2,384,128]{3,2,1,0:T(8,128)S(1)} %get-tuple-element.49.refs_1_, ...), custom_call_target="tpu_custom_call", output_to_operand_aliasing={{0}: (0, {}), {1}: (1, {})} | custom-call | bytes 9000000 | tf_op jit(solution)/shard_map/second_apply/pallas_call | solution.py:571
  42.0 29.0 %all_to_all.11 = f32[256,1,128]{2,1,0:T(1,128)S(1)} all-to-all(f32[256,1,128]{2,1,0:T(1,128)S(1)} %bitcast.6), channel_id=1, replica_groups=mesh['gx'=16,'gy'=16] {'gx','gy'}, dimensions={0} | all-to-all | bytes 262144 | tf_op jit(solution)/shard_map/all_to_all | solution.py:666
  71.0 1.9 %last_update.1 = (f32[2,256,512]{2,1,0:T(8,128)}, f32[2,256,512]{2,1,0:T(8,128)}) custom-call(f32[256,128]{1,0:T(8,128)S(1)} %bitcast.5, f32[2,256,512]{2,1,0:T(8,128)S(1)} %copy-done, f32[2,256,512]{2,1,0:T(8,128)S(1)} %get-tuple-element.38.field.refs_0_.refs_3_.w_vec, f32[2,256,512]{2,1,0:T(8,128)S(1)} %get-tuple-element.53.n_vec), custom_call_target="tpu_custom_call" | custom-call | tf_op jit(solution)/shard_map/last_update/pallas_call | solution.py:667
Async XLA Ops:
  0.6 6.5 %copy-start = (f32[2,256,512]{2,1,0:T(8,128)S(1)}, f32[2,256,512]{2,1,0:T(8,128)}, u32[]{:S(2)}) copy-start(f32[2,256,512]{2,1,0:T(8,128)} %base.1) | copy-start | bytes 3145732
  0.6 6.5 %copy-start.1 = (f32[2,256,512]{2,1,0:T(8,128)S(1)}, f32[2,256,512]{2,1,0:T(8,128)}, u32[]{:S(2)}) copy-start(f32[2,256,512]{2,1,0:T(8,128)} %refs_4_.1) | copy-start | bytes 3145732
  0.7 6.5 %copy-start.4 = (s32[2]{0:T(128)S(1)}, s32[2]{0:T(128)}, u32[]{:S(2)}) copy-start(s32[2]{0:T(128)} %refs_13_.3) | copy-start | bytes 28
  0.7 6.5 %copy-start.3 = (f32[35]{0:T(128)S(1)}, f32[35]{0:T(128)}, u32[]{:S(2)}) copy-start(f32[35]{0:T(128)} %refs_12_.1) | copy-start | bytes 424
  0.7 6.5 %copy-start.2 = (s32[6,2,2]{0,2,1:T(2,128)S(1)}, s32[6,2,2]{0,2,1:T(2,128)}, u32[]{:S(2)}) copy-start(s32[6,2,2]{0,2,1:T(2,128)} %param.9) | copy-start | bytes 292
  1.9 14.2 %collective-permute-start = (f32[2,72,512]{2,1,0:T(8,128)S(1)}, f32[2,72,512]{2,1,0:T(8,128)S(1)}, u32[]{:S(2)}, u32[]{:S(2)}) collective-permute-start(f32[2,72,512]{2,1,0:T(8,128)S(1)} %get-tuple-element.29), channel_id=1, source_target_pairs={{1,2},{3,4},{5,6},{7,8},{9,10},{11,12},{13,14},{2,1},{4,3},{6,5},{... | collective-permute-start | bytes 884744 | tf_op jit(solution)/shard_map/ppermute | solution.py:39
  2.6 13.6 %collective-permute-start.1 = (f32[2,72,512]{2,1,0:T(8,128)S(1)}, f32[2,72,512]{2,1,0:T(8,128)S(1)}, u32[]{:S(2)}, u32[]{:S(2)}) collective-permute-start(f32[2,72,512]{2,1,0:T(8,128)S(1)} %get-tuple-element.30), channel_id=1, source_target_pairs={{0,1},{2,3},{4,5},{6,7},{8,9},{10,11},{12,13},{14,15},{1,0},{3,2},... | collective-permute-start | bytes 884744 | tf_op jit(solution)/shard_map/ppermute | solution.py:40
  11.4 7.4 %collective-permute-start.2 = (f32[264,128]{1,0:T(8,128)S(1)}, f32[264,128]{1,0:T(8,128)S(1)}, u32[]{:S(2)}, u32[]{:S(2)}) collective-permute-start(f32[264,128]{1,0:T(8,128)S(1)} %get-tuple-element.32), channel_id=1, source_target_pairs={{0,16},{32,48},{64,80},{96,112},{128,144},{160,176},{192,208},{224... | collective-permute-start | bytes 405512 | tf_op jit(solution)/shard_map/ppermute | solution.py:39
  12.7 6.3 %collective-permute-start.3 = (f32[264,128]{1,0:T(8,128)S(1)}, f32[264,128]{1,0:T(8,128)S(1)}, u32[]{:S(2)}, u32[]{:S(2)}) collective-permute-start(f32[264,128]{1,0:T(8,128)S(1)} %get-tuple-element.33), channel_id=1, source_target_pairs={{16,32},{48,64},{80,96},{112,128},{144,160},{176,192},{208,224},{3... | collective-permute-start | bytes 405512 | tf_op jit(solution)/shard_map/ppermute | solution.py:40
  16.3 5.6 %collective-permute-start.5 = (f32[128,128]{1,0:T(8,128)S(1)}, f32[128,128]{1,0:T(8,128)S(1)}, u32[]{:S(2)}, u32[]{:S(2)}) collective-permute-start(f32[128,128]{1,0:T(8,128)S(1)} %get-tuple-element.36), channel_id=1, source_target_pairs={{16,32},{48,64},{80,96},{112,128},{144,160},{176,192},{208,224},{3... | collective-permute-start | bytes 196616 | tf_op jit(solution)/shard_map/ppermute | solution.py:40
  18.7 3.2 %collective-permute-start.4 = (f32[128,128]{1,0:T(8,128)S(1)}, f32[128,128]{1,0:T(8,128)S(1)}, u32[]{:S(2)}, u32[]{:S(2)}) collective-permute-start(f32[128,128]{1,0:T(8,128)S(1)} %get-tuple-element.31.packed), channel_id=1, source_target_pairs={{0,16},{32,48},{64,80},{96,112},{128,144},{160,176},{192,208},{224... | collective-permute-start | bytes 196616 | tf_op jit(solution)/shard_map/ppermute | solution.py:39
  23.1 11.9 %collective-permute-start.6 = (f32[2,64,512]{2,1,0:T(8,128)S(1)}, f32[2,64,512]{2,1,0:T(8,128)S(1)}, u32[]{:S(2)}, u32[]{:S(2)}) collective-permute-start(f32[2,64,512]{2,1,0:T(8,128)S(1)} %get-tuple-element.42), channel_id=1, source_target_pairs={{1,2},{3,4},{5,6},{7,8},{9,10},{11,12},{13,14},{2,1},{4,3},{6,5},{... | collective-permute-start | bytes 786440 | tf_op jit(solution)/shard_map/ppermute | solution.py:39
  23.7 11.2 %collective-permute-start.7 = (f32[2,64,512]{2,1,0:T(8,128)S(1)}, f32[2,64,512]{2,1,0:T(8,128)S(1)}, u32[]{:S(2)}, u32[]{:S(2)}) collective-permute-start(f32[2,64,512]{2,1,0:T(8,128)S(1)} %get-tuple-element.43), channel_id=1, source_target_pairs={{0,1},{2,3},{4,5},{6,7},{8,9},{10,11},{12,13},{14,15},{1,0},{3,2},... | collective-permute-start | bytes 786440 | tf_op jit(solution)/shard_map/ppermute | solution.py:40
  30.9 6.7 %collective-permute-start.8 = (f32[256,128]{1,0:T(8,128)S(1)}, f32[256,128]{1,0:T(8,128)S(1)}, u32[]{:S(2)}, u32[]{:S(2)}) collective-permute-start(f32[256,128]{1,0:T(8,128)S(1)} %get-tuple-element.45), channel_id=1, source_target_pairs={{0,16},{32,48},{64,80},{96,112},{128,144},{160,176},{192,208},{224... | collective-permute-start | bytes 393224 | tf_op jit(solution)/shard_map/ppermute | solution.py:39
  31.0 6.6 %collective-permute-start.9 = (f32[256,128]{1,0:T(8,128)S(1)}, f32[256,128]{1,0:T(8,128)S(1)}, u32[]{:S(2)}, u32[]{:S(2)}) collective-permute-start(f32[256,128]{1,0:T(8,128)S(1)} %get-tuple-element.46), channel_id=1, source_target_pairs={{16,32},{48,64},{80,96},{112,128},{144,160},{176,192},{208,224},{3... | collective-permute-start | bytes 393224 | tf_op jit(solution)/shard_map/ppermute | solution.py:40
  35.1 5.6 %collective-permute-start.11 = (f32[128,128]{1,0:T(8,128)S(1)}, f32[128,128]{1,0:T(8,128)S(1)}, u32[]{:S(2)}, u32[]{:S(2)}) collective-permute-start(f32[128,128]{1,0:T(8,128)S(1)} %get-tuple-element.50), channel_id=1, source_target_pairs={{16,32},{48,64},{80,96},{112,128},{144,160},{176,192},{208,224},{3... | collective-permute-start | bytes 196616 | tf_op jit(solution)/shard_map/ppermute | solution.py:40
  37.4 3.3 %collective-permute-start.10 = (f32[128,128]{1,0:T(8,128)S(1)}, f32[128,128]{1,0:T(8,128)S(1)}, u32[]{:S(2)}, u32[]{:S(2)}) collective-permute-start(f32[128,128]{1,0:T(8,128)S(1)} %get-tuple-element.44.packed), channel_id=1, source_target_pairs={{0,16},{32,48},{64,80},{96,112},{128,144},{160,176},{192,208},{224... | collective-permute-start | bytes 196616 | tf_op jit(solution)/shard_map/ppermute | solution.py:39
